TPU v7x, 32 devices: a whole 2x2x4 slice. The times are simulated.
32 devices in a mesh: dp: 4 (over z), expert: 8 (over y, x, core).
Axes of the slice: x: 2, y: 2, z: 4, core: 2. Of those that a mesh axis runs over, the one named last changes fastest.
Arguments:
- tokens: bfloat16 [16384, 1536], P(('dp', 'expert')), may hold values from -6 to 6
- cotangent: bfloat16 [16384, 1536], P(('dp', 'expert')), may hold values from -6 to 6
- routes: int32 [16384, 4], P(('dp', 'expert')), may hold values from 0 to 7, all different within a row; in each aligned block of 512 rows (0 to 511, 512 to 1023, ...) at most 384 rows name the same one
- doc_lengths: int32 [32, 3], P(('dp', 'expert')), may hold values from 1 to 384, 512 in all within a row
- query_weight: float32 [1536, 1536], P(('dp', 'expert')), may hold values from -0.15625 to 0.15625
- query_first: float32 [1536, 1536], P(('dp', 'expert')), may hold values from -160 to 160
- query_second: float32 [1536, 1536], P(('dp', 'expert')), may hold values from 65.536 to 262.144
- keyvalue_weight: float32 [1536, 512], P(('dp', 'expert')), may hold values from -0.15625 to 0.15625
- keyvalue_first: float32 [1536, 512], P(('dp', 'expert')), may hold values from -160 to 160
- keyvalue_second: float32 [1536, 512], P(('dp', 'expert')), may hold values from 65.536 to 262.144
- output_weight: float32 [1536, 1536], P(('dp', 'expert')), may hold values from -0.875 to 0.875
- output_first: float32 [1536, 1536], P(('dp', 'expert')), may hold values from -16 to 16
- output_second: float32 [1536, 1536], P(('dp', 'expert')), may hold values from 0.65536 to 2.62144
- router_weight: float32 [1536, 8], P(('dp', 'expert')), may hold values from -0.078125 to 0.078125
- router_first: float32 [1536, 8], P(('dp', 'expert')), may hold values from -896 to 896
- router_second: float32 [1536, 8], P(('dp', 'expert')), may hold values from 1843.2 to 7372.8
- norm_gains: float32 [2, 1536], P(None, ('dp', 'expert')), may hold values from 0.5 to 1.5
- gains_first: float32 [2, 1536], P(None, ('dp', 'expert')), may hold values from -160 to 160
- gains_second: float32 [2, 1536], P(None, ('dp', 'expert')), may hold values from 65.536 to 262.144
- expert_in: float32 [8, 1536, 1536], P('expert', 'dp'), may hold values from -0.15625 to 0.15625
- expert_in_first: float32 [8, 1536, 1536], P('expert', 'dp'), may hold values from -32 to 32
- expert_in_second: float32 [8, 1536, 1536], P('expert', 'dp'), may hold values from 2.048 to 8.192
- expert_out: float32 [8, 768, 1536], P('expert', 'dp'), may hold values from -0.625 to 0.625
- expert_out_first: float32 [8, 768, 1536], P('expert', 'dp'), may hold values from -8 to 8
- expert_out_second: float32 [8, 768, 1536], P('expert', 'dp'), may hold values from 0.18432 to 0.73728
Outputs:
- mixed: bfloat16 [16384, 1536], P(('dp', 'expert'))
- tokens_grad: float32 [16384, 1536], P(('dp', 'expert'))
- query_first_new: float32 [1536, 1536], P(('dp', 'expert'))
- query_second_new: float32 [1536, 1536], P(('dp', 'expert'))
- query_new: float32 [1536, 1536], P(('dp', 'expert'))
- keyvalue_first_new: float32 [1536, 512], P(('dp', 'expert'))
- keyvalue_second_new: float32 [1536, 512], P(('dp', 'expert'))
- keyvalue_new: float32 [1536, 512], P(('dp', 'expert'))
- output_first_new: float32 [1536, 1536], P(('dp', 'expert'))
- output_second_new: float32 [1536, 1536], P(('dp', 'expert'))
- output_new: float32 [1536, 1536], P(('dp', 'expert'))
- router_first_new: float32 [1536, 8], P(('dp', 'expert'))
- router_second_new: float32 [1536, 8], P(('dp', 'expert'))
- router_new: float32 [1536, 8], P(('dp', 'expert'))
- gains_first_new: float32 [2, 1536], P(None, ('dp', 'expert'))
- gains_second_new: float32 [2, 1536], P(None, ('dp', 'expert'))
- gains_new: float32 [2, 1536], P(None, ('dp', 'expert'))
- expert_in_first_new: float32 [8, 1536, 1536], P('expert', 'dp')
- expert_in_second_new: float32 [8, 1536, 1536], P('expert', 'dp')
- expert_in_new: float32 [8, 1536, 1536], P('expert', 'dp')
- expert_out_first_new: float32 [8, 768, 1536], P('expert', 'dp')
- expert_out_second_new: float32 [8, 768, 1536], P('expert', 'dp')
- expert_out_new: float32 [8, 768, 1536], P('expert', 'dp')
Inputs may be any that keep to these rules, and one draw needn't show every extreme that they name: `routes`: each row names 4 different experts. Among the rows of one device no expert is named more than 384 times, and some device's rows name some expert exactly 384 times. `doc_lengths`: each device's 3 lengths sum to 512, and the longest is exactly 384.
All inputs are finite; a program needn't handle non-finite values.
Results may differ from a plain program's by a relative error of at most 0.018.
Values may be sent and summed in bfloat16 or wider, within the bound.
No kernel may reach another device: no remote copies, remote signals or barrier semaphores. Data moves between devices by JAX's collectives and lax.ppermute only.
A program may use at most 256 MiB of HBM per device.

v0:
```python
import jax
import jax.numpy as jnp
from jax import lax
from jax.sharding import PartitionSpec as P

D = 1536
FF = 768
HEADS = 12
KV_HEADS = 2
HEAD_DIM = 128
TOP = 4
STEP = 10


EPS = 1e-06
NEG = -1e30
BETA_ONE = 0.9
BETA_TWO = 0.999
ADAM_EPS = 1e-08
DECAY = 0.1
ROPE_BASE = 10000.0
RATE_SCALE = 2.5
GAIN_RATE = 0.6


def doc_tables(lengths, rows_count):
    position = jnp.arange(rows_count, dtype=jnp.int32)
    doc_ends = jnp.cumsum(lengths)
    doc_starts = doc_ends - lengths
    doc_index = jnp.sum((position[:, None] >= doc_ends[None, :]).astype(jnp.int32), 1)
    doc_hot = doc_index[:, None] == jnp.arange(lengths.shape[0], dtype=jnp.int32)[None, :]
    start_of = jnp.sum(jnp.where(doc_hot, doc_starts[None, :], 0), 1)
    offset = (position - start_of).astype(jnp.float32)
    frequency = ROPE_BASE ** (-2.0 * jnp.arange(HEAD_DIM // 2, dtype=jnp.float32) / HEAD_DIM)
    angles = offset[:, None] * frequency[None, :]
    allowed = (doc_index[:, None] == doc_index[None, :]) & (position[None, :] <= position[:, None])
    return (jnp.cos(angles), jnp.sin(angles), allowed)


def rotate(values, cos_table, sin_table):
    half_width = values.shape[-1] // 2
    first_half = values[..., :half_width]
    second_half = values[..., half_width:]
    cosine = cos_table[:, None, :]
    sine_part = sin_table[:, None, :]
    return jnp.concatenate(
        [
            first_half * cosine - second_half * sine_part,
            second_half * cosine + first_half * sine_part,
        ],
        -1,
    )


def rotate_back(grads, cos_table, sin_table):
    half_width = grads.shape[-1] // 2
    first_half = grads[..., :half_width]
    second_half = grads[..., half_width:]
    cosine = cos_table[:, None, :]
    sine_part = sin_table[:, None, :]
    return jnp.concatenate(
        [
            first_half * cosine + second_half * sine_part,
            second_half * cosine - first_half * sine_part,
        ],
        -1,
    )


def gelu_tanh(values):
    return jax.nn.gelu(values, approximate=True)


def learning_rates():
    return (
        RATE_SCALE * D ** (-0.5),
        RATE_SCALE * D ** (-0.5),
        RATE_SCALE * (D // 32) ** (-0.5),
        RATE_SCALE * (4 * D) ** (-0.5),
        GAIN_RATE,
        RATE_SCALE * D ** (-0.5),
        RATE_SCALE * (FF // 8) ** (-0.5),
    )


def adam_update(weight, first, second, grad, rate, decay):
    new_first = BETA_ONE * first + (1.0 - BETA_ONE) * grad
    new_second = BETA_TWO * second + (1.0 - BETA_TWO) * grad * grad
    first_hat = new_first / (1.0 - BETA_ONE**STEP)
    second_hat = new_second / (1.0 - BETA_TWO**STEP)
    new_weight = weight - rate * (first_hat / (jnp.sqrt(second_hat) + ADAM_EPS) + decay * weight)
    return (new_first, new_second, new_weight)


def shards(
    tokens,
    cotangent,
    routes,
    doc_lengths,
    query_weight,
    query_first,
    query_second,
    keyvalue_weight,
    keyvalue_first,
    keyvalue_second,
    output_weight,
    output_first,
    output_second,
    router_weight,
    router_first,
    router_second,
    norm_gains,
    gains_first,
    gains_second,
    expert_in,
    expert_in_first,
    expert_in_second,
    expert_out,
    expert_out_first,
    expert_out_second,
):
    rows_count = tokens.shape[0]
    experts = router_weight.shape[1]
    owners = lax.axis_size("expert")
    per_owner = expert_in.shape[0]
    capacity = 3 * rows_count * TOP // (2 * experts)
    groups = HEADS // KV_HEADS
    width_kv = KV_HEADS * HEAD_DIM
    score_scale = HEAD_DIM ** (-0.5)
    query_full, keyvalue_full, output_full, router_full, gains_full = (
        lax.all_gather(query_weight.astype(jnp.bfloat16), ("dp", "expert"), axis=0, tiled=True),
        lax.all_gather(keyvalue_weight.astype(jnp.bfloat16), ("dp", "expert"), axis=0, tiled=True),
        lax.all_gather(output_weight.astype(jnp.bfloat16), ("dp", "expert"), axis=0, tiled=True),
        lax.all_gather(router_weight.astype(jnp.bfloat16), ("dp", "expert"), axis=0, tiled=True),
        lax.all_gather(norm_gains.astype(jnp.bfloat16), ("dp", "expert"), axis=1, tiled=True),
    )
    in_full, out_full = (
        lax.all_gather(expert_in.astype(jnp.bfloat16), "dp", axis=1, tiled=True),
        lax.all_gather(expert_out.astype(jnp.bfloat16), "dp", axis=1, tiled=True),
    )
    gain_attn = gains_full[0].astype(jnp.float32)
    gain_moe = gains_full[1].astype(jnp.float32)
    cos_table, sin_table, allowed = doc_tables(doc_lengths[0], rows_count)
    inputs = tokens.astype(jnp.float32)
    inv_one = lax.rsqrt(jnp.mean(inputs * inputs, -1, keepdims=True) + EPS)
    normed_one = inputs * inv_one
    attn_in = (normed_one * gain_attn).astype(jnp.bfloat16)
    query_raw = jnp.dot(attn_in, query_full, preferred_element_type=jnp.float32)
    keyvalue_raw = jnp.dot(attn_in, keyvalue_full, preferred_element_type=jnp.float32)
    queries = (
        rotate(query_raw.reshape(rows_count, HEADS, HEAD_DIM), cos_table, sin_table)
        .astype(jnp.bfloat16)
        .reshape(rows_count, KV_HEADS, groups, HEAD_DIM)
    )
    keys_rot = rotate(
        keyvalue_raw[:, :width_kv].reshape(rows_count, KV_HEADS, HEAD_DIM), cos_table, sin_table
    ).astype(jnp.bfloat16)
    values_in = (
        keyvalue_raw[:, width_kv:].reshape(rows_count, KV_HEADS, HEAD_DIM).astype(jnp.bfloat16)
    )

    def score_table():
        raw_scores = (
            jnp.einsum("tkgd,skd->kgts", queries, keys_rot, preferred_element_type=jnp.float32)
            * score_scale
        )
        return jnp.where(allowed[None, None], raw_scores, NEG)

    scores = score_table()
    row_max = jnp.max(scores, -1, keepdims=True)
    exponent = jnp.exp(scores - row_max)
    totals = jnp.sum(exponent, -1, keepdims=True)
    probabilities = exponent / totals
    log_sum = row_max + jnp.log(totals)
    attended = jnp.einsum(
        "kgts,skd->tkgd",
        probabilities.astype(jnp.bfloat16),
        values_in,
        preferred_element_type=jnp.float32,
    )
    attended = attended.reshape(rows_count, HEADS * HEAD_DIM).astype(jnp.bfloat16)
    residual_mid = inputs + jnp.dot(attended, output_full, preferred_element_type=jnp.float32)
    inv_two = lax.rsqrt(jnp.mean(residual_mid * residual_mid, -1, keepdims=True) + EPS)
    normed_two = residual_mid * inv_two
    moe_in = (normed_two * gain_moe).astype(jnp.bfloat16)
    logits = jnp.dot(tokens, router_full, preferred_element_type=jnp.float32)
    expert_ids = jnp.arange(experts, dtype=jnp.int32)
    route_hot = routes[:, :, None] == expert_ids[None, None, :]
    picked = jnp.sum(jnp.where(route_hot, logits[:, None, :], 0.0), -1)
    gate_weights = jax.nn.softmax(picked, axis=-1)
    flat_routes = routes.reshape(-1)
    flat_hot = (flat_routes[:, None] == expert_ids[None, :]).astype(jnp.int32)
    slot_index = jnp.sum((jnp.cumsum(flat_hot, 0) - 1) * flat_hot, 1)
    destination = flat_routes * capacity + slot_index
    route_ids = jnp.arange(rows_count * TOP, dtype=jnp.int32)
    source_route = jnp.zeros((experts * capacity,), jnp.int32).at[destination].set(route_ids)
    slot_used = jnp.zeros((experts * capacity,), jnp.bool_).at[destination].set(True)
    source_token = source_route // TOP
    zero_row = jnp.zeros((), jnp.bfloat16)
    send_rows = jnp.where(slot_used[:, None], moe_in[source_token], zero_row).reshape(
        owners, per_owner, capacity, D
    )
    received = lax.all_to_all(send_rows, "expert", split_axis=0, concat_axis=0, tiled=True)
    hidden_pre = jnp.einsum("sicd,idf->sicf", received, in_full, preferred_element_type=jnp.float32)
    gate_part = hidden_pre[..., :FF]
    up_part = hidden_pre[..., FF:]
    activated, gelu_pull = jax.vjp(gelu_tanh, gate_part)
    product = (activated * up_part).astype(jnp.bfloat16)
    expert_rows = jnp.einsum(
        "sicf,ifd->sicd", product, out_full, preferred_element_type=jnp.float32
    ).astype(jnp.bfloat16)
    returned = lax.all_to_all(
        expert_rows, "expert", split_axis=0, concat_axis=0, tiled=True
    ).reshape(experts * capacity, D)
    routed = returned[destination].reshape(rows_count, TOP, D)
    block_out = residual_mid + jnp.sum(gate_weights[:, :, None] * routed, 1)
    mixed_out = block_out.astype(jnp.bfloat16)
    upstream = cotangent.astype(jnp.float32)
    gate_grad = jnp.einsum("tjd,td->tj", routed, cotangent, preferred_element_type=jnp.float32)
    picked_grad = gate_weights * (gate_grad - jnp.sum(gate_weights * gate_grad, -1, keepdims=True))
    logits_grad = jnp.sum(jnp.where(route_hot, picked_grad[:, :, None], 0.0), 1).astype(
        jnp.bfloat16
    )
    rows_grad = (
        (gate_weights[:, :, None] * upstream[:, None, :])
        .astype(jnp.bfloat16)
        .reshape(rows_count * TOP, D)
    )
    send_grad = jnp.where(slot_used[:, None], rows_grad[source_route], zero_row).reshape(
        owners, per_owner, capacity, D
    )
    received_grad = lax.all_to_all(send_grad, "expert", split_axis=0, concat_axis=0, tiled=True)
    product_grad = jnp.einsum(
        "sicd,ifd->sicf", received_grad, out_full, preferred_element_type=jnp.float32
    )
    out_weight_grad = jnp.einsum(
        "sicf,sicd->ifd", product, received_grad, preferred_element_type=jnp.float32
    )
    gate_part_grad = gelu_pull(product_grad * up_part)[0]
    up_part_grad = product_grad * activated
    hidden_grad = jnp.concatenate([gate_part_grad, up_part_grad], -1).astype(jnp.bfloat16)
    in_weight_grad = jnp.einsum(
        "sicd,sicf->idf", received, hidden_grad, preferred_element_type=jnp.float32
    )
    input_rows_grad = jnp.einsum(
        "sicf,idf->sicd", hidden_grad, in_full, preferred_element_type=jnp.float32
    ).astype(jnp.bfloat16)
    returned_grad = lax.all_to_all(
        input_rows_grad, "expert", split_axis=0, concat_axis=0, tiled=True
    ).reshape(experts * capacity, D)
    moe_in_grad = jnp.sum(
        returned_grad[destination].reshape(rows_count, TOP, D).astype(jnp.float32), 1
    )
    gain_two_grad = jnp.sum(moe_in_grad * normed_two, 0)
    scaled_two = moe_in_grad * gain_moe
    mid_grad = upstream + inv_two * (
        scaled_two - normed_two * jnp.mean(scaled_two * normed_two, -1, keepdims=True)
    )
    attn_out_grad = mid_grad.astype(jnp.bfloat16)
    output_weight_grad = jnp.einsum(
        "tc,td->cd", attended, attn_out_grad, preferred_element_type=jnp.float32
    )
    attended_grad = jnp.einsum(
        "td,cd->tc", attn_out_grad, output_full, preferred_element_type=jnp.float32
    )
    attended_grad = attended_grad.astype(jnp.bfloat16).reshape(
        rows_count, KV_HEADS, groups, HEAD_DIM
    )
    probs_again = jnp.exp(score_table() - log_sum)
    prob_grad = jnp.einsum(
        "tkgd,skd->kgts", attended_grad, values_in, preferred_element_type=jnp.float32
    )
    delta_sum = jnp.sum(probs_again * prob_grad, -1, keepdims=True)
    score_grad = (probs_again * (prob_grad - delta_sum)).astype(jnp.bfloat16)
    values_grad = jnp.einsum(
        "kgts,tkgd->skd",
        probs_again.astype(jnp.bfloat16),
        attended_grad,
        preferred_element_type=jnp.float32,
    )
    queries_grad = (
        jnp.einsum("kgts,skd->tkgd", score_grad, keys_rot, preferred_element_type=jnp.float32)
        * score_scale
    )
    keys_grad = (
        jnp.einsum("kgts,tkgd->skd", score_grad, queries, preferred_element_type=jnp.float32)
        * score_scale
    )
    query_raw_grad = rotate_back(
        queries_grad.reshape(rows_count, HEADS, HEAD_DIM), cos_table, sin_table
    )
    query_raw_grad = query_raw_grad.astype(jnp.bfloat16).reshape(rows_count, HEADS * HEAD_DIM)
    key_raw_grad = (
        rotate_back(keys_grad, cos_table, sin_table)
        .astype(jnp.bfloat16)
        .reshape(rows_count, width_kv)
    )
    keyvalue_grad = jnp.concatenate(
        [key_raw_grad, values_grad.astype(jnp.bfloat16).reshape(rows_count, width_kv)], -1
    )
    query_weight_grad = jnp.einsum(
        "tc,tf->cf", attn_in, query_raw_grad, preferred_element_type=jnp.float32
    )
    keyvalue_weight_grad = jnp.einsum(
        "tc,tf->cf", attn_in, keyvalue_grad, preferred_element_type=jnp.float32
    )
    attn_in_grad = jnp.einsum(
        "tf,cf->tc", query_raw_grad, query_full, preferred_element_type=jnp.float32
    )
    attn_in_grad = attn_in_grad + jnp.einsum(
        "tf,cf->tc", keyvalue_grad, keyvalue_full, preferred_element_type=jnp.float32
    )
    gain_one_grad = jnp.sum(attn_in_grad * normed_one, 0)
    scaled_one = attn_in_grad * gain_attn
    tokens_grad = mid_grad + inv_one * (
        scaled_one - normed_one * jnp.mean(scaled_one * normed_one, -1, keepdims=True)
    )
    tokens_grad = tokens_grad + jnp.einsum(
        "te,ce->tc", logits_grad, router_full, preferred_element_type=jnp.float32
    )
    router_weight_grad = jnp.einsum(
        "tc,te->ce", tokens, logits_grad, preferred_element_type=jnp.float32
    )
    gains_grad = jnp.stack([gain_one_grad, gain_two_grad], 0)
    reduced = (
        lax.psum_scatter(query_weight_grad, ("dp", "expert"), scatter_dimension=0, tiled=True),
        lax.psum_scatter(keyvalue_weight_grad, ("dp", "expert"), scatter_dimension=0, tiled=True),
        lax.psum_scatter(output_weight_grad, ("dp", "expert"), scatter_dimension=0, tiled=True),
        lax.psum_scatter(router_weight_grad, ("dp", "expert"), scatter_dimension=0, tiled=True),
        lax.psum_scatter(gains_grad, ("dp", "expert"), scatter_dimension=1, tiled=True),
    )
    expert_sums = (
        lax.psum_scatter(
            in_weight_grad.astype(jnp.bfloat16), "dp", scatter_dimension=1, tiled=True
        ).astype(jnp.float32),
        lax.psum_scatter(
            out_weight_grad.astype(jnp.bfloat16), "dp", scatter_dimension=1, tiled=True
        ).astype(jnp.float32),
    )
    rates = learning_rates()
    query_upd = adam_update(query_weight, query_first, query_second, reduced[0], rates[0], DECAY)
    keyvalue_upd = adam_update(
        keyvalue_weight, keyvalue_first, keyvalue_second, reduced[1], rates[1], DECAY
    )
    output_upd = adam_update(
        output_weight, output_first, output_second, reduced[2], rates[2], DECAY
    )
    router_upd = adam_update(
        router_weight, router_first, router_second, reduced[3], rates[3], DECAY
    )
    gains_upd = adam_update(norm_gains, gains_first, gains_second, reduced[4], rates[4], 0.0)
    in_upd = adam_update(
        expert_in, expert_in_first, expert_in_second, expert_sums[0], rates[5], DECAY
    )
    out_upd = adam_update(
        expert_out, expert_out_first, expert_out_second, expert_sums[1], rates[6], DECAY
    )
    return (
        mixed_out,
        tokens_grad,
        query_upd[0],
        query_upd[1],
        query_upd[2],
        keyvalue_upd[0],
        keyvalue_upd[1],
        keyvalue_upd[2],
        output_upd[0],
        output_upd[1],
        output_upd[2],
        router_upd[0],
        router_upd[1],
        router_upd[2],
        gains_upd[0],
        gains_upd[1],
        gains_upd[2],
        in_upd[0],
        in_upd[1],
        in_upd[2],
        out_upd[0],
        out_upd[1],
        out_upd[2],
    )


def solution(mesh):
    in_specs = (
        P(("dp", "expert"), None),
        P(("dp", "expert"), None),
        P(("dp", "expert"), None),
        P(("dp", "expert"), None),
        P(("dp", "expert"), None),
        P(("dp", "expert"), None),
        P(("dp", "expert"), None),
        P(("dp", "expert"), None),
        P(("dp", "expert"), None),
        P(("dp", "expert"), None),
        P(("dp", "expert"), None),
        P(("dp", "expert"), None),
        P(("dp", "expert"), None),
        P(("dp", "expert"), None),
        P(("dp", "expert"), None),
        P(("dp", "expert"), None),
        P(None, ("dp", "expert")),
        P(None, ("dp", "expert")),
        P(None, ("dp", "expert")),
        P("expert", "dp", None),
        P("expert", "dp", None),
        P("expert", "dp", None),
        P("expert", "dp", None),
        P("expert", "dp", None),
        P("expert", "dp", None),
    )
    out_specs = (
        P(("dp", "expert"), None),
        P(("dp", "expert"), None),
        P(("dp", "expert"), None),
        P(("dp", "expert"), None),
        P(("dp", "expert"), None),
        P(("dp", "expert"), None),
        P(("dp", "expert"), None),
        P(("dp", "expert"), None),
        P(("dp", "expert"), None),
        P(("dp", "expert"), None),
        P(("dp", "expert"), None),
        P(("dp", "expert"), None),
        P(("dp", "expert"), None),
        P(("dp", "expert"), None),
        P(None, ("dp", "expert")),
        P(None, ("dp", "expert")),
        P(None, ("dp", "expert")),
        P("expert", "dp", None),
        P("expert", "dp", None),
        P("expert", "dp", None),
        P("expert", "dp", None),
        P("expert", "dp", None),
        P("expert", "dp", None),
    )
    return jax.shard_map(shards, mesh=mesh, in_specs=in_specs, out_specs=out_specs, check_vma=False)
```

profile of v0, /device:TPU:0, one launch (start us, length us, event | category | flops | bytes accessed | tf_op | source)
XLA Modules:
  0.0 1557.0 jit_solution(13038505224834028958)
XLA Ops:
  15.0 43.0 %all-gather = bf16[32,48,2]{1,2,0:T(2,128)(2,1)S(1)} all-gather(bf16[1,48,2]{1,2,0:T(2,128)(2,1)S(1)} %convert_bitcast_fusion.3), channel_id=1, replica_groups=mesh['dp'=4,'expert'=8] {'dp','expert'}, dimensions={0}, use_global_device_ids=true | all-gather | bytes 6336 | tf_op jit(solution)/shard_map/all_gather | solution.py:135
  64.0 8.1 scatter_custom_fusion.1
  72.1 9.1 scatter_custom_fusion
  90.8 45.3 %all-gather.10.cloned.1.call-done = bf16[1536,1536]{1,0:T(8,128)(2,1)} async-done(((bf16[48,1536]{1,0:T(8,128)(2,1)}), bf16[1536,1536]{1,0:T(8,128)(2,1)}) %all-gather.10.cloned.1.call-update) | async-done | bytes 4718608 | tf_op jit(solution)/shard_map/all_gather | solution.py:131
  136.1 4.9 fusion.117
  144.5 2.8 copy.163
  147.4 4.6 fusion.42
  152.1 2.6 fusion.3
  156.8 4.8 fusion.61
  161.6 40.4 %all-gather.12.cloned.1.call-done = bf16[1536,1536]{1,0:T(8,128)(2,1)} async-done(((bf16[48,1536]{1,0:T(8,128)(2,1)}), bf16[1536,1536]{1,0:T(8,128)(2,1)}) %all-gather.12.cloned.1.call-update) | async-done | bytes 4718608 | tf_op jit(solution)/shard_map/all_gather | solution.py:133
  202.1 4.8 multiply_reduce_fusion.3
  208.9 14.7 gather_fusion
  223.6 8.1 broadcast_select_fusion.1
  231.7 5.0 all-to-all-start
  237.0 2.9 convert_element_type.184
  240.9 88.5 %all-gather.14.cloned.1.call-done = bf16[1,1536,1536]{2,1,0:T(8,128)(2,1)} async-done(((bf16[1,384,1536]{2,1,0:T(8,128)(2,1)}), bf16[1,1536,1536]{2,1,0:T(8,128)(2,1)}) %all-gather.14.cloned.1.call-update) | async-done | bytes 4718608 | tf_op jit(solution)/shard_map/all_gather | solution.py:138
  329.4 12.6 all-to-all-done
  342.0 19.5 %fusion.21 = f32[8,1,384,1536]{3,2,0,1:T(8,128)S(1)} fusion(bf16[8,1,384,1536]{3,2,1,0:T(8,128)(2,1)} %all-to-all-done, bf16[1,1536,1536]{2,1,0:T(8,128)(2,1)} %all-gather.14.cloned.1.call-done), kind=kOutput, calls=%fused_computation.47 | convolution fusion | flops 14495514624 | bytes 33030144 | tf_op jit(solution)/shard_map/sicd,idf->sicf/dot_general | solution.py:204
  361.5 6.5 copy-done.8
  368.0 4.6 fusion.37
  372.6 7.3 all-gather.16.cloned.1.call-done
  379.9 12.2 convert_bitcast_fusion.1
  392.1 5.2 all-to-all-start.1
  397.3 5.6 mul.622
  403.0 14.9 mul.623
  417.9 114.7 %all-gather.1 = bf16[32,48,8]{1,2,0:T(8,128)(2,1)S(1)} all-gather(bf16[1,48,8]{1,2,0:T(8,128)(2,1)S(1)} %convert_bitcast_fusion.2), channel_id=1, replica_groups=mesh['dp'=4,'expert'=8] {'dp','expert'}, dimensions={0}, use_global_device_ids=true | all-gather | bytes 25344 | tf_op jit(solution)/shard_map/all_gather | solution.py:134
  533.3 18.2 %gather_fusion.1 = bf16[2048,1536]{1,0:T(8,128)(2,1)} fusion(bf16[3072,1536]{1,0:T(8,128)(2,1)} %bitcast.40, s32[2048]{0:T(1024)S(1)} %broadcast_clamp_fusion), kind=kCustom, calls=%fused_computation.1 | custom fusion | bytes 12591104 | tf_op jit(solution)/shard_map/gather | solution.py:215
  551.5 11.1 reshape.423
  562.7 8.4 fusion.52
  571.6 8.0 multiply_convert_fusion
  579.6 22.9 %gather_fusion.2 = bf16[3072,1536]{1,0:T(8,128)(2,1)} fusion(bf16[2048,1536]{1,0:T(8,128)(2,1)} %multiply_convert_fusion, s32[3072]{0:T(1024)S(1)} %copy-done.56), kind=kCustom, calls=%fused_computation.2 | custom fusion | bytes 18886656 | tf_op jit(solution)/shard_map/gather | solution.py:229
  602.4 8.0 broadcast_select_fusion
  610.4 111.6 %all_to_all.20 = bf16[8,1,384,1536]{3,2,1,0:T(8,128)(2,1)} all-to-all(bf16[8,1,384,1536]{3,2,1,0:T(8,128)(2,1)} %broadcast_select_fusion), channel_id=1, replica_groups=mesh['dp'=4,'expert'=8] {'expert'}, dimensions={0} | all-to-all | bytes 18874368 | tf_op jit(solution)/shard_map/all_to_all | solution.py:232
  722.0 21.4 %fusion.41 = (bf16[8,384,768]{2,1,0:T(8,128)(2,1)}, bf16[8,384,768]{2,1,0:T(8,128)(2,1)}) fusion(f32[8,1,384,1536]{3,2,0,1:T(8,128)} %copy-done.8, bf16[1,768,1536]{2,1,0:T(8,128)(2,1)S(1)} %copy-done.68, bf16[8,1,384,1536]{3,2,1,0:T(8,128)(2,1)} %all_to_all.20), kind=kOutput, calls=%fused_computation.64 | convolution fusion | flops 7304380416 | bytes 40108032 | tf_op jit(solution)/shard_map/sicd,ifd->sicf/dot_general | solution.py:233
  743.5 20.3 %convert_bitcast_fusion = bf16[8,1,384,1536]{3,2,1,0:T(8,128)(2,1)} fusion(bf16[8,384,768]{2,1,0:T(8,128)(2,1)} %get-tuple-element.53, bf16[8,384,768]{2,1,0:T(8,128)(2,1)} %get-tuple-element.52, bf16[1,1536,1536]{2,1,0:T(8,128)(2,1)} %all-gather.14.cloned.1.call-done), kind=kOutput, calls=%fused_computation.41 | convolution fusion | flops 14519107584 | bytes 23592960 | tf_op jit(solution)/shard_map/sicf,idf->sicd/dot_general | solution.py:245
  763.7 5.2 all-to-all-start.3
  770.6 12.7 multiply_reduce_fusion
  783.3 12.8 fusion.54
  796.4 79.7 %all-to-all-done.3 = bf16[8,1,384,1536]{3,2,1,0:T(8,128)(2,1)} async-done(((bf16[8,1,384,1536]{3,2,1,0:T(8,128)(2,1)}), bf16[8,1,384,1536]{3,2,1,0:T(8,128)(2,1)}, u32[]{:S(2)}, u32[]{:S(2)}) %all-to-all-start.3) | async-done | bytes 9437216 | tf_op jit(solution)/shard_map/all_to_all | solution.py:248
  876.1 18.2 %gather_fusion.3 = bf16[2048,1536]{1,0:T(8,128)(2,1)} fusion(bf16[3072,1536]{1,0:T(8,128)(2,1)} %bitcast.55, s32[2048]{0:T(1024)S(1)} %broadcast_clamp_fusion), kind=kCustom, calls=%fused_computation.3 | custom fusion | bytes 12591104 | tf_op jit(solution)/shard_map/gather | solution.py:252
  894.3 12.3 reshape.431
  906.5 13.2 reduce_sum.165
  919.7 3.8 multiply_reduce_fusion.1
  924.5 4.5 multiply_add_fusion
  930.7 3.7 convolution_convert_fusion
  934.4 2.7 copy.176
  937.1 11.7 fusion
  950.3 7.5 fusion.2
  961.6 4.3 convolution_multiply_fusion
  967.7 2.7 fusion.137
  971.7 3.1 fusion.67
  974.9 3.4 fusion.50
  979.6 21.7 %fusion.26 = bf16[1,1536,1536]{2,1,0:T(8,128)(2,1)} fusion(bf16[8,1,384,1536]{3,2,1,0:T(8,128)(2,1)} %all-to-all-done, bf16[8,384,768]{2,1,0:T(8,128)(2,1)} %get-tuple-element.53, bf16[8,384,768]{2,1,0:T(8,128)(2,1)} %get-tuple-element.52), kind=kOutput, calls=%fused_computation.48 | convolution fusion | flops 14516748288 | bytes 23592960 | tf_op jit(solution)/shard_map/sicd,sicf->idf/dot_general | solution.py:242
  1001.3 3.0 fusion.76
  1005.7 5.5 fusion.115
  1012.7 7.2 fusion.73
  1021.5 4.4 multiply_subtract_fusion.1
  1026.5 2.9 convolution_add_fusion
  1029.4 41.9 %reduce-scatter.24.cloned.1.call-done = f32[48,2]{1,0:T(8,128)} async-done(((f32[1536,2]{1,0:T(8,128)}), f32[48,2]{1,0:T(8,128)}) %reduce-scatter.24.cloned.1.call-update) | async-done | bytes 400
  1072.8 85.2 %reduce-scatter.18.cloned.1.call-done = bf16[1,384,1536]{2,1,0:T(8,128)(2,1)} async-done(((bf16[1,1536,1536]{2,1,0:T(8,128)(2,1)}), bf16[1,384,1536]{2,1,0:T(8,128)(2,1)}) %reduce-scatter.18.cloned.1.call-update) | async-done | bytes 1179664 | tf_op jit(solution)/shard_map/reduce_scatter | solution.py:333
  1157.9 7.6 multiply_subtract_fusion
  1165.6 99.8 %reduce-scatter.14.cloned.1.call-done = f32[48,512]{1,0:T(8,128)} async-done(((f32[1536,512]{1,0:T(8,128)}), f32[48,512]{1,0:T(8,128)}) %reduce-scatter.14.cloned.1.call-update) | async-done | bytes 98320 | tf_op jit(solution)/shard_map/reduce_scatter | solution.py:327
  1267.1 138.9 %reduce-scatter.12.cloned.1.call-done = f32[48,1536]{1,0:T(8,128)} async-done(((f32[1536,1536]{1,0:T(8,128)}), f32[48,1536]{1,0:T(8,128)}) %reduce-scatter.12.cloned.1.call-update) | async-done | bytes 294928 | tf_op jit(solution)/shard_map/reduce_scatter | solution.py:326
  1408.0 139.3 %reduce-scatter.16.cloned.1.call-done = f32[48,1536]{1,0:T(8,128)} async-done(((f32[1536,1536]{1,0:T(8,128)}), f32[48,1536]{1,0:T(8,128)}) %reduce-scatter.16.cloned.1.call-update) | async-done | bytes 294928 | tf_op jit(solution)/shard_map/reduce_scatter | solution.py:328
  (273 shorter events, 58.5 us)
Async XLA Ops:
  8.0 52.6 %copy-start.51 = (s32[512,4]{0,1:T(4,128)S(1)}, s32[512,4]{0,1:T(4,128)}, u32[]{:S(2)}) copy-start(s32[512,4]{0,1:T(4,128)} %param.27) | copy-start | bytes 24580
  8.0 73.2 %copy-start.2 = (bf16[512,1536]{1,0:T(8,128)(2,1)S(1)}, bf16[512,1536]{1,0:T(8,128)(2,1)}, u32[]{:S(2)}) copy-start(bf16[512,1536]{1,0:T(8,128)(2,1)} %param.25) | copy-start | bytes 4718596
  8.0 74.5 %all-gather.8.cloned.1.call-start = ((), (), s32[]{:S(2)}) async-start(), calls=%async_computation.11 | async-start | bytes 1622016 | tf_op jit(solution)/shard_map/all_gather | solution.py:132
  9.7 126.3 %all-gather.10.cloned.1.call-start = ((), (), s32[]{:S(2)}) async-start(), calls=%async_computation.12 | async-start | bytes 4866048 | tf_op jit(solution)/shard_map/all_gather | solution.py:131
  11.5 190.6 %all-gather.12.cloned.1.call-start = ((), (), s32[]{:S(2)}) async-start(), calls=%async_computation.13 | async-start | bytes 4866048 | tf_op jit(solution)/shard_map/all_gather | solution.py:133
  60.4 80.6 %copy-start.28 = (f32[512,64]{0,1:T(8,128)}, f32[512,64]{0,1:T(8,128)S(1)}, u32[]{:S(2)}) copy-start(f32[512,64]{0,1:T(8,128)S(1)} %get-tuple-element.68) | copy-start | bytes 393220
  60.4 80.6 %copy-start.30 = (f32[512,64]{0,1:T(8,128)}, f32[512,64]{0,1:T(8,128)S(1)}, u32[]{:S(2)}) copy-start(f32[512,64]{0,1:T(8,128)S(1)} %get-tuple-element.69) | copy-start | bytes 393220
  60.5 28.3 %copy-start.22 = (f32[512,64]{1,0:T(8,128)}, f32[512,64]{1,0:T(8,128)S(1)}, u32[]{:S(2)}) copy-start(f32[512,64]{1,0:T(8,128)S(1)} %copy.161) | copy-start | bytes 393220
  60.7 28.1 %copy-start.24 = (f32[512,64]{1,0:T(8,128)}, f32[512,64]{1,0:T(8,128)S(1)}, u32[]{:S(2)}) copy-start(f32[512,64]{1,0:T(8,128)S(1)} %copy.159) | copy-start | bytes 393220
  81.2 54.9 %copy-start.54 = (f32[1536]{0:T(1024)}, f32[1536]{0:T(1024)S(1)}, u32[]{:S(2)}) copy-start(f32[1536]{0:T(1024)S(1)} %get-tuple-element.28) | copy-start | bytes 18436
  81.3 125.7 %copy-start.47 = (f32[1536]{0:T(1024)}, f32[1536]{0:T(1024)S(1)}, u32[]{:S(2)}) copy-start(f32[1536]{0:T(1024)S(1)} %get-tuple-element.27) | copy-start | bytes 18436
  81.7 54.4 %copy-start.59 = (f32[512]{0:T(512)}, f32[512]{0:T(512)S(1)}, u32[]{:S(2)}) copy-start(f32[512]{0:T(512)S(1)} %add_rsqrt_fusion.1) | copy-start | bytes 6148
  82.5 72.2 %copy-start.12 = (pred[512,512]{0,1:T(8,128)(4,1)}, pred[512,512]{0,1:T(8,128)(4,1)S(1)}, u32[]{:S(2)}) copy-start(pred[512,512]{0,1:T(8,128)(4,1)S(1)} %fusion.72) | copy-start | bytes 786436
  144.5 7.5 copy-start.9
  152.0 4.6 copy-start
  152.0 4.7 copy-start.39
  161.6 45.2 %copy-start.26 = (bf16[2,128,6,512]{3,1,2,0:T(8,128)(2,1)}, bf16[2,128,6,512]{3,1,2,0:T(8,128)(2,1)S(1)}, u32[]{:S(2)}) copy-start(bf16[2,128,6,512]{3,1,2,0:T(8,128)(2,1)S(1)} %fusion.61) | copy-start | bytes 4718596
  206.9 16.7 %copy-start.57 = (f32[512]{0:T(512)}, f32[512]{0:T(512)S(1)}, u32[]{:S(2)}) copy-start(f32[512]{0:T(512)S(1)} %add_rsqrt_fusion) | copy-start | bytes 6148
  231.7 110.4 %all-to-all-start = ((bf16[8,1,384,1536]{3,2,1,0:T(8,128)(2,1)}), bf16[8,1,384,1536]{3,2,1,0:T(8,128)(2,1)}, u32[]{:S(2)}, u32[]{:S(2)}) async-start(bf16[8,1,384,1536]{3,2,1,0:T(8,128)(2,1)} %broadcast_select_fusion.1), calls=%async_computation | async-start | bytes 18874368 | tf_op jit(solution)/shard_map/all_to_all | solution.py:203
  236.7 92.7 %all-gather.14.cloned.1.call-start = ((), (), s32[]{:S(2)}) async-start(), calls=%async_computation.14 | async-start | bytes 5898240 | tf_op jit(solution)/shard_map/all_gather | solution.py:138
  239.9 140.0 %all-gather.16.cloned.1.call-start = ((), (), s32[]{:S(2)}) async-start(), calls=%async_computation.15 | async-start | bytes 2949120 | tf_op jit(solution)/shard_map/all_gather | solution.py:139
  361.5 6.5 copy-start.8
  392.1 5.2 copy-start.15
  392.1 141.2 %all-to-all-start.1 = ((bf16[8,1,384,1536]{3,2,1,0:T(8,128)(2,1)}), bf16[8,1,384,1536]{3,2,1,0:T(8,128)(2,1)}, u32[]{:S(2)}, u32[]{:S(2)}) async-start(bf16[8,1,384,1536]{3,2,1,0:T(8,128)(2,1)} %convert_bitcast_fusion.1), calls=%async_computation.1 | async-start | bytes 18874368 | tf_op jit(solution)/shard_map/all_to_all | solution.py:212
  403.0 14.9 copy-start.61
  532.7 18.8 %copy-start.45 = (bf16[1536,8]{0,1:T(8,128)(2,1)}, bf16[1536,8]{0,1:T(8,128)(2,1)S(1)}, u32[]{:S(2)}) copy-start(bf16[1536,8]{0,1:T(8,128)(2,1)S(1)} %reshape.485) | copy-start | bytes 73732
  571.6 8.0 copy-start.56
  610.4 111.6 %copy-start.68 = (bf16[1,768,1536]{2,1,0:T(8,128)(2,1)S(1)}, bf16[1,768,1536]{2,1,0:T(8,128)(2,1)}, u32[]{:S(2)}) copy-start(bf16[1,768,1536]{2,1,0:T(8,128)(2,1)} %all-gather.16.cloned.1.call-done) | copy-start | bytes 7077892
  763.7 5.2 copy-start.40
  763.7 5.3 copy-start.50
  763.7 112.3 %all-to-all-start.3 = ((bf16[8,1,384,1536]{3,2,1,0:T(8,128)(2,1)}), bf16[8,1,384,1536]{3,2,1,0:T(8,128)(2,1)}, u32[]{:S(2)}, u32[]{:S(2)}) async-start(bf16[8,1,384,1536]{3,2,1,0:T(8,128)(2,1)} %convert_bitcast_fusion), calls=%async_computation.3 | async-start | bytes 18874368 | tf_op jit(solution)/shard_map/all_to_all | solution.py:248
  768.9 251.0 %reduce-scatter.22.cloned.1.call-start = ((), (), s32[]{:S(2)}) async-start(), calls=%async_computation.21 | async-start | bytes 811008
  770.6 250.9 %reduce-scatter.20.cloned.1.call-start = ((), (), s32[]{:S(2)}) async-start(), calls=%async_computation.20 | async-start | bytes 2949120 | tf_op jit(solution)/shard_map/reduce_scatter | solution.py:336
  796.1 275.2 %reduce-scatter.24.cloned.1.call-start = ((), (), s32[]{:S(2)}) async-start(), calls=%async_computation.22 | async-start | bytes 811008
  906.5 13.2 copy-start.48
  906.5 13.2 copy-start.58
  906.5 17.0 %copy-start.16 = (bf16[512,1536]{1,0:T(8,128)(2,1)S(1)}, bf16[512,1536]{1,0:T(8,128)(2,1)}, u32[]{:S(2)}) copy-start(bf16[512,1536]{1,0:T(8,128)(2,1)} %param.26) | copy-start | bytes 4718596
  919.7 4.8 copy-start.5
  919.7 10.9 slice-start.8
  924.5 6.2 slice-start.9
  937.1 11.7 slice-start
  937.1 11.7 slice-start.1
  937.1 13.2 slice-start.2
  950.3 7.5 copy-start.10
  950.3 7.6 copy-start.11
  961.1 6.6 slice-start.6
  961.6 6.1 slice-start.7
  979.5 178.4 %reduce-scatter.18.cloned.1.call-start = ((), (), s32[]{:S(2)}) async-start(), calls=%async_computation.19 | async-start | bytes 5898240 | tf_op jit(solution)/shard_map/reduce_scatter | solution.py:333
  1001.3 264.2 %reduce-scatter.14.cloned.1.call-start = ((), (), s32[]{:S(2)}) async-start(), calls=%async_computation.17 | async-start | bytes 3244032 | tf_op jit(solution)/shard_map/reduce_scatter | solution.py:327
  1004.3 401.6 %reduce-scatter.12.cloned.1.call-start = ((), (), s32[]{:S(2)}) async-start(), calls=%async_computation.16 | async-start | bytes 9732096 | tf_op jit(solution)/shard_map/reduce_scatter | solution.py:326
  1011.3 536.0 %reduce-scatter.16.cloned.1.call-start = ((), (), s32[]{:S(2)}) async-start(), calls=%async_computation.18 | async-start | bytes 9732096 | tf_op jit(solution)/shard_map/reduce_scatter | solution.py:328
  1021.4 5.1 copy-start.14
  1026.5 45.6 %copy-start.65 = (f32[2,48]{1,0:T(2,128)S(1)}, f32[2,48]{1,0:T(2,128)}, u32[]{:S(2)}) copy-start(f32[2,48]{1,0:T(2,128)} %param.41) | copy-start | bytes 1156
  1026.5 45.6 %copy-start.66 = (f32[2,48]{1,0:T(2,128)S(1)}, f32[2,48]{1,0:T(2,128)}, u32[]{:S(2)}) copy-start(f32[2,48]{1,0:T(2,128)} %param.43) | copy-start | bytes 1156
  1026.5 45.6 %copy-start.67 = (f32[2,48]{1,0:T(2,128)S(1)}, f32[2,48]{1,0:T(2,128)}, u32[]{:S(2)}) copy-start(f32[2,48]{1,0:T(2,128)} %param.42) | copy-start | bytes 1156
  1072.7 192.7 %copy-start.38 = (f32[48,512]{1,0:T(8,128)S(1)}, f32[48,512]{1,0:T(8,128)}, u32[]{:S(2)}) copy-start(f32[48,512]{1,0:T(8,128)} %param.32) | copy-start | bytes 294916
  1072.7 192.7 %copy-start.52 = (f32[48,512]{1,0:T(8,128)S(1)}, f32[48,512]{1,0:T(8,128)}, u32[]{:S(2)}) copy-start(f32[48,512]{1,0:T(8,128)} %param.34) | copy-start | bytes 294916
  1072.7 192.7 %copy-start.53 = (f32[48,512]{1,0:T(8,128)S(1)}, f32[48,512]{1,0:T(8,128)}, u32[]{:S(2)}) copy-start(f32[48,512]{1,0:T(8,128)} %param.33) | copy-start | bytes 294916
  1072.7 333.3 %copy-start.35 = (f32[48,1536]{1,0:T(8,128)S(1)}, f32[48,1536]{1,0:T(8,128)}, u32[]{:S(2)}) copy-start(f32[48,1536]{1,0:T(8,128)} %param.29) | copy-start | bytes 884740
  1072.7 333.3 %copy-start.41 = (f32[48,1536]{1,0:T(8,128)S(1)}, f32[48,1536]{1,0:T(8,128)}, u32[]{:S(2)}) copy-start(f32[48,1536]{1,0:T(8,128)} %param.31) | copy-start | bytes 884740
  1072.7 333.2 %copy-start.42 = (f32[48,1536]{1,0:T(8,128)S(1)}, f32[48,1536]{1,0:T(8,128)}, u32[]{:S(2)}) copy-start(f32[48,1536]{1,0:T(8,128)} %param.30) | copy-start | bytes 884740
  1072.7 474.6 %copy-start.36 = (f32[48,1536]{1,0:T(8,128)S(1)}, f32[48,1536]{1,0:T(8,128)}, u32[]{:S(2)}) copy-start(f32[48,1536]{1,0:T(8,128)} %param.35) | copy-start | bytes 884740
  1072.7 474.6 %copy-start.43 = (f32[48,1536]{1,0:T(8,128)S(1)}, f32[48,1536]{1,0:T(8,128)}, u32[]{:S(2)}) copy-start(f32[48,1536]{1,0:T(8,128)} %param.37) | copy-start | bytes 884740
  1072.8 474.6 %copy-start.44 = (f32[48,1536]{1,0:T(8,128)S(1)}, f32[48,1536]{1,0:T(8,128)}, u32[]{:S(2)}) copy-start(f32[48,1536]{1,0:T(8,128)} %param.36) | copy-start | bytes 884740
  (30 other events, 77.9 us)
Sparse Core Ops, SparseCore 0:
  12.3 57.7 all-gather.7
  73.6 62.4 all-gather.9
  139.6 62.4 all-gather.11
  775.1 124.5 reduce-scatter.21
  902.5 47.0 reduce-scatter.19
  979.6 91.5 reduce-scatter.23
  1073.6 84.3 reduce-scatter.17
  1163.4 102.0 reduce-scatter.13
  1271.3 134.5 reduce-scatter.11
  1412.7 134.5 reduce-scatter.15
Sparse Core Ops, SparseCore 1:
  240.0 89.4 all-gather.13
  331.4 48.4 all-gather.15
where the time goes:
time: 1570 us; the launch traced here: 1560 us
  waiting for transfers between devices  779 us (50%)
  blocking collectives  269 us (17%)
  matrix products  188 us (12%)
  local copies, waits for them, and re-layouts  174 us (11%)
  other arithmetic  113 us (7%)
  between operations  16.9 us (1%)
  starting transfers between devices  16.3 us (1%)
    reduce_scatter x1, waiting for transfers between devices, shards(): lax.psum_scatter(output_weight_grad, ('dp', 'expert'), scatter_dimension=...  139 us
    reduce_scatter x1, waiting for transfers between devices, shards(): lax.psum_scatter(query_weight_grad, ('dp', 'expert'), scatter_dimension=0...  139 us
    all_gather x1, blocking collectives, shards(): lax.all_gather(router_weight.astype(jnp.bfloat16), ('dp', 'expert'), axis...  115 us
    all_to_all x1, blocking collectives, shards(): lax.all_to_all(send_grad, 'expert', split_axis=0, concat_axis=0, tiled=True)  112 us
    reduce_scatter x1, waiting for transfers between devices, shards(): lax.psum_scatter(keyvalue_weight_grad, ('dp', 'expert'), scatter_dimensio...  99.8 us
    all_gather x1, waiting for transfers between devices, shards(): lax.all_gather(expert_in.astype(jnp.bfloat16), 'dp', axis=1, tiled=True)  88.5 us
    reduce_scatter x1, waiting for transfers between devices, shards(): lax.psum_scatter(in_weight_grad.astype(jnp.bfloat16), 'dp', scatter_dimen...  85.2 us
    all_to_all x1, waiting for transfers between devices, shards(): lax.all_to_all(input_rows_grad, 'expert', split_axis=0, concat_axis=0, ti...  79.7 us
  transfers between devices with their start and end apart: 15, of which 11 were waited for; matrix products, arithmetic and copies ran while one was open for 19% of the time, Pallas kernels for 0%

commit v1 on v0

--- a/solution.py
+++ b/solution.py
@@ -1,6 +1,10 @@
+import functools
+
 import jax
 import jax.numpy as jnp
 from jax import lax
+from jax.experimental import pallas as pl
+from jax.experimental.pallas import tpu as pltpu
 from jax.sharding import PartitionSpec as P
 
 D = 1536
@@ -382,6 +386,1220 @@
     )
 
 
+def flip(mask):
+    return [(i, i ^ mask) for i in range(8)]
+
+
+ACROSS_X, ACROSS_Y, ACROSS_CORE = flip(2), flip(4), flip(1)
+FORWARD = [(i, i ^ (4 if i & 1 else 2)) for i in range(8)]
+
+
+def after(value, *earlier):
+    return lax.optimization_barrier((value, *earlier))[0]
+
+
+def hold(*values):
+    return lax.optimization_barrier(values)
+
+
+def to_x(value):
+    return lax.ppermute(value, "expert", ACROSS_X)
+
+
+def to_y(value):
+    return lax.ppermute(value, "expert", ACROSS_Y)
+
+
+def to_core(value):
+    return lax.ppermute(value, "expert", ACROSS_CORE)
+
+
+def forward(value):
+    return lax.ppermute(value, "expert", FORWARD)
+
+
+def gather_plane(value, core):
+    from_x, from_y = to_x(value), to_y(value)
+    from_core = to_core(value)
+    from_far = forward(jnp.where(core == 0, from_y, from_x))
+    return [
+        value,
+        from_core,
+        from_x,
+        to_core(from_x),
+        from_y,
+        to_core(from_y),
+        from_far,
+        to_core(from_far),
+    ]
+
+
+def add_low(*terms):
+    total = terms[0].astype(jnp.float32)
+    for term in terms[1:]:
+        total = total + term.astype(jnp.float32)
+    return total.astype(jnp.bfloat16)
+
+
+def add_low_wide(*terms):
+    return sum([term.astype(jnp.float32) for term in terms])
+
+
+def scatter_plane(parts, core):
+    far = add_low(parts[6], to_core(parts[7]))
+    relayed = forward(far)
+    by_x = add_low(parts[2], to_core(parts[3]))
+    by_y = add_low(parts[4], to_core(parts[5]))
+    own = add_low(parts[0], to_core(parts[1]))
+    zero = jnp.zeros((), jnp.bfloat16)
+    by_x = add_low(by_x, jnp.where(core == 1, relayed, zero))
+    by_y = add_low(by_y, jnp.where(core == 0, relayed, zero))
+    return own, to_x(by_x), to_y(by_y)
+
+
+def gather_column(value, ring):
+    values = [value]
+    for _ in range(len(ring) - 1):
+        values.append(lax.ppermute(values[-1], "dp", ring))
+    return values
+
+
+def scatter_column(value, ring, place):
+    count = len(ring)
+    rows = value.shape[0] // count
+
+    def piece(shard):
+        return lax.dynamic_slice_in_dim(value, (shard % count) * rows, rows, 0)
+
+    moving = piece(place + count - 1)
+    for step in range(count - 2):
+        moving = add_low(lax.ppermute(moving, "dp", ring), piece(place + count - 2 - step))
+    return lax.ppermute(moving, "dp", ring).astype(jnp.float32) + piece(place).astype(jnp.float32)
+
+
+def scatter_pieces(pieces, ring):
+    moving = pieces[1]
+    for piece in pieces[2:]:
+        moving = add_low(lax.ppermute(moving, "dp", ring), piece)
+    return lax.ppermute(moving, "dp", ring).astype(jnp.float32) + pieces[0].astype(jnp.float32)
+
+
+def anywhere():
+    return pl.BlockSpec(memory_space=pl.ANY)
+
+
+def scalars():
+    return pl.BlockSpec(memory_space=pltpu.SMEM)
+
+
+def whole():
+    return pl.BlockSpec(memory_space=pltpu.VMEM)
+
+
+def small_cost():
+    return pl.CostEstimate(flops=1024, bytes_accessed=1024, transcendentals=0)
+
+
+def load_rows(blocks, start_ref, joined, sems, column=0):
+    width = joined.shape[1]
+    pieces, rows = blocks[0].shape[0], blocks[0].shape[1]
+    copies = []
+    for i, block in enumerate(blocks):
+        for p in range(pieces):
+            at = pl.multiple_of(start_ref[i * pieces + p], 16)
+            copies.append(
+                pltpu.make_async_copy(
+                    block.at[p, :, pl.ds(column, width)],
+                    joined.at[pl.ds(at, rows)],
+                    sems.at[i * pieces + p],
+                )
+            )
+    for copy in copies:
+        copy.start()
+    return copies
+
+
+def wide_dot(left, right):
+    return lax.dot_general(
+        left, right, (((1,), (1,)), ((), ())), preferred_element_type=jnp.float32
+    )
+
+
+def tall_dot(left, right):
+    return lax.dot_general(
+        left, right, (((0,), (0,)), ((), ())), preferred_element_type=jnp.float32
+    )
+
+
+def load_weight(chunks, place_ref, buffer, sems, start=True):
+    total = sum([chunk.shape[0] for chunk in chunks[::4]])
+    copies, offset = [], 0
+    for j, chunk in enumerate(chunks):
+        rows = chunk.shape[0]
+        at = pl.multiple_of(place_ref[j % 4] * total + offset, 16)
+        copies.append(pltpu.make_async_copy(chunk, buffer.at[pl.ds(at, rows)], sems.at[j]))
+        if j % 4 == 3:
+            offset += rows
+    for copy in copies if start else []:
+        copy.start()
+    return copies
+
+
+LANES = 256
+WIDE = 512
+
+
+def turned(values, cosine, sine):
+    return values * cosine + pltpu.roll(values, HEAD_DIM // 2, 1) * sine
+
+
+def fill_bias(bias, first_ref):
+    row = lax.broadcasted_iota(jnp.int32, bias.shape, 0)
+    column = lax.broadcasted_iota(jnp.int32, bias.shape, 1)
+    bias[...] = jnp.where((column <= row) & (column >= first_ref[...]), 0.0, NEG)
+
+
+def attend_kernel(
+    planes, start_ref, tokens_ref, first_ref, cosine_ref, sine_ref, *refs
+):
+    blocks, refs = refs[:planes], refs[planes:]
+    attn_in_ref, heads_ref, attended_ref, log_ref, small_ref, weight, bias, sems = refs
+    rows_count = tokens_ref.shape[0]
+    copies = load_rows(blocks, start_ref, weight, sems)
+    fill_bias(bias, first_ref)
+    inputs = tokens_ref[...].astype(jnp.float32)
+    inverse = lax.rsqrt(jnp.mean(inputs * inputs, -1, keepdims=True) + EPS)
+    normed = inputs * inverse
+    for copy in copies:
+        copy.wait()
+    width_q, width_kv = HEADS * HEAD_DIM, KV_HEADS * HEAD_DIM
+    width = width_q + 2 * width_kv
+    small = jnp.transpose(weight[:, width:].astype(jnp.float32))
+    small_ref[...] = small[:16, :]
+    experts = small_ref.shape[0] - 8
+    attn_in_ref[...] = (normed * small[experts : experts + 1, :]).astype(jnp.bfloat16)
+    for at in range(0, width, LANES):
+        raw = jnp.dot(
+            attn_in_ref[...], weight[:, at : at + LANES], preferred_element_type=jnp.float32
+        )
+        for column in range(0, LANES, HEAD_DIM):
+            values = raw[:, column : column + HEAD_DIM]
+            if at + column < width_q + width_kv:
+                values = turned(values, cosine_ref[...], sine_ref[...])
+            heads_ref[:, at + column : at + column + HEAD_DIM] = values.astype(jnp.bfloat16)
+    half = rows_count // 2
+    for block in range(2):
+        rows, reach = pl.ds(block * half, half), (block + 1) * half
+        logs = jnp.zeros((half, 128), jnp.float32)
+        lane = lax.broadcasted_iota(jnp.int32, logs.shape, 1)
+        for head in range(HEADS):
+            key_at = width_q + head // (HEADS // KV_HEADS) * HEAD_DIM
+            value_at = key_at + width_kv
+            scores = wide_dot(
+                heads_ref[rows, head * HEAD_DIM : (head + 1) * HEAD_DIM],
+                heads_ref[:reach, key_at : key_at + HEAD_DIM],
+            )
+            scores = scores * HEAD_DIM ** (-0.5) + bias[rows, :reach]
+            peak = jnp.max(scores, -1, keepdims=True)
+            exponent = jnp.exp(scores - peak)
+            total = jnp.sum(exponent, -1, keepdims=True)
+            mixed = jnp.dot(
+                exponent.astype(jnp.bfloat16),
+                heads_ref[:reach, value_at : value_at + HEAD_DIM],
+                preferred_element_type=jnp.float32,
+            )
+            attended_ref[rows, head * HEAD_DIM : (head + 1) * HEAD_DIM] = (
+                mixed * (1.0 / total)
+            ).astype(jnp.bfloat16)
+            logs = jnp.where(lane == head, peak + jnp.log(total), logs)
+        log_ref[rows, :] = logs
+
+
+def attend_call(starts, tokens, first, cosine, sine, blocks, width_early):
+    rows_count = tokens.shape[0]
+    width = (HEADS + 2 * KV_HEADS) * HEAD_DIM
+    low = jnp.bfloat16
+    return pl.pallas_call(
+        functools.partial(attend_kernel, len(blocks)),
+        out_shape=[
+            jax.ShapeDtypeStruct((rows_count, D), low),
+            jax.ShapeDtypeStruct((rows_count, width), low),
+            jax.ShapeDtypeStruct((rows_count, HEADS * HEAD_DIM), low),
+            jax.ShapeDtypeStruct((rows_count, 128), jnp.float32),
+            jax.ShapeDtypeStruct((16, D), jnp.float32),
+        ],
+        in_specs=[scalars()] + [whole()] * 4 + [anywhere()] * len(blocks),
+        out_specs=[whole()] * 5,
+        scratch_shapes=[
+            pltpu.VMEM((D, width_early), low),
+            pltpu.VMEM((rows_count, rows_count), jnp.float32),
+            pltpu.SemaphoreType.DMA((len(blocks) * blocks[0].shape[0],)),
+        ],
+        compiler_params=pltpu.CompilerParams(vmem_limit_bytes=62 << 20),
+        cost_estimate=small_cost(),
+        name="attend",
+    )(starts, tokens, first, cosine, sine, *blocks)
+
+
+def middle_kernel(planes, column, start_ref, tokens_ref, attended_ref, routes_ref, small_ref, *refs):
+    blocks, refs = refs[:planes], refs[planes:]
+    residual_ref, packed_ref, gates_ref, weight, sems = refs
+    step = pl.program_id(0)
+    tile = tokens_ref.shape[0]
+    rows_count = packed_ref.shape[0] - 16
+    experts = gates_ref.shape[0]
+
+    @pl.when(step == 0)
+    def _():
+        for copy in load_rows(blocks, start_ref, weight, sems, column):
+            copy.wait()
+
+    for at in range(0, D, LANES):
+        residual_ref[:, at : at + LANES] = tokens_ref[:, at : at + LANES].astype(
+            jnp.float32
+        ) + jnp.dot(
+            attended_ref[...], weight[:, at : at + LANES], preferred_element_type=jnp.float32
+        )
+    residual = residual_ref[...]
+    inverse = lax.rsqrt(jnp.mean(residual * residual, -1, keepdims=True) + EPS)
+    rows = pl.ds(pl.multiple_of(step * tile, tile), tile)
+    packed_ref[rows, :] = (
+        residual * inverse * small_ref[experts + 1 : experts + 2, :]
+    ).astype(jnp.bfloat16)
+    logits = wide_dot(small_ref[...].astype(jnp.bfloat16), tokens_ref[...])[:experts, :]
+    expert = lax.broadcasted_iota(jnp.int32, logits.shape, 0)
+    routed = expert == routes_ref[:1, :]
+    for choice in range(1, TOP):
+        routed = routed | (expert == routes_ref[choice : choice + 1, :])
+    logits = jnp.where(routed, logits, NEG)
+    exponent = jnp.exp(logits - jnp.max(logits, 0, keepdims=True))
+    exponent = jnp.where(routed, exponent, 0.0)
+    gates = exponent / jnp.sum(exponent, 0, keepdims=True)
+    gates_ref[...] = gates
+    high = gates.astype(jnp.bfloat16)
+    rest = gates - high.astype(jnp.float32)
+    middle = rest.astype(jnp.bfloat16)
+    rest = rest - middle.astype(jnp.float32)
+    for part, values in enumerate((high.astype(jnp.float32), middle.astype(jnp.float32), rest)):
+        lanes = pl.ds(pl.multiple_of(part * rows_count + step * tile, tile), tile)
+        packed_ref[rows_count:, lanes] = jnp.concatenate(
+            [values, jnp.zeros((16 - experts, tile), jnp.float32)], 0
+        ).astype(jnp.bfloat16)
+
+
+def middle_call(starts, tokens, attended, routes, small, blocks, experts, column):
+    rows_count = tokens.shape[0]
+    tile = rows_count // 2
+    low = jnp.bfloat16
+    tiled = pl.BlockSpec((tile, D), lambda i: (i, 0))
+    lanes = lambda rows: pl.BlockSpec((rows, tile), lambda i: (0, i))
+    return pl.pallas_call(
+        functools.partial(middle_kernel, len(blocks), column),
+        grid=(2,),
+        out_shape=[
+            jax.ShapeDtypeStruct((rows_count, D), jnp.float32),
+            jax.ShapeDtypeStruct((rows_count + 16, D), low),
+            jax.ShapeDtypeStruct((experts, rows_count), jnp.float32),
+        ],
+        in_specs=[
+            scalars(),
+            tiled,
+            tiled,
+            lanes(routes.shape[0]),
+            pl.BlockSpec((16, D), lambda i: (0, 0)),
+        ]
+        + [anywhere()] * len(blocks),
+        out_specs=[
+            tiled,
+            pl.BlockSpec((rows_count + 16, D), lambda i: (0, 0)),
+            lanes(experts),
+        ],
+        scratch_shapes=[
+            pltpu.VMEM((D, D), low),
+            pltpu.SemaphoreType.DMA((len(blocks) * blocks[0].shape[0],)),
+        ],
+        compiler_params=pltpu.CompilerParams(vmem_limit_bytes=62 << 20),
+        cost_estimate=small_cost(),
+        name="middle",
+    )(starts, tokens, attended, routes, small, *blocks)
+
+
+def middle_back_kernel(planes, column, start_ref, *refs):
+    terms, tails, refs = refs[:4], refs[4:8], refs[8:]
+    residual_ref, small_ref, cot_ref, gates_ref, refs = *refs[:4], refs[4:]
+    blocks, refs = refs[:planes], refs[planes:]
+    mid_ref, low_ref, attended_grad_ref, logits_grad_ref, gain_ref, weight, sems = refs
+    step = pl.program_id(0)
+    experts = gates_ref.shape[0]
+    rows_count = gates_ref.shape[1]
+
+    @pl.when(step == 0)
+    def _():
+        copies = load_rows(blocks, start_ref, weight, sems, column)
+        gates = gates_ref[...]
+        parts = sum([tail[:experts, :].astype(jnp.float32) for tail in tails])
+        grad = (
+            parts[:, :rows_count]
+            + parts[:, rows_count : 2 * rows_count]
+            + parts[:, 2 * rows_count :]
+        )
+        grad = gates * (grad - jnp.sum(gates * grad, 0, keepdims=True))
+        logits_grad_ref[...] = jnp.concatenate(
+            [grad, jnp.zeros((16 - experts, rows_count), jnp.float32)], 0
+        ).astype(jnp.bfloat16)
+        gain_ref[...] = jnp.zeros_like(gain_ref)
+        for copy in copies:
+            copy.wait()
+
+    grad = sum([term[...].astype(jnp.float32) for term in terms])
+    residual = residual_ref[...]
+    inverse = lax.rsqrt(jnp.mean(residual * residual, -1, keepdims=True) + EPS)
+    normed = residual * inverse
+    product = grad * normed
+    gain_ref[...] += jnp.sum(product, 0, keepdims=True)
+    gain = small_ref[experts + 1 : experts + 2, :]
+    mean = jnp.mean(product * gain, -1, keepdims=True)
+    mid = cot_ref[...].astype(jnp.float32) + inverse * (grad * gain - normed * mean)
+    mid_ref[...] = mid
+    low_ref[...] = mid.astype(jnp.bfloat16)
+    for at in range(0, D, LANES):
+        attended_grad_ref[:, at : at + LANES] = wide_dot(
+            low_ref[...], weight[at : at + LANES, :]
+        ).astype(jnp.bfloat16)
+
+
+def middle_back_call(starts, terms, residual, small, cotangent, gates, blocks, column):
+    rows_count = residual.shape[0]
+    tile = rows_count // 2
+    low = jnp.bfloat16
+    tiled = pl.BlockSpec((tile, D), lambda i: (i, 0))
+    fixed = lambda rows, columns: pl.BlockSpec((rows, columns), lambda i: (0, 0))
+    tail = pl.BlockSpec((16, D), lambda i: (rows_count // 16, 0))
+    return pl.pallas_call(
+        functools.partial(middle_back_kernel, len(blocks), column),
+        grid=(2,),
+        out_shape=[
+            jax.ShapeDtypeStruct((rows_count, D), jnp.float32),
+            jax.ShapeDtypeStruct((rows_count, D), low),
+            jax.ShapeDtypeStruct((rows_count, D), low),
+            jax.ShapeDtypeStruct((16, rows_count), low),
+            jax.ShapeDtypeStruct((1, D), jnp.float32),
+        ],
+        in_specs=[scalars()]
+        + [tiled] * 4
+        + [tail] * 4
+        + [tiled, fixed(16, D), tiled, fixed(*gates.shape)]
+        + [anywhere()] * len(blocks),
+        out_specs=[tiled, tiled, tiled, fixed(16, rows_count), fixed(1, D)],
+        scratch_shapes=[
+            pltpu.VMEM((D, D), low),
+            pltpu.SemaphoreType.DMA((len(blocks) * blocks[0].shape[0],)),
+        ],
+        compiler_params=pltpu.CompilerParams(vmem_limit_bytes=62 << 20),
+        cost_estimate=small_cost(),
+        name="middle_back",
+    )(starts, *terms, *terms, residual, small, cotangent, gates, *blocks)
+
+
+def attend_back_kernel(heads_ref, grad_ref, log_ref, first_ref, cosine_ref, sine_ref, raw_ref, bias):
+    rows_count = heads_ref.shape[0]
+    width_q, width_kv = HEADS * HEAD_DIM, KV_HEADS * HEAD_DIM
+    half = rows_count // 2
+    scale = HEAD_DIM ** (-0.5)
+    fill_bias(bias, first_ref)
+    cosine, sine = cosine_ref[...], -sine_ref[...]
+    for key_head in range(KV_HEADS):
+        key_at = width_q + key_head * HEAD_DIM
+        value_at = key_at + width_kv
+        key_grads, value_grads = [], []
+        for block in range(2):
+            rows, reach = slice(block * half, (block + 1) * half), (block + 1) * half
+            keys = heads_ref[:reach, key_at : key_at + HEAD_DIM]
+            values = heads_ref[:reach, value_at : value_at + HEAD_DIM]
+            key_grad = jnp.zeros((reach, HEAD_DIM), jnp.float32)
+            value_grad = jnp.zeros((reach, HEAD_DIM), jnp.float32)
+            for head in range(key_head * HEADS // KV_HEADS, (key_head + 1) * HEADS // KV_HEADS):
+                columns = slice(head * HEAD_DIM, (head + 1) * HEAD_DIM)
+                queries, grads = heads_ref[rows, columns], grad_ref[rows, columns]
+                scores = wide_dot(queries, keys) * scale + bias[rows, :reach]
+                chances = jnp.exp(scores - log_ref[rows, head : head + 1])
+                pulled = wide_dot(grads, values)
+                shift = jnp.sum(chances * pulled, -1, keepdims=True)
+                score_grad = (chances * (pulled - shift)).astype(jnp.bfloat16)
+                value_grad = value_grad + tall_dot(chances.astype(jnp.bfloat16), grads)
+                key_grad = key_grad + tall_dot(score_grad, queries)
+                query_grad = (
+                    jnp.dot(score_grad, keys, preferred_element_type=jnp.float32) * scale
+                )
+                raw_ref[rows, columns] = turned(
+                    query_grad, cosine[rows, :], sine[rows, :]
+                ).astype(jnp.bfloat16)
+            key_grads.append(key_grad)
+            value_grads.append(value_grad)
+        key_grad = jnp.concatenate([key_grads[0] + key_grads[1][:half], key_grads[1][half:]], 0)
+        value_grad = jnp.concatenate(
+            [value_grads[0] + value_grads[1][:half], value_grads[1][half:]], 0
+        )
+        raw_ref[:, key_at : key_at + HEAD_DIM] = turned(key_grad * scale, cosine, sine).astype(
+            jnp.bfloat16
+        )
+        raw_ref[:, value_at : value_at + HEAD_DIM] = value_grad.astype(jnp.bfloat16)
+
+
+def attend_back_call(heads, grads, logs, first, cosine, sine):
+    rows_count = heads.shape[0]
+    return pl.pallas_call(
+        attend_back_kernel,
+        out_shape=jax.ShapeDtypeStruct(heads.shape, jnp.bfloat16),
+        in_specs=[whole()] * 6,
+        out_specs=whole(),
+        scratch_shapes=[pltpu.VMEM((rows_count, rows_count), jnp.float32)],
+        compiler_params=pltpu.CompilerParams(vmem_limit_bytes=62 << 20),
+        cost_estimate=small_cost(),
+        name="attend_back",
+    )(heads, grads, logs, first, cosine, sine)
+
+
+def shard_grad_kernel(start_ref, left_ref, right_ref, *refs):
+    parts, grad, sems = refs[:-2], refs[-2], refs[-1]
+    owners, width = len(parts), right_ref.shape[1]
+    pieces, rows = parts[0].shape[0], parts[0].shape[1]
+    tall = owners * rows
+    copies = []
+    for p in range(pieces):
+        for at in range(0, width, WIDE):
+            grad[p * tall : (p + 1) * tall, at : at + WIDE] = tall_dot(
+                left_ref[:, p * tall : (p + 1) * tall], right_ref[:, at : at + WIDE]
+            ).astype(jnp.bfloat16)
+        to = lax.rem(start_ref[0] + pieces - p, pieces)
+        for i, part in enumerate(parts):
+            at = pl.multiple_of(p * tall + start_ref[1 + i] * rows, 16)
+            copy = pltpu.make_async_copy(
+                grad.at[pl.ds(at, rows)], part.at[to], sems.at[p * owners + i]
+            )
+            copy.start()
+            copies.append(copy)
+    for copy in copies:
+        copy.wait()
+
+
+def shard_grad_call(spots, left, right, pieces, owners):
+    width, height = right.shape[1], left.shape[1]
+    rows = height // (pieces * owners)
+    return pl.pallas_call(
+        shard_grad_kernel,
+        out_shape=[jax.ShapeDtypeStruct((pieces, rows, width), jnp.bfloat16)] * owners,
+        in_specs=[scalars(), whole(), whole()],
+        out_specs=[anywhere()] * owners,
+        scratch_shapes=[
+            pltpu.VMEM((height, width), jnp.bfloat16),
+            pltpu.SemaphoreType.DMA((pieces * owners,)),
+        ],
+        compiler_params=pltpu.CompilerParams(vmem_limit_bytes=62 << 20),
+        cost_estimate=small_cost(),
+        name="shard_grad",
+    )(spots, left, right)
+
+
+def entry_back_kernel(planes, start_ref, *refs):
+    raw_ref, tokens_ref, mid_ref, small_ref, logits_grad_ref, gain_two_ref, refs = (
+        *refs[:6],
+        refs[6:],
+    )
+    blocks, refs = refs[:planes], refs[planes:]
+    grad_ref, small_grad_ref, weight, sems = refs
+    step = pl.program_id(0)
+    width = raw_ref.shape[1]
+    experts = small_ref.shape[0] - 8
+    tile = tokens_ref.shape[0]
+
+    @pl.when(step == 0)
+    def _():
+        for copy in load_rows(blocks, start_ref, weight, sems):
+            copy.wait()
+        small_grad_ref[...] = jnp.zeros_like(small_grad_ref)
+        small_grad_ref[experts + 1 : experts + 2, :] = gain_two_ref[...]
+
+    for at in range(0, D, LANES):
+        grad_ref[:, at : at + LANES] = wide_dot(raw_ref[...], weight[at : at + LANES, :width])
+    inputs = tokens_ref[...].astype(jnp.float32)
+    inverse = lax.rsqrt(jnp.mean(inputs * inputs, -1, keepdims=True) + EPS)
+    normed = inputs * inverse
+    grad = grad_ref[...]
+    gain = small_ref[experts : experts + 1, :]
+    product = grad * normed
+    small_grad_ref[experts : experts + 1, :] += jnp.sum(product, 0, keepdims=True)
+    small_grad_ref[:experts, :] += jnp.dot(
+        logits_grad_ref[...], tokens_ref[...], preferred_element_type=jnp.float32
+    )[:experts, :]
+    mean = jnp.mean(product * gain, -1, keepdims=True)
+    row = lax.broadcasted_iota(jnp.int32, (16, 1), 0)
+    router = jnp.where(row < experts, small_ref[...], 0.0).astype(jnp.bfloat16)
+    grad_ref[...] = (
+        mid_ref[...]
+        + inverse * (grad * gain - normed * mean)
+        + tall_dot(logits_grad_ref[...], router)
+    )
+
+
+def entry_back_call(
+    starts, raw_grad, tokens, mid_grad, small, logits_grad, gain_two, blocks, width_early
+):
+    rows_count = tokens.shape[0]
+    tile = rows_count // 2
+    tiled = lambda columns: pl.BlockSpec((tile, columns), lambda i: (i, 0))
+    fixed = lambda rows, columns: pl.BlockSpec((rows, columns), lambda i: (0, 0))
+    return pl.pallas_call(
+        functools.partial(entry_back_kernel, len(blocks)),
+        grid=(2,),
+        out_shape=[
+            jax.ShapeDtypeStruct((rows_count, D), jnp.float32),
+            jax.ShapeDtypeStruct((16, D), jnp.float32),
+        ],
+        in_specs=[
+            scalars(),
+            tiled(raw_grad.shape[1]),
+            tiled(D),
+            tiled(D),
+            fixed(16, D),
+            pl.BlockSpec((16, tile), lambda i: (0, i)),
+            fixed(1, D),
+        ]
+        + [anywhere()] * len(blocks),
+        out_specs=[tiled(D), fixed(16, D)],
+        scratch_shapes=[
+            pltpu.VMEM((D, width_early), jnp.bfloat16),
+            pltpu.SemaphoreType.DMA((len(blocks) * blocks[0].shape[0],)),
+        ],
+        compiler_params=pltpu.CompilerParams(vmem_limit_bytes=62 << 20),
+        cost_estimate=small_cost(),
+        name="entry_back",
+    )(starts, raw_grad, tokens, mid_grad, small, logits_grad, gain_two, *blocks)
+
+
+def pipeline(loads, stores, body, count, later=()):
+    coming = {}
+
+    def fetch(i):
+        coming[i] = loads(i, i % 2)
+        for copy in coming[i]:
+            copy.start()
+
+    leaving = {}
+    fetch(0)
+    for copy in later:
+        copy.start()
+    for i in range(count):
+        if i + 1 < count:
+            fetch(i + 1)
+        for copy in coming.pop(i):
+            copy.wait()
+        for copy in leaving.pop(i - 2, []):
+            copy.wait()
+        body(i, i % 2)
+        leaving[i] = stores(i, i % 2)
+        for copy in leaving[i]:
+            copy.start()
+    for i in sorted(leaving):
+        for copy in leaving[i]:
+            copy.wait()
+
+
+def copies_of(pairs, sems):
+    return [
+        pltpu.make_async_copy(source, target, sems.at[j])
+        for j, (source, target) in enumerate(pairs)
+    ]
+
+
+def hidden_kernel(count, pieces, tokens_count, place_ref, *refs):
+    rows_in, chunks, refs = refs[:count], refs[count : count + pieces], refs[count + pieces :]
+    outs, refs = refs[: 3 * count], refs[3 * count :]
+    weight, rows, slope, product, gated, sems, in_sems, out_sems = refs
+    weight_copies = load_weight(chunks, place_ref, weight, sems)
+
+    def loads(i, slot):
+        return copies_of([(rows_in[i], rows.at[slot])], in_sems.at[slot])
+
+    def stores(i, slot):
+        buffers = (slope, product, gated)
+        return copies_of(
+            [(buffer.at[slot], outs[j * count + i]) for j, buffer in enumerate(buffers)],
+            out_sems.at[slot],
+        )
+
+    def body(i, slot):
+        if i == 0:
+            for copy in weight_copies:
+                copy.wait()
+        weights = spread(expert_row(rows[slot, tokens_count:, :], place_ref[4]), tokens_count)
+        weights = jnp.concatenate([weights] * (LANES // 128), 1)
+        for at in range(0, FF, LANES):
+            gate = jnp.dot(
+                rows[slot, :tokens_count, :],
+                weight[:, at : at + LANES],
+                preferred_element_type=jnp.float32,
+            )
+            up = jnp.dot(
+                rows[slot, :tokens_count, :],
+                weight[:, FF + at : FF + at + LANES],
+                preferred_element_type=jnp.float32,
+            )
+            square = gate * gate
+            bend = jnp.tanh(0.7978845608028654 * gate * (1.0 + 0.044715 * square))
+            half = 0.5 + 0.5 * bend
+            steep = half + 0.5 * gate * (1.0 - bend * bend) * (
+                0.7978845608028654 + 0.10703222440890037 * square
+            )
+            active = gate * half
+            both = (active * up).astype(jnp.bfloat16)
+            slope[slot, :, at : at + LANES] = (up * steep).astype(jnp.bfloat16)
+            slope[slot, :, FF + at : FF + at + LANES] = active.astype(jnp.bfloat16)
+            product[slot, :, at : at + LANES] = both
+            gated[slot, :, at : at + LANES] = (both.astype(jnp.float32) * weights).astype(
+                jnp.bfloat16
+            )
+
+    pipeline(loads, stores, body, count)
+
+
+def hidden_call(rows_in, chunks, places, tokens_count):
+    count = len(rows_in)
+    low = jnp.bfloat16
+    widths = [2 * FF, FF, FF]
+    outs = pl.pallas_call(
+        functools.partial(hidden_kernel, count, len(chunks), tokens_count),
+        out_shape=[
+            jax.ShapeDtypeStruct((tokens_count, width), low)
+            for width in widths
+            for _ in range(count)
+        ],
+        in_specs=[scalars()] + [anywhere()] * (count + len(chunks)),
+        out_specs=[anywhere()] * (3 * count),
+        scratch_shapes=[
+            pltpu.VMEM((D, 2 * FF), low),
+            pltpu.VMEM((2, *rows_in[0].shape), low),
+            *[pltpu.VMEM((2, tokens_count, width), low) for width in widths],
+            pltpu.SemaphoreType.DMA((len(chunks),)),
+            pltpu.SemaphoreType.DMA((2, 1)),
+            pltpu.SemaphoreType.DMA((2, 3)),
+        ],
+        compiler_params=pltpu.CompilerParams(vmem_limit_bytes=62 << 20),
+        cost_estimate=small_cost(),
+        name="expert_hidden",
+    )(places, *rows_in, *chunks)
+    return outs[:count], outs[count : 2 * count], outs[2 * count :]
+
+
+def spread(row, tokens_count):
+    return jnp.transpose(jnp.broadcast_to(row, (128, tokens_count)))
+
+
+def expert_row(block, expert):
+    third = block.shape[1] // 3
+    index = lax.broadcasted_iota(jnp.int32, block.shape, 0)
+    row = jnp.sum(jnp.where(index == expert, block.astype(jnp.float32), 0.0), 0, keepdims=True)
+    return row[:, :third] + row[:, third : 2 * third] + row[:, 2 * third :]
+
+
+def split_row(row):
+    high = row.astype(jnp.bfloat16)
+    rest = row - high.astype(jnp.float32)
+    middle = rest.astype(jnp.bfloat16)
+    low = (rest - middle.astype(jnp.float32)).astype(jnp.bfloat16)
+    return jnp.concatenate(
+        [high.astype(jnp.float32), middle.astype(jnp.float32), low.astype(jnp.float32)], 1
+    )
+
+
+def pull_kernel(count, pieces, tokens_count, place_ref, *refs):
+    packed, cots, slopes, products = (refs[i * count : (i + 1) * count] for i in range(4))
+    refs = refs[4 * count :]
+    in_chunks, out_chunks, refs = refs[: pieces[0]], refs[pieces[0] : sum(pieces)], refs[sum(pieces) :]
+    row_grads, hidden_grads, refs = refs[:count], refs[count : 2 * count], refs[2 * count :]
+    in_weight, out_weight, tail, cot, slope, product, grad, hidden, *sems = refs
+    expert = place_ref[4]
+    in_copies, out_copies = [], []
+
+    def loads(i, slot):
+        copies = copies_of(
+            [
+                (packed[i].at[pl.ds(tokens_count, 16)], tail.at[slot]),
+                (cots[i], cot.at[slot]),
+                (slopes[i], slope.at[slot]),
+                (products[i], product.at[slot]),
+            ],
+            sems[2].at[slot],
+        )
+        return copies
+
+    def stores(i, slot):
+        return copies_of(
+            [(grad.at[slot], row_grads[i]), (hidden.at[slot], hidden_grads[i])], sems[3].at[slot]
+        )
+
+    def body(i, slot):
+        if i == 0:
+            for copy in out_copies:
+                copy.wait()
+        weights = spread(expert_row(tail[slot], expert), tokens_count)
+        weights = jnp.concatenate([weights] * (LANES // 128), 1)
+        gate_grad = jnp.zeros((tokens_count, 1), jnp.float32)
+        for at in range(0, FF, LANES):
+            pulled = wide_dot(cot[slot], out_weight[at : at + LANES, :])
+            both = product[slot, :, at : at + LANES].astype(jnp.float32)
+            gate_grad = gate_grad + jnp.sum(pulled * both, 1, keepdims=True)
+            pulled = pulled * weights
+            for base in (at, FF + at):
+                hidden[slot, :, base : base + LANES] = (
+                    pulled * slope[slot, :, base : base + LANES].astype(jnp.float32)
+                ).astype(jnp.bfloat16)
+        row = jnp.transpose(jnp.broadcast_to(gate_grad, (tokens_count, 128)))[:1, :]
+        parts = jnp.broadcast_to(split_row(row), (16, 3 * tokens_count))
+        index = lax.broadcasted_iota(jnp.int32, parts.shape, 0)
+        grad[slot, tokens_count:, :] = jnp.where(index == expert, parts, 0.0).astype(jnp.bfloat16)
+        if i == 0:
+            for copy in in_copies:
+                copy.wait()
+        for at in range(0, D, LANES):
+            grad[slot, :tokens_count, at : at + LANES] = wide_dot(
+                hidden[slot], in_weight[at : at + LANES, :]
+            ).astype(jnp.bfloat16)
+
+    out_copies += load_weight(out_chunks, place_ref, out_weight, sems[1])
+    in_copies += load_weight(in_chunks, place_ref, in_weight, sems[0], False)
+    pipeline(loads, stores, body, count, in_copies)
+
+
+def pull_call(packed, cots, slopes, products, in_chunks, out_chunks, places, tokens_count):
+    count = len(packed)
+    low = jnp.bfloat16
+    out_shapes = [(tokens_count + 16, D), (tokens_count, 2 * FF)]
+    outs = pl.pallas_call(
+        functools.partial(
+            pull_kernel, count, (len(in_chunks), len(out_chunks)), tokens_count
+        ),
+        out_shape=[jax.ShapeDtypeStruct(shape, low) for shape in out_shapes for _ in range(count)],
+        in_specs=[scalars()] + [anywhere()] * (4 * count + len(in_chunks) + len(out_chunks)),
+        out_specs=[anywhere()] * (2 * count),
+        scratch_shapes=[
+            pltpu.VMEM((D, 2 * FF), low),
+            pltpu.VMEM((FF, D), low),
+            pltpu.VMEM((2, 16, D), low),
+            pltpu.VMEM((2, tokens_count, D), low),
+            pltpu.VMEM((2, tokens_count, 2 * FF), low),
+            pltpu.VMEM((2, tokens_count, FF), low),
+            pltpu.VMEM((2, tokens_count + 16, D), low),
+            pltpu.VMEM((2, tokens_count, 2 * FF), low),
+            pltpu.SemaphoreType.DMA((len(in_chunks),)),
+            pltpu.SemaphoreType.DMA((len(out_chunks),)),
+            pltpu.SemaphoreType.DMA((2, 4)),
+            pltpu.SemaphoreType.DMA((2, 2)),
+        ],
+        compiler_params=pltpu.CompilerParams(vmem_limit_bytes=62 << 20),
+        cost_estimate=small_cost(),
+        name="expert_pull",
+    )(places, *packed, *cots, *slopes, *products, *in_chunks, *out_chunks)
+    return outs[:count], outs[count:]
+
+
+def product_kernel(count, place_ref, *refs):
+    gated, chunks, refs = refs[:count], refs[count : count + 4], refs[count + 4 :]
+    rows_out, (weight, left, total, *sems) = refs[:count], refs[count:]
+    weight_copies = load_weight(chunks, place_ref, weight, sems[0])
+
+    def loads(i, slot):
+        return copies_of([(gated[i], left.at[slot])], sems[1].at[slot])
+
+    def stores(i, slot):
+        return copies_of([(total.at[slot], rows_out[i])], sems[2].at[slot])
+
+    def body(i, slot):
+        if i == 0:
+            for copy in weight_copies:
+                copy.wait()
+        for at in range(0, D, LANES):
+            total[slot, :, at : at + LANES] = jnp.dot(
+                left[slot], weight[:, at : at + LANES], preferred_element_type=jnp.float32
+            ).astype(jnp.bfloat16)
+
+    pipeline(loads, stores, body, count)
+
+
+def product_call(gated, chunks, places):
+    count, rows = len(gated), gated[0].shape[0]
+    return pl.pallas_call(
+        functools.partial(product_kernel, count),
+        out_shape=[jax.ShapeDtypeStruct((rows, D), jnp.bfloat16)] * count,
+        in_specs=[scalars()] + [anywhere()] * (count + 4),
+        out_specs=[anywhere()] * count,
+        scratch_shapes=[
+            pltpu.VMEM((FF, D), jnp.bfloat16),
+            pltpu.VMEM((2, rows, FF), jnp.bfloat16),
+            pltpu.VMEM((2, rows, D), jnp.bfloat16),
+            pltpu.SemaphoreType.DMA((4,)),
+            pltpu.SemaphoreType.DMA((2, 1)),
+            pltpu.SemaphoreType.DMA((2, 1)),
+        ],
+        compiler_params=pltpu.CompilerParams(vmem_limit_bytes=62 << 20),
+        cost_estimate=small_cost(),
+        name="expert_rows",
+    )(places, *gated, *chunks)
+
+
+def weight_grad_kernel(count, rows, *refs):
+    left, right, grad = refs[:count], refs[count : 2 * count], refs[2 * count]
+    total = tall_dot(left[0][:rows, :], right[0][:rows, :])
+    for i in range(1, count):
+        total = total + tall_dot(left[i][:rows, :], right[i][:rows, :])
+    grad[...] = total.astype(grad.dtype)
+
+
+def weight_grad_call(left, right, rows, tall, name):
+    count = len(left)
+    height, width = left[0].shape[1], right[0].shape[1]
+    return pl.pallas_call(
+        functools.partial(weight_grad_kernel, count, rows),
+        grid=(height // tall, width // WIDE),
+        out_shape=jax.ShapeDtypeStruct((height, width), jnp.bfloat16),
+        in_specs=[pl.BlockSpec((rows, tall), lambda i, j: (0, i))] * count
+        + [pl.BlockSpec((rows, WIDE), lambda i, j: (0, j))] * count,
+        out_specs=pl.BlockSpec((tall, WIDE), lambda i, j: (i, j)),
+        compiler_params=pltpu.CompilerParams(vmem_limit_bytes=62 << 20),
+        cost_estimate=small_cost(),
+        name=name,
+    )(*left, *right)
+
+
+def plane_shards(
+    tokens,
+    cotangent,
+    routes,
+    doc_lengths,
+    query_weight,
+    query_first,
+    query_second,
+    keyvalue_weight,
+    keyvalue_first,
+    keyvalue_second,
+    output_weight,
+    output_first,
+    output_second,
+    router_weight,
+    router_first,
+    router_second,
+    norm_gains,
+    gains_first,
+    gains_second,
+    expert_in,
+    expert_in_first,
+    expert_in_second,
+    expert_out,
+    expert_out_first,
+    expert_out_second,
+):
+    rows_count = tokens.shape[0]
+    experts = router_weight.shape[1]
+    columns_dp, owners = lax.axis_size("dp"), lax.axis_size("expert")
+    dp_index, expert_index = lax.axis_index("dp"), lax.axis_index("expert")
+    core = expert_index & 1
+    ring = [(i, (i + 1) % columns_dp) for i in range(columns_dp)]
+    shard = query_weight.shape[0]
+    width_q = HEADS * HEAD_DIM
+    width_qkv = (HEADS + 2 * KV_HEADS) * HEAD_DIM
+    low = jnp.bfloat16
+    places = (dp_index - jnp.arange(columns_dp, dtype=jnp.int32)) % columns_dp
+    starts = (
+        (expert_index ^ jnp.arange(owners, dtype=jnp.int32))[:, None] + places[None, :] * owners
+    ).reshape(-1) * shard
+    places = jnp.concatenate([places, expert_index[None]]).astype(jnp.int32)
+    spots = jnp.concatenate([dp_index[None], expert_index ^ jnp.arange(owners)]).astype(jnp.int32)
+
+    position = jnp.arange(rows_count, dtype=jnp.int32)
+    ends = jnp.cumsum(doc_lengths[0])
+    first = jnp.max(jnp.where(position[:, None] >= ends[None, :], ends[None, :], 0), 1)
+    offset = (position - first).astype(jnp.float32)
+    frequency = ROPE_BASE ** (-2.0 * jnp.arange(HEAD_DIM // 2, dtype=jnp.float32) / HEAD_DIM)
+    angles = offset[:, None] * frequency[None, :]
+    cosine = jnp.tile(jnp.cos(angles), (1, 2))
+    sine = jnp.concatenate([-jnp.sin(angles), jnp.sin(angles)], 1)
+    first = first[:, None]
+
+    width_early = width_qkv + 128
+
+    def cross(block):
+        return to_x(block), to_y(block)
+
+    def onward(from_x, from_y):
+        return jnp.where(core == 0, from_y, from_x)
+
+    sent = jnp.concatenate(
+        [
+            query_weight.astype(low),
+            keyvalue_weight.astype(low),
+            router_weight.astype(low),
+            norm_gains.T.astype(low),
+            jnp.zeros((shard, 128 - experts - 2), low),
+            output_weight.astype(low),
+        ],
+        1,
+    )
+
+    def around(value):
+        return lax.ppermute(value, "dp", ring)
+
+    cot_x, cot_y = cross(cotangent)
+    in_low, out_low = expert_in[0].astype(low), expert_out[0].astype(low)
+    column = [sent, around(sent)]
+    column.append(around(column[1]))
+    column[2], in_low, out_low, cosine, sine, first, routes_t = hold(
+        column[2], in_low, out_low, cosine, sine, first, routes.T
+    )
+    column.append(around(column[2]))
+    joint = jnp.stack(column)
+    cut = in_low.shape[0] * 5 // 8
+    in_near, in_rest = [in_low[:cut]], [in_low[cut:]]
+    cot_x, cot_y, joint, in_near[0], in_rest[0] = hold(
+        cot_x, cot_y, joint, in_near[0], in_rest[0]
+    )
+
+    joint_x, joint_y = cross(joint)
+    joint_core, cot_core = to_core(joint), to_core(cotangent)
+    in_near.append(around(in_near[0]))
+    in_rest.append(around(in_rest[0]))
+    joint_x, joint_y, joint_core, cot_core, in_near[1], in_rest[1] = hold(
+        joint_x, joint_y, joint_core, cot_core, in_near[1], in_rest[1]
+    )
+
+    joint_far = forward(onward(joint_x, joint_y))
+    joint_x2, joint_y2 = to_core(joint_x), to_core(joint_y)
+    cot_x2, cot_y2 = to_core(cot_x), to_core(cot_y)
+    in_near.append(around(in_near[1]))
+    joint_far, joint_x2, joint_y2, cot_x2, cot_y2, in_near[2] = hold(
+        joint_far, joint_x2, joint_y2, cot_x2, cot_y2, in_near[2]
+    )
+    plane = [joint, joint_core, joint_x, joint_x2, joint_y, joint_y2, joint_far]
+    plane.append(to_core(joint_far))
+
+    plane[7], cot_x = hold(plane[7], cot_x)
+    cot_far = forward(onward(cot_x, cot_y))
+    in_near.append(around(in_near[2]))
+    attn_in, heads, attended, logs, small = attend_call(
+        starts, tokens, first, cosine, sine, plane, width_early
+    )
+    attended, cot_far, in_near[3], in_rest[1] = hold(attended, cot_far, in_near[3], in_rest[1])
+    in_rest.append(around(in_rest[1]))
+    residual_mid, packed, gates = middle_call(
+        starts, tokens, attended, routes_t, small, plane, experts, width_early
+    )
+    packed, in_rest[2], out_low, cot_far = hold(packed, in_rest[2], out_low, cot_far)
+
+    packed_x, packed_y = cross(packed)
+    packed_core, cot_far2 = to_core(packed), to_core(cot_far)
+    in_rest.append(around(in_rest[2]))
+    out_chunks = [out_low, around(out_low)]
+    packed_x, packed_y, packed_core, cot_far2, in_rest[3], out_chunks[1] = hold(
+        packed_x, packed_y, packed_core, cot_far2, in_rest[3], out_chunks[1]
+    )
+    cot_blocks = [cotangent, cot_core, cot_x, cot_x2, cot_y, cot_y2, cot_far, cot_far2]
+    in_chunks = in_near + in_rest
+    slopes, products, gated = [None] * 8, [None] * 8, [None] * 8
+
+    def hidden(k, *blocks):
+        outs = hidden_call(blocks, in_chunks, places, rows_count)
+        to = slice(k, k + len(blocks))
+        slopes[to], products[to], gated[to] = outs
+
+    packed_x2, packed_y2 = to_core(packed_x), to_core(packed_y)
+    packed_x, packed_x2, packed_y, packed_y2 = hold(packed_x, packed_x2, packed_y, packed_y2)
+    packed_far = forward(onward(packed_x, packed_y))
+    out_chunks.append(around(out_chunks[1]))
+    hidden(0, packed, packed_core, packed_x, packed_x2)
+    packed_far, gated[0], out_chunks[2] = hold(packed_far, gated[0], out_chunks[2])
+    packed_far2 = to_core(packed_far)
+    packed_far, packed_far2, out_chunks[2] = hold(packed_far, packed_far2, out_chunks[2])
+    out_chunks.append(around(out_chunks[2]))
+    hidden(4, packed_y, packed_y2, packed_far, packed_far2)
+    packed_blocks = [packed, packed_core, packed_x, packed_x2]
+    packed_blocks += [packed_y, packed_y2, packed_far, packed_far2]
+
+    def column_piece(value, back):
+        rows = value.shape[0] // columns_dp
+        return lax.dynamic_slice_in_dim(value, places[back] * rows, rows, 0)
+
+    out_grad = weight_grad_call(gated, cot_blocks, rows_count, FF, "expert_out_grad")
+    out_grad, out_chunks[3] = hold(out_grad, out_chunks[3])
+    moving = column_piece(out_grad, 1)
+    row_grads, hidden_grads = [None] * 8, [None] * 8
+
+    def pull(order, *earlier):
+        def pick(values):
+            return [values[k] for k in order]
+
+        first_cot = after(cot_blocks[order[0]], *earlier)
+        outs = pull_call(
+            pick(packed_blocks),
+            [first_cot] + pick(cot_blocks)[1:],
+            pick(slopes),
+            pick(products),
+            in_chunks,
+            out_chunks,
+            places,
+            rows_count,
+        )
+        for k, row_grad, hidden_grad in zip(order, *outs):
+            row_grads[k], hidden_grads[k] = row_grad, hidden_grad
+
+    moved = around(moving)
+    pull((7, 6), moving)
+    moved, row_grads[6], row_grads[7] = hold(moved, row_grads[6], row_grads[7])
+    far = add_low(row_grads[6], to_core(row_grads[7]))
+    moving = add_low(moved, column_piece(out_grad, 2))
+    far, moving = hold(far, moving)
+    relayed = forward(far)
+    moved = around(moving)
+    pull((0, 1, 3, 2, 5, 4), far, moving)
+    relayed, moved, row_grads[:6] = hold(relayed, moved, row_grads[:6])
+    zero = jnp.zeros((), low)
+    back_x = to_core(row_grads[3])
+    back_y = to_core(row_grads[5])
+    by_x = add_low(row_grads[2], back_x, jnp.where(core == 1, relayed, zero))
+    by_y = add_low(row_grads[4], back_y, jnp.where(core == 0, relayed, zero))
+    moving = add_low(moved, column_piece(out_grad, 3))
+    by_x, by_y, moving = hold(by_x, by_y, moving)
+
+    from_x, from_y = cross(by_x)[0], cross(by_y)[1]
+    moved = around(moving)
+    rows_out = [None] * 8
+
+    def rows_of(order, *earlier):
+        first_gated = after(gated[order[0]], *earlier)
+        outs = product_call(
+            [first_gated] + [gated[k] for k in order[1:]], out_chunks, places
+        )
+        for k, rows in zip(order, outs):
+            rows_out[k] = rows
+
+    rows_of((7, 6), by_x, by_y, moving)
+    hidden_grads[0], rows_out[6] = hold(hidden_grads[0], rows_out[6])
+    in_grad = weight_grad_call(packed_blocks, hidden_grads, rows_count, FF, "expert_in_grad")
+    moving = column_piece(in_grad, 1)
+    from_x, from_y, moved, moving, row_grads[1] = hold(
+        from_x, from_y, moved, moving, row_grads[1]
+    )
+    expert_out_sum = moved.astype(jnp.float32) + column_piece(out_grad, 0).astype(jnp.float32)
+    back_own, rows_back = to_core(row_grads[1]), to_core(rows_out[7])
+    rows_far = add_low(rows_out[6], rows_back)
+    back_own, rows_far, moving = hold(back_own, rows_far, moving)
+
+    rows_relayed = forward(rows_far)
+    moved = around(moving)
+    mid_grad, mid_low, attended_grad, logits_grad, gain_two = middle_back_call(
+        starts, [after(row_grads[0], rows_far, moving), back_own, from_x, from_y], residual_mid,
+        small, cotangent, gates, plane, width_early,
+    )
+    output_parts = shard_grad_call(spots, attended, mid_low, columns_dp, owners)
+    rows_of((5, 4, 3, 2, 1, 0), output_parts[0])
+    rows_relayed, moved, rows_out[:6], output_parts = hold(
+        rows_relayed, moved, rows_out[:6], output_parts
+    )
+    rows_x = add_low(
+        rows_out[2], to_core(rows_out[3]), jnp.where(core == 1, rows_relayed, zero)
+    )
+    rows_y = add_low(
+        rows_out[4], to_core(rows_out[5]), jnp.where(core == 0, rows_relayed, zero)
+    )
+    output_back = [to_core(output_parts[k]) for k in (1, 3, 5, 7)]
+    output_far = add_low(output_parts[6], output_back[3])
+    moving = add_low(moved, column_piece(in_grad, 2))
+    rows_x, rows_y, output_far, moving, output_back = hold(
+        rows_x, rows_y, output_far, moving, output_back
+    )
+
+    rows_from_x, rows_from_y = to_x(rows_x), to_y(rows_y)
+    output_relayed = forward(output_far)
+    moved = around(moving)
+    raw_grad = attend_back_call(
+        heads, after(attended_grad, rows_x, output_far, moving), logs, first, cosine, sine
+    )
+    early_parts = shard_grad_call(spots, attn_in, raw_grad, columns_dp, owners)
+    rows_from_x, rows_from_y, output_relayed, moved, early_parts, rows_out[0] = hold(
+        rows_from_x, rows_from_y, output_relayed, moved, early_parts, rows_out[0]
+    )
+    early_back = [to_core(early_parts[k]) for k in (1, 3, 5, 7)]
+    early_far = add_low(early_parts[6], early_back[3])
+    output_x = add_low(
+        output_parts[2], output_back[1], jnp.where(core == 1, output_relayed, zero)
+    )
+    output_y = add_low(
+        output_parts[4], output_back[2], jnp.where(core == 0, output_relayed, zero)
+    )
+    moving = add_low(moved, column_piece(in_grad, 3))
+    early_far, output_x, output_y, moving, early_back = hold(
+        early_far, output_x, output_y, moving, early_back
+    )
+
+    early_relayed = forward(early_far)
+    output_terms = [output_parts[0], output_back[0], to_x(output_x), to_y(output_y)]
+    tokens_grad, small_grad = entry_back_call(
+        starts, after(raw_grad, early_far, output_x), tokens, mid_grad, small, logits_grad,
+        gain_two, plane, width_early,
+    )
+    early_relayed, output_terms, small_grad = hold(early_relayed, output_terms, small_grad)
+    early_x = add_low(early_parts[2], early_back[1], jnp.where(core == 1, early_relayed, zero))
+    early_y = add_low(early_parts[4], early_back[2], jnp.where(core == 0, early_relayed, zero))
+    small_sum = small_grad + to_core(small_grad)
+    early_x, early_y, small_sum, output_terms = hold(early_x, early_y, small_sum, output_terms)
+    early_terms = [early_parts[0], early_back[0], to_x(early_x), to_y(early_y)]
+    moved = around(moving)
+    small_x = small_sum + to_x(small_sum)
+    small_sum = small_x + to_y(small_x)
+    output_total = add_low(*output_terms)
+    block_out = residual_mid + add_low_wide(
+        rows_out[0], to_core(rows_out[1]), rows_from_x, rows_from_y
+    )
+    mixed_out = block_out.astype(low)
+    early_terms, output_total, moved, small_sum = hold(
+        early_terms, output_total, moved, small_sum
+    )
+    total = jnp.concatenate([add_low(*early_terms), output_total], 2)
+    summed = scatter_pieces([total[p] for p in range(columns_dp)], ring)
+    small_total = small_sum
+    small_moving = small_sum
+    for _ in range(columns_dp - 1):
+        small_moving = around(small_moving)
+        small_total = small_total + small_moving
+    small_own = lax.dynamic_slice_in_dim(
+        small_total.T, (dp_index * owners + expert_index) * shard, shard, 0
+    )
+    expert_in_sum = moved.astype(jnp.float32) + column_piece(in_grad, 0).astype(jnp.float32)
+    at = width_qkv
+    sums = (
+        summed[:, :width_q],
+        summed[:, width_q:at],
+        summed[:, at:],
+        small_own[:, :experts],
+        small_own[:, experts : experts + 2].T,
+        expert_in_sum[None],
+        expert_out_sum[None],
+    )
+    weights = (
+        (query_weight, query_first, query_second),
+        (keyvalue_weight, keyvalue_first, keyvalue_second),
+        (output_weight, output_first, output_second),
+        (router_weight, router_first, router_second),
+        (norm_gains, gains_first, gains_second),
+        (expert_in, expert_in_first, expert_in_second),
+        (expert_out, expert_out_first, expert_out_second),
+    )
+    updates = []
+    for state, grad, rate, decay in zip(
+        weights, sums, learning_rates(), (DECAY, DECAY, DECAY, DECAY, 0.0, DECAY, DECAY)
+    ):
+        updates.extend(adam_update(*state, grad, rate, decay))
+    return (mixed_out, tokens_grad, *updates)
+
+
 def solution(mesh):
     in_specs = (
         P(("dp", "expert"), None),
@@ -435,4 +1653,9 @@
         P("expert", "dp", None),
         P("expert", "dp", None),
     )
-    return jax.shard_map(shards, mesh=mesh, in_specs=in_specs, out_specs=out_specs, check_vma=False)
+    def body(tokens, *rest):
+        one_plane = mesh.shape["expert"] == 8 and rest[12].shape[1] == 8
+        fits = one_plane and 3 * tokens.shape[0] == D
+        return (plane_shards if fits else shards)(tokens, *rest)
+
+    return jax.shard_map(body, mesh=mesh, in_specs=in_specs, out_specs=out_specs, check_vma=False)

time: 1570 us -> 563 us (0.36)
  waiting for transfers between devices: 779 us -> 181 us
  blocking collectives: 269 us -> 0 us
  Pallas kernels: 0 us -> 229 us
  matrix products: 188 us -> 0 us
  local copies, waits for them, and re-layouts: 174 us -> 17.4 us
  other arithmetic: 113 us -> 71.8 us
  starting transfers between devices: 16.3 us -> 51.7 us
    reduce_scatter x5 -> x0, waiting for transfers between devices: 463 us -> none  [the longest x1 139 us: shards(): lax.psum_scatter(output_weight_grad, ('dp', 'expert'), scatter_dimension=...]
    pallas_call x0 -> x15, Pallas kernels: none -> 229 us  [the longest x2 51.5 us: pull_call(): pl.pallas_call(functools.partial(pull_kernel, count, (len(in_chunks), len...]
    dot_general x25 -> x0, matrix products: 188 us -> none  [the longest x1 21.7 us: shards(): jnp.einsum('sicd,sicf->idf', received, hidden_grad, preferred_element_typ...]
    all_gather x5 -> x0, waiting for transfers between devices: 182 us -> none  [the longest x1 88.5 us: shards(): lax.all_gather(expert_in.astype(jnp.bfloat16), 'dp', axis=1, tiled=True)]
    ppermute x0 -> x76, waiting for transfers between devices: none -> 181 us  [the longest x21 112 us: around(): return lax.ppermute(value, 'dp', ring)]
    all_gather x2 -> x0, blocking collectives: 158 us -> none  [the longest x1 115 us: shards(): lax.all_gather(router_weight.astype(jnp.bfloat16), ('dp', 'expert'), axis...]
    all_to_all x1 -> x0, blocking collectives: 112 us -> none  [shards(): lax.all_to_all(send_grad, 'expert', split_axis=0, concat_axis=0, tiled=True)]
    all_to_all x3 -> x0, waiting for transfers between devices: 92.3 us -> none  [the longest x1 79.7 us: shards(): lax.all_to_all(input_rows_grad, 'expert', split_axis=0, concat_axis=0, ti...]
  transfers between devices with their start and end apart: 15 -> 76, of which waited for: 11 -> 30; matrix products, arithmetic and copies ran while one was open for 19% -> 12% of each run, Pallas kernels for 0% -> 41%
where the time goes in v1:
time: 563 us; the launch traced here: 558 us
  Pallas kernels  229 us (41%)
  waiting for transfers between devices  181 us (32%)
  other arithmetic  71.8 us (13%)
  starting transfers between devices  51.7 us (9%)
  local copies, waits for them, and re-layouts  17.4 us (3%)
  between operations  7.16 us (1%)
    ppermute x21, waiting for transfers between devices, around(): return lax.ppermute(value, 'dp', ring)  112 us
    pallas_call x2, Pallas kernels, pull_call(): pl.pallas_call(functools.partial(pull_kernel, count, (len(in_chunks), len...  51.5 us
    pallas_call x2, Pallas kernels, weight_grad_call(): pl.pallas_call(functools.partial(weight_grad_kernel, count, rows), grid=(...  42.9 us
    convert_element_type x16, other arithmetic, add_low(): return total.astype(jnp.bfloat16)  37.5 us
    pallas_call x2, Pallas kernels, hidden_call(): pl.pallas_call(functools.partial(hidden_kernel, count, len(chunks), token...  37.3 us
    ppermute x29, waiting for transfers between devices, to_core(): return lax.ppermute(value, 'expert', ACROSS_CORE)  19.4 us
    pallas_call x2, Pallas kernels, product_call(): pl.pallas_call(functools.partial(product_kernel, count), out_shape=[jax.S...  19.1 us
    pallas_call x1, Pallas kernels, attend_back_call(): pl.pallas_call(attend_back_kernel, out_shape=jax.ShapeDtypeStruct(heads.s...  16.3 us
  transfers between devices with their start and end apart: 76, of which 30 were waited for; matrix products, arithmetic and copies ran while one was open for 12% of the time, Pallas kernels for 41%

profile of v1, /device:TPU:0, one launch (start us, length us, event | category | flops | bytes accessed | tf_op | source)
XLA Modules:
  0.0 558.5 jit_solution(11646296325489647963)
XLA Ops:
  0.7 3.0 collective-permute-start.2
  12.2 1.8 convert_bitcast_fusion
  16.7 4.6 collective-permute-done
  21.4 10.6 %collective-permute-done.1 = bf16[48,3712]{1,0:T(8,128)(2,1)S(1)} collective-permute-done((bf16[48,3712]{1,0:T(8,128)(2,1)}, bf16[48,3712]{1,0:T(8,128)(2,1)S(1)}, u32[]{:S(2)}, u32[]{:S(2)}) %collective-permute-start.1) | collective-permute-done | bytes 356384 | tf_op jit(solution)/shard_map/ppermute | solution.py:1349
  34.5 7.7 %collective-permute-done.4 = bf16[48,3712]{1,0:T(8,128)(2,1)S(1)} collective-permute-done((bf16[48,3712]{1,0:T(8,128)(2,1)S(1)}, bf16[48,3712]{1,0:T(8,128)(2,1)S(1)}, u32[]{:S(2)}, u32[]{:S(2)}) %collective-permute-start.4) | collective-permute-done | bytes 356384 | tf_op jit(solution)/shard_map/ppermute | solution.py:1349
  46.2 29.3 %collective-permute-done.10.refs_9_.refs_13_.refs_29_ = bf16[144,1536]{1,0:T(8,128)(2,1)} collective-permute-done((bf16[144,1536]{1,0:T(8,128)(2,1)}, bf16[144,1536]{1,0:T(8,128)(2,1)}, u32[]{:S(2)}, u32[]{:S(2)}) %collective-permute-start.10) | collective-permute-done | bytes 442400 | tf_op jit(solution)/shard_map/ppermute | solution.py:1349
  76.0 2.0 broadcast_select_fusion.2
  79.7 1.7 collective-permute-done.14.refs_11_.refs_8_
  81.4 18.8 %collective-permute-done.16.refs_6_.refs_10_.refs_26_ = bf16[240,1536]{1,0:T(8,128)(2,1)S(1)} collective-permute-done((bf16[240,1536]{1,0:T(8,128)(2,1)}, bf16[240,1536]{1,0:T(8,128)(2,1)S(1)}, u32[]{:S(2)}, u32[]{:S(2)}) %collective-permute-start.16) | collective-permute-done | bytes 737312 | tf_op jit(solution)/shard_map/ppermute | solution.py:1349
  102.4 2.2 collective-permute-done.17.refs_7_.refs_19_.refs_13_
  104.7 2.7 broadcast_select_fusion.1
  111.0 16.1 %attend.1 = (bf16[512,1536]{1,0:T(8,128)(2,1)}, bf16[512,2048]{1,0:T(8,128)(2,1)}, bf16[512,1536]{1,0:T(8,128)(2,1)}, f32[512,128]{1,0:T(8,128)}, f32[16,1536]{1,0:T(8,128)}) custom-call(s32[32]{0:T(128)} %mul.326.start_ref, bf16[512,1536]{1,0:T(8,128)(2,1)} %refs_1_.1, s32[512,1]{1,0:T(8,128)} %copy.68.first_ref, f32[512,128]{1,0:T(8,128)} %copy.69.cosine_ref, ...), custom_call_target="tpu_custom_call" | custom-call | flops 1024 | bytes 1024 | tf_op jit(solution)/shard_map/attend/pallas_call | solution.py:622
  127.1 2.1 collective-permute-done.19.refs_7_.refs_11_.refs_27_
  129.2 9.6 %middle.1 = (f32[512,1536]{1,0:T(8,128)}, bf16[528,1536]{1,0:T(8,128)(2,1)}, f32[8,512]{1,0:T(8,128)}) custom-call(s32[32]{0:T(128)} %mul.326.start_ref, bf16[512,1536]{1,0:T(8,128)(2,1)} %refs_1_.1, bf16[512,1536]{1,0:T(8,128)(2,1)} %get-tuple-element.272.attended_ref.left_ref, s32[4,512]{1,0:T(4,128)} %bitcast.73, ...), custom_call_target="tpu_custom_call" | custom-call | flops 1024 | bytes 1024 | tf_op jit(solution)/shard_map/middle/pallas_call | solution.py:696
  138.8 4.1 collective-permute-done.20.refs_10_.refs_14_.refs_30_
  144.1 14.0 %collective-permute-done.25.refs_11_.refs_15_.refs_31_ = bf16[144,1536]{1,0:T(8,128)(2,1)} collective-permute-done((bf16[144,1536]{1,0:T(8,128)(2,1)S(1)}, bf16[144,1536]{1,0:T(8,128)(2,1)}, u32[]{:S(2)}, u32[]{:S(2)}) %collective-permute-start.25) | collective-permute-done | bytes 442400 | tf_op jit(solution)/shard_map/ppermute | solution.py:1349
  158.1 16.2 %collective-permute-done.26.refs_17_.refs_33_.refs_3_.refs_7_ = bf16[192,1536]{1,0:T(8,128)(2,1)S(1)} collective-permute-done((bf16[192,1536]{1,0:T(8,128)(2,1)S(1)}, bf16[192,1536]{1,0:T(8,128)(2,1)S(1)}, u32[]{:S(2)}, u32[]{:S(2)}) %collective-permute-start.26) | collective-permute-done | bytes 589856 | tf_op jit(solution)/shard_map/ppermute | solution.py:1349
  174.2 4.9 collective-permute-done.21.refs_2_.refs_3_
  179.7 4.5 collective-permute-done.27.refs_3_.refs_2_
  186.5 1.8 collective-permute-start.29
  189.1 18.6 %expert_hidden.2 = (bf16[512,1536]{1,0:T(8,128)(2,1)}, bf16[512,1536]{1,0:T(8,128)(2,1)}, bf16[512,1536]{1,0:T(8,128)(2,1)}, bf16[512,1536]{1,0:T(8,128)(2,1)}, ...) custom-call(s32[5]{0:T(128)} %pad_add_fusion.place_ref, ...), custom_call_target="tpu_custom_call" | custom-call | flops 1024 | bytes 1024 | tf_op jit(solution)/shard_map/expert_hidden/pallas_call | solution.py:1070
  208.5 3.7 collective-permute-done.31.refs_3_.refs_0_.refs_7_
  214.0 18.7 %expert_hidden.3 = (bf16[512,1536]{1,0:T(8,128)(2,1)}, bf16[512,1536]{1,0:T(8,128)(2,1)}, bf16[512,1536]{1,0:T(8,128)(2,1)}, bf16[512,1536]{1,0:T(8,128)(2,1)}, ...) custom-call(s32[5]{0:T(128)} %pad_add_fusion.place_ref, ...), custom_call_target="tpu_custom_call" | custom-call | flops 1024 | bytes 1024 | tf_op jit(solution)/shard_map/expert_hidden/pallas_call | solution.py:1070
  232.7 16.0 %expert_out_grad.1 = bf16[768,1536]{1,0:T(8,128)(2,1)} custom-call(bf16[512,768]{1,0:T(8,128)(2,1)} %get-tuple-element.294.refs_0_.refs_5_, bf16[512,768]{1,0:T(8,128)(2,1)} %get-tuple-element.295.refs_1_.refs_4_, bf16[512,768]{1,0:T(8,128)(2,1)} %get-tuple-element.296.refs_2_.refs_3_, bf16[512,768]{1,0:T(8,128)(2,1)} %get-tuple-element.297.refs_3_.refs_2_, ...), custom_call_target="tpu_custom_call" | custom-call | flops 1024 | bytes 1024 | tf_op jit(solution)/shard_map/expert_out_grad/pallas_call | solution.py:1261
  249.9 2.1 collective-permute-start.33
  252.0 16.8 %expert_pull.2 = (bf16[528,1536]{1,0:T(8,128)(2,1)}, bf16[528,1536]{1,0:T(8,128)(2,1)}, bf16[512,1536]{1,0:T(8,128)(2,1)}, bf16[512,1536]{1,0:T(8,128)(2,1)}) custom-call(s32[5]{0:T(128)} %pad_add_fusion.place_ref, bf16[528,1536]{1,0:T(8,128)(2,1)} %copy-done.10, bf16[528,1536]{1,0:T(8,128)(2,1)} %collective-permute-done.29.refs_2_.refs_1_.refs_6_, ...), custom_call_target="tpu_custom_call" | custom-call | flops 1024 | bytes 1024 | tf_op jit(solution)/shard_map/expert_pull/pallas_call | solution.py:1178
  269.6 2.1 add_convert_fusion.18
  272.8 1.8 add_convert_fusion.2
  275.0 2.9 collective-permute-start.36
  277.9 34.6 %expert_pull.3 = (bf16[528,1536]{1,0:T(8,128)(2,1)}, bf16[528,1536]{1,0:T(8,128)(2,1)}, bf16[528,1536]{1,0:T(8,128)(2,1)}, bf16[528,1536]{1,0:T(8,128)(2,1)}, bf...) custom-call(s32[5]{0:T(128)} %pad_add_fusion.place_ref, ...), custom_call_target="tpu_custom_call" | custom-call | flops 1024 | bytes 1024 | tf_op jit(solution)/shard_map/expert_pull/pallas_call | solution.py:1178
  313.8 2.2 add_convert_fusion.17
  316.0 1.9 collective-permute-done.37
  318.8 5.5 add_convert_fusion
  324.3 1.7 collective-permute-start.39
  326.5 6.7 %expert_rows.2 = (bf16[512,1536]{1,0:T(8,128)(2,1)}, bf16[512,1536]{1,0:T(8,128)(2,1)}) custom-call(s32[5]{0:T(128)} %pad_add_fusion.place_ref, bf16[512,768]{1,0:T(8,128)(2,1)} %get-tuple-element.355.refs_7_.refs_0_, bf16[512,768]{1,0:T(8,128)(2,1)} %get-tuple-element.305.refs_6_.refs_1_, bf16[192,1536]{1,0:T(8,128)(2,1)} %copy-done.7, ...), custom_call_target="tpu_custom_call" | custom-call | flops 1024 | bytes 1024 | tf_op jit(solution)/shard_map/expert_rows/pallas_call | solution.py:1231
  334.0 26.9 %expert_in_grad.1 = bf16[1536,1536]{1,0:T(8,128)(2,1)} custom-call(bf16[528,1536]{1,0:T(8,128)(2,1)} %get-tuple-element.280.refs_0_, bf16[528,1536]{1,0:T(8,128)(2,1)} %copy-done.8, bf16[528,1536]{1,0:T(8,128)(2,1)} %copy-done.2, bf16[528,1536]{1,0:T(8,128)(2,1)} %copy-done.9, bf16[528,1536]{1,0:T(8,128)(2,1)} %copy-done.3, ...), custom_call_target="tpu_custom_call" | custom-call | flops 1024 | bytes 1024 | tf_op jit(solution)/shard_map/expert_in_grad/pallas_call | solution.py:1261
  360.8 2.5 constant_dynamic-slice_fusion
  363.9 3.0 add_convert_fusion.6
  370.4 11.7 %middle_back.1 = (f32[512,1536]{1,0:T(8,128)}, bf16[512,1536]{1,0:T(8,128)(2,1)}, bf16[512,1536]{1,0:T(8,128)(2,1)}, bf16[16,512]{1,0:T(8,128)(2,1)}, f32[1,1536]{1,0:T(1,128)}) custom-call(s32[32]{0:T(128)} %mul.326.start_ref, bf16[528,1536]{1,0:T(8,128)(2,1)} %get-tuple-element.373.refs_0_.refs_4_, bf16[528,1536]{1,0:T(8,128)(2,1)} %copy-done.19, ...), custom_call_target="tpu_custom_call" | custom-call | flops 1024 | bytes 1024 | tf_op jit(solution)/shard_map/middle_back/pallas_call | solution.py:778
  382.1 5.8 %shard_grad.2 = (bf16[4,48,1536]{2,1,0:T(8,128)(2,1)}, bf16[4,48,1536]{2,1,0:T(8,128)(2,1)}, bf16[4,48,1536]{2,1,0:T(8,128)(2,1)}, bf16[4,48,1536]{2,1,0:T(8,128...) custom-call(s32[9]{0:T(128)} %pad_add_fusion.1.start_ref, ...), custom_call_target="tpu_custom_call" | custom-call | flops 1024 | bytes 1024 | tf_op jit(solution)/shard_map/shard_grad/pallas_call | solution.py:889
  387.9 12.3 %expert_rows.3 = (bf16[512,1536]{1,0:T(8,128)(2,1)}, bf16[512,1536]{1,0:T(8,128)(2,1)}, bf16[512,1536]{1,0:T(8,128)(2,1)}, bf16[512,1536]{1,0:T(8,128)(2,1)}, bf...) custom-call(s32[5]{0:T(128)} %pad_add_fusion.place_ref, bf16[512,768]{1,0:T(8,128)(2,1)} %get-tuple-element.380.refs_5_.refs_0_, ...), custom_call_target="tpu_custom_call" | custom-call | flops 1024 | bytes 1024 | tf_op jit(solution)/shard_map/expert_rows/pallas_call | solution.py:1231
  402.7 3.0 add_convert_fusion.8
  407.2 2.1 collective-permute-done.47
  409.3 4.9 add_convert_fusion.4
  417.6 2.2 collective-permute-start.55
  420.8 16.3 %attend_back.1.right_ref.refs_0_ = bf16[512,2048]{1,0:T(8,128)(2,1)} custom-call(bf16[512,2048]{1,0:T(8,128)(2,1)} %get-tuple-element.410.heads_ref, bf16[512,1536]{1,0:T(8,128)(2,1)} %get-tuple-element.412.grad_ref, f32[512,128]{1,0:T(8,128)} %get-tuple-element.413.log_ref, s32[512,1]{1,0:T(8,128)} %copy.68.first_ref, f32[512,128]{1,0:T(8,128)} %copy.69.cosine_ref, ...), custom_call_target="tpu_custom_call" | custom-call | flops 1024 | bytes 1024 | tf_op jit(solution)/shard_map/attend_back/pallas_call | solution.py:851
  437.1 7.3 %shard_grad.3 = (bf16[4,48,2048]{2,1,0:T(8,128)(2,1)}, bf16[4,48,2048]{2,1,0:T(8,128)(2,1)}, bf16[4,48,2048]{2,1,0:T(8,128)(2,1)}, bf16[4,48,2048]{2,1,0:T(8,128...) custom-call(s32[9]{0:T(128)} %pad_add_fusion.1.start_ref, ...), custom_call_target="tpu_custom_call" | custom-call | flops 1024 | bytes 1024 | tf_op jit(solution)/shard_map/shard_grad/pallas_call | solution.py:889
  444.4 14.1 %collective-permute-done.54 = bf16[4,48,1536]{2,1,0:T(8,128)(2,1)} collective-permute-done((bf16[4,48,1536]{2,1,0:T(8,128)(2,1)}, bf16[4,48,1536]{2,1,0:T(8,128)(2,1)}, u32[]{:S(2)}, u32[]{:S(2)}) %collective-permute-start.54) | collective-permute-done | bytes 589856 | tf_op jit(solution)/shard_map/ppermute | solution.py:418
  459.7 3.3 add_convert_fusion.14
  463.0 3.0 add_convert_fusion.7
  471.8 2.1 collective-permute-start.67
  473.9 11.4 %entry_back.1 = (f32[512,1536]{1,0:T(8,128)}, f32[16,1536]{1,0:T(8,128)}) custom-call(s32[32]{0:T(128)} %mul.326.start_ref, bf16[512,2048]{1,0:T(8,128)(2,1)} %attend_back.1.right_ref.refs_0_, bf16[512,1536]{1,0:T(8,128)(2,1)} %refs_1_.1, f32[512,1536]{1,0:T(8,128)} %get-tuple-element.441.refs_2_, f32[16,1536]{1,0:T(8,128)} %get-tuple-element.274.small_ref.refs_9_.refs_3_, ...), custom_call_target="tpu_custom_call" | custom-call | flops 1024 | bytes 1024 | tf_op jit(solution)/shard_map/entry_back/pallas_call | solution.py:952
  485.4 6.8 %collective-permute-done.62 = bf16[4,48,1536]{2,1,0:T(8,128)(2,1)} collective-permute-done((bf16[4,48,1536]{2,1,0:T(8,128)(2,1)}, bf16[4,48,1536]{2,1,0:T(8,128)(2,1)}, u32[]{:S(2)}, u32[]{:S(2)}) %collective-permute-start.62) | collective-permute-done | bytes 589856 | tf_op jit(solution)/shard_map/ppermute | solution.py:406
  492.3 3.0 add_convert_fusion.10
  498.6 3.7 multiply_subtract_fusion.1
  504.7 14.1 %collective-permute-done.69 = f32[16,1536]{1,0:T(8,128)S(1)} collective-permute-done((f32[16,1536]{1,0:T(8,128)S(1)}, f32[16,1536]{1,0:T(8,128)S(1)}, u32[]{:S(2)}, u32[]{:S(2)}) %collective-permute-start.69) | collective-permute-done | bytes 98336 | tf_op jit(solution)/shard_map/ppermute | solution.py:410
  518.9 1.8 collective-permute-start.73
  520.6 1.8 add_convert_fusion.9
  522.5 2.8 collective-permute-start.70
  526.6 4.2 add_convert_fusion.3
  530.9 4.2 collective-permute-done.74
  537.7 6.0 %multiply_subtract_fusion = (f32[1,384,1536]{2,1,0:T(8,128)}, f32[1,384,1536]{2,1,0:T(8,128)}, f32[1,384,1536]{2,1,0:T(8,128)}) fusion(f32[1,384,1536]{2,1,0:T(8,128)S(1)} %copy-done.14, bf16[1536,1536]{1,0:T(8,128)(2,1)} %expert_in_grad.1, s32[]{:T(128)S(6)} %select_n.147, bf16[384,1536]{1,0:T(8,128)(2,1)} %collective-permute-done.67, ...), kind=kLoop, calls=%fused_computation.11 | loop fusion | flops 10616832 | bytes 16515076 | tf_op jit(solution)/shard_map/sub | solution.py:95
  543.8 2.8 collective-permute-done.71
  548.6 7.3 %collective-permute-done.72 = bf16[48,3584]{1,0:T(8,128)(2,1)S(1)} collective-permute-done((bf16[48,3584]{1,0:T(8,128)(2,1)S(1)}, bf16[48,3584]{1,0:T(8,128)(2,1)S(1)}, u32[]{:S(2)}, u32[]{:S(2)}) %collective-permute-start.72) | collective-permute-done | bytes 344096 | tf_op jit(solution)/shard_map/ppermute | solution.py:484
  (305 shorter events, 68.0 us)
Async XLA Ops:
  0.7 42.7 %collective-permute-start.2 = (bf16[512,1536]{1,0:T(8,128)(2,1)}, bf16[512,1536]{1,0:T(8,128)(2,1)}, u32[]{:S(2)}, u32[]{:S(2)}) collective-permute-start(bf16[512,1536]{1,0:T(8,128)(2,1)} %refs_10_.1), channel_id=1, source_target_pairs={{0,2},{1,3},{2,0},{3,1},{4,6},{5,7},{6,4},{7,5},{8,10},{9,11},{10,... | collective-permute-start | bytes 4718600 | tf_op jit(solution)/shard_map/ppermute | solution.py:406
  3.7 39.7 %collective-permute-start.3 = (bf16[512,1536]{1,0:T(8,128)(2,1)}, bf16[512,1536]{1,0:T(8,128)(2,1)}, u32[]{:S(2)}, u32[]{:S(2)}) collective-permute-start(bf16[512,1536]{1,0:T(8,128)(2,1)} %refs_10_.1), channel_id=1, source_target_pairs={{0,4},{1,5},{2,6},{3,7},{4,0},{5,1},{6,2},{7,3},{8,12},{9,13},{10,... | collective-permute-start | bytes 4718600 | tf_op jit(solution)/shard_map/ppermute | solution.py:410
  9.8 11.5 %collective-permute-start = (bf16[48,3712]{1,0:T(8,128)(2,1)S(1)}, bf16[48,3712]{1,0:T(8,128)(2,1)}, u32[]{:S(2)}, u32[]{:S(2)}) collective-permute-start(bf16[48,3712]{1,0:T(8,128)(2,1)S(1)} %concatenate.15), channel_id=1, source_target_pairs={{0,8},{8,16},{16,24},{24,0},{1,9},{9,17},{17,25},{25,1},{2,10},{10... | collective-permute-start | bytes 1069064 | tf_op jit(solution)/shard_map/ppermute | solution.py:1349
  21.3 10.7 %collective-permute-start.1 = (bf16[48,3712]{1,0:T(8,128)(2,1)}, bf16[48,3712]{1,0:T(8,128)(2,1)S(1)}, u32[]{:S(2)}, u32[]{:S(2)}) collective-permute-start(bf16[48,3712]{1,0:T(8,128)(2,1)} %collective-permute-done), channel_id=1, source_target_pairs={{0,8},{8,16},{16,24},{24,0},{1,9},{9,17},{17,25},{25,1},{2,10},{10... | collective-permute-start | bytes 1069064 | tf_op jit(solution)/shard_map/ppermute | solution.py:1349
  32.7 9.5 %collective-permute-start.4 = (bf16[48,3712]{1,0:T(8,128)(2,1)S(1)}, bf16[48,3712]{1,0:T(8,128)(2,1)S(1)}, u32[]{:S(2)}, u32[]{:S(2)}) collective-permute-start(bf16[48,3712]{1,0:T(8,128)(2,1)S(1)} %collective-permute-done.1), channel_id=1, source_target_pairs={{0,8},{8,16},{16,24},{24,0},{1,9},{9,17},{17,25},{25,1},{2,10},{10... | collective-permute-start | bytes 1069064 | tf_op jit(solution)/shard_map/ppermute | solution.py:1349
  32.7 12.3 %collective-permute-start.8 = (bf16[512,1536]{1,0:T(8,128)(2,1)S(1)}, bf16[512,1536]{1,0:T(8,128)(2,1)S(1)}, u32[]{:S(2)}, u32[]{:S(2)}) collective-permute-start(bf16[512,1536]{1,0:T(8,128)(2,1)S(1)} %copy-done.11), channel_id=1, source_target_pairs={{0,1},{1,0},{2,3},{3,2},{4,5},{5,4},{6,7},{7,6},{8,9},{9,8},{10,11... | collective-permute-start | bytes 4718600 | tf_op jit(solution)/shard_map/ppermute | solution.py:414
  43.4 32.6 %collective-permute-start.5 = (bf16[4,48,3712]{2,1,0:T(8,128)(2,1)S(1)}, bf16[4,48,3712]{2,1,0:T(8,128)(2,1)S(1)}, u32[]{:S(2)}, u32[]{:S(2)}) collective-permute-start(bf16[4,48,3712]{2,1,0:T(8,128)(2,1)S(1)} %pad_maximum_fusion.refs_0_.refs_12_.refs_6_), channel_id=1, source_target_pairs={{0,2},{1,3},{2,0},{3,1},{4,6},{5,7},{6,4},{7,5},{8,10},{9,11},{10,... | collective-permute-start | bytes 4276232 | tf_op jit(solution)/shard_map/ppermute | solution.py:406
  44.0 32.0 %collective-permute-start.6 = (bf16[4,48,3712]{2,1,0:T(8,128)(2,1)S(1)}, bf16[4,48,3712]{2,1,0:T(8,128)(2,1)}, u32[]{:S(2)}, u32[]{:S(2)}) collective-permute-start(bf16[4,48,3712]{2,1,0:T(8,128)(2,1)S(1)} %pad_maximum_fusion.refs_0_.refs_12_.refs_6_), channel_id=1, source_target_pairs={{0,4},{1,5},{2,6},{3,7},{4,0},{5,1},{6,2},{7,3},{8,12},{9,13},{10,... | collective-permute-start | bytes 4276232 | tf_op jit(solution)/shard_map/ppermute | solution.py:410
  45.0 31.0 %collective-permute-start.7 = (bf16[4,48,3712]{2,1,0:T(8,128)(2,1)S(1)}, bf16[4,48,3712]{2,1,0:T(8,128)(2,1)}, u32[]{:S(2)}, u32[]{:S(2)}) collective-permute-start(bf16[4,48,3712]{2,1,0:T(8,128)(2,1)S(1)} %pad_maximum_fusion.refs_0_.refs_12_.refs_6_), channel_id=1, source_target_pairs={{0,1},{1,0},{2,3},{3,2},{4,5},{5,4},{6,7},{7,6},{8,9},{9,8},{10,11... | collective-permute-start | bytes 4276232 | tf_op jit(solution)/shard_map/ppermute | solution.py:414
  45.0 30.5 %collective-permute-start.9 = (bf16[240,1536]{1,0:T(8,128)(2,1)}, bf16[240,1536]{1,0:T(8,128)(2,1)}, u32[]{:S(2)}, u32[]{:S(2)}) collective-permute-start(bf16[240,1536]{1,0:T(8,128)(2,1)} %slice.49.refs_4_.refs_8_.refs_24_), channel_id=1, source_target_pairs={{0,8},{8,16},{16,24},{24,0},{1,9},{9,17},{17,25},{25,1},{2,10},{10... | collective-permute-start | bytes 2211848 | tf_op jit(solution)/shard_map/ppermute | solution.py:1349
  46.1 29.3 %collective-permute-start.10 = (bf16[144,1536]{1,0:T(8,128)(2,1)}, bf16[144,1536]{1,0:T(8,128)(2,1)}, u32[]{:S(2)}, u32[]{:S(2)}) collective-permute-start(bf16[144,1536]{1,0:T(8,128)(2,1)} %slice.50.refs_8_.refs_12_.refs_28_), channel_id=1, source_target_pairs={{0,8},{8,16},{16,24},{24,0},{1,9},{9,17},{17,25},{25,1},{2,10},{10... | collective-permute-start | bytes 1327112 | tf_op jit(solution)/shard_map/ppermute | solution.py:1349
  78.1 22.1 %collective-permute-start.11 = (bf16[4,48,3712]{2,1,0:T(8,128)(2,1)S(1)}, bf16[4,48,3712]{2,1,0:T(8,128)(2,1)S(1)}, u32[]{:S(2)}, u32[]{:S(2)}) collective-permute-start(bf16[4,48,3712]{2,1,0:T(8,128)(2,1)S(1)} %broadcast_select_fusion.2), channel_id=1, source_target_pairs={{0,2},{1,5},{2,0},{3,7},{4,6},{5,1},{6,4},{7,3},{8,10},{9,13},{10,... | collective-permute-start | bytes 4276232 | tf_op jit(solution)/shard_map/ppermute | solution.py:418
  79.2 21.0 %collective-permute-start.12 = (bf16[4,48,3712]{2,1,0:T(8,128)(2,1)S(1)}, bf16[4,48,3712]{2,1,0:T(8,128)(2,1)S(1)}, u32[]{:S(2)}, u32[]{:S(2)}) collective-permute-start(bf16[4,48,3712]{2,1,0:T(8,128)(2,1)S(1)} %collective-permute-done.5.refs_2_.refs_14_.refs_8_), channel_id=1, source_target_pairs={{0,1},{1,0},{2,3},{3,2},{4,5},{5,4},{6,7},{7,6},{8,9},{9,8},{10,11... | collective-permute-start | bytes 4276232 | tf_op jit(solution)/shard_map/ppermute | solution.py:414
  79.2 21.0 %collective-permute-start.13 = (bf16[4,48,3712]{2,1,0:T(8,128)(2,1)}, bf16[4,48,3712]{2,1,0:T(8,128)(2,1)S(1)}, u32[]{:S(2)}, u32[]{:S(2)}) collective-permute-start(bf16[4,48,3712]{2,1,0:T(8,128)(2,1)} %collective-permute-done.6.refs_4_.refs_16_.refs_10_), channel_id=1, source_target_pairs={{0,1},{1,0},{2,3},{3,2},{4,5},{5,4},{6,7},{7,6},{8,9},{9,8},{10,11... | collective-permute-start | bytes 4276232 | tf_op jit(solution)/shard_map/ppermute | solution.py:414
  79.7 20.5 %collective-permute-start.16 = (bf16[240,1536]{1,0:T(8,128)(2,1)}, bf16[240,1536]{1,0:T(8,128)(2,1)S(1)}, u32[]{:S(2)}, u32[]{:S(2)}) collective-permute-start(bf16[240,1536]{1,0:T(8,128)(2,1)} %collective-permute-done.9.refs_5_.refs_9_.refs_25_), channel_id=1, source_target_pairs={{0,8},{8,16},{16,24},{24,0},{1,9},{9,17},{17,25},{25,1},{2,10},{10... | collective-permute-start | bytes 2211848 | tf_op jit(solution)/shard_map/ppermute | solution.py:1349
  107.4 21.8 %collective-permute-start.18 = (bf16[512,1536]{1,0:T(8,128)(2,1)}, bf16[512,1536]{1,0:T(8,128)(2,1)}, u32[]{:S(2)}, u32[]{:S(2)}) collective-permute-start(bf16[512,1536]{1,0:T(8,128)(2,1)} %broadcast_select_fusion.1), channel_id=1, source_target_pairs={{0,2},{1,5},{2,0},{3,7},{4,6},{5,1},{6,4},{7,3},{8,10},{9,13},{10,... | collective-permute-start | bytes 4718600 | tf_op jit(solution)/shard_map/ppermute | solution.py:418
  108.4 20.8 %collective-permute-start.19 = (bf16[240,1536]{1,0:T(8,128)(2,1)S(1)}, bf16[240,1536]{1,0:T(8,128)(2,1)}, u32[]{:S(2)}, u32[]{:S(2)}) collective-permute-start(bf16[240,1536]{1,0:T(8,128)(2,1)S(1)} %collective-permute-done.16.refs_6_.refs_10_.refs_26_), channel_id=1, source_target_pairs={{0,8},{8,16},{16,24},{24,0},{1,9},{9,17},{17,25},{25,1},{2,10},{10... | collective-permute-start | bytes 2211848 | tf_op jit(solution)/shard_map/ppermute | solution.py:1349
  129.2 13.6 %collective-permute-start.20 = (bf16[144,1536]{1,0:T(8,128)(2,1)}, bf16[144,1536]{1,0:T(8,128)(2,1)S(1)}, u32[]{:S(2)}, u32[]{:S(2)}) collective-permute-start(bf16[144,1536]{1,0:T(8,128)(2,1)} %collective-permute-done.10.refs_9_.refs_13_.refs_29_), channel_id=1, source_target_pairs={{0,8},{8,16},{16,24},{24,0},{1,9},{9,17},{17,25},{25,1},{2,10},{10... | collective-permute-start | bytes 1327112 | tf_op jit(solution)/shard_map/ppermute | solution.py:1349
  142.9 36.2 %collective-permute-start.21 = (bf16[528,1536]{1,0:T(8,128)(2,1)}, bf16[528,1536]{1,0:T(8,128)(2,1)S(1)}, u32[]{:S(2)}, u32[]{:S(2)}) collective-permute-start(bf16[528,1536]{1,0:T(8,128)(2,1)} %get-tuple-element.280.refs_0_), channel_id=1, source_target_pairs={{0,2},{1,3},{2,0},{3,1},{4,6},{5,7},{6,4},{7,5},{8,10},{9,11},{10,... | collective-permute-start | bytes 4866056 | tf_op jit(solution)/shard_map/ppermute | solution.py:406
  142.9 36.2 %collective-permute-start.22 = (bf16[528,1536]{1,0:T(8,128)(2,1)}, bf16[528,1536]{1,0:T(8,128)(2,1)S(1)}, u32[]{:S(2)}, u32[]{:S(2)}) collective-permute-start(bf16[528,1536]{1,0:T(8,128)(2,1)} %get-tuple-element.280.refs_0_), channel_id=1, source_target_pairs={{0,4},{1,5},{2,6},{3,7},{4,0},{5,1},{6,2},{7,3},{8,12},{9,13},{10,... | collective-permute-start | bytes 4866056 | tf_op jit(solution)/shard_map/ppermute | solution.py:410
  143.6 35.5 %collective-permute-start.23 = (bf16[528,1536]{1,0:T(8,128)(2,1)}, bf16[528,1536]{1,0:T(8,128)(2,1)S(1)}, u32[]{:S(2)}, u32[]{:S(2)}) collective-permute-start(bf16[528,1536]{1,0:T(8,128)(2,1)} %get-tuple-element.280.refs_0_), channel_id=1, source_target_pairs={{0,1},{1,0},{2,3},{3,2},{4,5},{5,4},{6,7},{7,6},{8,9},{9,8},{10,11... | collective-permute-start | bytes 4866056 | tf_op jit(solution)/shard_map/ppermute | solution.py:414
  143.6 30.7 %collective-permute-start.24 = (bf16[512,1536]{1,0:T(8,128)(2,1)}, bf16[512,1536]{1,0:T(8,128)(2,1)S(1)}, u32[]{:S(2)}, u32[]{:S(2)}) collective-permute-start(bf16[512,1536]{1,0:T(8,128)(2,1)} %collective-permute-done.18.refs_14_.refs_3_), channel_id=1, source_target_pairs={{0,1},{1,0},{2,3},{3,2},{4,5},{5,4},{6,7},{7,6},{8,9},{9,8},{10,11... | collective-permute-start | bytes 4718600 | tf_op jit(solution)/shard_map/ppermute | solution.py:414
  144.1 14.0 %collective-permute-start.25 = (bf16[144,1536]{1,0:T(8,128)(2,1)S(1)}, bf16[144,1536]{1,0:T(8,128)(2,1)}, u32[]{:S(2)}, u32[]{:S(2)}) collective-permute-start(bf16[144,1536]{1,0:T(8,128)(2,1)S(1)} %collective-permute-done.20.refs_10_.refs_14_.refs_30_), channel_id=1, source_target_pairs={{0,8},{8,16},{16,24},{24,0},{1,9},{9,17},{17,25},{25,1},{2,10},{10... | collective-permute-start | bytes 1327112 | tf_op jit(solution)/shard_map/ppermute | solution.py:1349
  158.1 16.2 %collective-permute-start.26 = (bf16[192,1536]{1,0:T(8,128)(2,1)S(1)}, bf16[192,1536]{1,0:T(8,128)(2,1)S(1)}, u32[]{:S(2)}, u32[]{:S(2)}) collective-permute-start(bf16[192,1536]{1,0:T(8,128)(2,1)S(1)} %convert_bitcast_fusion.1.refs_16_.refs_32_.refs_2_.refs_6_), channel_id=1, source_target_pairs={{0,8},{8,16},{16,24},{24,0},{1,9},{9,17},{17,25},{25,1},{2,10},{10... | collective-permute-start | bytes 1769480 | tf_op jit(solution)/shard_map/ppermute | solution.py:1349
  186.5 21.3 %collective-permute-start.29 = (bf16[528,1536]{1,0:T(8,128)(2,1)}, bf16[528,1536]{1,0:T(8,128)(2,1)}, u32[]{:S(2)}, u32[]{:S(2)}) collective-permute-start(bf16[528,1536]{1,0:T(8,128)(2,1)} %broadcast_select_fusion), channel_id=1, source_target_pairs={{0,2},{1,5},{2,0},{3,7},{4,6},{5,1},{6,4},{7,3},{8,10},{9,13},{10,... | collective-permute-start | bytes 4866056 | tf_op jit(solution)/shard_map/ppermute | solution.py:418
  188.2 19.4 %collective-permute-start.30 = (bf16[192,1536]{1,0:T(8,128)(2,1)S(1)}, bf16[192,1536]{1,0:T(8,128)(2,1)S(1)}, u32[]{:S(2)}, u32[]{:S(2)}) collective-permute-start(bf16[192,1536]{1,0:T(8,128)(2,1)S(1)} %collective-permute-done.26.refs_17_.refs_33_.refs_3_.refs_7_), channel_id=1, source_target_pairs={{0,8},{8,16},{16,24},{24,0},{1,9},{9,17},{17,25},{25,1},{2,10},{10... | collective-permute-start | bytes 1769480 | tf_op jit(solution)/shard_map/ppermute | solution.py:1349
  212.2 36.5 %collective-permute-start.32 = (bf16[192,1536]{1,0:T(8,128)(2,1)}, bf16[192,1536]{1,0:T(8,128)(2,1)}, u32[]{:S(2)}, u32[]{:S(2)}) collective-permute-start(bf16[192,1536]{1,0:T(8,128)(2,1)} %copy-done.16), channel_id=1, source_target_pairs={{0,8},{8,16},{16,24},{24,0},{1,9},{9,17},{17,25},{25,1},{2,10},{10... | collective-permute-start | bytes 1769480 | tf_op jit(solution)/shard_map/ppermute | solution.py:1349
  249.9 19.0 %collective-permute-start.33 = (bf16[192,1536]{1,0:T(8,128)(2,1)S(1)}, bf16[192,1536]{1,0:T(8,128)(2,1)S(1)}, u32[]{:S(2)}, u32[]{:S(2)}) collective-permute-start(bf16[192,1536]{1,0:T(8,128)(2,1)S(1)} %constant_dynamic-slice_fusion.1), channel_id=1, source_target_pairs={{0,8},{8,16},{16,24},{24,0},{1,9},{9,17},{17,25},{25,1},{2,10},{10... | collective-permute-start | bytes 1769480 | tf_op jit(solution)/shard_map/ppermute | solution.py:1349
  274.6 38.0 %collective-permute-start.35 = (bf16[528,1536]{1,0:T(8,128)(2,1)S(1)}, bf16[528,1536]{1,0:T(8,128)(2,1)}, u32[]{:S(2)}, u32[]{:S(2)}) collective-permute-start(bf16[528,1536]{1,0:T(8,128)(2,1)S(1)} %add_convert_fusion.2), channel_id=1, source_target_pairs={{0,2},{1,5},{2,0},{3,7},{4,6},{5,1},{6,4},{7,3},{8,10},{9,13},{10,... | collective-permute-start | bytes 4866056 | tf_op jit(solution)/shard_map/ppermute | solution.py:418
  275.0 37.6 %collective-permute-start.36 = (bf16[192,1536]{1,0:T(8,128)(2,1)}, bf16[192,1536]{1,0:T(8,128)(2,1)}, u32[]{:S(2)}, u32[]{:S(2)}) collective-permute-start(bf16[192,1536]{1,0:T(8,128)(2,1)} %add_convert_fusion.18), channel_id=1, source_target_pairs={{0,8},{8,16},{16,24},{24,0},{1,9},{9,17},{17,25},{25,1},{2,10},{10... | collective-permute-start | bytes 1769480 | tf_op jit(solution)/shard_map/ppermute | solution.py:1349
  324.3 39.0 %collective-permute-start.39 = (bf16[528,1536]{1,0:T(8,128)(2,1)}, bf16[528,1536]{1,0:T(8,128)(2,1)S(1)}, u32[]{:S(2)}, u32[]{:S(2)}) collective-permute-start(bf16[528,1536]{1,0:T(8,128)(2,1)} %get-tuple-element.351), channel_id=1, source_target_pairs={{0,2},{1,3},{2,0},{3,1},{4,6},{5,7},{6,4},{7,5},{8,10},{9,11},{10,... | collective-permute-start | bytes 4866056 | tf_op jit(solution)/shard_map/ppermute | solution.py:406
  326.1 37.5 %collective-permute-start.40 = (bf16[528,1536]{1,0:T(8,128)(2,1)}, bf16[528,1536]{1,0:T(8,128)(2,1)}, u32[]{:S(2)}, u32[]{:S(2)}) collective-permute-start(bf16[528,1536]{1,0:T(8,128)(2,1)} %get-tuple-element.352), channel_id=1, source_target_pairs={{0,4},{1,5},{2,6},{3,7},{4,0},{5,1},{6,2},{7,3},{8,12},{9,13},{10,... | collective-permute-start | bytes 4866056 | tf_op jit(solution)/shard_map/ppermute | solution.py:410
  326.4 36.9 %collective-permute-start.41 = (bf16[192,1536]{1,0:T(8,128)(2,1)}, bf16[192,1536]{1,0:T(8,128)(2,1)}, u32[]{:S(2)}, u32[]{:S(2)}) collective-permute-start(bf16[192,1536]{1,0:T(8,128)(2,1)} %add_convert_fusion.17), channel_id=1, source_target_pairs={{0,8},{8,16},{16,24},{24,0},{1,9},{9,17},{17,25},{25,1},{2,10},{10... | collective-permute-start | bytes 1769480 | tf_op jit(solution)/shard_map/ppermute | solution.py:1349
  333.2 30.7 %collective-permute-start.43 = (bf16[512,1536]{1,0:T(8,128)(2,1)}, bf16[512,1536]{1,0:T(8,128)(2,1)}, u32[]{:S(2)}, u32[]{:S(2)}) collective-permute-start(bf16[512,1536]{1,0:T(8,128)(2,1)} %get-tuple-element.368), channel_id=1, source_target_pairs={{0,1},{1,0},{2,3},{3,2},{4,5},{5,4},{6,7},{7,6},{8,9},{9,8},{10,11... | collective-permute-start | bytes 4718600 | tf_op jit(solution)/shard_map/ppermute | solution.py:414
  368.4 32.1 %collective-permute-start.44 = (bf16[512,1536]{1,0:T(8,128)(2,1)}, bf16[512,1536]{1,0:T(8,128)(2,1)S(1)}, u32[]{:S(2)}, u32[]{:S(2)}) collective-permute-start(bf16[512,1536]{1,0:T(8,128)(2,1)} %add_convert_fusion.6), channel_id=1, source_target_pairs={{0,2},{1,5},{2,0},{3,7},{4,6},{5,1},{6,4},{7,3},{8,10},{9,13},{10,... | collective-permute-start | bytes 4718600 | tf_op jit(solution)/shard_map/ppermute | solution.py:418
  369.6 30.9 %collective-permute-start.45 = (bf16[384,1536]{1,0:T(8,128)(2,1)}, bf16[384,1536]{1,0:T(8,128)(2,1)}, u32[]{:S(2)}, u32[]{:S(2)}) collective-permute-start(bf16[384,1536]{1,0:T(8,128)(2,1)} %constant_dynamic-slice_fusion), channel_id=1, source_target_pairs={{0,8},{8,16},{16,24},{24,0},{1,9},{9,17},{17,25},{25,1},{2,10},{10... | collective-permute-start | bytes 3538952 | tf_op jit(solution)/shard_map/ppermute | solution.py:1349
  400.5 6.7 %collective-permute-start.46 = (bf16[512,1536]{1,0:T(8,128)(2,1)}, bf16[512,1536]{1,0:T(8,128)(2,1)}, u32[]{:S(2)}, u32[]{:S(2)}) collective-permute-start(bf16[512,1536]{1,0:T(8,128)(2,1)} %get-tuple-element.395), channel_id=1, source_target_pairs={{0,1},{1,0},{2,3},{3,2},{4,5},{5,4},{6,7},{7,6},{8,9},{9,8},{10,11... | collective-permute-start | bytes 4718600 | tf_op jit(solution)/shard_map/ppermute | solution.py:414
  400.9 8.5 %collective-permute-start.47 = (bf16[512,1536]{1,0:T(8,128)(2,1)}, bf16[512,1536]{1,0:T(8,128)(2,1)}, u32[]{:S(2)}, u32[]{:S(2)}) collective-permute-start(bf16[512,1536]{1,0:T(8,128)(2,1)} %get-tuple-element.398), channel_id=1, source_target_pairs={{0,1},{1,0},{2,3},{3,2},{4,5},{5,4},{6,7},{7,6},{8,9},{9,8},{10,11... | collective-permute-start | bytes 4718600 | tf_op jit(solution)/shard_map/ppermute | solution.py:414
  402.1 12.1 %collective-permute-start.49 = (bf16[4,48,1536]{2,1,0:T(8,128)(2,1)}, bf16[4,48,1536]{2,1,0:T(8,128)(2,1)S(1)}, u32[]{:S(2)}, u32[]{:S(2)}) collective-permute-start(bf16[4,48,1536]{2,1,0:T(8,128)(2,1)} %get-tuple-element.402), channel_id=1, source_target_pairs={{0,1},{1,0},{2,3},{3,2},{4,5},{5,4},{6,7},{7,6},{8,9},{9,8},{10,11... | collective-permute-start | bytes 1769480 | tf_op jit(solution)/shard_map/ppermute | solution.py:414
  402.3 11.9 %collective-permute-start.50 = (bf16[4,48,1536]{2,1,0:T(8,128)(2,1)}, bf16[4,48,1536]{2,1,0:T(8,128)(2,1)S(1)}, u32[]{:S(2)}, u32[]{:S(2)}) collective-permute-start(bf16[4,48,1536]{2,1,0:T(8,128)(2,1)} %get-tuple-element.403), channel_id=1, source_target_pairs={{0,1},{1,0},{2,3},{3,2},{4,5},{5,4},{6,7},{7,6},{8,9},{9,8},{10,11... | collective-permute-start | bytes 1769480 | tf_op jit(solution)/shard_map/ppermute | solution.py:414
  405.8 8.4 %collective-permute-start.51 = (bf16[4,48,1536]{2,1,0:T(8,128)(2,1)S(1)}, bf16[4,48,1536]{2,1,0:T(8,128)(2,1)S(1)}, u32[]{:S(2)}, u32[]{:S(2)}) collective-permute-start(bf16[4,48,1536]{2,1,0:T(8,128)(2,1)S(1)} %copy-done.66), channel_id=1, source_target_pairs={{0,1},{1,0},{2,3},{3,2},{4,5},{5,4},{6,7},{7,6},{8,9},{9,8},{10,11... | collective-permute-start | bytes 1769480 | tf_op jit(solution)/shard_map/ppermute | solution.py:414
  415.2 43.3 %collective-permute-start.52 = (bf16[512,1536]{1,0:T(8,128)(2,1)}, bf16[512,1536]{1,0:T(8,128)(2,1)S(1)}, u32[]{:S(2)}, u32[]{:S(2)}) collective-permute-start(bf16[512,1536]{1,0:T(8,128)(2,1)} %get-tuple-element.405), channel_id=1, source_target_pairs={{0,2},{1,3},{2,0},{3,1},{4,6},{5,7},{6,4},{7,5},{8,10},{9,11},{10,... | collective-permute-start | bytes 4718600 | tf_op jit(solution)/shard_map/ppermute | solution.py:406
  416.1 42.4 %collective-permute-start.53 = (bf16[512,1536]{1,0:T(8,128)(2,1)}, bf16[512,1536]{1,0:T(8,128)(2,1)}, u32[]{:S(2)}, u32[]{:S(2)}) collective-permute-start(bf16[512,1536]{1,0:T(8,128)(2,1)} %get-tuple-element.406), channel_id=1, source_target_pairs={{0,4},{1,5},{2,6},{3,7},{4,0},{5,1},{6,2},{7,3},{8,12},{9,13},{10,... | collective-permute-start | bytes 4718600 | tf_op jit(solution)/shard_map/ppermute | solution.py:410
  417.6 40.9 %collective-permute-start.55 = (bf16[384,1536]{1,0:T(8,128)(2,1)}, bf16[384,1536]{1,0:T(8,128)(2,1)}, u32[]{:S(2)}, u32[]{:S(2)}) collective-permute-start(bf16[384,1536]{1,0:T(8,128)(2,1)} %add_convert_fusion.8), channel_id=1, source_target_pairs={{0,8},{8,16},{16,24},{24,0},{1,9},{9,17},{17,25},{25,1},{2,10},{10... | collective-permute-start | bytes 3538952 | tf_op jit(solution)/shard_map/ppermute | solution.py:1349
  419.8 38.7 %collective-permute-start.54 = (bf16[4,48,1536]{2,1,0:T(8,128)(2,1)}, bf16[4,48,1536]{2,1,0:T(8,128)(2,1)}, u32[]{:S(2)}, u32[]{:S(2)}) collective-permute-start(bf16[4,48,1536]{2,1,0:T(8,128)(2,1)} %add_convert_fusion.16), channel_id=1, source_target_pairs={{0,2},{1,5},{2,0},{3,7},{4,6},{5,1},{6,4},{7,3},{8,10},{9,13},{10,... | collective-permute-start | bytes 1769480 | tf_op jit(solution)/shard_map/ppermute | solution.py:418
  458.5 7.4 %collective-permute-start.57 = (bf16[4,48,2048]{2,1,0:T(8,128)(2,1)}, bf16[4,48,2048]{2,1,0:T(8,128)(2,1)S(1)}, u32[]{:S(2)}, u32[]{:S(2)}) collective-permute-start(bf16[4,48,2048]{2,1,0:T(8,128)(2,1)} %get-tuple-element.428), channel_id=1, source_target_pairs={{0,1},{1,0},{2,3},{3,2},{4,5},{5,4},{6,7},{7,6},{8,9},{9,8},{10,11... | collective-permute-start | bytes 2359304 | tf_op jit(solution)/shard_map/ppermute | solution.py:414
  459.1 8.0 %collective-permute-start.58 = (bf16[4,48,2048]{2,1,0:T(8,128)(2,1)}, bf16[4,48,2048]{2,1,0:T(8,128)(2,1)}, u32[]{:S(2)}, u32[]{:S(2)}) collective-permute-start(bf16[4,48,2048]{2,1,0:T(8,128)(2,1)} %get-tuple-element.435), channel_id=1, source_target_pairs={{0,1},{1,0},{2,3},{3,2},{4,5},{5,4},{6,7},{7,6},{8,9},{9,8},{10,11... | collective-permute-start | bytes 2359304 | tf_op jit(solution)/shard_map/ppermute | solution.py:414
  459.1 8.0 %collective-permute-start.59 = (bf16[4,48,2048]{2,1,0:T(8,128)(2,1)}, bf16[4,48,2048]{2,1,0:T(8,128)(2,1)}, u32[]{:S(2)}, u32[]{:S(2)}) collective-permute-start(bf16[4,48,2048]{2,1,0:T(8,128)(2,1)} %get-tuple-element.436), channel_id=1, source_target_pairs={{0,1},{1,0},{2,3},{3,2},{4,5},{5,4},{6,7},{7,6},{8,9},{9,8},{10,11... | collective-permute-start | bytes 2359304 | tf_op jit(solution)/shard_map/ppermute | solution.py:414
  459.6 7.5 %collective-permute-start.60 = (bf16[4,48,2048]{2,1,0:T(8,128)(2,1)}, bf16[4,48,2048]{2,1,0:T(8,128)(2,1)}, u32[]{:S(2)}, u32[]{:S(2)}) collective-permute-start(bf16[4,48,2048]{2,1,0:T(8,128)(2,1)} %get-tuple-element.437), channel_id=1, source_target_pairs={{0,1},{1,0},{2,3},{3,2},{4,5},{5,4},{6,7},{7,6},{8,9},{9,8},{10,11... | collective-permute-start | bytes 2359304 | tf_op jit(solution)/shard_map/ppermute | solution.py:414
  467.1 25.0 %collective-permute-start.61 = (bf16[4,48,2048]{2,1,0:T(8,128)(2,1)}, bf16[4,48,2048]{2,1,0:T(8,128)(2,1)}, u32[]{:S(2)}, u32[]{:S(2)}) collective-permute-start(bf16[4,48,2048]{2,1,0:T(8,128)(2,1)} %add_convert_fusion.12), channel_id=1, source_target_pairs={{0,2},{1,5},{2,0},{3,7},{4,6},{5,1},{6,4},{7,3},{8,10},{9,13},{10,... | collective-permute-start | bytes 2359304 | tf_op jit(solution)/shard_map/ppermute | solution.py:418
  468.3 23.8 %collective-permute-start.62 = (bf16[4,48,1536]{2,1,0:T(8,128)(2,1)}, bf16[4,48,1536]{2,1,0:T(8,128)(2,1)}, u32[]{:S(2)}, u32[]{:S(2)}) collective-permute-start(bf16[4,48,1536]{2,1,0:T(8,128)(2,1)} %get-tuple-element.439), channel_id=1, source_target_pairs={{0,2},{1,3},{2,0},{3,1},{4,6},{5,7},{6,4},{7,5},{8,10},{9,11},{10,... | collective-permute-start | bytes 1769480 | tf_op jit(solution)/shard_map/ppermute | solution.py:406
  469.2 22.9 %collective-permute-start.63 = (bf16[4,48,1536]{2,1,0:T(8,128)(2,1)}, bf16[4,48,1536]{2,1,0:T(8,128)(2,1)}, u32[]{:S(2)}, u32[]{:S(2)}) collective-permute-start(bf16[4,48,1536]{2,1,0:T(8,128)(2,1)} %get-tuple-element.451), channel_id=1, source_target_pairs={{0,4},{1,5},{2,6},{3,7},{4,0},{5,1},{6,2},{7,3},{8,12},{9,13},{10,... | collective-permute-start | bytes 1769480 | tf_op jit(solution)/shard_map/ppermute | solution.py:410
  471.8 54.8 %collective-permute-start.56 = (bf16[512,1536]{1,0:T(8,128)(2,1)}, bf16[512,1536]{1,0:T(8,128)(2,1)}, u32[]{:S(2)}, u32[]{:S(2)}) collective-permute-start(bf16[512,1536]{1,0:T(8,128)(2,1)} %get-tuple-element.424), channel_id=1, source_target_pairs={{0,1},{1,0},{2,3},{3,2},{4,5},{5,4},{6,7},{7,6},{8,9},{9,8},{10,11... | collective-permute-start | bytes 4718600 | tf_op jit(solution)/shard_map/ppermute | solution.py:414
  471.8 47.0 %collective-permute-start.67 = (bf16[384,1536]{1,0:T(8,128)(2,1)}, bf16[384,1536]{1,0:T(8,128)(2,1)}, u32[]{:S(2)}, u32[]{:S(2)}) collective-permute-start(bf16[384,1536]{1,0:T(8,128)(2,1)} %add_convert_fusion.7), channel_id=1, source_target_pairs={{0,8},{8,16},{16,24},{24,0},{1,9},{9,17},{17,25},{25,1},{2,10},{10... | collective-permute-start | bytes 3538952 | tf_op jit(solution)/shard_map/ppermute | solution.py:1349
  495.3 7.0 %collective-permute-start.68 = (f32[16,1536]{1,0:T(8,128)S(1)}, f32[16,1536]{1,0:T(8,128)S(1)}, u32[]{:S(2)}, u32[]{:S(2)}) collective-permute-start(f32[16,1536]{1,0:T(8,128)S(1)} %add.327), channel_id=1, source_target_pairs={{0,2},{1,3},{2,0},{3,1},{4,6},{5,7},{6,4},{7,5},{8,10},{9,11},{10,... | collective-permute-start | bytes 294920 | tf_op jit(solution)/shard_map/ppermute | solution.py:406
  496.5 22.4 %collective-permute-start.65 = (bf16[4,48,2048]{2,1,0:T(8,128)(2,1)S(1)}, bf16[4,48,2048]{2,1,0:T(8,128)(2,1)S(1)}, u32[]{:S(2)}, u32[]{:S(2)}) collective-permute-start(bf16[4,48,2048]{2,1,0:T(8,128)(2,1)S(1)} %get-tuple-element.461), channel_id=1, source_target_pairs={{0,2},{1,3},{2,0},{3,1},{4,6},{5,7},{6,4},{7,5},{8,10},{9,11},{10,... | collective-permute-start | bytes 2359304 | tf_op jit(solution)/shard_map/ppermute | solution.py:406
  497.4 21.5 %collective-permute-start.66 = (bf16[4,48,2048]{2,1,0:T(8,128)(2,1)S(1)}, bf16[4,48,2048]{2,1,0:T(8,128)(2,1)S(1)}, u32[]{:S(2)}, u32[]{:S(2)}) collective-permute-start(bf16[4,48,2048]{2,1,0:T(8,128)(2,1)S(1)} %get-tuple-element.462), channel_id=1, source_target_pairs={{0,4},{1,5},{2,6},{3,7},{4,0},{5,1},{6,2},{7,3},{8,12},{9,13},{10,... | collective-permute-start | bytes 2359304 | tf_op jit(solution)/shard_map/ppermute | solution.py:410
  502.3 16.5 %collective-permute-start.69 = (f32[16,1536]{1,0:T(8,128)S(1)}, f32[16,1536]{1,0:T(8,128)S(1)}, u32[]{:S(2)}, u32[]{:S(2)}) collective-permute-start(f32[16,1536]{1,0:T(8,128)S(1)} %add.331), channel_id=1, source_target_pairs={{0,4},{1,5},{2,6},{3,7},{4,0},{5,1},{6,2},{7,3},{8,12},{9,13},{10,... | collective-permute-start | bytes 294920 | tf_op jit(solution)/shard_map/ppermute | solution.py:410
  518.9 6.5 %collective-permute-start.73 = (f32[16,1536]{1,0:T(8,128)S(1)}, f32[16,1536]{1,0:T(8,128)S(1)}, u32[]{:S(2)}, u32[]{:S(2)}) collective-permute-start(f32[16,1536]{1,0:T(8,128)S(1)} %add.332), channel_id=1, source_target_pairs={{0,8},{8,16},{16,24},{24,0},{1,9},{9,17},{17,25},{25,1},{2,10},{10... | collective-permute-start | bytes 294920 | tf_op jit(solution)/shard_map/ppermute | solution.py:1349
  522.5 13.5 %collective-permute-start.70 = (bf16[48,3584]{1,0:T(8,128)(2,1)S(1)}, bf16[48,3584]{1,0:T(8,128)(2,1)S(1)}, u32[]{:S(2)}, u32[]{:S(2)}) collective-permute-start(bf16[48,3584]{1,0:T(8,128)(2,1)S(1)} %fusion.9), channel_id=1, source_target_pairs={{0,8},{8,16},{16,24},{24,0},{1,9},{9,17},{17,25},{25,1},{2,10},{10... | collective-permute-start | bytes 1032200 | tf_op jit(solution)/shard_map/ppermute | solution.py:483
  525.3 9.7 %collective-permute-start.74 = (f32[16,1536]{1,0:T(8,128)S(1)}, f32[16,1536]{1,0:T(8,128)S(1)}, u32[]{:S(2)}, u32[]{:S(2)}) collective-permute-start(f32[16,1536]{1,0:T(8,128)S(1)} %collective-permute-done.73), channel_id=1, source_target_pairs={{0,8},{8,16},{16,24},{24,0},{1,9},{9,17},{17,25},{25,1},{2,10},{10... | collective-permute-start | bytes 294920 | tf_op jit(solution)/shard_map/ppermute | solution.py:1349
  535.0 8.7 %collective-permute-start.75 = (f32[16,1536]{1,0:T(8,128)S(1)}, f32[16,1536]{1,0:T(8,128)S(1)}, u32[]{:S(2)}, u32[]{:S(2)}) collective-permute-start(f32[16,1536]{1,0:T(8,128)S(1)} %collective-permute-done.74), channel_id=1, source_target_pairs={{0,8},{8,16},{16,24},{24,0},{1,9},{9,17},{17,25},{25,1},{2,10},{10... | collective-permute-start | bytes 294920 | tf_op jit(solution)/shard_map/ppermute | solution.py:1349
  536.1 10.5 %collective-permute-start.71 = (bf16[48,3584]{1,0:T(8,128)(2,1)S(1)}, bf16[48,3584]{1,0:T(8,128)(2,1)S(1)}, u32[]{:S(2)}, u32[]{:S(2)}) collective-permute-start(bf16[48,3584]{1,0:T(8,128)(2,1)S(1)} %fusion.5), channel_id=1, source_target_pairs={{0,8},{8,16},{16,24},{24,0},{1,9},{9,17},{17,25},{25,1},{2,10},{10... | collective-permute-start | bytes 1032200 | tf_op jit(solution)/shard_map/ppermute | solution.py:483
  546.8 9.1 %collective-permute-start.72 = (bf16[48,3584]{1,0:T(8,128)(2,1)S(1)}, bf16[48,3584]{1,0:T(8,128)(2,1)S(1)}, u32[]{:S(2)}, u32[]{:S(2)}) collective-permute-start(bf16[48,3584]{1,0:T(8,128)(2,1)S(1)} %fusion.4), channel_id=1, source_target_pairs={{0,8},{8,16},{16,24},{24,0},{1,9},{9,17},{17,25},{25,1},{2,10},{10... | collective-permute-start | bytes 1032200 | tf_op jit(solution)/shard_map/ppermute | solution.py:484
  (80 other events, 830.0 us)

commit v2 on v1

--- a/solution.py
+++ b/solution.py
@@ -414,6 +414,10 @@
     return lax.ppermute(value, "expert", ACROSS_CORE)
 
 
+def to_far(value):
+    return lax.ppermute(value, "expert", flip(6))
+
+
 def forward(value):
     return lax.ppermute(value, "expert", FORWARD)
 
@@ -500,7 +504,7 @@
     return pl.CostEstimate(flops=1024, bytes_accessed=1024, transcendentals=0)
 
 
-def load_rows(blocks, start_ref, joined, sems, column=0):
+def load_rows(blocks, start_ref, joined, sems, column=0, start=True):
     width = joined.shape[1]
     pieces, rows = blocks[0].shape[0], blocks[0].shape[1]
     copies = []
@@ -514,7 +518,7 @@
                     sems.at[i * pieces + p],
                 )
             )
-    for copy in copies:
+    for copy in copies if start else []:
         copy.start()
     return copies
 
@@ -726,9 +730,9 @@
 
 def middle_back_kernel(planes, column, start_ref, *refs):
     terms, tails, refs = refs[:4], refs[4:8], refs[8:]
-    residual_ref, small_ref, cot_ref, gates_ref, refs = *refs[:4], refs[4:]
+    residual_ref, small_ref, cot_ref, tokens_ref, gates_ref, refs = *refs[:5], refs[5:]
     blocks, refs = refs[:planes], refs[planes:]
-    mid_ref, low_ref, attended_grad_ref, logits_grad_ref, gain_ref, weight, sems = refs
+    mid_ref, low_ref, attended_grad_ref, logits_grad_ref, small_grad_ref, weight, sems = refs
     step = pl.program_id(0)
     experts = gates_ref.shape[0]
     rows_count = gates_ref.shape[1]
@@ -736,6 +740,7 @@
     @pl.when(step == 0)
     def _():
         copies = load_rows(blocks, start_ref, weight, sems, column)
+        del copies
         gates = gates_ref[...]
         parts = sum([tail[:experts, :].astype(jnp.float32) for tail in tails])
         grad = (
@@ -747,28 +752,39 @@
         logits_grad_ref[...] = jnp.concatenate(
             [grad, jnp.zeros((16 - experts, rows_count), jnp.float32)], 0
         ).astype(jnp.bfloat16)
-        gain_ref[...] = jnp.zeros_like(gain_ref)
-        for copy in copies:
-            copy.wait()
+        small_grad_ref[...] = jnp.zeros_like(small_grad_ref)
 
     grad = sum([term[...].astype(jnp.float32) for term in terms])
     residual = residual_ref[...]
     inverse = lax.rsqrt(jnp.mean(residual * residual, -1, keepdims=True) + EPS)
     normed = residual * inverse
     product = grad * normed
-    gain_ref[...] += jnp.sum(product, 0, keepdims=True)
+    small_grad_ref[experts : experts + 1, :] += jnp.sum(product, 0, keepdims=True)
+    tile = tokens_ref.shape[0]
+    lanes = pl.ds(pl.multiple_of(step * tile, tile), tile)
+    small_grad_ref[:experts, :] += jnp.dot(
+        logits_grad_ref[:, lanes], tokens_ref[...], preferred_element_type=jnp.float32
+    )[:experts, :]
     gain = small_ref[experts + 1 : experts + 2, :]
     mean = jnp.mean(product * gain, -1, keepdims=True)
     mid = cot_ref[...].astype(jnp.float32) + inverse * (grad * gain - normed * mean)
     mid_ref[...] = mid
     low_ref[...] = mid.astype(jnp.bfloat16)
+
+    @pl.when(step == 0)
+    def _():
+        for copy in load_rows(blocks, start_ref, weight, sems, column, False):
+            copy.wait()
+
     for at in range(0, D, LANES):
         attended_grad_ref[:, at : at + LANES] = wide_dot(
             low_ref[...], weight[at : at + LANES, :]
         ).astype(jnp.bfloat16)
 
 
-def middle_back_call(starts, terms, residual, small, cotangent, gates, blocks, column):
+def middle_back_call(
+    starts, terms, residual, small, cotangent, tokens, gates, blocks, column
+):
     rows_count = residual.shape[0]
     tile = rows_count // 2
     low = jnp.bfloat16
@@ -783,14 +799,14 @@
             jax.ShapeDtypeStruct((rows_count, D), low),
             jax.ShapeDtypeStruct((rows_count, D), low),
             jax.ShapeDtypeStruct((16, rows_count), low),
-            jax.ShapeDtypeStruct((1, D), jnp.float32),
+            jax.ShapeDtypeStruct((16, D), jnp.float32),
         ],
         in_specs=[scalars()]
         + [tiled] * 4
         + [tail] * 4
-        + [tiled, fixed(16, D), tiled, fixed(*gates.shape)]
+        + [tiled, fixed(16, D), tiled, tiled, fixed(*gates.shape)]
         + [anywhere()] * len(blocks),
-        out_specs=[tiled, tiled, tiled, fixed(16, rows_count), fixed(1, D)],
+        out_specs=[tiled, tiled, tiled, fixed(16, rows_count), fixed(16, D)],
         scratch_shapes=[
             pltpu.VMEM((D, D), low),
             pltpu.SemaphoreType.DMA((len(blocks) * blocks[0].shape[0],)),
@@ -798,7 +814,7 @@
         compiler_params=pltpu.CompilerParams(vmem_limit_bytes=62 << 20),
         cost_estimate=small_cost(),
         name="middle_back",
-    )(starts, *terms, *terms, residual, small, cotangent, gates, *blocks)
+    )(starts, *terms, *terms, residual, small, cotangent, tokens, gates, *blocks)
 
 
 def attend_back_kernel(heads_ref, grad_ref, log_ref, first_ref, cosine_ref, sine_ref, raw_ref, bias):
@@ -860,22 +876,27 @@
     )(heads, grads, logs, first, cosine, sine)
 
 
-def shard_grad_kernel(start_ref, left_ref, right_ref, *refs):
-    parts, grad, sems = refs[:-2], refs[-2], refs[-1]
-    owners, width = len(parts), right_ref.shape[1]
-    pieces, rows = parts[0].shape[0], parts[0].shape[1]
+def shard_grad_kernel(extra, start_ref, left_ref, right_ref, *refs):
+    parts, grad, sems = refs[extra:-2], refs[-2], refs[-1]
+    width = right_ref.shape[1]
+    pairs, pieces, rows = parts[0].shape[:3]
+    owners = 2 * pairs
     tall = owners * rows
     copies = []
+    if extra:
+        small = refs[0][...]
+        small = jnp.concatenate([small, jnp.zeros((128 - small.shape[0], D), jnp.float32)], 0)
+        grad[:, width:] = jnp.transpose(small).astype(jnp.bfloat16)
     for p in range(pieces):
         for at in range(0, width, WIDE):
             grad[p * tall : (p + 1) * tall, at : at + WIDE] = tall_dot(
                 left_ref[:, p * tall : (p + 1) * tall], right_ref[:, at : at + WIDE]
             ).astype(jnp.bfloat16)
         to = lax.rem(start_ref[0] + pieces - p, pieces)
-        for i, part in enumerate(parts):
+        for i in range(owners):
             at = pl.multiple_of(p * tall + start_ref[1 + i] * rows, 16)
             copy = pltpu.make_async_copy(
-                grad.at[pl.ds(at, rows)], part.at[to], sems.at[p * owners + i]
+                grad.at[pl.ds(at, rows)], parts[i % 2].at[i // 2, to], sems.at[p * owners + i]
             )
             copy.start()
             copies.append(copy)
@@ -883,14 +904,15 @@
         copy.wait()
 
 
-def shard_grad_call(spots, left, right, pieces, owners):
-    width, height = right.shape[1], left.shape[1]
+def shard_grad_call(spots, left, right, pieces, owners, small=None):
+    extra = [] if small is None else [small]
+    width, height = right.shape[1] + 128 * len(extra), left.shape[1]
     rows = height // (pieces * owners)
     return pl.pallas_call(
-        shard_grad_kernel,
-        out_shape=[jax.ShapeDtypeStruct((pieces, rows, width), jnp.bfloat16)] * owners,
-        in_specs=[scalars(), whole(), whole()],
-        out_specs=[anywhere()] * owners,
+        functools.partial(shard_grad_kernel, len(extra)),
+        out_shape=[jax.ShapeDtypeStruct((owners // 2, pieces, rows, width), jnp.bfloat16)] * 2,
+        in_specs=[scalars()] + [whole()] * (2 + len(extra)),
+        out_specs=[anywhere()] * 2,
         scratch_shapes=[
             pltpu.VMEM((height, width), jnp.bfloat16),
             pltpu.SemaphoreType.DMA((pieces * owners,)),
@@ -898,16 +920,13 @@
         compiler_params=pltpu.CompilerParams(vmem_limit_bytes=62 << 20),
         cost_estimate=small_cost(),
         name="shard_grad",
-    )(spots, left, right)
+    )(spots, left, right, *extra)
 
 
 def entry_back_kernel(planes, start_ref, *refs):
-    raw_ref, tokens_ref, mid_ref, small_ref, logits_grad_ref, gain_two_ref, refs = (
-        *refs[:6],
-        refs[6:],
-    )
+    raw_ref, tokens_ref, mid_ref, small_ref, logits_grad_ref, refs = *refs[:5], refs[5:]
     blocks, refs = refs[:planes], refs[planes:]
-    grad_ref, small_grad_ref, weight, sems = refs
+    grad_ref, weight, sems = refs
     step = pl.program_id(0)
     width = raw_ref.shape[1]
     experts = small_ref.shape[0] - 8
@@ -917,8 +936,6 @@
     def _():
         for copy in load_rows(blocks, start_ref, weight, sems):
             copy.wait()
-        small_grad_ref[...] = jnp.zeros_like(small_grad_ref)
-        small_grad_ref[experts + 1 : experts + 2, :] = gain_two_ref[...]
 
     for at in range(0, D, LANES):
         grad_ref[:, at : at + LANES] = wide_dot(raw_ref[...], weight[at : at + LANES, :width])
@@ -927,12 +944,7 @@
     normed = inputs * inverse
     grad = grad_ref[...]
     gain = small_ref[experts : experts + 1, :]
-    product = grad * normed
-    small_grad_ref[experts : experts + 1, :] += jnp.sum(product, 0, keepdims=True)
-    small_grad_ref[:experts, :] += jnp.dot(
-        logits_grad_ref[...], tokens_ref[...], preferred_element_type=jnp.float32
-    )[:experts, :]
-    mean = jnp.mean(product * gain, -1, keepdims=True)
+    mean = jnp.mean(grad * normed * gain, -1, keepdims=True)
     row = lax.broadcasted_iota(jnp.int32, (16, 1), 0)
     router = jnp.where(row < experts, small_ref[...], 0.0).astype(jnp.bfloat16)
     grad_ref[...] = (
@@ -943,7 +955,7 @@
 
 
 def entry_back_call(
-    starts, raw_grad, tokens, mid_grad, small, logits_grad, gain_two, blocks, width_early
+    starts, raw_grad, tokens, mid_grad, small, logits_grad, blocks, width_early
 ):
     rows_count = tokens.shape[0]
     tile = rows_count // 2
@@ -952,10 +964,7 @@
     return pl.pallas_call(
         functools.partial(entry_back_kernel, len(blocks)),
         grid=(2,),
-        out_shape=[
-            jax.ShapeDtypeStruct((rows_count, D), jnp.float32),
-            jax.ShapeDtypeStruct((16, D), jnp.float32),
-        ],
+        out_shape=jax.ShapeDtypeStruct((rows_count, D), jnp.float32),
         in_specs=[
             scalars(),
             tiled(raw_grad.shape[1]),
@@ -963,10 +972,9 @@
             tiled(D),
             fixed(16, D),
             pl.BlockSpec((16, tile), lambda i: (0, i)),
-            fixed(1, D),
         ]
         + [anywhere()] * len(blocks),
-        out_specs=[tiled(D), fixed(16, D)],
+        out_specs=tiled(D),
         scratch_shapes=[
             pltpu.VMEM((D, width_early), jnp.bfloat16),
             pltpu.SemaphoreType.DMA((len(blocks) * blocks[0].shape[0],)),
@@ -974,7 +982,7 @@
         compiler_params=pltpu.CompilerParams(vmem_limit_bytes=62 << 20),
         cost_estimate=small_cost(),
         name="entry_back",
-    )(starts, raw_grad, tokens, mid_grad, small, logits_grad, gain_two, *blocks)
+    )(starts, raw_grad, tokens, mid_grad, small, logits_grad, *blocks)
 
 
 def pipeline(loads, stores, body, count, later=()):
@@ -1358,90 +1366,97 @@
     column.append(around(column[2]))
     joint = jnp.stack(column)
     cut = in_low.shape[0] * 5 // 8
-    in_near, in_rest = [in_low[:cut]], [in_low[cut:]]
-    cot_x, cot_y, joint, in_near[0], in_rest[0] = hold(
-        cot_x, cot_y, joint, in_near[0], in_rest[0]
-    )
+    cot_x, cot_y, joint, in_low, out_low = hold(cot_x, cot_y, joint, in_low, out_low)
+    in_near, in_rest, out_chunks = [in_low[:cut]], [in_low[cut:]], [out_low]
 
     joint_x, joint_y = cross(joint)
-    joint_core, cot_core = to_core(joint), to_core(cotangent)
+    joint_core = to_core(joint)
     in_near.append(around(in_near[0]))
     in_rest.append(around(in_rest[0]))
-    joint_x, joint_y, joint_core, cot_core, in_near[1], in_rest[1] = hold(
-        joint_x, joint_y, joint_core, cot_core, in_near[1], in_rest[1]
-    )
-
+    joint_x, joint_y, joint_core, in_near, in_rest, cot_x, cot_y = hold(
+        joint_x, joint_y, joint_core, in_near, in_rest, cot_x, cot_y
+    )
     joint_far = forward(onward(joint_x, joint_y))
     joint_x2, joint_y2 = to_core(joint_x), to_core(joint_y)
-    cot_x2, cot_y2 = to_core(cot_x), to_core(cot_y)
+    cot_x2 = to_core(cot_x)
     in_near.append(around(in_near[1]))
-    joint_far, joint_x2, joint_y2, cot_x2, cot_y2, in_near[2] = hold(
-        joint_far, joint_x2, joint_y2, cot_x2, cot_y2, in_near[2]
-    )
-    plane = [joint, joint_core, joint_x, joint_x2, joint_y, joint_y2, joint_far]
-    plane.append(to_core(joint_far))
-
-    plane[7], cot_x = hold(plane[7], cot_x)
-    cot_far = forward(onward(cot_x, cot_y))
+    outward = onward(cot_x, cot_y)
+    joint_far, joint_x2, joint_y2, in_near, in_rest, cot_x2, cot_y, outward = hold(
+        joint_far, joint_x2, joint_y2, in_near, in_rest, cot_x2, cot_y, outward
+    )
+    joint_far2 = to_core(joint_far)
+    joint_far2, outward, cot_y, in_near, in_rest = hold(
+        joint_far2, outward, cot_y, in_near, in_rest
+    )
+    plane = [joint, joint_core, joint_x, joint_x2, joint_y, joint_y2, joint_far, joint_far2]
+
+    cot_far = forward(outward)
+    cot_core, cot_y2 = to_core(cotangent), to_core(cot_y)
     in_near.append(around(in_near[2]))
+    in_rest.append(around(in_rest[1]))
     attn_in, heads, attended, logs, small = attend_call(
         starts, tokens, first, cosine, sine, plane, width_early
     )
-    attended, cot_far, in_near[3], in_rest[1] = hold(attended, cot_far, in_near[3], in_rest[1])
-    in_rest.append(around(in_rest[1]))
     residual_mid, packed, gates = middle_call(
         starts, tokens, attended, routes_t, small, plane, experts, width_early
     )
-    packed, in_rest[2], out_low, cot_far = hold(packed, in_rest[2], out_low, cot_far)
+    packed, cot_far, cot_core, cot_y2, in_near, in_rest, out_chunks = hold(
+        packed, cot_far, cot_core, cot_y2, in_near, in_rest, out_chunks
+    )
 
     packed_x, packed_y = cross(packed)
-    packed_core, cot_far2 = to_core(packed), to_core(cot_far)
+    packed_core = to_core(packed)
     in_rest.append(around(in_rest[2]))
-    out_chunks = [out_low, around(out_low)]
-    packed_x, packed_y, packed_core, cot_far2, in_rest[3], out_chunks[1] = hold(
-        packed_x, packed_y, packed_core, cot_far2, in_rest[3], out_chunks[1]
-    )
+    in_chunks = in_near + in_rest
+    out_chunks.append(around(after(out_chunks[0], in_rest[3])))
+    slopes, products, gated = [None] * 8, [None] * 8, [None] * 8
+    packed_blocks = [packed, packed_core] + [None] * 6
+
+    def hidden(order, *earlier):
+        blocks = [packed_blocks[k] for k in order]
+        blocks[0] = after(blocks[0], *earlier)
+        for k, *outs in zip(order, *hidden_call(blocks, in_chunks, places, rows_count)):
+            slopes[k], products[k], gated[k] = outs
+
+    hidden((0, 1))
+    packed_x, packed_y, gated[0], out_chunks, cot_far = hold(
+        packed_x, packed_y, gated[0], out_chunks, cot_far
+    )
+    outward = onward(packed_x, packed_y)
+    outward, packed_x, packed_y = hold(outward, packed_x, packed_y)
+    packed_x2, packed_y2 = to_core(packed_x), to_core(packed_y)
+    packed_far = forward(outward)
+    cot_far2 = to_core(cot_far)
+    out_chunks.append(around(out_chunks[1]))
     cot_blocks = [cotangent, cot_core, cot_x, cot_x2, cot_y, cot_y2, cot_far, cot_far2]
-    in_chunks = in_near + in_rest
-    slopes, products, gated = [None] * 8, [None] * 8, [None] * 8
-
-    def hidden(k, *blocks):
-        outs = hidden_call(blocks, in_chunks, places, rows_count)
-        to = slice(k, k + len(blocks))
-        slopes[to], products[to], gated[to] = outs
-
-    packed_x2, packed_y2 = to_core(packed_x), to_core(packed_y)
-    packed_x, packed_x2, packed_y, packed_y2 = hold(packed_x, packed_x2, packed_y, packed_y2)
-    packed_far = forward(onward(packed_x, packed_y))
-    out_chunks.append(around(out_chunks[1]))
-    hidden(0, packed, packed_core, packed_x, packed_x2)
-    packed_far, gated[0], out_chunks[2] = hold(packed_far, gated[0], out_chunks[2])
+    packed_blocks[2:6] = [packed_x, packed_x2, packed_y, packed_y2]
+    hidden((2, 4))
+    hidden((3, 5), gated[2])
+    packed_far, out_chunks, gated[3] = hold(packed_far, out_chunks, gated[3])
     packed_far2 = to_core(packed_far)
-    packed_far, packed_far2, out_chunks[2] = hold(packed_far, packed_far2, out_chunks[2])
-    out_chunks.append(around(out_chunks[2]))
-    hidden(4, packed_y, packed_y2, packed_far, packed_far2)
-    packed_blocks = [packed, packed_core, packed_x, packed_x2]
-    packed_blocks += [packed_y, packed_y2, packed_far, packed_far2]
+    packed_blocks[6:] = hold(packed_far, packed_far2)
+    out_chunks.append(around(after(out_chunks[2], packed_far2)))
+    hidden((6, 7))
+    out_grad = weight_grad_call(gated, cot_blocks, rows_count, FF, "expert_out_grad")
+    out_grad, out_chunks = hold(out_grad, out_chunks)
 
     def column_piece(value, back):
         rows = value.shape[0] // columns_dp
         return lax.dynamic_slice_in_dim(value, places[back] * rows, rows, 0)
 
-    out_grad = weight_grad_call(gated, cot_blocks, rows_count, FF, "expert_out_grad")
-    out_grad, out_chunks[3] = hold(out_grad, out_chunks[3])
     moving = column_piece(out_grad, 1)
-    row_grads, hidden_grads = [None] * 8, [None] * 8
+    row_grads, hidden_grads, rows_out = [None] * 8, [None] * 8, [None] * 8
+
+    def pick(values, order):
+        return [values[k] for k in order]
 
     def pull(order, *earlier):
-        def pick(values):
-            return [values[k] for k in order]
-
         first_cot = after(cot_blocks[order[0]], *earlier)
         outs = pull_call(
-            pick(packed_blocks),
-            [first_cot] + pick(cot_blocks)[1:],
-            pick(slopes),
-            pick(products),
+            pick(packed_blocks, order),
+            [first_cot] + pick(cot_blocks, order[1:]),
+            pick(slopes, order),
+            pick(products, order),
             in_chunks,
             out_chunks,
             places,
@@ -1450,138 +1465,167 @@
         for k, row_grad, hidden_grad in zip(order, *outs):
             row_grads[k], hidden_grads[k] = row_grad, hidden_grad
 
-    moved = around(moving)
-    pull((7, 6), moving)
-    moved, row_grads[6], row_grads[7] = hold(moved, row_grads[6], row_grads[7])
-    far = add_low(row_grads[6], to_core(row_grads[7]))
-    moving = add_low(moved, column_piece(out_grad, 2))
-    far, moving = hold(far, moving)
-    relayed = forward(far)
-    moved = around(moving)
-    pull((0, 1, 3, 2, 5, 4), far, moving)
-    relayed, moved, row_grads[:6] = hold(relayed, moved, row_grads[:6])
-    zero = jnp.zeros((), low)
-    back_x = to_core(row_grads[3])
-    back_y = to_core(row_grads[5])
-    by_x = add_low(row_grads[2], back_x, jnp.where(core == 1, relayed, zero))
-    by_y = add_low(row_grads[4], back_y, jnp.where(core == 0, relayed, zero))
-    moving = add_low(moved, column_piece(out_grad, 3))
-    by_x, by_y, moving = hold(by_x, by_y, moving)
-
-    from_x, from_y = cross(by_x)[0], cross(by_y)[1]
-    moved = around(moving)
-    rows_out = [None] * 8
-
     def rows_of(order, *earlier):
         first_gated = after(gated[order[0]], *earlier)
-        outs = product_call(
-            [first_gated] + [gated[k] for k in order[1:]], out_chunks, places
-        )
+        outs = product_call([first_gated] + pick(gated, order[1:]), out_chunks, places)
         for k, rows in zip(order, outs):
             rows_out[k] = rows
 
-    rows_of((7, 6), by_x, by_y, moving)
-    hidden_grads[0], rows_out[6] = hold(hidden_grads[0], rows_out[6])
+    zero = jnp.zeros((), low)
+
+    def by_core(value, wanted):
+        return jnp.where(core == wanted, value, zero)
+
+    rows_of((7, 6), moving)
+    rows_out[6], rows_out[7], moving = hold(rows_out[6], rows_out[7], moving)
+    moved = around(moving)
+    rows_back = to_core(rows_out[7])
+    pull((7, 6), rows_out[6])
+    moved, rows_back, row_grads[6], row_grads[7] = hold(
+        moved, rows_back, row_grads[6], row_grads[7]
+    )
+    far_back = to_core(row_grads[7])
+    rows_far = add_low(rows_out[6], rows_back)
+    moving = add_low(moved, column_piece(out_grad, 2))
+    far_back, rows_far, moving = hold(far_back, rows_far, moving)
+    far = add_low(row_grads[6], far_back)
+    far, rows_far, moving = hold(far, rows_far, moving)
+    relayed, rows_relayed = forward(far), forward(rows_far)
+    moved = around(moving)
+    pull((0, 1, 3, 2, 5, 4), far, rows_far, moving)
+    relayed, moved, row_grads[:6] = hold(relayed, moved, row_grads[:6])
+    back_x, back_y = to_core(row_grads[3]), to_core(row_grads[5])
+    back_own = to_core(row_grads[1])
+    rows_of((5, 4, 3, 2, 1, 0), row_grads[0])
+    moving = add_low(moved, column_piece(out_grad, 3))
+    back_x, back_y, back_own, rows_out[:6], moving = hold(
+        back_x, back_y, back_own, rows_out[:6], moving
+    )
+    by_x = add_low(row_grads[2], back_x, by_core(relayed, 1))
+    by_y = add_low(row_grads[4], back_y, by_core(relayed, 0))
+    by_x, by_y, moving, hidden_grads[0], rows_out[:6], rows_relayed = hold(
+        by_x, by_y, moving, hidden_grads[0], rows_out[:6], rows_relayed
+    )
+
+    from_x, from_y = to_x(by_x), to_y(by_y)
+    moved = around(moving)
+    rows_backs = [to_core(rows_out[k]) for k in (3, 5)]
     in_grad = weight_grad_call(packed_blocks, hidden_grads, rows_count, FF, "expert_in_grad")
-    moving = column_piece(in_grad, 1)
-    from_x, from_y, moved, moving, row_grads[1] = hold(
-        from_x, from_y, moved, moving, row_grads[1]
+    rows_x = add_low(rows_out[2], rows_backs[0], by_core(rows_relayed, 1))
+    rows_y = add_low(rows_out[4], rows_backs[1], by_core(rows_relayed, 0))
+    cut = in_low.shape[0] * 5 // 8
+
+    def in_pieces(back):
+        piece = column_piece(in_grad, back)
+        return piece[:cut], piece[cut:]
+
+    near, rest = in_pieces(1)
+    from_x, from_y, moved, near, rest, rows_out[:2], rows_x, rows_y = hold(
+        from_x, from_y, moved, near, rest, rows_out[:2], rows_x, rows_y
     )
     expert_out_sum = moved.astype(jnp.float32) + column_piece(out_grad, 0).astype(jnp.float32)
-    back_own, rows_back = to_core(row_grads[1]), to_core(rows_out[7])
-    rows_far = add_low(rows_out[6], rows_back)
-    back_own, rows_far, moving = hold(back_own, rows_far, moving)
-
-    rows_relayed = forward(rows_far)
-    moved = around(moving)
-    mid_grad, mid_low, attended_grad, logits_grad, gain_two = middle_back_call(
-        starts, [after(row_grads[0], rows_far, moving), back_own, from_x, from_y], residual_mid,
-        small, cotangent, gates, plane, width_early,
-    )
-    output_parts = shard_grad_call(spots, attended, mid_low, columns_dp, owners)
-    rows_of((5, 4, 3, 2, 1, 0), output_parts[0])
-    rows_relayed, moved, rows_out[:6], output_parts = hold(
-        rows_relayed, moved, rows_out[:6], output_parts
-    )
-    rows_x = add_low(
-        rows_out[2], to_core(rows_out[3]), jnp.where(core == 1, rows_relayed, zero)
-    )
-    rows_y = add_low(
-        rows_out[4], to_core(rows_out[5]), jnp.where(core == 0, rows_relayed, zero)
-    )
-    output_back = [to_core(output_parts[k]) for k in (1, 3, 5, 7)]
-    output_far = add_low(output_parts[6], output_back[3])
-    moving = add_low(moved, column_piece(in_grad, 2))
-    rows_x, rows_y, output_far, moving, output_back = hold(
-        rows_x, rows_y, output_far, moving, output_back
-    )
 
     rows_from_x, rows_from_y = to_x(rows_x), to_y(rows_y)
-    output_relayed = forward(output_far)
-    moved = around(moving)
-    raw_grad = attend_back_call(
-        heads, after(attended_grad, rows_x, output_far, moving), logs, first, cosine, sine
-    )
-    early_parts = shard_grad_call(spots, attn_in, raw_grad, columns_dp, owners)
-    rows_from_x, rows_from_y, output_relayed, moved, early_parts, rows_out[0] = hold(
-        rows_from_x, rows_from_y, output_relayed, moved, early_parts, rows_out[0]
-    )
-    early_back = [to_core(early_parts[k]) for k in (1, 3, 5, 7)]
-    early_far = add_low(early_parts[6], early_back[3])
-    output_x = add_low(
-        output_parts[2], output_back[1], jnp.where(core == 1, output_relayed, zero)
-    )
-    output_y = add_low(
-        output_parts[4], output_back[2], jnp.where(core == 0, output_relayed, zero)
-    )
-    moving = add_low(moved, column_piece(in_grad, 3))
-    early_far, output_x, output_y, moving, early_back = hold(
-        early_far, output_x, output_y, moving, early_back
-    )
+    rows_back = to_core(rows_out[1])
+    near_moved, rest_moved = around(near), around(rest)
+    mid_grad, mid_low, attended_grad, logits_grad, small_grad = middle_back_call(
+        starts, [after(row_grads[0], rows_x), back_own, from_x, from_y], residual_mid,
+        small, cotangent, tokens, gates, plane, width_early,
+    )
+    raw_grad = attend_back_call(heads, attended_grad, logs, first, cosine, sine)
+    early_even, early_odd = shard_grad_call(spots, attn_in, raw_grad, columns_dp, owners)
+    early_even, early_odd, mid_low, rows_back, near_moved, rest_moved = hold(
+        early_even, early_odd, mid_low, rows_back, near_moved, rest_moved
+    )
+    rest = add_low(rest_moved, in_pieces(2)[1])
+    rest, early_odd, rows_from_x, rows_from_y = hold(rest, early_odd, rows_from_x, rows_from_y)
+    early_back = to_core(early_odd)
+    rest_moved = around(rest)
+    near = add_low(near_moved, in_pieces(2)[0])
+    output_even, output_odd = shard_grad_call(
+        spots, attended, mid_low, columns_dp, owners, small_grad
+    )
+    early_back, output_even, output_odd, near, rest_moved = hold(
+        early_back, output_even, output_odd, near, rest_moved
+    )
+    near_moved = around(near)
+    early_far = add_low(early_even[3], early_back[3])
+    early_far, output_odd, output_even = hold(early_far, output_odd, output_even)
 
     early_relayed = forward(early_far)
-    output_terms = [output_parts[0], output_back[0], to_x(output_x), to_y(output_y)]
-    tokens_grad, small_grad = entry_back_call(
-        starts, after(raw_grad, early_far, output_x), tokens, mid_grad, small, logits_grad,
-        gain_two, plane, width_early,
-    )
-    early_relayed, output_terms, small_grad = hold(early_relayed, output_terms, small_grad)
-    early_x = add_low(early_parts[2], early_back[1], jnp.where(core == 1, early_relayed, zero))
-    early_y = add_low(early_parts[4], early_back[2], jnp.where(core == 0, early_relayed, zero))
-    small_sum = small_grad + to_core(small_grad)
-    early_x, early_y, small_sum, output_terms = hold(early_x, early_y, small_sum, output_terms)
-    early_terms = [early_parts[0], early_back[0], to_x(early_x), to_y(early_y)]
-    moved = around(moving)
-    small_x = small_sum + to_x(small_sum)
-    small_sum = small_x + to_y(small_x)
-    output_total = add_low(*output_terms)
-    block_out = residual_mid + add_low_wide(
-        rows_out[0], to_core(rows_out[1]), rows_from_x, rows_from_y
-    )
+    output_back = to_core(output_odd)
+    tokens_grad = entry_back_call(
+        starts, after(raw_grad, early_far), tokens, mid_grad, small, logits_grad,
+        plane, width_early,
+    )
+    early_pairs = add_low(early_even[:3], early_back[:3])
+    rest = add_low(rest_moved, in_pieces(3)[1])
+    early_relayed, output_back, tokens_grad, early_pairs, near_moved, rest = hold(
+        early_relayed, output_back, tokens_grad, early_pairs, near_moved, rest
+    )
+    early_x = add_low(early_pairs[1], by_core(early_relayed, 1))
+    early_y = add_low(early_pairs[2], by_core(early_relayed, 0))
+    output_far = add_low(output_even[3], output_back[3])
+    near = add_low(near_moved, in_pieces(3)[0])
+    early_x, early_y, output_far, near, expert_out_sum, rows_back = hold(
+        early_x, early_y, output_far, near, expert_out_sum, rows_back
+    )
+    early_x, early_y, output_relayed = to_x(early_x), to_y(early_y), forward(output_far)
+    near_moved, rest_moved = around(near), around(rest)
+    output_pairs = add_low(output_even[:3], output_back[:3])
+    block_out = residual_mid + add_low_wide(rows_out[0], rows_back, rows_from_x, rows_from_y)
     mixed_out = block_out.astype(low)
-    early_terms, output_total, moved, small_sum = hold(
-        early_terms, output_total, moved, small_sum
-    )
-    total = jnp.concatenate([add_low(*early_terms), output_total], 2)
-    summed = scatter_pieces([total[p] for p in range(columns_dp)], ring)
-    small_total = small_sum
-    small_moving = small_sum
-    for _ in range(columns_dp - 1):
-        small_moving = around(small_moving)
-        small_total = small_total + small_moving
-    small_own = lax.dynamic_slice_in_dim(
-        small_total.T, (dp_index * owners + expert_index) * shard, shard, 0
-    )
-    expert_in_sum = moved.astype(jnp.float32) + column_piece(in_grad, 0).astype(jnp.float32)
+    early_x, early_y, output_relayed, output_pairs, near_moved, rest_moved = hold(
+        early_x, early_y, output_relayed, output_pairs, near_moved, rest_moved
+    )
+    early_total = add_low(early_pairs[0], early_x, early_y)
+    output_x = add_low(output_pairs[1], by_core(output_relayed, 1))
+    output_y = add_low(output_pairs[2], by_core(output_relayed, 0))
+    early_total, output_x, output_y = hold(early_total, output_x, output_y)
+
+    def spread_pieces(total):
+        return [total[0]] + [
+            lax.ppermute(total[p], "dp", [(i, (i - p) % columns_dp) for i in range(columns_dp)])
+            for p in range(1, columns_dp)
+        ]
+
+    early_pieces = spread_pieces(early_total)
+    output_x, output_y = to_x(output_x), to_y(output_y)
+    expert_in_sum = jnp.concatenate([near_moved, rest_moved]).astype(
+        jnp.float32
+    ) + column_piece(in_grad, 0).astype(jnp.float32)
+    early_pieces, output_x, output_y = hold(early_pieces, output_x, output_y)
+    output_total = add_low(output_pairs[0], output_x, output_y)
+    output_pieces = spread_pieces(output_total)
+    output_sum = add_low_wide(*output_pieces)
+    summed = add_low_wide(*early_pieces)
+    used = sent[:, :width_qkv].astype(jnp.float32)
+    gain_one = sent[:, width_qkv + experts].astype(jnp.float32)
+    gain_one_sum = jnp.sum(used * summed, 1) / gain_one
     at = width_qkv
     sums = (
         summed[:, :width_q],
         summed[:, width_q:at],
-        summed[:, at:],
-        small_own[:, :experts],
-        small_own[:, experts : experts + 2].T,
+        output_sum[:, :D],
+        output_sum[:, D : D + experts],
+        jnp.stack([gain_one_sum, output_sum[:, D + experts]]),
         expert_in_sum[None],
         expert_out_sum[None],
+    )
+    (
+        (query_weight, query_first, query_second),
+        (keyvalue_weight, keyvalue_first, keyvalue_second),
+        (output_weight, output_first, output_second),
+        (router_weight, router_first, router_second),
+        (norm_gains, gains_first, gains_second),
+        _,
+    ) = hold(
+        (query_weight, query_first, query_second),
+        (keyvalue_weight, keyvalue_first, keyvalue_second),
+        (output_weight, output_first, output_second),
+        (router_weight, router_first, router_second),
+        (norm_gains, gains_first, gains_second),
+        early_total,
     )
     weights = (
         (query_weight, query_first, query_second),

time: 563 us -> 543 us (0.964)
  waiting for transfers between devices: 181 us -> 150 us
  Pallas kernels: 229 us -> 239 us
  other arithmetic: 71.8 us -> 79.3 us
  starting transfers between devices: 51.7 us -> 45.5 us
    ppermute x29 -> x22, waiting for transfers between devices: 19.4 us -> 8.7 us  [to_core(): return lax.ppermute(value, 'expert', ACROSS_CORE)]
    pallas_call x2 -> x4, Pallas kernels: 37.3 us -> 47.7 us  [hidden_call(): pl.pallas_call(functools.partial(hidden_kernel, count, len(chunks), token...]
    ppermute x3 -> x6, waiting for transfers between devices: 10 us -> 19.7 us  [spread_pieces(): lax.ppermute(total[p], 'dp', [(i, (i - p) % columns_dp) for i in range(co...]
    ppermute x7, waiting for transfers between devices: 14.2 us -> 4.84 us  [forward(): return lax.ppermute(value, 'expert', FORWARD)]
    ppermute x8 -> x7, waiting for transfers between devices: 11.6 us -> 3.66 us  [to_x(): return lax.ppermute(value, 'expert', ACROSS_X)]
    ppermute x21, waiting for transfers between devices: 112 us -> 104 us  [around(): return lax.ppermute(value, 'dp', ring)]
    ppermute x8 -> x7, waiting for transfers between devices: 14.3 us -> 8.34 us  [to_y(): return lax.ppermute(value, 'expert', ACROSS_Y)]
    sub x6 -> x7, other arithmetic: 13.1 us -> 10.5 us  [adam_update(): weight - rate * (first_hat / (jnp.sqrt(second_hat) + ADAM_EPS) + decay *...]
  transfers between devices with their start and end apart: 76 -> 70, of which waited for: 30 -> 24; matrix products, arithmetic and copies ran while one was open for 12% -> 15% of each run, Pallas kernels for 41% -> 43%
where the time goes in v2:
time: 543 us; the launch traced here: 538 us
  Pallas kernels  239 us (44%)
  waiting for transfers between devices  150 us (28%)
  other arithmetic  79.3 us (15%)
  starting transfers between devices  45.5 us (8%)
  local copies, waits for them, and re-layouts  18.2 us (3%)
  between operations  7.23 us (1%)
    ppermute x21, waiting for transfers between devices, around(): return lax.ppermute(value, 'dp', ring)  104 us
    pallas_call x2, Pallas kernels, pull_call(): pl.pallas_call(functools.partial(pull_kernel, count, (len(in_chunks), len...  51.2 us
    pallas_call x4, Pallas kernels, hidden_call(): pl.pallas_call(functools.partial(hidden_kernel, count, len(chunks), token...  47.7 us
    pallas_call x2, Pallas kernels, weight_grad_call(): pl.pallas_call(functools.partial(weight_grad_kernel, count, rows), grid=(...  42.5 us
    convert_element_type x18, other arithmetic, add_low(): return total.astype(jnp.bfloat16)  39.8 us
    ppermute x6, waiting for transfers between devices, spread_pieces(): lax.ppermute(total[p], 'dp', [(i, (i - p) % columns_dp) for i in range(co...  19.7 us
    pallas_call x2, Pallas kernels, product_call(): pl.pallas_call(functools.partial(product_kernel, count), out_shape=[jax.S...  19.1 us
    pallas_call x1, Pallas kernels, attend_back_call(): pl.pallas_call(attend_back_kernel, out_shape=jax.ShapeDtypeStruct(heads.s...  16.3 us
  transfers between devices with their start and end apart: 70, of which 24 were waited for; matrix products, arithmetic and copies ran while one was open for 15% of the time, Pallas kernels for 43%

profile of v2, /device:TPU:0, one launch (start us, length us, event | category | flops | bytes accessed | tf_op | source)
XLA Modules:
  0.0 538.4 jit_solution(8615504705252570675)
XLA Ops:
  0.7 3.0 collective-permute-start.3
  9.8 1.6 collective-permute-start
  11.7 2.8 convert_bitcast_fusion
  14.6 1.8 fusion.19
  17.5 1.9 pad_maximum_fusion.2.sine_ref
  19.3 2.0 collective-permute-done
  22.2 9.8 %collective-permute-done.1 = bf16[48,3712]{1,0:T(8,128)(2,1)S(1)} collective-permute-done((bf16[48,3712]{1,0:T(8,128)(2,1)}, bf16[48,3712]{1,0:T(8,128)(2,1)S(1)}, u32[]{:S(2)}, u32[]{:S(2)}) %collective-permute-start.1) | collective-permute-done | bytes 356384 | tf_op jit(solution)/shard_map/ppermute | solution.py:1357
  32.7 9.5 %collective-permute-done.4 = bf16[48,3712]{1,0:T(8,128)(2,1)S(1)} collective-permute-done((bf16[48,3712]{1,0:T(8,128)(2,1)S(1)}, bf16[48,3712]{1,0:T(8,128)(2,1)S(1)}, u32[]{:S(2)}, u32[]{:S(2)}) %collective-permute-start.4) | collective-permute-done | bytes 356384 | tf_op jit(solution)/shard_map/ppermute | solution.py:1357
  45.8 29.1 %collective-permute-done.9.refs_7_.refs_13_.refs_29_ = bf16[144,1536]{1,0:T(8,128)(2,1)} collective-permute-done((bf16[144,1536]{1,0:T(8,128)(2,1)S(1)}, bf16[144,1536]{1,0:T(8,128)(2,1)}, u32[]{:S(2)}, u32[]{:S(2)}) %collective-permute-start.9) | collective-permute-done | bytes 442400 | tf_op jit(solution)/shard_map/ppermute | solution.py:1357
  74.9 2.4 collective-permute-done.6.refs_4_.refs_17_.refs_9_
  80.9 2.8 broadcast_select_fusion.1
  83.7 17.9 %collective-permute-done.13.refs_4_.refs_10_.refs_26_ = bf16[240,1536]{1,0:T(8,128)(2,1)S(1)} collective-permute-done((bf16[240,1536]{1,0:T(8,128)(2,1)S(1)}, bf16[240,1536]{1,0:T(8,128)(2,1)S(1)}, u32[]{:S(2)}, u32[]{:S(2)}) %collective-permute-start.13) | collective-permute-done | bytes 737312 | tf_op jit(solution)/shard_map/ppermute | solution.py:1357
  102.3 3.9 collective-permute-done.15.refs_7_.refs_20_.refs_12_
  109.9 16.1 %attend.1 = (bf16[512,1536]{1,0:T(8,128)(2,1)}, bf16[512,2048]{1,0:T(8,128)(2,1)}, bf16[512,1536]{1,0:T(8,128)(2,1)}, f32[512,128]{1,0:T(8,128)}, f32[16,1536]{1,0:T(8,128)}) custom-call(s32[32]{0:T(128)} %mul.325.start_ref, bf16[512,1536]{1,0:T(8,128)(2,1)} %refs_1_.1, s32[512,1]{1,0:T(8,128)} %copy.98.first_ref, f32[512,128]{1,0:T(8,128)} %copy.99.cosine_ref, ...), custom_call_target="tpu_custom_call" | custom-call | flops 1024 | bytes 1024 | tf_op jit(solution)/shard_map/attend/pallas_call | solution.py:626
  126.0 9.6 %middle.1 = (f32[512,1536]{1,0:T(8,128)}, bf16[528,1536]{1,0:T(8,128)(2,1)}, f32[8,512]{1,0:T(8,128)}) custom-call(s32[32]{0:T(128)} %mul.325.start_ref, bf16[512,1536]{1,0:T(8,128)(2,1)} %refs_1_.1, bf16[512,1536]{1,0:T(8,128)(2,1)} %get-tuple-element.311.attended_ref.left_ref, s32[4,512]{1,0:T(4,128)} %bitcast.93, ...), custom_call_target="tpu_custom_call" | custom-call | flops 1024 | bytes 1024 | tf_op jit(solution)/shard_map/middle/pallas_call | solution.py:700
  135.6 1.5 collective-permute-done.20.refs_8_.refs_14_.refs_30_
  139.1 13.8 %collective-permute-done.24.refs_9_.refs_15_.refs_31_ = bf16[144,1536]{1,0:T(8,128)(2,1)S(1)} collective-permute-done((bf16[144,1536]{1,0:T(8,128)(2,1)S(1)}, bf16[144,1536]{1,0:T(8,128)(2,1)S(1)}, u32[]{:S(2)}, u32[]{:S(2)}) %collective-permute-start.24) | collective-permute-done | bytes 442400 | tf_op jit(solution)/shard_map/ppermute | solution.py:1357
  153.7 11.9 %expert_hidden.4 = (bf16[512,1536]{1,0:T(8,128)(2,1)}, bf16[512,1536]{1,0:T(8,128)(2,1)}, bf16[512,768]{1,0:T(8,128)(2,1)}, bf16[512,768]{1,0:T(8,128)(2,1)}, bf...) custom-call(s32[5]{0:T(128)} %pad_add_fusion.place_ref, bf16[528,1536]{1,0:T(8,128)(2,1)} %get-tuple-element.324.refs_0_, ...), custom_call_target="tpu_custom_call" | custom-call | flops 1024 | bytes 1024 | tf_op jit(solution)/shard_map/expert_hidden/pallas_call | solution.py:1078
  165.7 3.8 collective-permute-done.25.refs_3_.refs_17_.refs_33_.refs_7_
  169.5 5.9 %collective-permute-done.22.refs_1_.refs_5_.refs_4_ = bf16[528,1536]{1,0:T(8,128)(2,1)} collective-permute-done((bf16[528,1536]{1,0:T(8,128)(2,1)}, bf16[528,1536]{1,0:T(8,128)(2,1)}, u32[]{:S(2)}, u32[]{:S(2)}) %collective-permute-start.22) | collective-permute-done | bytes 1622048 | tf_op jit(solution)/shard_map/ppermute | solution.py:410
  176.3 2.8 broadcast_select_fusion
  180.2 11.9 %expert_hidden.5 = (bf16[512,1536]{1,0:T(8,128)(2,1)}, bf16[512,1536]{1,0:T(8,128)(2,1)}, bf16[512,768]{1,0:T(8,128)(2,1)}, bf16[512,768]{1,0:T(8,128)(2,1)}, bf...) custom-call(s32[5]{0:T(128)} %pad_add_fusion.place_ref, ...), custom_call_target="tpu_custom_call" | custom-call | flops 1024 | bytes 1024 | tf_op jit(solution)/shard_map/expert_hidden/pallas_call | solution.py:1078
  193.3 11.9 %expert_hidden.6 = (bf16[512,1536]{1,0:T(8,128)(2,1)}, bf16[512,1536]{1,0:T(8,128)(2,1)}, bf16[512,768]{1,0:T(8,128)(2,1)}, bf16[512,768]{1,0:T(8,128)(2,1)}, bf...) custom-call(s32[5]{0:T(128)} %pad_add_fusion.place_ref, bf16[528,1536]{1,0:T(8,128)(2,1)} %copy-done.12, ...), custom_call_target="tpu_custom_call" | custom-call | flops 1024 | bytes 1024 | tf_op jit(solution)/shard_map/expert_hidden/pallas_call | solution.py:1078
  205.9 4.7 collective-permute-done.30.refs_1_.refs_0_.refs_7_
  210.6 3.8 collective-permute-start.32
  215.6 11.9 %expert_hidden.7 = (bf16[512,1536]{1,0:T(8,128)(2,1)}, bf16[512,1536]{1,0:T(8,128)(2,1)}, bf16[512,768]{1,0:T(8,128)(2,1)}, bf16[512,768]{1,0:T(8,128)(2,1)}, bf...) custom-call(s32[5]{0:T(128)} %pad_add_fusion.place_ref, ...), custom_call_target="tpu_custom_call" | custom-call | flops 1024 | bytes 1024 | tf_op jit(solution)/shard_map/expert_hidden/pallas_call | solution.py:1078
  227.6 15.8 %expert_out_grad.1 = bf16[768,1536]{1,0:T(8,128)(2,1)} custom-call(bf16[512,768]{1,0:T(8,128)(2,1)} %get-tuple-element.350.refs_0_.refs_5_, bf16[512,768]{1,0:T(8,128)(2,1)} %get-tuple-element.351.refs_1_.refs_4_, bf16[512,768]{1,0:T(8,128)(2,1)} %get-tuple-element.343.refs_2_.refs_3_, bf16[512,768]{1,0:T(8,128)(2,1)} %get-tuple-element.352.refs_3_.refs_2_, ...), custom_call_target="tpu_custom_call" | custom-call | flops 1024 | bytes 1024 | tf_op jit(solution)/shard_map/expert_out_grad/pallas_call | solution.py:1269
  243.4 2.0 constant_dynamic-slice_fusion.2
  245.4 6.7 %expert_rows.2 = (bf16[512,1536]{1,0:T(8,128)(2,1)}, bf16[512,1536]{1,0:T(8,128)(2,1)}) custom-call(s32[5]{0:T(128)} %pad_add_fusion.place_ref, bf16[512,768]{1,0:T(8,128)(2,1)} %get-tuple-element.365.refs_7_.refs_0_, bf16[512,768]{1,0:T(8,128)(2,1)} %get-tuple-element.355.refs_6_.refs_1_, ...), custom_call_target="tpu_custom_call" | custom-call | flops 1024 | bytes 1024 | tf_op jit(solution)/shard_map/expert_rows/pallas_call | solution.py:1239
  252.6 16.6 %expert_pull.2 = (bf16[528,1536]{1,0:T(8,128)(2,1)}, bf16[528,1536]{1,0:T(8,128)(2,1)}, bf16[512,1536]{1,0:T(8,128)(2,1)}, bf16[512,1536]{1,0:T(8,128)(2,1)}) custom-call(s32[5]{0:T(128)} %pad_add_fusion.place_ref, bf16[528,1536]{1,0:T(8,128)(2,1)} %copy-done.13, bf16[528,1536]{1,0:T(8,128)(2,1)} %collective-permute-done.26.refs_0_.refs_1_.refs_6_, ...), custom_call_target="tpu_custom_call" | custom-call | flops 1024 | bytes 1024 | tf_op jit(solution)/shard_map/expert_pull/pallas_call | solution.py:1186
  270.9 2.2 add_convert_fusion.14
  274.7 1.8 add_convert_fusion.4
  278.9 34.6 %expert_pull.3 = (bf16[528,1536]{1,0:T(8,128)(2,1)}, bf16[528,1536]{1,0:T(8,128)(2,1)}, bf16[528,1536]{1,0:T(8,128)(2,1)}, bf16[528,1536]{1,0:T(8,128)(2,1)}, bf...) custom-call(s32[5]{0:T(128)} %pad_add_fusion.place_ref, ...), custom_call_target="tpu_custom_call" | custom-call | flops 1024 | bytes 1024 | tf_op jit(solution)/shard_map/expert_pull/pallas_call | solution.py:1186
  315.6 12.4 %expert_rows.3 = (bf16[512,1536]{1,0:T(8,128)(2,1)}, bf16[512,1536]{1,0:T(8,128)(2,1)}, bf16[512,1536]{1,0:T(8,128)(2,1)}, bf16[512,1536]{1,0:T(8,128)(2,1)}, bf...) custom-call(s32[5]{0:T(128)} %pad_add_fusion.place_ref, bf16[512,768]{1,0:T(8,128)(2,1)} %get-tuple-element.416.refs_5_.refs_0_, ...), custom_call_target="tpu_custom_call" | custom-call | flops 1024 | bytes 1024 | tf_op jit(solution)/shard_map/expert_rows/pallas_call | solution.py:1239
  328.0 2.3 add_convert_fusion.13
  330.4 6.6 %add_convert_fusion.2 = (bf16[528,1536]{1,0:T(8,128)(2,1)}, bf16[528,1536]{1,0:T(8,128)(2,1)}) fusion(bf16[528,1536]{1,0:T(8,128)(2,1)} %collective-permute-done.39, bf16[528,1536]{1,0:T(8,128)(2,1)} %get-tuple-element.426, bf16[528,1536]{1,0:T(8,128)(2,1)} %collective-permute-done.36, pred[]{:T(512)S(6)} %eq.6, pred[]{:T(512)S(6)} %eq.7, ...), kind=kLoop, calls=%fused_computation.3 | loop fusion | flops 11354112 | bytes 11354114 | tf_op jit(solution)/shard_map/convert_element_type | solution.py:445
  340.7 26.6 %expert_in_grad.1 = bf16[1536,1536]{1,0:T(8,128)(2,1)} custom-call(bf16[528,1536]{1,0:T(8,128)(2,1)} %get-tuple-element.324.refs_0_, bf16[528,1536]{1,0:T(8,128)(2,1)} %collective-permute-done.23.refs_1_, bf16[528,1536]{1,0:T(8,128)(2,1)} %collective-permute-done.21.refs_0_.refs_3_.refs_2_, bf16[528,1536]{1,0:T(8,128)(2,1)} %copy-done.12, ...), custom_call_target="tpu_custom_call" | custom-call | flops 1024 | bytes 1024 | tf_op jit(solution)/shard_map/expert_in_grad/pallas_call | solution.py:1269
  367.3 1.9 constant_dynamic-slice_fusion.1
  369.2 2.0 constant_dynamic-slice_fusion
  371.3 5.8 %add_convert_fusion.6 = (bf16[512,1536]{1,0:T(8,128)(2,1)}, bf16[512,1536]{1,0:T(8,128)(2,1)}) fusion(bf16[512,1536]{1,0:T(8,128)(2,1)} %collective-permute-done.46, bf16[512,1536]{1,0:T(8,128)(2,1)S(1)} %copy-done.31, bf16[512,1536]{1,0:T(8,128)(2,1)} %collective-permute-done.41, pred[]{:T(512)S(6)} %eq.6, pred[]{:T(512)S(6)} %eq.7, ...), kind=kLoop, calls=%fused_computation.7 | loop fusion | flops 11010048 | bytes 11010050 | tf_op jit(solution)/shard_map/convert_element_type | solution.py:445
  379.1 3.1 collective-permute-start.48
  384.4 11.7 %middle_back.1 = (f32[512,1536]{1,0:T(8,128)}, bf16[512,1536]{1,0:T(8,128)(2,1)}, bf16[512,1536]{1,0:T(8,128)(2,1)}, bf16[16,512]{1,0:T(8,128)(2,1)}, f32[16,1536]{1,0:T(8,128)}) custom-call(s32[32]{0:T(128)} %mul.325.start_ref, bf16[528,1536]{1,0:T(8,128)(2,1)} %get-tuple-element.458.refs_0_.refs_4_, bf16[528,1536]{1,0:T(8,128)(2,1)} %copy-done.18, ...), custom_call_target="tpu_custom_call" | custom-call | flops 1024 | bytes 1024 | tf_op jit(solution)/shard_map/middle_back/pallas_call | solution.py:794
  396.1 16.3 %attend_back.1.right_ref.refs_0_ = bf16[512,2048]{1,0:T(8,128)(2,1)} custom-call(bf16[512,2048]{1,0:T(8,128)(2,1)} %get-tuple-element.456.heads_ref, bf16[512,1536]{1,0:T(8,128)(2,1)} %get-tuple-element.463.grad_ref, f32[512,128]{1,0:T(8,128)} %get-tuple-element.464.log_ref, s32[512,1]{1,0:T(8,128)} %copy.98.first_ref, f32[512,128]{1,0:T(8,128)} %copy.99.cosine_ref, ...), custom_call_target="tpu_custom_call" | custom-call | flops 1024 | bytes 1024 | tf_op jit(solution)/shard_map/attend_back/pallas_call | solution.py:867
  412.3 7.3 %shard_grad.2 = (bf16[4,4,48,2048]{3,2,1,0:T(8,128)(2,1)}, bf16[4,4,48,2048]{3,2,1,0:T(8,128)(2,1)}) custom-call(s32[9]{0:T(128)} %pad_add_fusion.1.start_ref, bf16[512,1536]{1,0:T(8,128)(2,1)} %get-tuple-element.455.left_ref, bf16[512,2048]{1,0:T(8,128)(2,1)} %attend_back.1.right_ref.refs_0_), custom_call_target="tpu_custom_call" | custom-call | flops 1024 | bytes 1024 | tf_op jit(solution)/shard_map/shard_grad/pallas_call | solution.py:911
  421.8 6.0 %shard_grad.3 = (bf16[4,4,48,1664]{3,2,1,0:T(8,128)(2,1)}, bf16[4,4,48,1664]{3,2,1,0:T(8,128)(2,1)}) custom-call(s32[9]{0:T(128)} %pad_add_fusion.1.start_ref, bf16[512,1536]{1,0:T(8,128)(2,1)} %get-tuple-element.311.attended_ref.left_ref, bf16[512,1536]{1,0:T(8,128)(2,1)} %get-tuple-element.476.right_ref, f32[16,1536]{1,0:T(8,128)} %get-tuple-element.477.refs_0_), custom_call_target="tpu_custom_call" | custom-call | flops 1024 | bytes 1024 | tf_op jit(solution)/shard_map/shard_grad/pallas_call | solution.py:911
  427.8 2.4 add_convert_fusion.11
  430.2 5.3 collective-permute-done.53
  435.4 1.8 fusion.12
  442.0 1.9 add_convert_fusion.15
  443.9 11.3 %entry_back.1 = f32[512,1536]{1,0:T(8,128)} custom-call(s32[32]{0:T(128)} %mul.325.start_ref, bf16[512,2048]{1,0:T(8,128)(2,1)} %attend_back.1.right_ref.refs_0_, bf16[512,1536]{1,0:T(8,128)(2,1)} %refs_1_.1, f32[512,1536]{1,0:T(8,128)} %get-tuple-element.488.refs_2_, f32[16,1536]{1,0:T(8,128)} %get-tuple-element.313.small_ref.refs_9_.refs_3_, ...), custom_call_target="tpu_custom_call" | custom-call | flops 1024 | bytes 1024 | tf_op jit(solution)/shard_map/entry_back/pallas_call | solution.py:964
  455.2 3.4 add_convert_fusion
  458.6 3.3 collective-permute-done.56
  464.9 1.8 fusion.4
  470.2 4.5 add_convert_fusion.5
  474.8 2.4 multiply_subtract_fusion.1
  477.2 2.0 add_convert_fusion.1
  479.3 4.8 collective-permute-done.59
  484.1 7.3 %collective-permute-done.60 = bf16[240,1536]{1,0:T(8,128)(2,1)S(1)} collective-permute-done((bf16[240,1536]{1,0:T(8,128)(2,1)S(1)}, bf16[240,1536]{1,0:T(8,128)(2,1)S(1)}, u32[]{:S(2)}, u32[]{:S(2)}) %collective-permute-start.60) | collective-permute-done | bytes 737312 | tf_op jit(solution)/shard_map/ppermute | solution.py:1357
  491.4 2.5 collective-permute-done.57
  498.5 3.8 collective-permute-start.62
  502.3 4.6 multiply_subtract_fusion
  508.8 10.0 %collective-permute-done.63 = bf16[48,2048]{1,0:T(8,128)(2,1)} collective-permute-done((bf16[48,2048]{1,0:T(8,128)(2,1)}, bf16[48,2048]{1,0:T(8,128)(2,1)}, u32[]{:S(2)}, u32[]{:S(2)}) %collective-permute-start.63) | collective-permute-done | bytes 196640 | tf_op jit(solution)/shard_map/ppermute | solution.py:1588
  524.5 4.0 collective-permute-done.67
  528.8 5.5 %collective-permute-done.68 = bf16[48,1664]{1,0:T(8,128)(2,1)S(1)} collective-permute-done((bf16[48,1664]{1,0:T(8,128)(2,1)S(1)}, bf16[48,1664]{1,0:T(8,128)(2,1)S(1)}, u32[]{:S(2)}, u32[]{:S(2)}) %collective-permute-start.68) | collective-permute-done | bytes 159776 | tf_op jit(solution)/shard_map/ppermute | solution.py:1588
  (290 shorter events, 68.5 us)
Async XLA Ops:
  0.7 42.8 %collective-permute-start.3 = (bf16[512,1536]{1,0:T(8,128)(2,1)}, bf16[512,1536]{1,0:T(8,128)(2,1)}, u32[]{:S(2)}, u32[]{:S(2)}) collective-permute-start(bf16[512,1536]{1,0:T(8,128)(2,1)} %refs_10_.1), channel_id=1, source_target_pairs={{0,4},{1,5},{2,6},{3,7},{4,0},{5,1},{6,2},{7,3},{8,12},{9,13},{10,... | collective-permute-start | bytes 4718600 | tf_op jit(solution)/shard_map/ppermute | solution.py:410
  3.7 39.8 %collective-permute-start.2 = (bf16[512,1536]{1,0:T(8,128)(2,1)}, bf16[512,1536]{1,0:T(8,128)(2,1)S(1)}, u32[]{:S(2)}, u32[]{:S(2)}) collective-permute-start(bf16[512,1536]{1,0:T(8,128)(2,1)} %refs_10_.1), channel_id=1, source_target_pairs={{0,2},{1,3},{2,0},{3,1},{4,6},{5,7},{6,4},{7,5},{8,10},{9,11},{10,... | collective-permute-start | bytes 4718600 | tf_op jit(solution)/shard_map/ppermute | solution.py:406
  9.8 11.5 %collective-permute-start = (bf16[48,3712]{1,0:T(8,128)(2,1)S(1)}, bf16[48,3712]{1,0:T(8,128)(2,1)}, u32[]{:S(2)}, u32[]{:S(2)}) collective-permute-start(bf16[48,3712]{1,0:T(8,128)(2,1)S(1)} %concatenate.18), channel_id=1, source_target_pairs={{0,8},{8,16},{16,24},{24,0},{1,9},{9,17},{17,25},{25,1},{2,10},{10... | collective-permute-start | bytes 1069064 | tf_op jit(solution)/shard_map/ppermute | solution.py:1357
  21.3 10.7 %collective-permute-start.1 = (bf16[48,3712]{1,0:T(8,128)(2,1)}, bf16[48,3712]{1,0:T(8,128)(2,1)S(1)}, u32[]{:S(2)}, u32[]{:S(2)}) collective-permute-start(bf16[48,3712]{1,0:T(8,128)(2,1)} %collective-permute-done), channel_id=1, source_target_pairs={{0,8},{8,16},{16,24},{24,0},{1,9},{9,17},{17,25},{25,1},{2,10},{10... | collective-permute-start | bytes 1069064 | tf_op jit(solution)/shard_map/ppermute | solution.py:1357
  43.5 31.4 %collective-permute-start.7 = (bf16[4,48,3712]{2,1,0:T(8,128)(2,1)S(1)}, bf16[4,48,3712]{2,1,0:T(8,128)(2,1)}, u32[]{:S(2)}, u32[]{:S(2)}) collective-permute-start(bf16[4,48,3712]{2,1,0:T(8,128)(2,1)S(1)} %pad_maximum_fusion.refs_0_.refs_13_.refs_5_), channel_id=1, source_target_pairs={{0,1},{1,0},{2,3},{3,2},{4,5},{5,4},{6,7},{7,6},{8,9},{9,8},{10,11... | collective-permute-start | bytes 4276232 | tf_op jit(solution)/shard_map/ppermute | solution.py:414
  43.6 33.8 %collective-permute-start.6 = (bf16[4,48,3712]{2,1,0:T(8,128)(2,1)S(1)}, bf16[4,48,3712]{2,1,0:T(8,128)(2,1)}, u32[]{:S(2)}, u32[]{:S(2)}) collective-permute-start(bf16[4,48,3712]{2,1,0:T(8,128)(2,1)S(1)} %pad_maximum_fusion.refs_0_.refs_13_.refs_5_), channel_id=1, source_target_pairs={{0,4},{1,5},{2,6},{3,7},{4,0},{5,1},{6,2},{7,3},{8,12},{9,13},{10,... | collective-permute-start | bytes 4276232 | tf_op jit(solution)/shard_map/ppermute | solution.py:410
  44.7 32.8 %collective-permute-start.5 = (bf16[4,48,3712]{2,1,0:T(8,128)(2,1)S(1)}, bf16[4,48,3712]{2,1,0:T(8,128)(2,1)}, u32[]{:S(2)}, u32[]{:S(2)}) collective-permute-start(bf16[4,48,3712]{2,1,0:T(8,128)(2,1)S(1)} %pad_maximum_fusion.refs_0_.refs_13_.refs_5_), channel_id=1, source_target_pairs={{0,2},{1,3},{2,0},{3,1},{4,6},{5,7},{6,4},{7,5},{8,10},{9,11},{10,... | collective-permute-start | bytes 4276232 | tf_op jit(solution)/shard_map/ppermute | solution.py:406
  45.3 29.6 %collective-permute-start.8 = (bf16[240,1536]{1,0:T(8,128)(2,1)S(1)}, bf16[240,1536]{1,0:T(8,128)(2,1)S(1)}, u32[]{:S(2)}, u32[]{:S(2)}) collective-permute-start(bf16[240,1536]{1,0:T(8,128)(2,1)S(1)} %slice.128.refs_2_.refs_8_.refs_24_), channel_id=1, source_target_pairs={{0,8},{8,16},{16,24},{24,0},{1,9},{9,17},{17,25},{25,1},{2,10},{10... | collective-permute-start | bytes 2211848 | tf_op jit(solution)/shard_map/ppermute | solution.py:1357
  45.4 29.5 %collective-permute-start.9 = (bf16[144,1536]{1,0:T(8,128)(2,1)S(1)}, bf16[144,1536]{1,0:T(8,128)(2,1)}, u32[]{:S(2)}, u32[]{:S(2)}) collective-permute-start(bf16[144,1536]{1,0:T(8,128)(2,1)S(1)} %slice.129.refs_6_.refs_12_.refs_28_), channel_id=1, source_target_pairs={{0,8},{8,16},{16,24},{24,0},{1,9},{9,17},{17,25},{25,1},{2,10},{10... | collective-permute-start | bytes 1327112 | tf_op jit(solution)/shard_map/ppermute | solution.py:1357
  77.5 24.1 %collective-permute-start.14 = (bf16[512,1536]{1,0:T(8,128)(2,1)}, bf16[512,1536]{1,0:T(8,128)(2,1)S(1)}, u32[]{:S(2)}, u32[]{:S(2)}) collective-permute-start(bf16[512,1536]{1,0:T(8,128)(2,1)} %copy-done.14), channel_id=1, source_target_pairs={{0,1},{1,0},{2,3},{3,2},{4,5},{5,4},{6,7},{7,6},{8,9},{9,8},{10,11... | collective-permute-start | bytes 4718600 | tf_op jit(solution)/shard_map/ppermute | solution.py:414
  79.1 22.5 %collective-permute-start.10 = (bf16[4,48,3712]{2,1,0:T(8,128)(2,1)S(1)}, bf16[4,48,3712]{2,1,0:T(8,128)(2,1)S(1)}, u32[]{:S(2)}, u32[]{:S(2)}) collective-permute-start(bf16[4,48,3712]{2,1,0:T(8,128)(2,1)S(1)} %broadcast_select_fusion.2), channel_id=1, source_target_pairs={{0,2},{1,5},{2,0},{3,7},{4,6},{5,1},{6,4},{7,3},{8,10},{9,13},{10,... | collective-permute-start | bytes 4276232 | tf_op jit(solution)/shard_map/ppermute | solution.py:422
  80.2 21.5 %collective-permute-start.11 = (bf16[4,48,3712]{2,1,0:T(8,128)(2,1)}, bf16[4,48,3712]{2,1,0:T(8,128)(2,1)S(1)}, u32[]{:S(2)}, u32[]{:S(2)}) collective-permute-start(bf16[4,48,3712]{2,1,0:T(8,128)(2,1)} %collective-permute-done.5.refs_2_.refs_15_.refs_7_), channel_id=1, source_target_pairs={{0,1},{1,0},{2,3},{3,2},{4,5},{5,4},{6,7},{7,6},{8,9},{9,8},{10,11... | collective-permute-start | bytes 4276232 | tf_op jit(solution)/shard_map/ppermute | solution.py:414
  80.9 20.7 %collective-permute-start.12 = (bf16[4,48,3712]{2,1,0:T(8,128)(2,1)}, bf16[4,48,3712]{2,1,0:T(8,128)(2,1)S(1)}, u32[]{:S(2)}, u32[]{:S(2)}) collective-permute-start(bf16[4,48,3712]{2,1,0:T(8,128)(2,1)} %collective-permute-done.6.refs_4_.refs_17_.refs_9_), channel_id=1, source_target_pairs={{0,1},{1,0},{2,3},{3,2},{4,5},{5,4},{6,7},{7,6},{8,9},{9,8},{10,11... | collective-permute-start | bytes 4276232 | tf_op jit(solution)/shard_map/ppermute | solution.py:414
  80.9 20.7 %collective-permute-start.13 = (bf16[240,1536]{1,0:T(8,128)(2,1)S(1)}, bf16[240,1536]{1,0:T(8,128)(2,1)S(1)}, u32[]{:S(2)}, u32[]{:S(2)}) collective-permute-start(bf16[240,1536]{1,0:T(8,128)(2,1)S(1)} %collective-permute-done.8.refs_3_.refs_9_.refs_25_), channel_id=1, source_target_pairs={{0,8},{8,16},{16,24},{24,0},{1,9},{9,17},{17,25},{25,1},{2,10},{10... | collective-permute-start | bytes 2211848 | tf_op jit(solution)/shard_map/ppermute | solution.py:1357
  101.8 33.8 %collective-permute-start.17 = (bf16[512,1536]{1,0:T(8,128)(2,1)}, bf16[512,1536]{1,0:T(8,128)(2,1)}, u32[]{:S(2)}, u32[]{:S(2)}) collective-permute-start(bf16[512,1536]{1,0:T(8,128)(2,1)} %refs_10_.1), channel_id=1, source_target_pairs={{0,1},{1,0},{2,3},{3,2},{4,5},{5,4},{6,7},{7,6},{8,9},{9,8},{10,11... | collective-permute-start | bytes 4718600 | tf_op jit(solution)/shard_map/ppermute | solution.py:414
  106.2 30.9 %collective-permute-start.16 = (bf16[512,1536]{1,0:T(8,128)(2,1)}, bf16[512,1536]{1,0:T(8,128)(2,1)}, u32[]{:S(2)}, u32[]{:S(2)}) collective-permute-start(bf16[512,1536]{1,0:T(8,128)(2,1)} %broadcast_select_fusion.1), channel_id=1, source_target_pairs={{0,2},{1,5},{2,0},{3,7},{4,6},{5,1},{6,4},{7,3},{8,10},{9,13},{10,... | collective-permute-start | bytes 4718600 | tf_op jit(solution)/shard_map/ppermute | solution.py:422
  106.7 30.4 %collective-permute-start.18 = (bf16[512,1536]{1,0:T(8,128)(2,1)}, bf16[512,1536]{1,0:T(8,128)(2,1)}, u32[]{:S(2)}, u32[]{:S(2)}) collective-permute-start(bf16[512,1536]{1,0:T(8,128)(2,1)} %collective-permute-done.3.refs_12_.refs_11_), channel_id=1, source_target_pairs={{0,1},{1,0},{2,3},{3,2},{4,5},{5,4},{6,7},{7,6},{8,9},{9,8},{10,11... | collective-permute-start | bytes 4718600 | tf_op jit(solution)/shard_map/ppermute | solution.py:414
  107.3 29.8 %collective-permute-start.19 = (bf16[240,1536]{1,0:T(8,128)(2,1)S(1)}, bf16[240,1536]{1,0:T(8,128)(2,1)S(1)}, u32[]{:S(2)}, u32[]{:S(2)}) collective-permute-start(bf16[240,1536]{1,0:T(8,128)(2,1)S(1)} %collective-permute-done.13.refs_4_.refs_10_.refs_26_), channel_id=1, source_target_pairs={{0,8},{8,16},{16,24},{24,0},{1,9},{9,17},{17,25},{25,1},{2,10},{10... | collective-permute-start | bytes 2211848 | tf_op jit(solution)/shard_map/ppermute | solution.py:1357
  107.3 29.8 %collective-permute-start.20 = (bf16[144,1536]{1,0:T(8,128)(2,1)}, bf16[144,1536]{1,0:T(8,128)(2,1)S(1)}, u32[]{:S(2)}, u32[]{:S(2)}) collective-permute-start(bf16[144,1536]{1,0:T(8,128)(2,1)} %collective-permute-done.9.refs_7_.refs_13_.refs_29_), channel_id=1, source_target_pairs={{0,8},{8,16},{16,24},{24,0},{1,9},{9,17},{17,25},{25,1},{2,10},{10... | collective-permute-start | bytes 1327112 | tf_op jit(solution)/shard_map/ppermute | solution.py:1357
  137.1 16.6 %collective-permute-start.23 = (bf16[528,1536]{1,0:T(8,128)(2,1)}, bf16[528,1536]{1,0:T(8,128)(2,1)}, u32[]{:S(2)}, u32[]{:S(2)}) collective-permute-start(bf16[528,1536]{1,0:T(8,128)(2,1)} %get-tuple-element.324.refs_0_), channel_id=1, source_target_pairs={{0,1},{1,0},{2,3},{3,2},{4,5},{5,4},{6,7},{7,6},{8,9},{9,8},{10,11... | collective-permute-start | bytes 4866056 | tf_op jit(solution)/shard_map/ppermute | solution.py:414
  137.2 38.2 %collective-permute-start.22 = (bf16[528,1536]{1,0:T(8,128)(2,1)}, bf16[528,1536]{1,0:T(8,128)(2,1)}, u32[]{:S(2)}, u32[]{:S(2)}) collective-permute-start(bf16[528,1536]{1,0:T(8,128)(2,1)} %get-tuple-element.324.refs_0_), channel_id=1, source_target_pairs={{0,4},{1,5},{2,6},{3,7},{4,0},{5,1},{6,2},{7,3},{8,12},{9,13},{10,... | collective-permute-start | bytes 4866056 | tf_op jit(solution)/shard_map/ppermute | solution.py:410
  138.4 37.8 %collective-permute-start.21 = (bf16[528,1536]{1,0:T(8,128)(2,1)}, bf16[528,1536]{1,0:T(8,128)(2,1)}, u32[]{:S(2)}, u32[]{:S(2)}) collective-permute-start(bf16[528,1536]{1,0:T(8,128)(2,1)} %get-tuple-element.324.refs_0_), channel_id=1, source_target_pairs={{0,2},{1,3},{2,0},{3,1},{4,6},{5,7},{6,4},{7,5},{8,10},{9,11},{10,... | collective-permute-start | bytes 4866056 | tf_op jit(solution)/shard_map/ppermute | solution.py:406
  139.1 13.8 %collective-permute-start.24 = (bf16[144,1536]{1,0:T(8,128)(2,1)S(1)}, bf16[144,1536]{1,0:T(8,128)(2,1)S(1)}, u32[]{:S(2)}, u32[]{:S(2)}) collective-permute-start(bf16[144,1536]{1,0:T(8,128)(2,1)S(1)} %collective-permute-done.20.refs_8_.refs_14_.refs_30_), channel_id=1, source_target_pairs={{0,8},{8,16},{16,24},{24,0},{1,9},{9,17},{17,25},{25,1},{2,10},{10... | collective-permute-start | bytes 1327112 | tf_op jit(solution)/shard_map/ppermute | solution.py:1357
  152.9 16.6 %collective-permute-start.25 = (bf16[192,1536]{1,0:T(8,128)(2,1)}, bf16[192,1536]{1,0:T(8,128)(2,1)}, u32[]{:S(2)}, u32[]{:S(2)}) collective-permute-start(bf16[192,1536]{1,0:T(8,128)(2,1)} %convert_bitcast_fusion.1.refs_2_.refs_16_.refs_32_.refs_6_), channel_id=1, source_target_pairs={{0,8},{8,16},{16,24},{24,0},{1,9},{9,17},{17,25},{25,1},{2,10},{10... | collective-permute-start | bytes 1769480 | tf_op jit(solution)/shard_map/ppermute | solution.py:1357
  179.0 13.2 %collective-permute-start.28 = (bf16[528,1536]{1,0:T(8,128)(2,1)}, bf16[528,1536]{1,0:T(8,128)(2,1)S(1)}, u32[]{:S(2)}, u32[]{:S(2)}) collective-permute-start(bf16[528,1536]{1,0:T(8,128)(2,1)} %collective-permute-done.21.refs_0_.refs_3_.refs_2_), channel_id=1, source_target_pairs={{0,1},{1,0},{2,3},{3,2},{4,5},{5,4},{6,7},{7,6},{8,9},{9,8},{10,11... | collective-permute-start | bytes 4866056 | tf_op jit(solution)/shard_map/ppermute | solution.py:414
  179.0 13.2 %collective-permute-start.29 = (bf16[528,1536]{1,0:T(8,128)(2,1)}, bf16[528,1536]{1,0:T(8,128)(2,1)}, u32[]{:S(2)}, u32[]{:S(2)}) collective-permute-start(bf16[528,1536]{1,0:T(8,128)(2,1)} %collective-permute-done.22.refs_1_.refs_5_.refs_4_), channel_id=1, source_target_pairs={{0,1},{1,0},{2,3},{3,2},{4,5},{5,4},{6,7},{7,6},{8,9},{9,8},{10,11... | collective-permute-start | bytes 4866056 | tf_op jit(solution)/shard_map/ppermute | solution.py:414
  179.5 25.8 %collective-permute-start.26 = (bf16[528,1536]{1,0:T(8,128)(2,1)}, bf16[528,1536]{1,0:T(8,128)(2,1)}, u32[]{:S(2)}, u32[]{:S(2)}) collective-permute-start(bf16[528,1536]{1,0:T(8,128)(2,1)} %broadcast_select_fusion), channel_id=1, source_target_pairs={{0,2},{1,5},{2,0},{3,7},{4,6},{5,1},{6,4},{7,3},{8,10},{9,13},{10,... | collective-permute-start | bytes 4866056 | tf_op jit(solution)/shard_map/ppermute | solution.py:422
  180.2 25.0 %collective-permute-start.27 = (bf16[192,1536]{1,0:T(8,128)(2,1)}, bf16[192,1536]{1,0:T(8,128)(2,1)}, u32[]{:S(2)}, u32[]{:S(2)}) collective-permute-start(bf16[192,1536]{1,0:T(8,128)(2,1)} %collective-permute-done.25.refs_3_.refs_17_.refs_33_.refs_7_), channel_id=1, source_target_pairs={{0,8},{8,16},{16,24},{24,0},{1,9},{9,17},{17,25},{25,1},{2,10},{10... | collective-permute-start | bytes 1769480 | tf_op jit(solution)/shard_map/ppermute | solution.py:1357
  205.4 22.2 %collective-permute-start.31 = (bf16[512,1536]{1,0:T(8,128)(2,1)}, bf16[512,1536]{1,0:T(8,128)(2,1)}, u32[]{:S(2)}, u32[]{:S(2)}) collective-permute-start(bf16[512,1536]{1,0:T(8,128)(2,1)} %collective-permute-done.16.refs_14_.refs_3_), channel_id=1, source_target_pairs={{0,1},{1,0},{2,3},{3,2},{4,5},{5,4},{6,7},{7,6},{8,9},{9,8},{10,11... | collective-permute-start | bytes 4718600 | tf_op jit(solution)/shard_map/ppermute | solution.py:414
  210.6 32.8 %collective-permute-start.32 = (bf16[192,1536]{1,0:T(8,128)(2,1)}, bf16[192,1536]{1,0:T(8,128)(2,1)}, u32[]{:S(2)}, u32[]{:S(2)}) collective-permute-start(bf16[192,1536]{1,0:T(8,128)(2,1)} %collective-permute-done.27.refs_4_.refs_18_.refs_34_.refs_8_), channel_id=1, source_target_pairs={{0,8},{8,16},{16,24},{24,0},{1,9},{9,17},{17,25},{25,1},{2,10},{10... | collective-permute-start | bytes 1769480 | tf_op jit(solution)/shard_map/ppermute | solution.py:1357
  252.1 18.1 %collective-permute-start.34 = (bf16[512,1536]{1,0:T(8,128)(2,1)}, bf16[512,1536]{1,0:T(8,128)(2,1)S(1)}, u32[]{:S(2)}, u32[]{:S(2)}) collective-permute-start(bf16[512,1536]{1,0:T(8,128)(2,1)} %get-tuple-element.373), channel_id=1, source_target_pairs={{0,1},{1,0},{2,3},{3,2},{4,5},{5,4},{6,7},{7,6},{8,9},{9,8},{10,11... | collective-permute-start | bytes 4718600 | tf_op jit(solution)/shard_map/ppermute | solution.py:414
  252.2 18.0 %collective-permute-start.33 = (bf16[192,1536]{1,0:T(8,128)(2,1)}, bf16[192,1536]{1,0:T(8,128)(2,1)}, u32[]{:S(2)}, u32[]{:S(2)}) collective-permute-start(bf16[192,1536]{1,0:T(8,128)(2,1)} %constant_dynamic-slice_fusion.2), channel_id=1, source_target_pairs={{0,8},{8,16},{16,24},{24,0},{1,9},{9,17},{17,25},{25,1},{2,10},{10... | collective-permute-start | bytes 1769480 | tf_op jit(solution)/shard_map/ppermute | solution.py:1357
  276.6 37.0 %collective-permute-start.36 = (bf16[528,1536]{1,0:T(8,128)(2,1)S(1)}, bf16[528,1536]{1,0:T(8,128)(2,1)}, u32[]{:S(2)}, u32[]{:S(2)}) collective-permute-start(bf16[528,1536]{1,0:T(8,128)(2,1)S(1)} %add_convert_fusion.4), channel_id=1, source_target_pairs={{0,2},{1,5},{2,0},{3,7},{4,6},{5,1},{6,4},{7,3},{8,10},{9,13},{10,... | collective-permute-start | bytes 4866056 | tf_op jit(solution)/shard_map/ppermute | solution.py:422
  277.7 35.9 %collective-permute-start.37 = (bf16[192,1536]{1,0:T(8,128)(2,1)}, bf16[192,1536]{1,0:T(8,128)(2,1)}, u32[]{:S(2)}, u32[]{:S(2)}) collective-permute-start(bf16[192,1536]{1,0:T(8,128)(2,1)} %add_convert_fusion.14), channel_id=1, source_target_pairs={{0,8},{8,16},{16,24},{24,0},{1,9},{9,17},{17,25},{25,1},{2,10},{10... | collective-permute-start | bytes 1769480 | tf_op jit(solution)/shard_map/ppermute | solution.py:1357
  313.6 16.7 %collective-permute-start.38 = (bf16[528,1536]{1,0:T(8,128)(2,1)}, bf16[528,1536]{1,0:T(8,128)(2,1)}, u32[]{:S(2)}, u32[]{:S(2)}) collective-permute-start(bf16[528,1536]{1,0:T(8,128)(2,1)} %get-tuple-element.412), channel_id=1, source_target_pairs={{0,1},{1,0},{2,3},{3,2},{4,5},{5,4},{6,7},{7,6},{8,9},{9,8},{10,11... | collective-permute-start | bytes 4866056 | tf_op jit(solution)/shard_map/ppermute | solution.py:414
  313.7 16.7 %collective-permute-start.39 = (bf16[528,1536]{1,0:T(8,128)(2,1)}, bf16[528,1536]{1,0:T(8,128)(2,1)}, u32[]{:S(2)}, u32[]{:S(2)}) collective-permute-start(bf16[528,1536]{1,0:T(8,128)(2,1)} %get-tuple-element.413), channel_id=1, source_target_pairs={{0,1},{1,0},{2,3},{3,2},{4,5},{5,4},{6,7},{7,6},{8,9},{9,8},{10,11... | collective-permute-start | bytes 4866056 | tf_op jit(solution)/shard_map/ppermute | solution.py:414
  314.2 16.2 %collective-permute-start.40 = (bf16[528,1536]{1,0:T(8,128)(2,1)}, bf16[528,1536]{1,0:T(8,128)(2,1)S(1)}, u32[]{:S(2)}, u32[]{:S(2)}) collective-permute-start(bf16[528,1536]{1,0:T(8,128)(2,1)} %get-tuple-element.414), channel_id=1, source_target_pairs={{0,1},{1,0},{2,3},{3,2},{4,5},{5,4},{6,7},{7,6},{8,9},{9,8},{10,11... | collective-permute-start | bytes 4866056 | tf_op jit(solution)/shard_map/ppermute | solution.py:414
  314.2 22.7 %collective-permute-start.41 = (bf16[512,1536]{1,0:T(8,128)(2,1)}, bf16[512,1536]{1,0:T(8,128)(2,1)}, u32[]{:S(2)}, u32[]{:S(2)}) collective-permute-start(bf16[512,1536]{1,0:T(8,128)(2,1)} %add_convert_fusion.8), channel_id=1, source_target_pairs={{0,2},{1,5},{2,0},{3,7},{4,6},{5,1},{6,4},{7,3},{8,10},{9,13},{10,... | collective-permute-start | bytes 4718600 | tf_op jit(solution)/shard_map/ppermute | solution.py:422
  337.0 34.3 %collective-permute-start.45 = (bf16[512,1536]{1,0:T(8,128)(2,1)}, bf16[512,1536]{1,0:T(8,128)(2,1)}, u32[]{:S(2)}, u32[]{:S(2)}) collective-permute-start(bf16[512,1536]{1,0:T(8,128)(2,1)} %get-tuple-element.450), channel_id=1, source_target_pairs={{0,1},{1,0},{2,3},{3,2},{4,5},{5,4},{6,7},{7,6},{8,9},{9,8},{10,11... | collective-permute-start | bytes 4718600 | tf_op jit(solution)/shard_map/ppermute | solution.py:414
  337.3 33.9 %collective-permute-start.46 = (bf16[512,1536]{1,0:T(8,128)(2,1)}, bf16[512,1536]{1,0:T(8,128)(2,1)}, u32[]{:S(2)}, u32[]{:S(2)}) collective-permute-start(bf16[512,1536]{1,0:T(8,128)(2,1)} %get-tuple-element.453), channel_id=1, source_target_pairs={{0,1},{1,0},{2,3},{3,2},{4,5},{5,4},{6,7},{7,6},{8,9},{9,8},{10,11... | collective-permute-start | bytes 4718600 | tf_op jit(solution)/shard_map/ppermute | solution.py:414
  337.5 39.5 %collective-permute-start.42 = (bf16[528,1536]{1,0:T(8,128)(2,1)}, bf16[528,1536]{1,0:T(8,128)(2,1)S(1)}, u32[]{:S(2)}, u32[]{:S(2)}) collective-permute-start(bf16[528,1536]{1,0:T(8,128)(2,1)} %get-tuple-element.436), channel_id=1, source_target_pairs={{0,2},{1,3},{2,0},{3,1},{4,6},{5,7},{6,4},{7,5},{8,10},{9,11},{10,... | collective-permute-start | bytes 4866056 | tf_op jit(solution)/shard_map/ppermute | solution.py:406
  338.8 38.2 %collective-permute-start.43 = (bf16[528,1536]{1,0:T(8,128)(2,1)}, bf16[528,1536]{1,0:T(8,128)(2,1)}, u32[]{:S(2)}, u32[]{:S(2)}) collective-permute-start(bf16[528,1536]{1,0:T(8,128)(2,1)} %get-tuple-element.437), channel_id=1, source_target_pairs={{0,4},{1,5},{2,6},{3,7},{4,0},{5,1},{6,2},{7,3},{8,12},{9,13},{10,... | collective-permute-start | bytes 4866056 | tf_op jit(solution)/shard_map/ppermute | solution.py:410
  340.4 36.7 %collective-permute-start.44 = (bf16[192,1536]{1,0:T(8,128)(2,1)}, bf16[192,1536]{1,0:T(8,128)(2,1)}, u32[]{:S(2)}, u32[]{:S(2)}) collective-permute-start(bf16[192,1536]{1,0:T(8,128)(2,1)} %add_convert_fusion.13), channel_id=1, source_target_pairs={{0,8},{8,16},{16,24},{24,0},{1,9},{9,17},{17,25},{25,1},{2,10},{10... | collective-permute-start | bytes 1769480 | tf_op jit(solution)/shard_map/ppermute | solution.py:1357
  377.1 42.6 %collective-permute-start.47 = (bf16[512,1536]{1,0:T(8,128)(2,1)}, bf16[512,1536]{1,0:T(8,128)(2,1)}, u32[]{:S(2)}, u32[]{:S(2)}) collective-permute-start(bf16[512,1536]{1,0:T(8,128)(2,1)} %get-tuple-element.468), channel_id=1, source_target_pairs={{0,1},{1,0},{2,3},{3,2},{4,5},{5,4},{6,7},{7,6},{8,9},{9,8},{10,11... | collective-permute-start | bytes 4718600 | tf_op jit(solution)/shard_map/ppermute | solution.py:414
  377.2 43.8 %collective-permute-start.51 = (bf16[512,1536]{1,0:T(8,128)(2,1)}, bf16[512,1536]{1,0:T(8,128)(2,1)}, u32[]{:S(2)}, u32[]{:S(2)}) collective-permute-start(bf16[512,1536]{1,0:T(8,128)(2,1)} %get-tuple-element.474), channel_id=1, source_target_pairs={{0,4},{1,5},{2,6},{3,7},{4,0},{5,1},{6,2},{7,3},{8,12},{9,13},{10,... | collective-permute-start | bytes 4718600 | tf_op jit(solution)/shard_map/ppermute | solution.py:410
  378.4 42.6 %collective-permute-start.50 = (bf16[512,1536]{1,0:T(8,128)(2,1)}, bf16[512,1536]{1,0:T(8,128)(2,1)}, u32[]{:S(2)}, u32[]{:S(2)}) collective-permute-start(bf16[512,1536]{1,0:T(8,128)(2,1)} %get-tuple-element.457), channel_id=1, source_target_pairs={{0,2},{1,3},{2,0},{3,1},{4,6},{5,7},{6,4},{7,5},{8,10},{9,11},{10,... | collective-permute-start | bytes 4718600 | tf_op jit(solution)/shard_map/ppermute | solution.py:406
  379.1 40.6 %collective-permute-start.48 = (bf16[240,1536]{1,0:T(8,128)(2,1)}, bf16[240,1536]{1,0:T(8,128)(2,1)}, u32[]{:S(2)}, u32[]{:S(2)}) collective-permute-start(bf16[240,1536]{1,0:T(8,128)(2,1)} %constant_dynamic-slice_fusion), channel_id=1, source_target_pairs={{0,8},{8,16},{16,24},{24,0},{1,9},{9,17},{17,25},{25,1},{2,10},{10... | collective-permute-start | bytes 2211848 | tf_op jit(solution)/shard_map/ppermute | solution.py:1357
  382.3 37.4 %collective-permute-start.49 = (bf16[144,1536]{1,0:T(8,128)(2,1)}, bf16[144,1536]{1,0:T(8,128)(2,1)}, u32[]{:S(2)}, u32[]{:S(2)}) collective-permute-start(bf16[144,1536]{1,0:T(8,128)(2,1)} %constant_dynamic-slice_fusion.1), channel_id=1, source_target_pairs={{0,8},{8,16},{16,24},{24,0},{1,9},{9,17},{17,25},{25,1},{2,10},{10... | collective-permute-start | bytes 1327112 | tf_op jit(solution)/shard_map/ppermute | solution.py:1357
  421.0 14.5 %collective-permute-start.52 = (bf16[4,4,48,2048]{3,2,1,0:T(8,128)(2,1)}, bf16[4,4,48,2048]{3,2,1,0:T(8,128)(2,1)}, u32[]{:S(2)}, u32[]{:S(2)}) collective-permute-start(bf16[4,4,48,2048]{3,2,1,0:T(8,128)(2,1)} %get-tuple-element.475), channel_id=1, source_target_pairs={{0,1},{1,0},{2,3},{3,2},{4,5},{5,4},{6,7},{7,6},{8,9},{9,8},{10,11... | collective-permute-start | bytes 9437192 | tf_op jit(solution)/shard_map/ppermute | solution.py:414
  421.1 14.4 %collective-permute-start.53 = (bf16[144,1536]{1,0:T(8,128)(2,1)S(1)}, bf16[144,1536]{1,0:T(8,128)(2,1)S(1)}, u32[]{:S(2)}, u32[]{:S(2)}) collective-permute-start(bf16[144,1536]{1,0:T(8,128)(2,1)S(1)} %add_convert_fusion.16), channel_id=1, source_target_pairs={{0,8},{8,16},{16,24},{24,0},{1,9},{9,17},{17,25},{25,1},{2,10},{10... | collective-permute-start | bytes 1327112 | tf_op jit(solution)/shard_map/ppermute | solution.py:1357
  437.2 24.7 %collective-permute-start.55 = (bf16[4,4,48,1664]{3,2,1,0:T(8,128)(2,1)}, bf16[4,4,48,1664]{3,2,1,0:T(8,128)(2,1)}, u32[]{:S(2)}, u32[]{:S(2)}) collective-permute-start(bf16[4,4,48,1664]{3,2,1,0:T(8,128)(2,1)} %get-tuple-element.486), channel_id=1, source_target_pairs={{0,1},{1,0},{2,3},{3,2},{4,5},{5,4},{6,7},{7,6},{8,9},{9,8},{10,11... | collective-permute-start | bytes 7667720 | tf_op jit(solution)/shard_map/ppermute | solution.py:414
  440.9 21.1 %collective-permute-start.56 = (bf16[240,1536]{1,0:T(8,128)(2,1)}, bf16[240,1536]{1,0:T(8,128)(2,1)}, u32[]{:S(2)}, u32[]{:S(2)}) collective-permute-start(bf16[240,1536]{1,0:T(8,128)(2,1)} %add_convert_fusion.11), channel_id=1, source_target_pairs={{0,8},{8,16},{16,24},{24,0},{1,9},{9,17},{17,25},{25,1},{2,10},{10... | collective-permute-start | bytes 2211848 | tf_op jit(solution)/shard_map/ppermute | solution.py:1357
  440.9 21.0 %collective-permute-start.54 = (bf16[4,48,2048]{2,1,0:T(8,128)(2,1)S(1)}, bf16[4,48,2048]{2,1,0:T(8,128)(2,1)}, u32[]{:S(2)}, u32[]{:S(2)}) collective-permute-start(bf16[4,48,2048]{2,1,0:T(8,128)(2,1)S(1)} %fusion.12), channel_id=1, source_target_pairs={{0,2},{1,5},{2,0},{3,7},{4,6},{5,1},{6,4},{7,3},{8,10},{9,13},{10,... | collective-permute-start | bytes 2359304 | tf_op jit(solution)/shard_map/ppermute | solution.py:422
  461.9 17.3 %collective-permute-start.61 = (bf16[144,1536]{1,0:T(8,128)(2,1)S(1)}, bf16[144,1536]{1,0:T(8,128)(2,1)S(1)}, u32[]{:S(2)}, u32[]{:S(2)}) collective-permute-start(bf16[144,1536]{1,0:T(8,128)(2,1)S(1)} %copy-done.39), channel_id=1, source_target_pairs={{0,8},{8,16},{16,24},{24,0},{1,9},{9,17},{17,25},{25,1},{2,10},{10... | collective-permute-start | bytes 1327112 | tf_op jit(solution)/shard_map/ppermute | solution.py:1357
  466.8 17.3 %collective-permute-start.59 = (bf16[4,48,1664]{2,1,0:T(8,128)(2,1)S(1)}, bf16[4,48,1664]{2,1,0:T(8,128)(2,1)S(1)}, u32[]{:S(2)}, u32[]{:S(2)}) collective-permute-start(bf16[4,48,1664]{2,1,0:T(8,128)(2,1)S(1)} %fusion.13), channel_id=1, source_target_pairs={{0,2},{1,5},{2,0},{3,7},{4,6},{5,1},{6,4},{7,3},{8,10},{9,13},{10,... | collective-permute-start | bytes 1916936 | tf_op jit(solution)/shard_map/ppermute | solution.py:422
  467.9 23.5 %collective-permute-start.60 = (bf16[240,1536]{1,0:T(8,128)(2,1)S(1)}, bf16[240,1536]{1,0:T(8,128)(2,1)S(1)}, u32[]{:S(2)}, u32[]{:S(2)}) collective-permute-start(bf16[240,1536]{1,0:T(8,128)(2,1)S(1)} %add_convert_fusion.10), channel_id=1, source_target_pairs={{0,8},{8,16},{16,24},{24,0},{1,9},{9,17},{17,25},{25,1},{2,10},{10... | collective-permute-start | bytes 2211848 | tf_op jit(solution)/shard_map/ppermute | solution.py:1357
  468.0 25.9 %collective-permute-start.57 = (bf16[4,48,2048]{2,1,0:T(8,128)(2,1)S(1)}, bf16[4,48,2048]{2,1,0:T(8,128)(2,1)S(1)}, u32[]{:S(2)}, u32[]{:S(2)}) collective-permute-start(bf16[4,48,2048]{2,1,0:T(8,128)(2,1)S(1)} %get-tuple-element.503), channel_id=1, source_target_pairs={{0,2},{1,3},{2,0},{3,1},{4,6},{5,7},{6,4},{7,5},{8,10},{9,11},{10,... | collective-permute-start | bytes 2359304 | tf_op jit(solution)/shard_map/ppermute | solution.py:406
  469.1 24.8 %collective-permute-start.58 = (bf16[4,48,2048]{2,1,0:T(8,128)(2,1)S(1)}, bf16[4,48,2048]{2,1,0:T(8,128)(2,1)S(1)}, u32[]{:S(2)}, u32[]{:S(2)}) collective-permute-start(bf16[4,48,2048]{2,1,0:T(8,128)(2,1)S(1)} %get-tuple-element.504), channel_id=1, source_target_pairs={{0,4},{1,5},{2,6},{3,7},{4,0},{5,1},{6,2},{7,3},{8,12},{9,13},{10,... | collective-permute-start | bytes 2359304 | tf_op jit(solution)/shard_map/ppermute | solution.py:410
  495.8 23.0 %collective-permute-start.65 = (bf16[4,48,1664]{2,1,0:T(8,128)(2,1)}, bf16[4,48,1664]{2,1,0:T(8,128)(2,1)S(1)}, u32[]{:S(2)}, u32[]{:S(2)}) collective-permute-start(bf16[4,48,1664]{2,1,0:T(8,128)(2,1)} %get-tuple-element.514), channel_id=1, source_target_pairs={{0,2},{1,3},{2,0},{3,1},{4,6},{5,7},{6,4},{7,5},{8,10},{9,11},{10,... | collective-permute-start | bytes 1916936 | tf_op jit(solution)/shard_map/ppermute | solution.py:406
  496.8 22.0 %collective-permute-start.66 = (bf16[4,48,1664]{2,1,0:T(8,128)(2,1)}, bf16[4,48,1664]{2,1,0:T(8,128)(2,1)S(1)}, u32[]{:S(2)}, u32[]{:S(2)}) collective-permute-start(bf16[4,48,1664]{2,1,0:T(8,128)(2,1)} %get-tuple-element.515), channel_id=1, source_target_pairs={{0,4},{1,5},{2,6},{3,7},{4,0},{5,1},{6,2},{7,3},{8,12},{9,13},{10,... | collective-permute-start | bytes 1916936 | tf_op jit(solution)/shard_map/ppermute | solution.py:410
  498.5 10.3 %collective-permute-start.64 = (bf16[48,2048]{1,0:T(8,128)(2,1)}, bf16[48,2048]{1,0:T(8,128)(2,1)}, u32[]{:S(2)}, u32[]{:S(2)}) collective-permute-start(bf16[48,2048]{1,0:T(8,128)(2,1)} %get-tuple-element.662), channel_id=1, source_target_pairs={{0,8},{8,16},{16,24},{24,0},{1,9},{9,17},{17,25},{25,1},{2,10},{10... | collective-permute-start | bytes 589832 | tf_op jit(solution)/shard_map/ppermute | solution.py:1588
  498.5 20.3 %collective-permute-start.62 = (bf16[48,2048]{1,0:T(8,128)(2,1)}, bf16[48,2048]{1,0:T(8,128)(2,1)}, u32[]{:S(2)}, u32[]{:S(2)}) collective-permute-start(bf16[48,2048]{1,0:T(8,128)(2,1)} %get-tuple-element.664), channel_id=1, source_target_pairs={{0,24},{8,0},{16,8},{24,16},{1,25},{9,1},{17,9},{25,17},{2,26},{10... | collective-permute-start | bytes 589832 | tf_op jit(solution)/shard_map/ppermute | solution.py:1588
  507.1 11.6 %collective-permute-start.63 = (bf16[48,2048]{1,0:T(8,128)(2,1)}, bf16[48,2048]{1,0:T(8,128)(2,1)}, u32[]{:S(2)}, u32[]{:S(2)}) collective-permute-start(bf16[48,2048]{1,0:T(8,128)(2,1)} %get-tuple-element.663), channel_id=1, source_target_pairs={{0,16},{8,24},{16,0},{24,8},{1,17},{9,25},{17,1},{25,9},{2,18},{10... | collective-permute-start | bytes 589832 | tf_op jit(solution)/shard_map/ppermute | solution.py:1588
  521.2 13.0 %collective-permute-start.68 = (bf16[48,1664]{1,0:T(8,128)(2,1)S(1)}, bf16[48,1664]{1,0:T(8,128)(2,1)S(1)}, u32[]{:S(2)}, u32[]{:S(2)}) collective-permute-start(bf16[48,1664]{1,0:T(8,128)(2,1)S(1)} %get-tuple-element.668), channel_id=1, source_target_pairs={{0,16},{8,24},{16,0},{24,8},{1,17},{9,25},{17,1},{25,9},{2,18},{10... | collective-permute-start | bytes 479240 | tf_op jit(solution)/shard_map/ppermute | solution.py:1588
  (64 other events, 597.4 us)

commit v3 on v2

--- a/solution.py
+++ b/solution.py
@@ -557,31 +557,45 @@
     return values * cosine + pltpu.roll(values, HEAD_DIM // 2, 1) * sine
 
 
-def fill_bias(bias, first_ref):
+def fill_bias(bias, first):
     row = lax.broadcasted_iota(jnp.int32, bias.shape, 0)
-    column = lax.broadcasted_iota(jnp.int32, bias.shape, 1)
-    bias[...] = jnp.where((column <= row) & (column >= first_ref[...]), 0.0, NEG)
-
-
-def attend_kernel(
-    planes, start_ref, tokens_ref, first_ref, cosine_ref, sine_ref, *refs
-):
+    column = lax.broadcasted_iota(jnp.int32, bias.shape, 1).astype(jnp.float32)
+    row = row.astype(jnp.float32)
+    bias[...] = jnp.where((column <= row) & (column >= first), 0.0, NEG)
+
+
+def attend_kernel(planes, start_ref, tokens_ref, table_ref, routes_ref, *refs):
     blocks, refs = refs[:planes], refs[planes:]
-    attn_in_ref, heads_ref, attended_ref, log_ref, small_ref, weight, bias, sems = refs
+    attn_in_out, heads_out, attended_out, residual_out, packed_out, *refs = refs
+    log_ref, small_ref, gates_ref, *refs = refs
+    weight, late, bias, table, attn_in_ref, heads_ref, attended_ref, *refs = refs
+    residual_ref, packed_ref, sems, late_sems, out_sems = refs
     rows_count = tokens_ref.shape[0]
+    width_q, width_kv = HEADS * HEAD_DIM, KV_HEADS * HEAD_DIM
+    width = width_q + 2 * width_kv
+    table_copy = pltpu.make_async_copy(table_ref, table, out_sems.at[0])
+    table_copy.start()
     copies = load_rows(blocks, start_ref, weight, sems)
-    fill_bias(bias, first_ref)
+    late_copies = load_rows(blocks, start_ref, late, late_sems, weight.shape[1])
+    table_copy.wait()
+    leaving = []
+
+    def store(source, target):
+        leaving.append(pltpu.make_async_copy(source, target, out_sems.at[1 + len(leaving)]))
+        leaving[-1].start()
+
+    fill_bias(bias, table[:, 2 * HEAD_DIM : 2 * HEAD_DIM + 1])
     inputs = tokens_ref[...].astype(jnp.float32)
     inverse = lax.rsqrt(jnp.mean(inputs * inputs, -1, keepdims=True) + EPS)
     normed = inputs * inverse
     for copy in copies:
         copy.wait()
-    width_q, width_kv = HEADS * HEAD_DIM, KV_HEADS * HEAD_DIM
-    width = width_q + 2 * width_kv
     small = jnp.transpose(weight[:, width:].astype(jnp.float32))
     small_ref[...] = small[:16, :]
     experts = small_ref.shape[0] - 8
     attn_in_ref[...] = (normed * small[experts : experts + 1, :]).astype(jnp.bfloat16)
+    store(attn_in_ref, attn_in_out)
+    cosine, sine = table[:, :HEAD_DIM], table[:, HEAD_DIM : 2 * HEAD_DIM]
     for at in range(0, width, LANES):
         raw = jnp.dot(
             attn_in_ref[...], weight[:, at : at + LANES], preferred_element_type=jnp.float32
@@ -589,8 +603,25 @@
         for column in range(0, LANES, HEAD_DIM):
             values = raw[:, column : column + HEAD_DIM]
             if at + column < width_q + width_kv:
-                values = turned(values, cosine_ref[...], sine_ref[...])
+                values = turned(values, cosine, sine)
             heads_ref[:, at + column : at + column + HEAD_DIM] = values.astype(jnp.bfloat16)
+    store(heads_ref, heads_out)
+
+    logits = wide_dot(small_ref[...].astype(jnp.bfloat16), tokens_ref[...])[:experts, :]
+    expert = lax.broadcasted_iota(jnp.int32, logits.shape, 0)
+    routed = expert == routes_ref[:1, :]
+    for choice in range(1, TOP):
+        routed = routed | (expert == routes_ref[choice : choice + 1, :])
+    logits = jnp.where(routed, logits, NEG)
+    exponent = jnp.exp(logits - jnp.max(logits, 0, keepdims=True))
+    exponent = jnp.where(routed, exponent, 0.0)
+    gates = exponent / jnp.sum(exponent, 0, keepdims=True)
+    gates_ref[...] = gates
+    packed_ref[rows_count:, :] = jnp.concatenate(
+        [split_row(gates), jnp.zeros((16 - experts, D), jnp.float32)], 0
+    ).astype(jnp.bfloat16)
+    store(packed_ref.at[pl.ds(rows_count, 16)], packed_out.at[pl.ds(rows_count, 16)])
+
     half = rows_count // 2
     for block in range(2):
         rows, reach = pl.ds(block * half, half), (block + 1) * half
@@ -617,115 +648,63 @@
             ).astype(jnp.bfloat16)
             logs = jnp.where(lane == head, peak + jnp.log(total), logs)
         log_ref[rows, :] = logs
-
-
-def attend_call(starts, tokens, first, cosine, sine, blocks, width_early):
+        store(attended_ref.at[rows], attended_out.at[rows])
+        if block == 0:
+            for copy in late_copies:
+                copy.wait()
+        for at in range(0, D, LANES):
+            residual_ref[rows, at : at + LANES] = tokens_ref[rows, at : at + LANES].astype(
+                jnp.float32
+            ) + jnp.dot(
+                attended_ref[rows, :], late[:, at : at + LANES], preferred_element_type=jnp.float32
+            )
+        residual = residual_ref[rows, :]
+        inverse = lax.rsqrt(jnp.mean(residual * residual, -1, keepdims=True) + EPS)
+        packed_ref[rows, :] = (
+            residual * inverse * small_ref[experts + 1 : experts + 2, :]
+        ).astype(jnp.bfloat16)
+        store(packed_ref.at[rows], packed_out.at[rows])
+        store(residual_ref.at[rows], residual_out.at[rows])
+    for copy in leaving:
+        copy.wait()
+
+
+def attend_call(starts, tokens, table, routes, blocks, width_early, experts):
     rows_count = tokens.shape[0]
     width = (HEADS + 2 * KV_HEADS) * HEAD_DIM
     low = jnp.bfloat16
+    copies = len(blocks) * blocks[0].shape[0]
+    moved = [
+        ((rows_count, D), low),
+        ((rows_count, width), low),
+        ((rows_count, HEADS * HEAD_DIM), low),
+        ((rows_count, D), jnp.float32),
+        ((rows_count + 16, D), low),
+    ]
+    kept = [
+        ((rows_count, 128), jnp.float32),
+        ((16, D), jnp.float32),
+        ((experts, rows_count), jnp.float32),
+    ]
     return pl.pallas_call(
         functools.partial(attend_kernel, len(blocks)),
-        out_shape=[
-            jax.ShapeDtypeStruct((rows_count, D), low),
-            jax.ShapeDtypeStruct((rows_count, width), low),
-            jax.ShapeDtypeStruct((rows_count, HEADS * HEAD_DIM), low),
-            jax.ShapeDtypeStruct((rows_count, 128), jnp.float32),
-            jax.ShapeDtypeStruct((16, D), jnp.float32),
-        ],
-        in_specs=[scalars()] + [whole()] * 4 + [anywhere()] * len(blocks),
-        out_specs=[whole()] * 5,
+        out_shape=[jax.ShapeDtypeStruct(*shape) for shape in moved + kept],
+        in_specs=[scalars(), whole(), anywhere(), whole()] + [anywhere()] * len(blocks),
+        out_specs=[anywhere()] * len(moved) + [whole()] * len(kept),
         scratch_shapes=[
             pltpu.VMEM((D, width_early), low),
+            pltpu.VMEM((D, D), low),
             pltpu.VMEM((rows_count, rows_count), jnp.float32),
-            pltpu.SemaphoreType.DMA((len(blocks) * blocks[0].shape[0],)),
+            pltpu.VMEM(table.shape, jnp.float32),
+            *[pltpu.VMEM(*shape) for shape in moved],
+            pltpu.SemaphoreType.DMA((copies,)),
+            pltpu.SemaphoreType.DMA((copies,)),
+            pltpu.SemaphoreType.DMA((10,)),
         ],
         compiler_params=pltpu.CompilerParams(vmem_limit_bytes=62 << 20),
         cost_estimate=small_cost(),
         name="attend",
-    )(starts, tokens, first, cosine, sine, *blocks)
-
-
-def middle_kernel(planes, column, start_ref, tokens_ref, attended_ref, routes_ref, small_ref, *refs):
-    blocks, refs = refs[:planes], refs[planes:]
-    residual_ref, packed_ref, gates_ref, weight, sems = refs
-    step = pl.program_id(0)
-    tile = tokens_ref.shape[0]
-    rows_count = packed_ref.shape[0] - 16
-    experts = gates_ref.shape[0]
-
-    @pl.when(step == 0)
-    def _():
-        for copy in load_rows(blocks, start_ref, weight, sems, column):
-            copy.wait()
-
-    for at in range(0, D, LANES):
-        residual_ref[:, at : at + LANES] = tokens_ref[:, at : at + LANES].astype(
-            jnp.float32
-        ) + jnp.dot(
-            attended_ref[...], weight[:, at : at + LANES], preferred_element_type=jnp.float32
-        )
-    residual = residual_ref[...]
-    inverse = lax.rsqrt(jnp.mean(residual * residual, -1, keepdims=True) + EPS)
-    rows = pl.ds(pl.multiple_of(step * tile, tile), tile)
-    packed_ref[rows, :] = (
-        residual * inverse * small_ref[experts + 1 : experts + 2, :]
-    ).astype(jnp.bfloat16)
-    logits = wide_dot(small_ref[...].astype(jnp.bfloat16), tokens_ref[...])[:experts, :]
-    expert = lax.broadcasted_iota(jnp.int32, logits.shape, 0)
-    routed = expert == routes_ref[:1, :]
-    for choice in range(1, TOP):
-        routed = routed | (expert == routes_ref[choice : choice + 1, :])
-    logits = jnp.where(routed, logits, NEG)
-    exponent = jnp.exp(logits - jnp.max(logits, 0, keepdims=True))
-    exponent = jnp.where(routed, exponent, 0.0)
-    gates = exponent / jnp.sum(exponent, 0, keepdims=True)
-    gates_ref[...] = gates
-    high = gates.astype(jnp.bfloat16)
-    rest = gates - high.astype(jnp.float32)
-    middle = rest.astype(jnp.bfloat16)
-    rest = rest - middle.astype(jnp.float32)
-    for part, values in enumerate((high.astype(jnp.float32), middle.astype(jnp.float32), rest)):
-        lanes = pl.ds(pl.multiple_of(part * rows_count + step * tile, tile), tile)
-        packed_ref[rows_count:, lanes] = jnp.concatenate(
-            [values, jnp.zeros((16 - experts, tile), jnp.float32)], 0
-        ).astype(jnp.bfloat16)
-
-
-def middle_call(starts, tokens, attended, routes, small, blocks, experts, column):
-    rows_count = tokens.shape[0]
-    tile = rows_count // 2
-    low = jnp.bfloat16
-    tiled = pl.BlockSpec((tile, D), lambda i: (i, 0))
-    lanes = lambda rows: pl.BlockSpec((rows, tile), lambda i: (0, i))
-    return pl.pallas_call(
-        functools.partial(middle_kernel, len(blocks), column),
-        grid=(2,),
-        out_shape=[
-            jax.ShapeDtypeStruct((rows_count, D), jnp.float32),
-            jax.ShapeDtypeStruct((rows_count + 16, D), low),
-            jax.ShapeDtypeStruct((experts, rows_count), jnp.float32),
-        ],
-        in_specs=[
-            scalars(),
-            tiled,
-            tiled,
-            lanes(routes.shape[0]),
-            pl.BlockSpec((16, D), lambda i: (0, 0)),
-        ]
-        + [anywhere()] * len(blocks),
-        out_specs=[
-            tiled,
-            pl.BlockSpec((rows_count + 16, D), lambda i: (0, 0)),
-            lanes(experts),
-        ],
-        scratch_shapes=[
-            pltpu.VMEM((D, D), low),
-            pltpu.SemaphoreType.DMA((len(blocks) * blocks[0].shape[0],)),
-        ],
-        compiler_params=pltpu.CompilerParams(vmem_limit_bytes=62 << 20),
-        cost_estimate=small_cost(),
-        name="middle",
-    )(starts, tokens, attended, routes, small, *blocks)
+    )(starts, tokens, table, routes, *blocks)
 
 
 def middle_back_kernel(planes, column, start_ref, *refs):
@@ -817,13 +796,13 @@
     )(starts, *terms, *terms, residual, small, cotangent, tokens, gates, *blocks)
 
 
-def attend_back_kernel(heads_ref, grad_ref, log_ref, first_ref, cosine_ref, sine_ref, raw_ref, bias):
+def attend_back_kernel(heads_ref, grad_ref, log_ref, table_ref, raw_ref, bias):
     rows_count = heads_ref.shape[0]
     width_q, width_kv = HEADS * HEAD_DIM, KV_HEADS * HEAD_DIM
     half = rows_count // 2
     scale = HEAD_DIM ** (-0.5)
-    fill_bias(bias, first_ref)
-    cosine, sine = cosine_ref[...], -sine_ref[...]
+    fill_bias(bias, table_ref[:, 2 * HEAD_DIM : 2 * HEAD_DIM + 1])
+    cosine, sine = table_ref[:, :HEAD_DIM], -table_ref[:, HEAD_DIM : 2 * HEAD_DIM]
     for key_head in range(KV_HEADS):
         key_at = width_q + key_head * HEAD_DIM
         value_at = key_at + width_kv
@@ -862,18 +841,18 @@
         raw_ref[:, value_at : value_at + HEAD_DIM] = value_grad.astype(jnp.bfloat16)
 
 
-def attend_back_call(heads, grads, logs, first, cosine, sine):
+def attend_back_call(heads, grads, logs, table):
     rows_count = heads.shape[0]
     return pl.pallas_call(
         attend_back_kernel,
         out_shape=jax.ShapeDtypeStruct(heads.shape, jnp.bfloat16),
-        in_specs=[whole()] * 6,
+        in_specs=[whole()] * 4,
         out_specs=whole(),
         scratch_shapes=[pltpu.VMEM((rows_count, rows_count), jnp.float32)],
         compiler_params=pltpu.CompilerParams(vmem_limit_bytes=62 << 20),
         cost_estimate=small_cost(),
         name="attend_back",
-    )(heads, grads, logs, first, cosine, sine)
+    )(heads, grads, logs, table)
 
 
 def shard_grad_kernel(extra, start_ref, left_ref, right_ref, *refs):
@@ -1142,14 +1121,16 @@
         return copies
 
     def stores(i, slot):
-        return copies_of(
-            [(grad.at[slot], row_grads[i]), (hidden.at[slot], hidden_grads[i])], sems[3].at[slot]
-        )
+        return copies_of([(grad.at[slot], row_grads[i])], sems[3].at[slot])
+
+    leaving = {}
 
     def body(i, slot):
         if i == 0:
             for copy in out_copies:
                 copy.wait()
+        if i >= 2:
+            leaving.pop(i - 2).wait()
         weights = spread(expert_row(tail[slot], expert), tokens_count)
         weights = jnp.concatenate([weights] * (LANES // 128), 1)
         gate_grad = jnp.zeros((tokens_count, 1), jnp.float32)
@@ -1166,6 +1147,8 @@
         parts = jnp.broadcast_to(split_row(row), (16, 3 * tokens_count))
         index = lax.broadcasted_iota(jnp.int32, parts.shape, 0)
         grad[slot, tokens_count:, :] = jnp.where(index == expert, parts, 0.0).astype(jnp.bfloat16)
+        leaving[i] = pltpu.make_async_copy(hidden.at[slot], hidden_grads[i], sems[4].at[slot])
+        leaving[i].start()
         if i == 0:
             for copy in in_copies:
                 copy.wait()
@@ -1177,6 +1160,8 @@
     out_copies += load_weight(out_chunks, place_ref, out_weight, sems[1])
     in_copies += load_weight(in_chunks, place_ref, in_weight, sems[0], False)
     pipeline(loads, stores, body, count, in_copies)
+    for i in sorted(leaving):
+        leaving[i].wait()
 
 
 def pull_call(packed, cots, slopes, products, in_chunks, out_chunks, places, tokens_count):
@@ -1202,7 +1187,8 @@
             pltpu.SemaphoreType.DMA((len(in_chunks),)),
             pltpu.SemaphoreType.DMA((len(out_chunks),)),
             pltpu.SemaphoreType.DMA((2, 4)),
-            pltpu.SemaphoreType.DMA((2, 2)),
+            pltpu.SemaphoreType.DMA((2, 1)),
+            pltpu.SemaphoreType.DMA((2,)),
         ],
         compiler_params=pltpu.CompilerParams(vmem_limit_bytes=62 << 20),
         cost_estimate=small_cost(),
@@ -1329,9 +1315,9 @@
     offset = (position - first).astype(jnp.float32)
     frequency = ROPE_BASE ** (-2.0 * jnp.arange(HEAD_DIM // 2, dtype=jnp.float32) / HEAD_DIM)
     angles = offset[:, None] * frequency[None, :]
-    cosine = jnp.tile(jnp.cos(angles), (1, 2))
-    sine = jnp.concatenate([-jnp.sin(angles), jnp.sin(angles)], 1)
-    first = first[:, None]
+    cosine, sine = jnp.cos(angles), jnp.sin(angles)
+    first = jnp.broadcast_to(first.astype(jnp.float32)[:, None], (rows_count, HEAD_DIM))
+    table = jnp.concatenate([cosine, cosine, -sine, sine, first], 1)
 
     width_early = width_qkv + 128
 
@@ -1360,12 +1346,12 @@
     in_low, out_low = expert_in[0].astype(low), expert_out[0].astype(low)
     column = [sent, around(sent)]
     column.append(around(column[1]))
-    column[2], in_low, out_low, cosine, sine, first, routes_t = hold(
-        column[2], in_low, out_low, cosine, sine, first, routes.T
+    column[2], in_low, out_low, table, routes_t = hold(
+        column[2], in_low, out_low, table, routes.T
     )
     column.append(around(column[2]))
     joint = jnp.stack(column)
-    cut = in_low.shape[0] * 5 // 8
+    cut = in_low.shape[0] * 3 // 4
     cot_x, cot_y, joint, in_low, out_low = hold(cot_x, cot_y, joint, in_low, out_low)
     in_near, in_rest, out_chunks = [in_low[:cut]], [in_low[cut:]], [out_low]
 
@@ -1393,12 +1379,8 @@
     cot_far = forward(outward)
     cot_core, cot_y2 = to_core(cotangent), to_core(cot_y)
     in_near.append(around(in_near[2]))
-    in_rest.append(around(in_rest[1]))
-    attn_in, heads, attended, logs, small = attend_call(
-        starts, tokens, first, cosine, sine, plane, width_early
-    )
-    residual_mid, packed, gates = middle_call(
-        starts, tokens, attended, routes_t, small, plane, experts, width_early
+    attn_in, heads, attended, residual_mid, packed, logs, small, gates = attend_call(
+        starts, tokens, table, routes_t, plane, width_early, experts
     )
     packed, cot_far, cot_core, cot_y2, in_near, in_rest, out_chunks = hold(
         packed, cot_far, cot_core, cot_y2, in_near, in_rest, out_chunks
@@ -1406,6 +1388,7 @@
 
     packed_x, packed_y = cross(packed)
     packed_core = to_core(packed)
+    in_rest.append(around(in_rest[1]))
     in_rest.append(around(in_rest[2]))
     in_chunks = in_near + in_rest
     out_chunks.append(around(after(out_chunks[0], in_rest[3])))
@@ -1422,16 +1405,13 @@
     packed_x, packed_y, gated[0], out_chunks, cot_far = hold(
         packed_x, packed_y, gated[0], out_chunks, cot_far
     )
-    outward = onward(packed_x, packed_y)
-    outward, packed_x, packed_y = hold(outward, packed_x, packed_y)
     packed_x2, packed_y2 = to_core(packed_x), to_core(packed_y)
-    packed_far = forward(outward)
+    packed_far = forward(onward(packed_x, packed_y))
     cot_far2 = to_core(cot_far)
     out_chunks.append(around(out_chunks[1]))
     cot_blocks = [cotangent, cot_core, cot_x, cot_x2, cot_y, cot_y2, cot_far, cot_far2]
     packed_blocks[2:6] = [packed_x, packed_x2, packed_y, packed_y2]
-    hidden((2, 4))
-    hidden((3, 5), gated[2])
+    hidden((2, 4, 3, 5))
     packed_far, out_chunks, gated[3] = hold(packed_far, out_chunks, gated[3])
     packed_far2 = to_core(packed_far)
     packed_blocks[6:] = hold(packed_far, packed_far2)
@@ -1532,7 +1512,7 @@
         starts, [after(row_grads[0], rows_x), back_own, from_x, from_y], residual_mid,
         small, cotangent, tokens, gates, plane, width_early,
     )
-    raw_grad = attend_back_call(heads, attended_grad, logs, first, cosine, sine)
+    raw_grad = attend_back_call(heads, attended_grad, logs, table)
     early_even, early_odd = shard_grad_call(spots, attn_in, raw_grad, columns_dp, owners)
     early_even, early_odd, mid_low, rows_back, near_moved, rest_moved = hold(
         early_even, early_odd, mid_low, rows_back, near_moved, rest_moved

time: 543 us -> 533 us (0.982)
  Pallas kernels: 239 us -> 229 us
    pallas_call x1 -> x0, Pallas kernels: 9.57 us -> none  [middle_call(): pl.pallas_call(functools.partial(middle_kernel, len(blocks), column), gri...]
    ppermute x21, waiting for transfers between devices: 104 us -> 111 us  [around(): return lax.ppermute(value, 'dp', ring)]
    ppermute x7, waiting for transfers between devices: 8.34 us -> 2.4 us  [to_y(): return lax.ppermute(value, 'expert', ACROSS_Y)]
    pallas_call x1, Pallas kernels: 16.1 us -> 22 us  [attend_call(): pl.pallas_call(functools.partial(attend_kernel, len(blocks)), out_shape=[...]
    pallas_call x4 -> x3, Pallas kernels: 47.7 us -> 42.5 us  [hidden_call(): pl.pallas_call(functools.partial(hidden_kernel, count, len(chunks), token...]
  transfers between devices with their start and end apart: 70 -> 70, of which waited for: 24 -> 24; matrix products, arithmetic and copies ran while one was open for 15% -> 15% of each run, Pallas kernels for 43% -> 42%
where the time goes in v3:
time: 533 us; the launch traced here: 529 us
  Pallas kernels  229 us (43%)
  waiting for transfers between devices  151 us (28%)
  other arithmetic  76.2 us (14%)
  starting transfers between devices  46 us (9%)
  local copies, waits for them, and re-layouts  19.2 us (4%)
  between operations  7.31 us (1%)
    ppermute x21, waiting for transfers between devices, around(): return lax.ppermute(value, 'dp', ring)  111 us
    pallas_call x2, Pallas kernels, pull_call(): pl.pallas_call(functools.partial(pull_kernel, count, (len(in_chunks), len...  50.1 us
    pallas_call x3, Pallas kernels, hidden_call(): pl.pallas_call(functools.partial(hidden_kernel, count, len(chunks), token...  42.5 us
    pallas_call x2, Pallas kernels, weight_grad_call(): pl.pallas_call(functools.partial(weight_grad_kernel, count, rows), grid=(...  42.5 us
    convert_element_type x18, other arithmetic, add_low(): return total.astype(jnp.bfloat16)  39.8 us
    pallas_call x1, Pallas kernels, attend_call(): pl.pallas_call(functools.partial(attend_kernel, len(blocks)), out_shape=[...  22 us
    ppermute x6, waiting for transfers between devices, spread_pieces(): lax.ppermute(total[p], 'dp', [(i, (i - p) % columns_dp) for i in range(co...  20.1 us
    pallas_call x2, Pallas kernels, product_call(): pl.pallas_call(functools.partial(product_kernel, count), out_shape=[jax.S...  19.1 us
  transfers between devices with their start and end apart: 70, of which 24 were waited for; matrix products, arithmetic and copies ran while one was open for 15% of the time, Pallas kernels for 42%

profile of v3, /device:TPU:0, one launch (start us, length us, event | category | flops | bytes accessed | tf_op | source)
XLA Modules:
  0.0 528.7 jit_solution(3435348168252198299)
XLA Ops:
  0.7 3.0 collective-permute-start.3
  10.6 1.6 collective-permute-start
  12.4 2.8 convert_bitcast_fusion
  15.3 1.8 multiply_sine_fusion
  17.2 2.2 concatenate.19.table_ref
  19.4 2.8 collective-permute-done
  23.2 9.7 %collective-permute-done.1 = bf16[48,3712]{1,0:T(8,128)(2,1)S(1)} collective-permute-done((bf16[48,3712]{1,0:T(8,128)(2,1)}, bf16[48,3712]{1,0:T(8,128)(2,1)S(1)}, u32[]{:S(2)}, u32[]{:S(2)}) %collective-permute-start.1) | collective-permute-done | bytes 356384 | tf_op jit(solution)/shard_map/ppermute | solution.py:1343
  32.9 9.5 %collective-permute-done.4 = bf16[48,3712]{1,0:T(8,128)(2,1)S(1)} collective-permute-done((bf16[48,3712]{1,0:T(8,128)(2,1)S(1)}, bf16[48,3712]{1,0:T(8,128)(2,1)S(1)}, u32[]{:S(2)}, u32[]{:S(2)}) %collective-permute-start.4) | collective-permute-done | bytes 356384 | tf_op jit(solution)/shard_map/ppermute | solution.py:1343
  46.6 28.6 %collective-permute-done.9.refs_7_.refs_9_.refs_13_.refs_29_ = bf16[96,1536]{1,0:T(8,128)(2,1)} collective-permute-done((bf16[96,1536]{1,0:T(8,128)(2,1)}, bf16[96,1536]{1,0:T(8,128)(2,1)}, u32[]{:S(2)}, u32[]{:S(2)}) %collective-permute-start.9) | collective-permute-done | bytes 294944 | tf_op jit(solution)/shard_map/ppermute | solution.py:1343
  75.2 2.4 collective-permute-done.6.refs_4_.refs_17_.refs_9_
  81.2 2.8 broadcast_select_fusion.1
  84.0 21.1 %collective-permute-done.13.refs_4_.refs_6_.refs_10_.refs_26_ = bf16[288,1536]{1,0:T(8,128)(2,1)S(1)} collective-permute-done((bf16[288,1536]{1,0:T(8,128)(2,1)S(1)}, bf16[288,1536]{1,0:T(8,128)(2,1)S(1)}, u32[]{:S(2)}, u32[]{:S(2)}) %collective-permute-start.13) | collective-permute-done | bytes 884768 | tf_op jit(solution)/shard_map/ppermute | solution.py:1343
  105.7 3.9 collective-permute-done.15.refs_7_.refs_20_.refs_12_
  111.6 22.0 %attend.1 = (bf16[512,1536]{1,0:T(8,128)(2,1)}, bf16[512,2048]{1,0:T(8,128)(2,1)}, bf16[512,1536]{1,0:T(8,128)(2,1)}, f32[512,1536]{1,0:T(8,128)}, bf16[528,1536...) custom-call(s32[32]{0:T(128)} %mul.321.start_ref, bf16[512,1536]{1,0:T(8,128)(2,1)} %refs_1_.1, ...), custom_call_target="tpu_custom_call" | custom-call | flops 1024 | bytes 1024 | tf_op jit(solution)/shard_map/attend/pallas_call | solution.py:689
  137.2 10.9 %collective-permute-done.23.refs_8_.refs_10_.refs_14_.refs_30_ = bf16[96,1536]{1,0:T(8,128)(2,1)S(1)} collective-permute-done((bf16[96,1536]{1,0:T(8,128)(2,1)}, bf16[96,1536]{1,0:T(8,128)(2,1)S(1)}, u32[]{:S(2)}, u32[]{:S(2)}) %collective-permute-start.23) | collective-permute-done | bytes 294944 | tf_op jit(solution)/shard_map/ppermute | solution.py:1343
  148.1 9.8 %collective-permute-done.24.refs_9_.refs_11_.refs_15_.refs_31_ = bf16[96,1536]{1,0:T(8,128)(2,1)S(1)} collective-permute-done((bf16[96,1536]{1,0:T(8,128)(2,1)S(1)}, bf16[96,1536]{1,0:T(8,128)(2,1)S(1)}, u32[]{:S(2)}, u32[]{:S(2)}) %collective-permute-start.24) | collective-permute-done | bytes 294944 | tf_op jit(solution)/shard_map/ppermute | solution.py:1343
  159.6 11.9 %expert_hidden.3 = (bf16[512,1536]{1,0:T(8,128)(2,1)}, bf16[512,1536]{1,0:T(8,128)(2,1)}, bf16[512,768]{1,0:T(8,128)(2,1)}, bf16[512,768]{1,0:T(8,128)(2,1)}, bf...) custom-call(s32[5]{0:T(128)} %pad_add_fusion.place_ref, bf16[528,1536]{1,0:T(8,128)(2,1)} %get-tuple-element.313.refs_0_, ...), custom_call_target="tpu_custom_call" | custom-call | flops 1024 | bytes 1024 | tf_op jit(solution)/shard_map/expert_hidden/pallas_call | solution.py:1057
  171.5 3.0 collective-permute-done.25.refs_3_.refs_17_.refs_33_.refs_7_
  177.7 1.9 collective-permute-done.29.refs_3_.refs_4_.refs_5_
  180.7 18.7 %expert_hidden.4 = (bf16[512,1536]{1,0:T(8,128)(2,1)}, bf16[512,1536]{1,0:T(8,128)(2,1)}, bf16[512,1536]{1,0:T(8,128)(2,1)}, bf16[512,1536]{1,0:T(8,128)(2,1)}, ...) custom-call(s32[5]{0:T(128)} %pad_add_fusion.place_ref, ...), custom_call_target="tpu_custom_call" | custom-call | flops 1024 | bytes 1024 | tf_op jit(solution)/shard_map/expert_hidden/pallas_call | solution.py:1057
  200.0 4.2 collective-permute-done.30.refs_1_.refs_0_.refs_7_
  205.8 11.9 %expert_hidden.5 = (bf16[512,1536]{1,0:T(8,128)(2,1)}, bf16[512,1536]{1,0:T(8,128)(2,1)}, bf16[512,768]{1,0:T(8,128)(2,1)}, bf16[512,768]{1,0:T(8,128)(2,1)}, bf...) custom-call(s32[5]{0:T(128)} %pad_add_fusion.place_ref, ...), custom_call_target="tpu_custom_call" | custom-call | flops 1024 | bytes 1024 | tf_op jit(solution)/shard_map/expert_hidden/pallas_call | solution.py:1057
  217.8 15.8 %expert_out_grad.1 = bf16[768,1536]{1,0:T(8,128)(2,1)} custom-call(bf16[512,768]{1,0:T(8,128)(2,1)} %get-tuple-element.333.refs_0_.refs_5_, bf16[512,768]{1,0:T(8,128)(2,1)} %get-tuple-element.334.refs_1_.refs_4_, bf16[512,768]{1,0:T(8,128)(2,1)} %get-tuple-element.335.refs_2_.refs_3_, bf16[512,768]{1,0:T(8,128)(2,1)} %get-tuple-element.336.refs_3_.refs_2_, ...), custom_call_target="tpu_custom_call" | custom-call | flops 1024 | bytes 1024 | tf_op jit(solution)/shard_map/expert_out_grad/pallas_call | solution.py:1255
  233.6 1.9 constant_dynamic-slice_fusion.2
  235.5 6.7 %expert_rows.2 = (bf16[512,1536]{1,0:T(8,128)(2,1)}, bf16[512,1536]{1,0:T(8,128)(2,1)}) custom-call(s32[5]{0:T(128)} %pad_add_fusion.place_ref, bf16[512,768]{1,0:T(8,128)(2,1)} %get-tuple-element.349.refs_7_.refs_0_, bf16[512,768]{1,0:T(8,128)(2,1)} %get-tuple-element.339.refs_6_.refs_1_, ...), custom_call_target="tpu_custom_call" | custom-call | flops 1024 | bytes 1024 | tf_op jit(solution)/shard_map/expert_rows/pallas_call | solution.py:1225
  242.5 2.7 collective-permute-start.33
  245.2 16.2 %expert_pull.2 = (bf16[528,1536]{1,0:T(8,128)(2,1)}, bf16[528,1536]{1,0:T(8,128)(2,1)}, bf16[512,1536]{1,0:T(8,128)(2,1)}, bf16[512,1536]{1,0:T(8,128)(2,1)}) custom-call(s32[5]{0:T(128)} %pad_add_fusion.place_ref, bf16[528,1536]{1,0:T(8,128)(2,1)} %copy-done.7, bf16[528,1536]{1,0:T(8,128)(2,1)} %collective-permute-done.26.refs_0_.refs_1_.refs_6_, ...), custom_call_target="tpu_custom_call" | custom-call | flops 1024 | bytes 1024 | tf_op jit(solution)/shard_map/expert_pull/pallas_call | solution.py:1171
  262.4 2.2 add_convert_fusion.14
  264.6 1.5 add_convert_fusion.8
  266.3 1.8 add_convert_fusion.4
  269.2 2.0 collective-permute-start.37
  271.3 33.9 %expert_pull.3 = (bf16[528,1536]{1,0:T(8,128)(2,1)}, bf16[528,1536]{1,0:T(8,128)(2,1)}, bf16[528,1536]{1,0:T(8,128)(2,1)}, bf16[528,1536]{1,0:T(8,128)(2,1)}, bf...) custom-call(s32[5]{0:T(128)} %pad_add_fusion.place_ref, ...), custom_call_target="tpu_custom_call" | custom-call | flops 1024 | bytes 1024 | tf_op jit(solution)/shard_map/expert_pull/pallas_call | solution.py:1171
  307.5 12.3 %expert_rows.3 = (bf16[512,1536]{1,0:T(8,128)(2,1)}, bf16[512,1536]{1,0:T(8,128)(2,1)}, bf16[512,1536]{1,0:T(8,128)(2,1)}, bf16[512,1536]{1,0:T(8,128)(2,1)}, bf...) custom-call(s32[5]{0:T(128)} %pad_add_fusion.place_ref, bf16[512,768]{1,0:T(8,128)(2,1)} %get-tuple-element.400.refs_5_.refs_0_, ...), custom_call_target="tpu_custom_call" | custom-call | flops 1024 | bytes 1024 | tf_op jit(solution)/shard_map/expert_rows/pallas_call | solution.py:1225
  319.8 2.3 add_convert_fusion.13
  322.2 6.7 %add_convert_fusion.2 = (bf16[528,1536]{1,0:T(8,128)(2,1)}, bf16[528,1536]{1,0:T(8,128)(2,1)}) fusion(bf16[528,1536]{1,0:T(8,128)(2,1)} %collective-permute-done.39, bf16[528,1536]{1,0:T(8,128)(2,1)} %get-tuple-element.410, bf16[528,1536]{1,0:T(8,128)(2,1)} %collective-permute-done.36, pred[]{:T(512)S(6)} %eq.6, pred[]{:T(512)S(6)} %eq.7, ...), kind=kLoop, calls=%fused_computation.3 | loop fusion | flops 11354112 | bytes 11354114 | tf_op jit(solution)/shard_map/convert_element_type | solution.py:445
  333.0 26.7 %expert_in_grad.1 = bf16[1536,1536]{1,0:T(8,128)(2,1)} custom-call(bf16[528,1536]{1,0:T(8,128)(2,1)} %get-tuple-element.313.refs_0_, bf16[528,1536]{1,0:T(8,128)(2,1)} %collective-permute-done.22.refs_1_, bf16[528,1536]{1,0:T(8,128)(2,1)} %collective-permute-done.20.refs_0_.refs_3_.refs_2_, bf16[528,1536]{1,0:T(8,128)(2,1)} %collective-permute-done.28.refs_2_.refs_3_, ...), custom_call_target="tpu_custom_call" | custom-call | flops 1024 | bytes 1024 | tf_op jit(solution)/shard_map/expert_in_grad/pallas_call | solution.py:1255
  359.7 1.9 constant_dynamic-slice_fusion.1
  361.6 2.0 constant_dynamic-slice_fusion
  363.6 5.7 %add_convert_fusion.6 = (bf16[512,1536]{1,0:T(8,128)(2,1)}, bf16[512,1536]{1,0:T(8,128)(2,1)}) fusion(bf16[512,1536]{1,0:T(8,128)(2,1)} %collective-permute-done.46, bf16[512,1536]{1,0:T(8,128)(2,1)S(1)} %copy-done.31, bf16[512,1536]{1,0:T(8,128)(2,1)} %collective-permute-done.41, pred[]{:T(512)S(6)} %eq.6, pred[]{:T(512)S(6)} %eq.7, ...), kind=kLoop, calls=%fused_computation.7 | loop fusion | flops 11010048 | bytes 11010050 | tf_op jit(solution)/shard_map/convert_element_type | solution.py:445
  371.6 2.5 collective-permute-start.49
  375.3 11.9 %middle_back.1 = (f32[512,1536]{1,0:T(8,128)}, bf16[512,1536]{1,0:T(8,128)(2,1)}, bf16[512,1536]{1,0:T(8,128)(2,1)}, bf16[16,512]{1,0:T(8,128)(2,1)}, f32[16,1536]{1,0:T(8,128)}) custom-call(s32[32]{0:T(128)} %mul.321.start_ref, bf16[528,1536]{1,0:T(8,128)(2,1)} %get-tuple-element.442.refs_0_.refs_4_, bf16[528,1536]{1,0:T(8,128)(2,1)} %copy-done.18, ...), custom_call_target="tpu_custom_call" | custom-call | flops 1024 | bytes 1024 | tf_op jit(solution)/shard_map/middle_back/pallas_call | solution.py:773
  387.2 16.3 %attend_back.1.right_ref.refs_0_ = bf16[512,2048]{1,0:T(8,128)(2,1)} custom-call(bf16[512,2048]{1,0:T(8,128)(2,1)} %get-tuple-element.440.heads_ref, bf16[512,1536]{1,0:T(8,128)(2,1)} %get-tuple-element.448.grad_ref, f32[512,128]{1,0:T(8,128)} %get-tuple-element.449.log_ref, f32[512,384]{1,0:T(8,128)} %concatenate.19.table_ref), custom_call_target="tpu_custom_call" | custom-call | flops 1024 | bytes 1024 | tf_op jit(solution)/shard_map/attend_back/pallas_call | solution.py:846
  403.5 7.1 %shard_grad.2 = (bf16[4,4,48,2048]{3,2,1,0:T(8,128)(2,1)}, bf16[4,4,48,2048]{3,2,1,0:T(8,128)(2,1)}) custom-call(s32[9]{0:T(128)} %pad_add_fusion.1.start_ref, bf16[512,1536]{1,0:T(8,128)(2,1)} %get-tuple-element.439.left_ref, bf16[512,2048]{1,0:T(8,128)(2,1)} %attend_back.1.right_ref.refs_0_), custom_call_target="tpu_custom_call" | custom-call | flops 1024 | bytes 1024 | tf_op jit(solution)/shard_map/shard_grad/pallas_call | solution.py:890
  412.0 1.7 collective-permute-start.53
  413.7 6.1 %shard_grad.3 = (bf16[4,4,48,1664]{3,2,1,0:T(8,128)(2,1)}, bf16[4,4,48,1664]{3,2,1,0:T(8,128)(2,1)}) custom-call(s32[9]{0:T(128)} %pad_add_fusion.1.start_ref, bf16[512,1536]{1,0:T(8,128)(2,1)} %get-tuple-element.461.left_ref, bf16[512,1536]{1,0:T(8,128)(2,1)} %get-tuple-element.462.right_ref, f32[16,1536]{1,0:T(8,128)} %get-tuple-element.463.refs_0_), custom_call_target="tpu_custom_call" | custom-call | flops 1024 | bytes 1024 | tf_op jit(solution)/shard_map/shard_grad/pallas_call | solution.py:890
  419.8 2.4 add_convert_fusion.11
  422.2 4.2 collective-permute-done.53
  426.4 1.8 fusion.12
  433.0 1.9 add_convert_fusion.15
  434.9 11.3 %entry_back.1 = f32[512,1536]{1,0:T(8,128)} custom-call(s32[32]{0:T(128)} %mul.321.start_ref, bf16[512,2048]{1,0:T(8,128)(2,1)} %attend_back.1.right_ref.refs_0_, bf16[512,1536]{1,0:T(8,128)(2,1)} %refs_1_.1, f32[512,1536]{1,0:T(8,128)} %get-tuple-element.474.refs_2_, f32[16,1536]{1,0:T(8,128)} %get-tuple-element.446.refs_9_.refs_3_, ...), custom_call_target="tpu_custom_call" | custom-call | flops 1024 | bytes 1024 | tf_op jit(solution)/shard_map/entry_back/pallas_call | solution.py:943
  446.2 3.4 add_convert_fusion
  449.6 3.3 collective-permute-done.56
  455.9 1.8 fusion.4
  461.0 4.5 add_convert_fusion.5
  465.5 2.4 multiply_subtract_fusion.1
  468.0 2.0 add_convert_fusion.1
  470.0 5.0 collective-permute-done.59
  474.9 7.4 %collective-permute-done.60 = bf16[240,1536]{1,0:T(8,128)(2,1)S(1)} collective-permute-done((bf16[240,1536]{1,0:T(8,128)(2,1)S(1)}, bf16[240,1536]{1,0:T(8,128)(2,1)S(1)}, u32[]{:S(2)}, u32[]{:S(2)}) %collective-permute-start.60) | collective-permute-done | bytes 737312 | tf_op jit(solution)/shard_map/ppermute | solution.py:1343
  482.3 2.3 collective-permute-done.57
  489.5 3.8 collective-permute-start.62
  493.4 4.6 multiply_subtract_fusion
  499.1 10.3 %collective-permute-done.63 = bf16[48,2048]{1,0:T(8,128)(2,1)} collective-permute-done((bf16[48,2048]{1,0:T(8,128)(2,1)}, bf16[48,2048]{1,0:T(8,128)(2,1)}, u32[]{:S(2)}, u32[]{:S(2)}) %collective-permute-start.63) | collective-permute-done | bytes 196640 | tf_op jit(solution)/shard_map/ppermute | solution.py:1568
  515.2 3.4 collective-permute-done.67
  519.5 5.0 collective-permute-done.68
  (283 shorter events, 65.8 us)
Async XLA Ops:
  0.7 43.1 %collective-permute-start.3 = (bf16[512,1536]{1,0:T(8,128)(2,1)}, bf16[512,1536]{1,0:T(8,128)(2,1)}, u32[]{:S(2)}, u32[]{:S(2)}) collective-permute-start(bf16[512,1536]{1,0:T(8,128)(2,1)} %refs_10_.1), channel_id=1, source_target_pairs={{0,4},{1,5},{2,6},{3,7},{4,0},{5,1},{6,2},{7,3},{8,12},{9,13},{10,... | collective-permute-start | bytes 4718600 | tf_op jit(solution)/shard_map/ppermute | solution.py:410
  3.7 40.0 %collective-permute-start.2 = (bf16[512,1536]{1,0:T(8,128)(2,1)}, bf16[512,1536]{1,0:T(8,128)(2,1)S(1)}, u32[]{:S(2)}, u32[]{:S(2)}) collective-permute-start(bf16[512,1536]{1,0:T(8,128)(2,1)} %refs_10_.1), channel_id=1, source_target_pairs={{0,2},{1,3},{2,0},{3,1},{4,6},{5,7},{6,4},{7,5},{8,10},{9,11},{10,... | collective-permute-start | bytes 4718600 | tf_op jit(solution)/shard_map/ppermute | solution.py:406
  10.6 11.7 %collective-permute-start = (bf16[48,3712]{1,0:T(8,128)(2,1)}, bf16[48,3712]{1,0:T(8,128)(2,1)}, u32[]{:S(2)}, u32[]{:S(2)}) collective-permute-start(bf16[48,3712]{1,0:T(8,128)(2,1)} %concatenate.18), channel_id=1, source_target_pairs={{0,8},{8,16},{16,24},{24,0},{1,9},{9,17},{17,25},{25,1},{2,10},{10... | collective-permute-start | bytes 1069064 | tf_op jit(solution)/shard_map/ppermute | solution.py:1343
  22.2 10.7 %collective-permute-start.1 = (bf16[48,3712]{1,0:T(8,128)(2,1)}, bf16[48,3712]{1,0:T(8,128)(2,1)S(1)}, u32[]{:S(2)}, u32[]{:S(2)}) collective-permute-start(bf16[48,3712]{1,0:T(8,128)(2,1)} %collective-permute-done), channel_id=1, source_target_pairs={{0,8},{8,16},{16,24},{24,0},{1,9},{9,17},{17,25},{25,1},{2,10},{10... | collective-permute-start | bytes 1069064 | tf_op jit(solution)/shard_map/ppermute | solution.py:1343
  32.9 9.5 %collective-permute-start.4 = (bf16[48,3712]{1,0:T(8,128)(2,1)S(1)}, bf16[48,3712]{1,0:T(8,128)(2,1)S(1)}, u32[]{:S(2)}, u32[]{:S(2)}) collective-permute-start(bf16[48,3712]{1,0:T(8,128)(2,1)S(1)} %collective-permute-done.1), channel_id=1, source_target_pairs={{0,8},{8,16},{16,24},{24,0},{1,9},{9,17},{17,25},{25,1},{2,10},{10... | collective-permute-start | bytes 1069064 | tf_op jit(solution)/shard_map/ppermute | solution.py:1343
  43.8 31.4 %collective-permute-start.7 = (bf16[4,48,3712]{2,1,0:T(8,128)(2,1)S(1)}, bf16[4,48,3712]{2,1,0:T(8,128)(2,1)}, u32[]{:S(2)}, u32[]{:S(2)}) collective-permute-start(bf16[4,48,3712]{2,1,0:T(8,128)(2,1)S(1)} %pad_maximum_fusion.refs_0_.refs_13_.refs_5_), channel_id=1, source_target_pairs={{0,1},{1,0},{2,3},{3,2},{4,5},{5,4},{6,7},{7,6},{8,9},{9,8},{10,11... | collective-permute-start | bytes 4276232 | tf_op jit(solution)/shard_map/ppermute | solution.py:414
  43.8 33.8 %collective-permute-start.6 = (bf16[4,48,3712]{2,1,0:T(8,128)(2,1)S(1)}, bf16[4,48,3712]{2,1,0:T(8,128)(2,1)}, u32[]{:S(2)}, u32[]{:S(2)}) collective-permute-start(bf16[4,48,3712]{2,1,0:T(8,128)(2,1)S(1)} %pad_maximum_fusion.refs_0_.refs_13_.refs_5_), channel_id=1, source_target_pairs={{0,4},{1,5},{2,6},{3,7},{4,0},{5,1},{6,2},{7,3},{8,12},{9,13},{10,... | collective-permute-start | bytes 4276232 | tf_op jit(solution)/shard_map/ppermute | solution.py:410
  45.0 32.8 %collective-permute-start.5 = (bf16[4,48,3712]{2,1,0:T(8,128)(2,1)S(1)}, bf16[4,48,3712]{2,1,0:T(8,128)(2,1)}, u32[]{:S(2)}, u32[]{:S(2)}) collective-permute-start(bf16[4,48,3712]{2,1,0:T(8,128)(2,1)S(1)} %pad_maximum_fusion.refs_0_.refs_13_.refs_5_), channel_id=1, source_target_pairs={{0,2},{1,3},{2,0},{3,1},{4,6},{5,7},{6,4},{7,5},{8,10},{9,11},{10,... | collective-permute-start | bytes 4276232 | tf_op jit(solution)/shard_map/ppermute | solution.py:406
  45.7 29.6 %collective-permute-start.8 = (bf16[288,1536]{1,0:T(8,128)(2,1)S(1)}, bf16[288,1536]{1,0:T(8,128)(2,1)S(1)}, u32[]{:S(2)}, u32[]{:S(2)}) collective-permute-start(bf16[288,1536]{1,0:T(8,128)(2,1)S(1)} %slice.128.refs_2_.refs_4_.refs_8_.refs_24_), channel_id=1, source_target_pairs={{0,8},{8,16},{16,24},{24,0},{1,9},{9,17},{17,25},{25,1},{2,10},{10... | collective-permute-start | bytes 2654216 | tf_op jit(solution)/shard_map/ppermute | solution.py:1343
  46.6 28.6 %collective-permute-start.9 = (bf16[96,1536]{1,0:T(8,128)(2,1)}, bf16[96,1536]{1,0:T(8,128)(2,1)}, u32[]{:S(2)}, u32[]{:S(2)}) collective-permute-start(bf16[96,1536]{1,0:T(8,128)(2,1)} %slice.129.refs_6_.refs_8_.refs_12_.refs_28_), channel_id=1, source_target_pairs={{0,8},{8,16},{16,24},{24,0},{1,9},{9,17},{17,25},{25,1},{2,10},{10... | collective-permute-start | bytes 884744 | tf_op jit(solution)/shard_map/ppermute | solution.py:1343
  77.8 27.3 %collective-permute-start.14 = (bf16[512,1536]{1,0:T(8,128)(2,1)}, bf16[512,1536]{1,0:T(8,128)(2,1)S(1)}, u32[]{:S(2)}, u32[]{:S(2)}) collective-permute-start(bf16[512,1536]{1,0:T(8,128)(2,1)} %copy-done.8), channel_id=1, source_target_pairs={{0,1},{1,0},{2,3},{3,2},{4,5},{5,4},{6,7},{7,6},{8,9},{9,8},{10,11... | collective-permute-start | bytes 4718600 | tf_op jit(solution)/shard_map/ppermute | solution.py:414
  79.4 25.7 %collective-permute-start.10 = (bf16[4,48,3712]{2,1,0:T(8,128)(2,1)S(1)}, bf16[4,48,3712]{2,1,0:T(8,128)(2,1)S(1)}, u32[]{:S(2)}, u32[]{:S(2)}) collective-permute-start(bf16[4,48,3712]{2,1,0:T(8,128)(2,1)S(1)} %broadcast_select_fusion.2), channel_id=1, source_target_pairs={{0,2},{1,5},{2,0},{3,7},{4,6},{5,1},{6,4},{7,3},{8,10},{9,13},{10,... | collective-permute-start | bytes 4276232 | tf_op jit(solution)/shard_map/ppermute | solution.py:422
  80.4 24.6 %collective-permute-start.11 = (bf16[4,48,3712]{2,1,0:T(8,128)(2,1)}, bf16[4,48,3712]{2,1,0:T(8,128)(2,1)S(1)}, u32[]{:S(2)}, u32[]{:S(2)}) collective-permute-start(bf16[4,48,3712]{2,1,0:T(8,128)(2,1)} %collective-permute-done.5.refs_2_.refs_15_.refs_7_), channel_id=1, source_target_pairs={{0,1},{1,0},{2,3},{3,2},{4,5},{5,4},{6,7},{7,6},{8,9},{9,8},{10,11... | collective-permute-start | bytes 4276232 | tf_op jit(solution)/shard_map/ppermute | solution.py:414
  81.2 23.9 %collective-permute-start.12 = (bf16[4,48,3712]{2,1,0:T(8,128)(2,1)}, bf16[4,48,3712]{2,1,0:T(8,128)(2,1)S(1)}, u32[]{:S(2)}, u32[]{:S(2)}) collective-permute-start(bf16[4,48,3712]{2,1,0:T(8,128)(2,1)} %collective-permute-done.6.refs_4_.refs_17_.refs_9_), channel_id=1, source_target_pairs={{0,1},{1,0},{2,3},{3,2},{4,5},{5,4},{6,7},{7,6},{8,9},{9,8},{10,11... | collective-permute-start | bytes 4276232 | tf_op jit(solution)/shard_map/ppermute | solution.py:414
  81.2 23.9 %collective-permute-start.13 = (bf16[288,1536]{1,0:T(8,128)(2,1)S(1)}, bf16[288,1536]{1,0:T(8,128)(2,1)S(1)}, u32[]{:S(2)}, u32[]{:S(2)}) collective-permute-start(bf16[288,1536]{1,0:T(8,128)(2,1)S(1)} %collective-permute-done.8.refs_3_.refs_5_.refs_9_.refs_25_), channel_id=1, source_target_pairs={{0,8},{8,16},{16,24},{24,0},{1,9},{9,17},{17,25},{25,1},{2,10},{10... | collective-permute-start | bytes 2654216 | tf_op jit(solution)/shard_map/ppermute | solution.py:1343
  105.2 28.5 %collective-permute-start.17 = (bf16[512,1536]{1,0:T(8,128)(2,1)}, bf16[512,1536]{1,0:T(8,128)(2,1)}, u32[]{:S(2)}, u32[]{:S(2)}) collective-permute-start(bf16[512,1536]{1,0:T(8,128)(2,1)} %refs_10_.1), channel_id=1, source_target_pairs={{0,1},{1,0},{2,3},{3,2},{4,5},{5,4},{6,7},{7,6},{8,9},{9,8},{10,11... | collective-permute-start | bytes 4718600 | tf_op jit(solution)/shard_map/ppermute | solution.py:414
  109.6 24.8 %collective-permute-start.16 = (bf16[512,1536]{1,0:T(8,128)(2,1)}, bf16[512,1536]{1,0:T(8,128)(2,1)}, u32[]{:S(2)}, u32[]{:S(2)}) collective-permute-start(bf16[512,1536]{1,0:T(8,128)(2,1)} %broadcast_select_fusion.1), channel_id=1, source_target_pairs={{0,2},{1,5},{2,0},{3,7},{4,6},{5,1},{6,4},{7,3},{8,10},{9,13},{10,... | collective-permute-start | bytes 4718600 | tf_op jit(solution)/shard_map/ppermute | solution.py:422
  110.2 24.2 %collective-permute-start.18 = (bf16[512,1536]{1,0:T(8,128)(2,1)}, bf16[512,1536]{1,0:T(8,128)(2,1)}, u32[]{:S(2)}, u32[]{:S(2)}) collective-permute-start(bf16[512,1536]{1,0:T(8,128)(2,1)} %collective-permute-done.3.refs_12_.refs_11_), channel_id=1, source_target_pairs={{0,1},{1,0},{2,3},{3,2},{4,5},{5,4},{6,7},{7,6},{8,9},{9,8},{10,11... | collective-permute-start | bytes 4718600 | tf_op jit(solution)/shard_map/ppermute | solution.py:414
  110.7 23.6 %collective-permute-start.19 = (bf16[288,1536]{1,0:T(8,128)(2,1)S(1)}, bf16[288,1536]{1,0:T(8,128)(2,1)S(1)}, u32[]{:S(2)}, u32[]{:S(2)}) collective-permute-start(bf16[288,1536]{1,0:T(8,128)(2,1)S(1)} %collective-permute-done.13.refs_4_.refs_6_.refs_10_.refs_26_), channel_id=1, source_target_pairs={{0,8},{8,16},{16,24},{24,0},{1,9},{9,17},{17,25},{25,1},{2,10},{10... | collective-permute-start | bytes 2654216 | tf_op jit(solution)/shard_map/ppermute | solution.py:1343
  135.3 24.3 %collective-permute-start.22 = (bf16[528,1536]{1,0:T(8,128)(2,1)}, bf16[528,1536]{1,0:T(8,128)(2,1)}, u32[]{:S(2)}, u32[]{:S(2)}) collective-permute-start(bf16[528,1536]{1,0:T(8,128)(2,1)} %get-tuple-element.313.refs_0_), channel_id=1, source_target_pairs={{0,1},{1,0},{2,3},{3,2},{4,5},{5,4},{6,7},{7,6},{8,9},{9,8},{10,11... | collective-permute-start | bytes 4866056 | tf_op jit(solution)/shard_map/ppermute | solution.py:414
  135.3 39.2 %collective-permute-start.21 = (bf16[528,1536]{1,0:T(8,128)(2,1)}, bf16[528,1536]{1,0:T(8,128)(2,1)S(1)}, u32[]{:S(2)}, u32[]{:S(2)}) collective-permute-start(bf16[528,1536]{1,0:T(8,128)(2,1)} %get-tuple-element.313.refs_0_), channel_id=1, source_target_pairs={{0,4},{1,5},{2,6},{3,7},{4,0},{5,1},{6,2},{7,3},{8,12},{9,13},{10,... | collective-permute-start | bytes 4866056 | tf_op jit(solution)/shard_map/ppermute | solution.py:410
  136.5 38.0 %collective-permute-start.20 = (bf16[528,1536]{1,0:T(8,128)(2,1)}, bf16[528,1536]{1,0:T(8,128)(2,1)}, u32[]{:S(2)}, u32[]{:S(2)}) collective-permute-start(bf16[528,1536]{1,0:T(8,128)(2,1)} %get-tuple-element.313.refs_0_), channel_id=1, source_target_pairs={{0,2},{1,3},{2,0},{3,1},{4,6},{5,7},{6,4},{7,5},{8,10},{9,11},{10,... | collective-permute-start | bytes 4866056 | tf_op jit(solution)/shard_map/ppermute | solution.py:406
  137.2 10.9 %collective-permute-start.23 = (bf16[96,1536]{1,0:T(8,128)(2,1)}, bf16[96,1536]{1,0:T(8,128)(2,1)S(1)}, u32[]{:S(2)}, u32[]{:S(2)}) collective-permute-start(bf16[96,1536]{1,0:T(8,128)(2,1)} %collective-permute-done.9.refs_7_.refs_9_.refs_13_.refs_29_), channel_id=1, source_target_pairs={{0,8},{8,16},{16,24},{24,0},{1,9},{9,17},{17,25},{25,1},{2,10},{10... | collective-permute-start | bytes 884744 | tf_op jit(solution)/shard_map/ppermute | solution.py:1343
  148.1 9.8 %collective-permute-start.24 = (bf16[96,1536]{1,0:T(8,128)(2,1)S(1)}, bf16[96,1536]{1,0:T(8,128)(2,1)S(1)}, u32[]{:S(2)}, u32[]{:S(2)}) collective-permute-start(bf16[96,1536]{1,0:T(8,128)(2,1)S(1)} %collective-permute-done.23.refs_8_.refs_10_.refs_14_.refs_30_), channel_id=1, source_target_pairs={{0,8},{8,16},{16,24},{24,0},{1,9},{9,17},{17,25},{25,1},{2,10},{10... | collective-permute-start | bytes 884744 | tf_op jit(solution)/shard_map/ppermute | solution.py:1343
  158.6 15.9 %collective-permute-start.25 = (bf16[192,1536]{1,0:T(8,128)(2,1)}, bf16[192,1536]{1,0:T(8,128)(2,1)}, u32[]{:S(2)}, u32[]{:S(2)}) collective-permute-start(bf16[192,1536]{1,0:T(8,128)(2,1)} %convert_bitcast_fusion.1.refs_2_.refs_16_.refs_32_.refs_6_), channel_id=1, source_target_pairs={{0,8},{8,16},{16,24},{24,0},{1,9},{9,17},{17,25},{25,1},{2,10},{10... | collective-permute-start | bytes 1769480 | tf_op jit(solution)/shard_map/ppermute | solution.py:1343
  176.4 23.0 %collective-permute-start.26 = (bf16[528,1536]{1,0:T(8,128)(2,1)}, bf16[528,1536]{1,0:T(8,128)(2,1)}, u32[]{:S(2)}, u32[]{:S(2)}) collective-permute-start(bf16[528,1536]{1,0:T(8,128)(2,1)} %broadcast_select_fusion), channel_id=1, source_target_pairs={{0,2},{1,5},{2,0},{3,7},{4,6},{5,1},{6,4},{7,3},{8,10},{9,13},{10,... | collective-permute-start | bytes 4866056 | tf_op jit(solution)/shard_map/ppermute | solution.py:422
  177.7 21.7 %collective-permute-start.27 = (bf16[192,1536]{1,0:T(8,128)(2,1)}, bf16[192,1536]{1,0:T(8,128)(2,1)}, u32[]{:S(2)}, u32[]{:S(2)}) collective-permute-start(bf16[192,1536]{1,0:T(8,128)(2,1)} %collective-permute-done.25.refs_3_.refs_17_.refs_33_.refs_7_), channel_id=1, source_target_pairs={{0,8},{8,16},{16,24},{24,0},{1,9},{9,17},{17,25},{25,1},{2,10},{10... | collective-permute-start | bytes 1769480 | tf_op jit(solution)/shard_map/ppermute | solution.py:1343
  199.6 18.1 %collective-permute-start.31 = (bf16[512,1536]{1,0:T(8,128)(2,1)}, bf16[512,1536]{1,0:T(8,128)(2,1)}, u32[]{:S(2)}, u32[]{:S(2)}) collective-permute-start(bf16[512,1536]{1,0:T(8,128)(2,1)} %collective-permute-done.16.refs_14_.refs_3_), channel_id=1, source_target_pairs={{0,1},{1,0},{2,3},{3,2},{4,5},{5,4},{6,7},{7,6},{8,9},{9,8},{10,11... | collective-permute-start | bytes 4718600 | tf_op jit(solution)/shard_map/ppermute | solution.py:414
  204.2 29.4 %collective-permute-start.32 = (bf16[192,1536]{1,0:T(8,128)(2,1)}, bf16[192,1536]{1,0:T(8,128)(2,1)}, u32[]{:S(2)}, u32[]{:S(2)}) collective-permute-start(bf16[192,1536]{1,0:T(8,128)(2,1)} %collective-permute-done.27.refs_4_.refs_18_.refs_34_.refs_8_), channel_id=1, source_target_pairs={{0,8},{8,16},{16,24},{24,0},{1,9},{9,17},{17,25},{25,1},{2,10},{10... | collective-permute-start | bytes 1769480 | tf_op jit(solution)/shard_map/ppermute | solution.py:1343
  242.3 19.1 %collective-permute-start.34 = (bf16[512,1536]{1,0:T(8,128)(2,1)}, bf16[512,1536]{1,0:T(8,128)(2,1)S(1)}, u32[]{:S(2)}, u32[]{:S(2)}) collective-permute-start(bf16[512,1536]{1,0:T(8,128)(2,1)} %get-tuple-element.357), channel_id=1, source_target_pairs={{0,1},{1,0},{2,3},{3,2},{4,5},{5,4},{6,7},{7,6},{8,9},{9,8},{10,11... | collective-permute-start | bytes 4718600 | tf_op jit(solution)/shard_map/ppermute | solution.py:414
  242.5 18.9 %collective-permute-start.33 = (bf16[192,1536]{1,0:T(8,128)(2,1)}, bf16[192,1536]{1,0:T(8,128)(2,1)}, u32[]{:S(2)}, u32[]{:S(2)}) collective-permute-start(bf16[192,1536]{1,0:T(8,128)(2,1)} %constant_dynamic-slice_fusion.2), channel_id=1, source_target_pairs={{0,8},{8,16},{16,24},{24,0},{1,9},{9,17},{17,25},{25,1},{2,10},{10... | collective-permute-start | bytes 1769480 | tf_op jit(solution)/shard_map/ppermute | solution.py:1343
  268.1 37.1 %collective-permute-start.36 = (bf16[528,1536]{1,0:T(8,128)(2,1)S(1)}, bf16[528,1536]{1,0:T(8,128)(2,1)}, u32[]{:S(2)}, u32[]{:S(2)}) collective-permute-start(bf16[528,1536]{1,0:T(8,128)(2,1)S(1)} %add_convert_fusion.4), channel_id=1, source_target_pairs={{0,2},{1,5},{2,0},{3,7},{4,6},{5,1},{6,4},{7,3},{8,10},{9,13},{10,... | collective-permute-start | bytes 4866056 | tf_op jit(solution)/shard_map/ppermute | solution.py:422
  269.2 36.0 %collective-permute-start.37 = (bf16[192,1536]{1,0:T(8,128)(2,1)}, bf16[192,1536]{1,0:T(8,128)(2,1)}, u32[]{:S(2)}, u32[]{:S(2)}) collective-permute-start(bf16[192,1536]{1,0:T(8,128)(2,1)} %add_convert_fusion.14), channel_id=1, source_target_pairs={{0,8},{8,16},{16,24},{24,0},{1,9},{9,17},{17,25},{25,1},{2,10},{10... | collective-permute-start | bytes 1769480 | tf_op jit(solution)/shard_map/ppermute | solution.py:1343
  305.2 16.9 %collective-permute-start.38 = (bf16[528,1536]{1,0:T(8,128)(2,1)}, bf16[528,1536]{1,0:T(8,128)(2,1)}, u32[]{:S(2)}, u32[]{:S(2)}) collective-permute-start(bf16[528,1536]{1,0:T(8,128)(2,1)} %get-tuple-element.396), channel_id=1, source_target_pairs={{0,1},{1,0},{2,3},{3,2},{4,5},{5,4},{6,7},{7,6},{8,9},{9,8},{10,11... | collective-permute-start | bytes 4866056 | tf_op jit(solution)/shard_map/ppermute | solution.py:414
  305.3 16.9 %collective-permute-start.39 = (bf16[528,1536]{1,0:T(8,128)(2,1)}, bf16[528,1536]{1,0:T(8,128)(2,1)}, u32[]{:S(2)}, u32[]{:S(2)}) collective-permute-start(bf16[528,1536]{1,0:T(8,128)(2,1)} %get-tuple-element.397), channel_id=1, source_target_pairs={{0,1},{1,0},{2,3},{3,2},{4,5},{5,4},{6,7},{7,6},{8,9},{9,8},{10,11... | collective-permute-start | bytes 4866056 | tf_op jit(solution)/shard_map/ppermute | solution.py:414
  305.8 16.4 %collective-permute-start.40 = (bf16[528,1536]{1,0:T(8,128)(2,1)}, bf16[528,1536]{1,0:T(8,128)(2,1)S(1)}, u32[]{:S(2)}, u32[]{:S(2)}) collective-permute-start(bf16[528,1536]{1,0:T(8,128)(2,1)} %get-tuple-element.398), channel_id=1, source_target_pairs={{0,1},{1,0},{2,3},{3,2},{4,5},{5,4},{6,7},{7,6},{8,9},{9,8},{10,11... | collective-permute-start | bytes 4866056 | tf_op jit(solution)/shard_map/ppermute | solution.py:414
  305.9 23.0 %collective-permute-start.41 = (bf16[512,1536]{1,0:T(8,128)(2,1)}, bf16[512,1536]{1,0:T(8,128)(2,1)}, u32[]{:S(2)}, u32[]{:S(2)}) collective-permute-start(bf16[512,1536]{1,0:T(8,128)(2,1)} %add_convert_fusion.8), channel_id=1, source_target_pairs={{0,2},{1,5},{2,0},{3,7},{4,6},{5,1},{6,4},{7,3},{8,10},{9,13},{10,... | collective-permute-start | bytes 4718600 | tf_op jit(solution)/shard_map/ppermute | solution.py:422
  328.9 34.7 %collective-permute-start.45 = (bf16[512,1536]{1,0:T(8,128)(2,1)}, bf16[512,1536]{1,0:T(8,128)(2,1)}, u32[]{:S(2)}, u32[]{:S(2)}) collective-permute-start(bf16[512,1536]{1,0:T(8,128)(2,1)} %get-tuple-element.434), channel_id=1, source_target_pairs={{0,1},{1,0},{2,3},{3,2},{4,5},{5,4},{6,7},{7,6},{8,9},{9,8},{10,11... | collective-permute-start | bytes 4718600 | tf_op jit(solution)/shard_map/ppermute | solution.py:414
  329.2 34.4 %collective-permute-start.46 = (bf16[512,1536]{1,0:T(8,128)(2,1)}, bf16[512,1536]{1,0:T(8,128)(2,1)}, u32[]{:S(2)}, u32[]{:S(2)}) collective-permute-start(bf16[512,1536]{1,0:T(8,128)(2,1)} %get-tuple-element.437), channel_id=1, source_target_pairs={{0,1},{1,0},{2,3},{3,2},{4,5},{5,4},{6,7},{7,6},{8,9},{9,8},{10,11... | collective-permute-start | bytes 4718600 | tf_op jit(solution)/shard_map/ppermute | solution.py:414
  329.4 39.9 %collective-permute-start.42 = (bf16[528,1536]{1,0:T(8,128)(2,1)}, bf16[528,1536]{1,0:T(8,128)(2,1)S(1)}, u32[]{:S(2)}, u32[]{:S(2)}) collective-permute-start(bf16[528,1536]{1,0:T(8,128)(2,1)} %get-tuple-element.420), channel_id=1, source_target_pairs={{0,2},{1,3},{2,0},{3,1},{4,6},{5,7},{6,4},{7,5},{8,10},{9,11},{10,... | collective-permute-start | bytes 4866056 | tf_op jit(solution)/shard_map/ppermute | solution.py:406
  330.5 38.9 %collective-permute-start.43 = (bf16[528,1536]{1,0:T(8,128)(2,1)}, bf16[528,1536]{1,0:T(8,128)(2,1)}, u32[]{:S(2)}, u32[]{:S(2)}) collective-permute-start(bf16[528,1536]{1,0:T(8,128)(2,1)} %get-tuple-element.421), channel_id=1, source_target_pairs={{0,4},{1,5},{2,6},{3,7},{4,0},{5,1},{6,2},{7,3},{8,12},{9,13},{10,... | collective-permute-start | bytes 4866056 | tf_op jit(solution)/shard_map/ppermute | solution.py:410
  332.2 37.1 %collective-permute-start.44 = (bf16[192,1536]{1,0:T(8,128)(2,1)}, bf16[192,1536]{1,0:T(8,128)(2,1)}, u32[]{:S(2)}, u32[]{:S(2)}) collective-permute-start(bf16[192,1536]{1,0:T(8,128)(2,1)} %add_convert_fusion.13), channel_id=1, source_target_pairs={{0,8},{8,16},{16,24},{24,0},{1,9},{9,17},{17,25},{25,1},{2,10},{10... | collective-permute-start | bytes 1769480 | tf_op jit(solution)/shard_map/ppermute | solution.py:1343
  369.4 41.2 %collective-permute-start.47 = (bf16[512,1536]{1,0:T(8,128)(2,1)}, bf16[512,1536]{1,0:T(8,128)(2,1)}, u32[]{:S(2)}, u32[]{:S(2)}) collective-permute-start(bf16[512,1536]{1,0:T(8,128)(2,1)} %get-tuple-element.453), channel_id=1, source_target_pairs={{0,1},{1,0},{2,3},{3,2},{4,5},{5,4},{6,7},{7,6},{8,9},{9,8},{10,11... | collective-permute-start | bytes 4718600 | tf_op jit(solution)/shard_map/ppermute | solution.py:414
  369.5 42.4 %collective-permute-start.51 = (bf16[512,1536]{1,0:T(8,128)(2,1)}, bf16[512,1536]{1,0:T(8,128)(2,1)}, u32[]{:S(2)}, u32[]{:S(2)}) collective-permute-start(bf16[512,1536]{1,0:T(8,128)(2,1)} %get-tuple-element.459), channel_id=1, source_target_pairs={{0,4},{1,5},{2,6},{3,7},{4,0},{5,1},{6,2},{7,3},{8,12},{9,13},{10,... | collective-permute-start | bytes 4718600 | tf_op jit(solution)/shard_map/ppermute | solution.py:410
  370.7 41.2 %collective-permute-start.50 = (bf16[512,1536]{1,0:T(8,128)(2,1)}, bf16[512,1536]{1,0:T(8,128)(2,1)}, u32[]{:S(2)}, u32[]{:S(2)}) collective-permute-start(bf16[512,1536]{1,0:T(8,128)(2,1)} %get-tuple-element.441), channel_id=1, source_target_pairs={{0,2},{1,3},{2,0},{3,1},{4,6},{5,7},{6,4},{7,5},{8,10},{9,11},{10,... | collective-permute-start | bytes 4718600 | tf_op jit(solution)/shard_map/ppermute | solution.py:406
  371.3 39.3 %collective-permute-start.48 = (bf16[240,1536]{1,0:T(8,128)(2,1)}, bf16[240,1536]{1,0:T(8,128)(2,1)}, u32[]{:S(2)}, u32[]{:S(2)}) collective-permute-start(bf16[240,1536]{1,0:T(8,128)(2,1)} %constant_dynamic-slice_fusion), channel_id=1, source_target_pairs={{0,8},{8,16},{16,24},{24,0},{1,9},{9,17},{17,25},{25,1},{2,10},{10... | collective-permute-start | bytes 2211848 | tf_op jit(solution)/shard_map/ppermute | solution.py:1343
  371.6 39.0 %collective-permute-start.49 = (bf16[144,1536]{1,0:T(8,128)(2,1)}, bf16[144,1536]{1,0:T(8,128)(2,1)}, u32[]{:S(2)}, u32[]{:S(2)}) collective-permute-start(bf16[144,1536]{1,0:T(8,128)(2,1)} %constant_dynamic-slice_fusion.1), channel_id=1, source_target_pairs={{0,8},{8,16},{16,24},{24,0},{1,9},{9,17},{17,25},{25,1},{2,10},{10... | collective-permute-start | bytes 1327112 | tf_op jit(solution)/shard_map/ppermute | solution.py:1343
  411.9 14.5 %collective-permute-start.52 = (bf16[4,4,48,2048]{3,2,1,0:T(8,128)(2,1)}, bf16[4,4,48,2048]{3,2,1,0:T(8,128)(2,1)}, u32[]{:S(2)}, u32[]{:S(2)}) collective-permute-start(bf16[4,4,48,2048]{3,2,1,0:T(8,128)(2,1)} %get-tuple-element.460), channel_id=1, source_target_pairs={{0,1},{1,0},{2,3},{3,2},{4,5},{5,4},{6,7},{7,6},{8,9},{9,8},{10,11... | collective-permute-start | bytes 9437192 | tf_op jit(solution)/shard_map/ppermute | solution.py:414
  412.0 14.4 %collective-permute-start.53 = (bf16[144,1536]{1,0:T(8,128)(2,1)S(1)}, bf16[144,1536]{1,0:T(8,128)(2,1)S(1)}, u32[]{:S(2)}, u32[]{:S(2)}) collective-permute-start(bf16[144,1536]{1,0:T(8,128)(2,1)S(1)} %add_convert_fusion.16), channel_id=1, source_target_pairs={{0,8},{8,16},{16,24},{24,0},{1,9},{9,17},{17,25},{25,1},{2,10},{10... | collective-permute-start | bytes 1327112 | tf_op jit(solution)/shard_map/ppermute | solution.py:1343
  428.2 24.7 %collective-permute-start.55 = (bf16[4,4,48,1664]{3,2,1,0:T(8,128)(2,1)}, bf16[4,4,48,1664]{3,2,1,0:T(8,128)(2,1)}, u32[]{:S(2)}, u32[]{:S(2)}) collective-permute-start(bf16[4,4,48,1664]{3,2,1,0:T(8,128)(2,1)} %get-tuple-element.472), channel_id=1, source_target_pairs={{0,1},{1,0},{2,3},{3,2},{4,5},{5,4},{6,7},{7,6},{8,9},{9,8},{10,11... | collective-permute-start | bytes 7667720 | tf_op jit(solution)/shard_map/ppermute | solution.py:414
  431.8 21.1 %collective-permute-start.56 = (bf16[240,1536]{1,0:T(8,128)(2,1)}, bf16[240,1536]{1,0:T(8,128)(2,1)}, u32[]{:S(2)}, u32[]{:S(2)}) collective-permute-start(bf16[240,1536]{1,0:T(8,128)(2,1)} %add_convert_fusion.11), channel_id=1, source_target_pairs={{0,8},{8,16},{16,24},{24,0},{1,9},{9,17},{17,25},{25,1},{2,10},{10... | collective-permute-start | bytes 2211848 | tf_op jit(solution)/shard_map/ppermute | solution.py:1343
  431.9 21.0 %collective-permute-start.54 = (bf16[4,48,2048]{2,1,0:T(8,128)(2,1)S(1)}, bf16[4,48,2048]{2,1,0:T(8,128)(2,1)}, u32[]{:S(2)}, u32[]{:S(2)}) collective-permute-start(bf16[4,48,2048]{2,1,0:T(8,128)(2,1)S(1)} %fusion.12), channel_id=1, source_target_pairs={{0,2},{1,5},{2,0},{3,7},{4,6},{5,1},{6,4},{7,3},{8,10},{9,13},{10,... | collective-permute-start | bytes 2359304 | tf_op jit(solution)/shard_map/ppermute | solution.py:422
  452.9 17.1 %collective-permute-start.61 = (bf16[144,1536]{1,0:T(8,128)(2,1)S(1)}, bf16[144,1536]{1,0:T(8,128)(2,1)S(1)}, u32[]{:S(2)}, u32[]{:S(2)}) collective-permute-start(bf16[144,1536]{1,0:T(8,128)(2,1)S(1)} %copy-done.40), channel_id=1, source_target_pairs={{0,8},{8,16},{16,24},{24,0},{1,9},{9,17},{17,25},{25,1},{2,10},{10... | collective-permute-start | bytes 1327112 | tf_op jit(solution)/shard_map/ppermute | solution.py:1343
  457.7 17.2 %collective-permute-start.59 = (bf16[4,48,1664]{2,1,0:T(8,128)(2,1)S(1)}, bf16[4,48,1664]{2,1,0:T(8,128)(2,1)S(1)}, u32[]{:S(2)}, u32[]{:S(2)}) collective-permute-start(bf16[4,48,1664]{2,1,0:T(8,128)(2,1)S(1)} %fusion.13), channel_id=1, source_target_pairs={{0,2},{1,5},{2,0},{3,7},{4,6},{5,1},{6,4},{7,3},{8,10},{9,13},{10,... | collective-permute-start | bytes 1916936 | tf_op jit(solution)/shard_map/ppermute | solution.py:422
  458.8 23.5 %collective-permute-start.60 = (bf16[240,1536]{1,0:T(8,128)(2,1)S(1)}, bf16[240,1536]{1,0:T(8,128)(2,1)S(1)}, u32[]{:S(2)}, u32[]{:S(2)}) collective-permute-start(bf16[240,1536]{1,0:T(8,128)(2,1)S(1)} %add_convert_fusion.10), channel_id=1, source_target_pairs={{0,8},{8,16},{16,24},{24,0},{1,9},{9,17},{17,25},{25,1},{2,10},{10... | collective-permute-start | bytes 2211848 | tf_op jit(solution)/shard_map/ppermute | solution.py:1343
  459.0 25.6 %collective-permute-start.57 = (bf16[4,48,2048]{2,1,0:T(8,128)(2,1)S(1)}, bf16[4,48,2048]{2,1,0:T(8,128)(2,1)S(1)}, u32[]{:S(2)}, u32[]{:S(2)}) collective-permute-start(bf16[4,48,2048]{2,1,0:T(8,128)(2,1)S(1)} %get-tuple-element.489), channel_id=1, source_target_pairs={{0,2},{1,3},{2,0},{3,1},{4,6},{5,7},{6,4},{7,5},{8,10},{9,11},{10,... | collective-permute-start | bytes 2359304 | tf_op jit(solution)/shard_map/ppermute | solution.py:406
  460.1 24.6 %collective-permute-start.58 = (bf16[4,48,2048]{2,1,0:T(8,128)(2,1)S(1)}, bf16[4,48,2048]{2,1,0:T(8,128)(2,1)S(1)}, u32[]{:S(2)}, u32[]{:S(2)}) collective-permute-start(bf16[4,48,2048]{2,1,0:T(8,128)(2,1)S(1)} %get-tuple-element.490), channel_id=1, source_target_pairs={{0,4},{1,5},{2,6},{3,7},{4,0},{5,1},{6,2},{7,3},{8,12},{9,13},{10,... | collective-permute-start | bytes 2359304 | tf_op jit(solution)/shard_map/ppermute | solution.py:410
  486.5 22.9 %collective-permute-start.65 = (bf16[4,48,1664]{2,1,0:T(8,128)(2,1)}, bf16[4,48,1664]{2,1,0:T(8,128)(2,1)S(1)}, u32[]{:S(2)}, u32[]{:S(2)}) collective-permute-start(bf16[4,48,1664]{2,1,0:T(8,128)(2,1)} %get-tuple-element.500), channel_id=1, source_target_pairs={{0,2},{1,3},{2,0},{3,1},{4,6},{5,7},{6,4},{7,5},{8,10},{9,11},{10,... | collective-permute-start | bytes 1916936 | tf_op jit(solution)/shard_map/ppermute | solution.py:406
  487.5 22.0 %collective-permute-start.66 = (bf16[4,48,1664]{2,1,0:T(8,128)(2,1)}, bf16[4,48,1664]{2,1,0:T(8,128)(2,1)S(1)}, u32[]{:S(2)}, u32[]{:S(2)}) collective-permute-start(bf16[4,48,1664]{2,1,0:T(8,128)(2,1)} %get-tuple-element.501), channel_id=1, source_target_pairs={{0,4},{1,5},{2,6},{3,7},{4,0},{5,1},{6,2},{7,3},{8,12},{9,13},{10,... | collective-permute-start | bytes 1916936 | tf_op jit(solution)/shard_map/ppermute | solution.py:410
  489.5 9.6 %collective-permute-start.64 = (bf16[48,2048]{1,0:T(8,128)(2,1)}, bf16[48,2048]{1,0:T(8,128)(2,1)}, u32[]{:S(2)}, u32[]{:S(2)}) collective-permute-start(bf16[48,2048]{1,0:T(8,128)(2,1)} %get-tuple-element.648), channel_id=1, source_target_pairs={{0,8},{8,16},{16,24},{24,0},{1,9},{9,17},{17,25},{25,1},{2,10},{10... | collective-permute-start | bytes 589832 | tf_op jit(solution)/shard_map/ppermute | solution.py:1568
  489.5 19.9 %collective-permute-start.62 = (bf16[48,2048]{1,0:T(8,128)(2,1)}, bf16[48,2048]{1,0:T(8,128)(2,1)}, u32[]{:S(2)}, u32[]{:S(2)}) collective-permute-start(bf16[48,2048]{1,0:T(8,128)(2,1)} %get-tuple-element.650), channel_id=1, source_target_pairs={{0,24},{8,0},{16,8},{24,16},{1,25},{9,1},{17,9},{25,17},{2,26},{10... | collective-permute-start | bytes 589832 | tf_op jit(solution)/shard_map/ppermute | solution.py:1568
  498.1 11.3 %collective-permute-start.63 = (bf16[48,2048]{1,0:T(8,128)(2,1)}, bf16[48,2048]{1,0:T(8,128)(2,1)}, u32[]{:S(2)}, u32[]{:S(2)}) collective-permute-start(bf16[48,2048]{1,0:T(8,128)(2,1)} %get-tuple-element.649), channel_id=1, source_target_pairs={{0,16},{8,24},{16,0},{24,8},{1,17},{9,25},{17,1},{25,9},{2,18},{10... | collective-permute-start | bytes 589832 | tf_op jit(solution)/shard_map/ppermute | solution.py:1568
  510.6 9.0 %collective-permute-start.69 = (bf16[48,1664]{1,0:T(8,128)(2,1)S(1)}, bf16[48,1664]{1,0:T(8,128)(2,1)S(1)}, u32[]{:S(2)}, u32[]{:S(2)}) collective-permute-start(bf16[48,1664]{1,0:T(8,128)(2,1)S(1)} %get-tuple-element.653), channel_id=1, source_target_pairs={{0,8},{8,16},{16,24},{24,0},{1,9},{9,17},{17,25},{25,1},{2,10},{10... | collective-permute-start | bytes 479240 | tf_op jit(solution)/shard_map/ppermute | solution.py:1568
  511.9 12.6 %collective-permute-start.68 = (bf16[48,1664]{1,0:T(8,128)(2,1)S(1)}, bf16[48,1664]{1,0:T(8,128)(2,1)S(1)}, u32[]{:S(2)}, u32[]{:S(2)}) collective-permute-start(bf16[48,1664]{1,0:T(8,128)(2,1)S(1)} %get-tuple-element.654), channel_id=1, source_target_pairs={{0,16},{8,24},{16,0},{24,8},{1,17},{9,25},{17,1},{25,9},{2,18},{10... | collective-permute-start | bytes 479240 | tf_op jit(solution)/shard_map/ppermute | solution.py:1568
  (63 other events, 504.7 us)

commit v4 on v3

--- a/solution.py
+++ b/solution.py
@@ -1249,16 +1249,16 @@
     grad[...] = total.astype(grad.dtype)
 
 
-def weight_grad_call(left, right, rows, tall, name):
+def weight_grad_call(left, right, rows, tall, wide, name):
     count = len(left)
     height, width = left[0].shape[1], right[0].shape[1]
     return pl.pallas_call(
         functools.partial(weight_grad_kernel, count, rows),
-        grid=(height // tall, width // WIDE),
+        grid=(height // tall, width // wide),
         out_shape=jax.ShapeDtypeStruct((height, width), jnp.bfloat16),
         in_specs=[pl.BlockSpec((rows, tall), lambda i, j: (0, i))] * count
-        + [pl.BlockSpec((rows, WIDE), lambda i, j: (0, j))] * count,
-        out_specs=pl.BlockSpec((tall, WIDE), lambda i, j: (i, j)),
+        + [pl.BlockSpec((rows, wide), lambda i, j: (0, j))] * count,
+        out_specs=pl.BlockSpec((tall, wide), lambda i, j: (i, j)),
         compiler_params=pltpu.CompilerParams(vmem_limit_bytes=62 << 20),
         cost_estimate=small_cost(),
         name=name,
@@ -1351,7 +1351,7 @@
     )
     column.append(around(column[2]))
     joint = jnp.stack(column)
-    cut = in_low.shape[0] * 3 // 4
+    cut = in_low.shape[0] * 2 // 3
     cot_x, cot_y, joint, in_low, out_low = hold(cot_x, cot_y, joint, in_low, out_low)
     in_near, in_rest, out_chunks = [in_low[:cut]], [in_low[cut:]], [out_low]
 
@@ -1417,7 +1417,7 @@
     packed_blocks[6:] = hold(packed_far, packed_far2)
     out_chunks.append(around(after(out_chunks[2], packed_far2)))
     hidden((6, 7))
-    out_grad = weight_grad_call(gated, cot_blocks, rows_count, FF, "expert_out_grad")
+    out_grad = weight_grad_call(gated, cot_blocks, rows_count, FF, LANES, "expert_out_grad")
     out_grad, out_chunks = hold(out_grad, out_chunks)
 
     def column_piece(value, back):
@@ -1490,7 +1490,9 @@
     from_x, from_y = to_x(by_x), to_y(by_y)
     moved = around(moving)
     rows_backs = [to_core(rows_out[k]) for k in (3, 5)]
-    in_grad = weight_grad_call(packed_blocks, hidden_grads, rows_count, FF, "expert_in_grad")
+    in_grad = weight_grad_call(
+        packed_blocks, hidden_grads, rows_count, FF, WIDE, "expert_in_grad"
+    )
     rows_x = add_low(rows_out[2], rows_backs[0], by_core(rows_relayed, 1))
     rows_y = add_low(rows_out[4], rows_backs[1], by_core(rows_relayed, 0))
     cut = in_low.shape[0] * 5 // 8

time: 533 us -> 535 us (level)
  transfers between devices with their start and end apart: 70 -> 70, of which waited for: 24 -> 23; matrix products, arithmetic and copies ran while one was open for 15% -> 15% of each run, Pallas kernels for 42% -> 42%
where the time goes in v4:
time: 535 us; the launch traced here: 530 us
  Pallas kernels  229 us (43%)
  waiting for transfers between devices  156 us (29%)
  other arithmetic  76.3 us (14%)
  starting transfers between devices  44 us (8%)
  local copies, waits for them, and re-layouts  18.1 us (3%)
  between operations  7.21 us (1%)
    ppermute x21, waiting for transfers between devices, around(): return lax.ppermute(value, 'dp', ring)  114 us
    pallas_call x2, Pallas kernels, pull_call(): pl.pallas_call(functools.partial(pull_kernel, count, (len(in_chunks), len...  50.3 us
    pallas_call x2, Pallas kernels, weight_grad_call(): pl.pallas_call(functools.partial(weight_grad_kernel, count, rows), grid=(...  42.5 us
    pallas_call x3, Pallas kernels, hidden_call(): pl.pallas_call(functools.partial(hidden_kernel, count, len(chunks), token...  42.4 us
    convert_element_type x18, other arithmetic, add_low(): return total.astype(jnp.bfloat16)  39.9 us
    pallas_call x1, Pallas kernels, attend_call(): pl.pallas_call(functools.partial(attend_kernel, len(blocks)), out_shape=[...  22.1 us
    ppermute x6, waiting for transfers between devices, spread_pieces(): lax.ppermute(total[p], 'dp', [(i, (i - p) % columns_dp) for i in range(co...  21.4 us
    pallas_call x2, Pallas kernels, product_call(): pl.pallas_call(functools.partial(product_kernel, count), out_shape=[jax.S...  19.1 us
  transfers between devices with their start and end apart: 70, of which 23 were waited for; matrix products, arithmetic and copies ran while one was open for 15% of the time, Pallas kernels for 42%

profile of v4, /device:TPU:0, one launch (start us, length us, event | category | flops | bytes accessed | tf_op | source)
XLA Modules:
  0.0 530.2 jit_solution(11740837072377687202)
XLA Ops:
  0.7 3.0 collective-permute-start.3
  12.4 2.8 convert_bitcast_fusion
  15.3 1.8 multiply_sine_fusion
  17.2 2.2 concatenate.19.table_ref
  19.4 2.9 collective-permute-done
  23.1 9.8 %collective-permute-done.1 = bf16[48,3712]{1,0:T(8,128)(2,1)S(1)} collective-permute-done((bf16[48,3712]{1,0:T(8,128)(2,1)}, bf16[48,3712]{1,0:T(8,128)(2,1)S(1)}, u32[]{:S(2)}, u32[]{:S(2)}) %collective-permute-start.1) | collective-permute-done | bytes 356384 | tf_op jit(solution)/shard_map/ppermute | solution.py:1343
  32.9 9.5 %collective-permute-done.4 = bf16[48,3712]{1,0:T(8,128)(2,1)S(1)} collective-permute-done((bf16[48,3712]{1,0:T(8,128)(2,1)S(1)}, bf16[48,3712]{1,0:T(8,128)(2,1)S(1)}, u32[]{:S(2)}, u32[]{:S(2)}) %collective-permute-start.4) | collective-permute-done | bytes 356384 | tf_op jit(solution)/shard_map/ppermute | solution.py:1343
  45.8 29.4 %collective-permute-done.9.refs_7_.refs_9_.refs_13_.refs_29_ = bf16[128,1536]{1,0:T(8,128)(2,1)} collective-permute-done((bf16[128,1536]{1,0:T(8,128)(2,1)S(1)}, bf16[128,1536]{1,0:T(8,128)(2,1)}, u32[]{:S(2)}, u32[]{:S(2)}) %collective-permute-start.9) | collective-permute-done | bytes 393248 | tf_op jit(solution)/shard_map/ppermute | solution.py:1343
  75.2 2.4 collective-permute-done.6.refs_4_.refs_17_.refs_9_
  81.2 2.8 broadcast_select_fusion.1
  84.0 19.0 %collective-permute-done.13.refs_4_.refs_6_.refs_10_.refs_26_ = bf16[256,1536]{1,0:T(8,128)(2,1)S(1)} collective-permute-done((bf16[256,1536]{1,0:T(8,128)(2,1)S(1)}, bf16[256,1536]{1,0:T(8,128)(2,1)S(1)}, u32[]{:S(2)}, u32[]{:S(2)}) %collective-permute-start.13) | collective-permute-done | bytes 786464 | tf_op jit(solution)/shard_map/ppermute | solution.py:1343
  103.6 3.9 collective-permute-done.15.refs_7_.refs_20_.refs_12_
  109.5 22.1 %attend.1 = (bf16[512,1536]{1,0:T(8,128)(2,1)}, bf16[512,2048]{1,0:T(8,128)(2,1)}, bf16[512,1536]{1,0:T(8,128)(2,1)}, f32[512,1536]{1,0:T(8,128)}, bf16[528,1536...) custom-call(s32[32]{0:T(128)} %mul.321.start_ref, bf16[512,1536]{1,0:T(8,128)(2,1)} %refs_1_.1, ...), custom_call_target="tpu_custom_call" | custom-call | flops 1024 | bytes 1024 | tf_op jit(solution)/shard_map/attend/pallas_call | solution.py:689
  134.6 13.0 %collective-permute-done.23.refs_8_.refs_10_.refs_14_.refs_30_ = bf16[128,1536]{1,0:T(8,128)(2,1)S(1)} collective-permute-done((bf16[128,1536]{1,0:T(8,128)(2,1)}, bf16[128,1536]{1,0:T(8,128)(2,1)S(1)}, u32[]{:S(2)}, u32[]{:S(2)}) %collective-permute-start.23) | collective-permute-done | bytes 393248 | tf_op jit(solution)/shard_map/ppermute | solution.py:1343
  147.6 11.9 %collective-permute-done.24.refs_9_.refs_11_.refs_15_.refs_31_ = bf16[128,1536]{1,0:T(8,128)(2,1)S(1)} collective-permute-done((bf16[128,1536]{1,0:T(8,128)(2,1)S(1)}, bf16[128,1536]{1,0:T(8,128)(2,1)S(1)}, u32[]{:S(2)}, u32[]{:S(2)}) %collective-permute-start.24) | collective-permute-done | bytes 393248 | tf_op jit(solution)/shard_map/ppermute | solution.py:1343
  161.1 11.9 %expert_hidden.3 = (bf16[512,1536]{1,0:T(8,128)(2,1)}, bf16[512,1536]{1,0:T(8,128)(2,1)}, bf16[512,768]{1,0:T(8,128)(2,1)}, bf16[512,768]{1,0:T(8,128)(2,1)}, bf...) custom-call(s32[5]{0:T(128)} %pad_add_fusion.place_ref, bf16[528,1536]{1,0:T(8,128)(2,1)} %get-tuple-element.313.refs_0_, ...), custom_call_target="tpu_custom_call" | custom-call | flops 1024 | bytes 1024 | tf_op jit(solution)/shard_map/expert_hidden/pallas_call | solution.py:1057
  173.0 3.0 collective-permute-done.25.refs_3_.refs_17_.refs_33_.refs_7_
  178.6 2.5 collective-permute-done.29.refs_3_.refs_4_.refs_5_
  182.3 18.6 %expert_hidden.4 = (bf16[512,1536]{1,0:T(8,128)(2,1)}, bf16[512,1536]{1,0:T(8,128)(2,1)}, bf16[512,1536]{1,0:T(8,128)(2,1)}, bf16[512,1536]{1,0:T(8,128)(2,1)}, ...) custom-call(s32[5]{0:T(128)} %pad_add_fusion.place_ref, ...), custom_call_target="tpu_custom_call" | custom-call | flops 1024 | bytes 1024 | tf_op jit(solution)/shard_map/expert_hidden/pallas_call | solution.py:1057
  201.5 4.2 collective-permute-done.30.refs_1_.refs_0_.refs_7_
  207.4 11.9 %expert_hidden.5 = (bf16[512,1536]{1,0:T(8,128)(2,1)}, bf16[512,1536]{1,0:T(8,128)(2,1)}, bf16[512,768]{1,0:T(8,128)(2,1)}, bf16[512,768]{1,0:T(8,128)(2,1)}, bf...) custom-call(s32[5]{0:T(128)} %pad_add_fusion.place_ref, ...), custom_call_target="tpu_custom_call" | custom-call | flops 1024 | bytes 1024 | tf_op jit(solution)/shard_map/expert_hidden/pallas_call | solution.py:1057
  219.3 15.8 %expert_out_grad.1 = bf16[768,1536]{1,0:T(8,128)(2,1)} custom-call(bf16[512,768]{1,0:T(8,128)(2,1)} %get-tuple-element.333.refs_0_.refs_5_, bf16[512,768]{1,0:T(8,128)(2,1)} %get-tuple-element.334.refs_1_.refs_4_, bf16[512,768]{1,0:T(8,128)(2,1)} %get-tuple-element.335.refs_2_.refs_3_, bf16[512,768]{1,0:T(8,128)(2,1)} %get-tuple-element.336.refs_3_.refs_2_, ...), custom_call_target="tpu_custom_call" | custom-call | flops 1024 | bytes 1024 | tf_op jit(solution)/shard_map/expert_out_grad/pallas_call | solution.py:1255
  235.1 1.9 constant_dynamic-slice_fusion.2
  237.1 6.8 %expert_rows.2 = (bf16[512,1536]{1,0:T(8,128)(2,1)}, bf16[512,1536]{1,0:T(8,128)(2,1)}) custom-call(s32[5]{0:T(128)} %pad_add_fusion.place_ref, bf16[512,768]{1,0:T(8,128)(2,1)} %get-tuple-element.349.refs_7_.refs_0_, bf16[512,768]{1,0:T(8,128)(2,1)} %get-tuple-element.339.refs_6_.refs_1_, ...), custom_call_target="tpu_custom_call" | custom-call | flops 1024 | bytes 1024 | tf_op jit(solution)/shard_map/expert_rows/pallas_call | solution.py:1225
  245.0 16.1 %expert_pull.2 = (bf16[528,1536]{1,0:T(8,128)(2,1)}, bf16[528,1536]{1,0:T(8,128)(2,1)}, bf16[512,1536]{1,0:T(8,128)(2,1)}, bf16[512,1536]{1,0:T(8,128)(2,1)}) custom-call(s32[5]{0:T(128)} %pad_add_fusion.place_ref, bf16[528,1536]{1,0:T(8,128)(2,1)} %copy-done.7, bf16[528,1536]{1,0:T(8,128)(2,1)} %collective-permute-done.26.refs_0_.refs_1_.refs_6_, ...), custom_call_target="tpu_custom_call" | custom-call | flops 1024 | bytes 1024 | tf_op jit(solution)/shard_map/expert_pull/pallas_call | solution.py:1171
  262.8 2.2 add_convert_fusion.14
  266.6 1.8 add_convert_fusion.4
  269.3 3.1 collective-permute-start.37
  272.5 34.1 %expert_pull.3 = (bf16[528,1536]{1,0:T(8,128)(2,1)}, bf16[528,1536]{1,0:T(8,128)(2,1)}, bf16[528,1536]{1,0:T(8,128)(2,1)}, bf16[528,1536]{1,0:T(8,128)(2,1)}, bf...) custom-call(s32[5]{0:T(128)} %pad_add_fusion.place_ref, ...), custom_call_target="tpu_custom_call" | custom-call | flops 1024 | bytes 1024 | tf_op jit(solution)/shard_map/expert_pull/pallas_call | solution.py:1171
  308.2 12.3 %expert_rows.3 = (bf16[512,1536]{1,0:T(8,128)(2,1)}, bf16[512,1536]{1,0:T(8,128)(2,1)}, bf16[512,1536]{1,0:T(8,128)(2,1)}, bf16[512,1536]{1,0:T(8,128)(2,1)}, bf...) custom-call(s32[5]{0:T(128)} %pad_add_fusion.place_ref, bf16[512,768]{1,0:T(8,128)(2,1)} %get-tuple-element.400.refs_5_.refs_0_, ...), custom_call_target="tpu_custom_call" | custom-call | flops 1024 | bytes 1024 | tf_op jit(solution)/shard_map/expert_rows/pallas_call | solution.py:1225
  320.6 2.3 add_convert_fusion.13
  322.9 6.7 %add_convert_fusion.2 = (bf16[528,1536]{1,0:T(8,128)(2,1)}, bf16[528,1536]{1,0:T(8,128)(2,1)}) fusion(bf16[528,1536]{1,0:T(8,128)(2,1)} %collective-permute-done.39, bf16[528,1536]{1,0:T(8,128)(2,1)} %get-tuple-element.410, bf16[528,1536]{1,0:T(8,128)(2,1)} %collective-permute-done.36, pred[]{:T(512)S(6)} %eq.6, pred[]{:T(512)S(6)} %eq.7, ...), kind=kLoop, calls=%fused_computation.3 | loop fusion | flops 11354112 | bytes 11354114 | tf_op jit(solution)/shard_map/convert_element_type | solution.py:445
  330.2 1.8 collective-permute-start.42
  333.0 1.7 collective-permute-start.44
  334.7 26.7 %expert_in_grad.1 = bf16[1536,1536]{1,0:T(8,128)(2,1)} custom-call(bf16[528,1536]{1,0:T(8,128)(2,1)} %get-tuple-element.313.refs_0_, bf16[528,1536]{1,0:T(8,128)(2,1)} %collective-permute-done.22.refs_1_, bf16[528,1536]{1,0:T(8,128)(2,1)} %collective-permute-done.20.refs_0_.refs_3_.refs_2_, bf16[528,1536]{1,0:T(8,128)(2,1)} %collective-permute-done.28.refs_2_.refs_3_, ...), custom_call_target="tpu_custom_call" | custom-call | flops 1024 | bytes 1024 | tf_op jit(solution)/shard_map/expert_in_grad/pallas_call | solution.py:1255
  361.4 2.0 constant_dynamic-slice_fusion.1
  363.4 2.0 constant_dynamic-slice_fusion
  365.4 5.8 %add_convert_fusion.6 = (bf16[512,1536]{1,0:T(8,128)(2,1)}, bf16[512,1536]{1,0:T(8,128)(2,1)}) fusion(bf16[512,1536]{1,0:T(8,128)(2,1)} %collective-permute-done.46, bf16[512,1536]{1,0:T(8,128)(2,1)S(1)} %copy-done.32, bf16[512,1536]{1,0:T(8,128)(2,1)} %collective-permute-done.41, pred[]{:T(512)S(6)} %eq.6, pred[]{:T(512)S(6)} %eq.7, ...), kind=kLoop, calls=%fused_computation.7 | loop fusion | flops 11010048 | bytes 11010050 | tf_op jit(solution)/shard_map/convert_element_type | solution.py:445
  376.1 11.7 %middle_back.1 = (f32[512,1536]{1,0:T(8,128)}, bf16[512,1536]{1,0:T(8,128)(2,1)}, bf16[512,1536]{1,0:T(8,128)(2,1)}, bf16[16,512]{1,0:T(8,128)(2,1)}, f32[16,1536]{1,0:T(8,128)}) custom-call(s32[32]{0:T(128)} %mul.321.start_ref, bf16[528,1536]{1,0:T(8,128)(2,1)} %get-tuple-element.442.refs_0_.refs_4_, bf16[528,1536]{1,0:T(8,128)(2,1)} %copy-done.19, ...), custom_call_target="tpu_custom_call" | custom-call | flops 1024 | bytes 1024 | tf_op jit(solution)/shard_map/middle_back/pallas_call | solution.py:773
  387.8 16.3 %attend_back.1.right_ref.refs_0_ = bf16[512,2048]{1,0:T(8,128)(2,1)} custom-call(bf16[512,2048]{1,0:T(8,128)(2,1)} %get-tuple-element.440.heads_ref, bf16[512,1536]{1,0:T(8,128)(2,1)} %get-tuple-element.448.grad_ref, f32[512,128]{1,0:T(8,128)} %get-tuple-element.449.log_ref, f32[512,384]{1,0:T(8,128)} %concatenate.19.table_ref), custom_call_target="tpu_custom_call" | custom-call | flops 1024 | bytes 1024 | tf_op jit(solution)/shard_map/attend_back/pallas_call | solution.py:846
  404.1 7.3 %shard_grad.2 = (bf16[4,4,48,2048]{3,2,1,0:T(8,128)(2,1)}, bf16[4,4,48,2048]{3,2,1,0:T(8,128)(2,1)}) custom-call(s32[9]{0:T(128)} %pad_add_fusion.1.start_ref, bf16[512,1536]{1,0:T(8,128)(2,1)} %get-tuple-element.439.left_ref, bf16[512,2048]{1,0:T(8,128)(2,1)} %attend_back.1.right_ref.refs_0_), custom_call_target="tpu_custom_call" | custom-call | flops 1024 | bytes 1024 | tf_op jit(solution)/shard_map/shard_grad/pallas_call | solution.py:890
  412.8 1.8 collective-permute-start.53
  414.7 6.0 %shard_grad.3 = (bf16[4,4,48,1664]{3,2,1,0:T(8,128)(2,1)}, bf16[4,4,48,1664]{3,2,1,0:T(8,128)(2,1)}) custom-call(s32[9]{0:T(128)} %pad_add_fusion.1.start_ref, bf16[512,1536]{1,0:T(8,128)(2,1)} %get-tuple-element.461.left_ref, bf16[512,1536]{1,0:T(8,128)(2,1)} %get-tuple-element.462.right_ref, f32[16,1536]{1,0:T(8,128)} %get-tuple-element.463.refs_0_), custom_call_target="tpu_custom_call" | custom-call | flops 1024 | bytes 1024 | tf_op jit(solution)/shard_map/shard_grad/pallas_call | solution.py:890
  420.7 2.4 add_convert_fusion.11
  423.0 4.1 collective-permute-done.53
  427.2 1.8 fusion.12
  432.7 1.7 collective-permute-start.54
  434.4 1.9 add_convert_fusion.15
  436.3 11.3 %entry_back.1 = f32[512,1536]{1,0:T(8,128)} custom-call(s32[32]{0:T(128)} %mul.321.start_ref, bf16[512,2048]{1,0:T(8,128)(2,1)} %attend_back.1.right_ref.refs_0_, bf16[512,1536]{1,0:T(8,128)(2,1)} %refs_1_.1, f32[512,1536]{1,0:T(8,128)} %get-tuple-element.474.refs_2_, f32[16,1536]{1,0:T(8,128)} %get-tuple-element.446.refs_9_.refs_3_, ...), custom_call_target="tpu_custom_call" | custom-call | flops 1024 | bytes 1024 | tf_op jit(solution)/shard_map/entry_back/pallas_call | solution.py:943
  447.6 3.4 add_convert_fusion
  451.0 2.7 collective-permute-done.56
  456.7 1.8 fusion.4
  461.5 4.5 add_convert_fusion.5
  466.0 2.4 multiply_subtract_fusion.1
  468.5 2.0 add_convert_fusion.1
  470.5 5.3 %collective-permute-done.59 = bf16[4,48,1664]{2,1,0:T(8,128)(2,1)S(1)} collective-permute-done((bf16[4,48,1664]{2,1,0:T(8,128)(2,1)S(1)}, bf16[4,48,1664]{2,1,0:T(8,128)(2,1)S(1)}, u32[]{:S(2)}, u32[]{:S(2)}) %collective-permute-start.59) | collective-permute-done | bytes 639008 | tf_op jit(solution)/shard_map/ppermute | solution.py:422
  475.8 7.3 %collective-permute-done.60 = bf16[240,1536]{1,0:T(8,128)(2,1)S(1)} collective-permute-done((bf16[240,1536]{1,0:T(8,128)(2,1)S(1)}, bf16[240,1536]{1,0:T(8,128)(2,1)S(1)}, u32[]{:S(2)}, u32[]{:S(2)}) %collective-permute-start.60) | collective-permute-done | bytes 737312 | tf_op jit(solution)/shard_map/ppermute | solution.py:1343
  483.1 2.0 collective-permute-done.57
  490.5 3.2 collective-permute-start.62
  493.7 4.6 multiply_subtract_fusion
  499.9 10.7 %collective-permute-done.63 = bf16[48,2048]{1,0:T(8,128)(2,1)} collective-permute-done((bf16[48,2048]{1,0:T(8,128)(2,1)}, bf16[48,2048]{1,0:T(8,128)(2,1)}, u32[]{:S(2)}, u32[]{:S(2)}) %collective-permute-start.63) | collective-permute-done | bytes 196640 | tf_op jit(solution)/shard_map/ppermute | solution.py:1570
  511.3 1.7 collective-permute-start.69
  516.3 4.5 collective-permute-done.67
  520.8 5.3 collective-permute-done.68
  (289 shorter events, 63.3 us)
Async XLA Ops:
  0.7 43.1 %collective-permute-start.3 = (bf16[512,1536]{1,0:T(8,128)(2,1)}, bf16[512,1536]{1,0:T(8,128)(2,1)}, u32[]{:S(2)}, u32[]{:S(2)}) collective-permute-start(bf16[512,1536]{1,0:T(8,128)(2,1)} %refs_10_.1), channel_id=1, source_target_pairs={{0,4},{1,5},{2,6},{3,7},{4,0},{5,1},{6,2},{7,3},{8,12},{9,13},{10,... | collective-permute-start | bytes 4718600 | tf_op jit(solution)/shard_map/ppermute | solution.py:410
  3.7 40.0 %collective-permute-start.2 = (bf16[512,1536]{1,0:T(8,128)(2,1)}, bf16[512,1536]{1,0:T(8,128)(2,1)S(1)}, u32[]{:S(2)}, u32[]{:S(2)}) collective-permute-start(bf16[512,1536]{1,0:T(8,128)(2,1)} %refs_10_.1), channel_id=1, source_target_pairs={{0,2},{1,3},{2,0},{3,1},{4,6},{5,7},{6,4},{7,5},{8,10},{9,11},{10,... | collective-permute-start | bytes 4718600 | tf_op jit(solution)/shard_map/ppermute | solution.py:406
  10.6 11.7 %collective-permute-start = (bf16[48,3712]{1,0:T(8,128)(2,1)}, bf16[48,3712]{1,0:T(8,128)(2,1)}, u32[]{:S(2)}, u32[]{:S(2)}) collective-permute-start(bf16[48,3712]{1,0:T(8,128)(2,1)} %concatenate.18), channel_id=1, source_target_pairs={{0,8},{8,16},{16,24},{24,0},{1,9},{9,17},{17,25},{25,1},{2,10},{10... | collective-permute-start | bytes 1069064 | tf_op jit(solution)/shard_map/ppermute | solution.py:1343
  22.2 10.7 %collective-permute-start.1 = (bf16[48,3712]{1,0:T(8,128)(2,1)}, bf16[48,3712]{1,0:T(8,128)(2,1)S(1)}, u32[]{:S(2)}, u32[]{:S(2)}) collective-permute-start(bf16[48,3712]{1,0:T(8,128)(2,1)} %collective-permute-done), channel_id=1, source_target_pairs={{0,8},{8,16},{16,24},{24,0},{1,9},{9,17},{17,25},{25,1},{2,10},{10... | collective-permute-start | bytes 1069064 | tf_op jit(solution)/shard_map/ppermute | solution.py:1343
  32.9 9.5 %collective-permute-start.4 = (bf16[48,3712]{1,0:T(8,128)(2,1)S(1)}, bf16[48,3712]{1,0:T(8,128)(2,1)S(1)}, u32[]{:S(2)}, u32[]{:S(2)}) collective-permute-start(bf16[48,3712]{1,0:T(8,128)(2,1)S(1)} %collective-permute-done.1), channel_id=1, source_target_pairs={{0,8},{8,16},{16,24},{24,0},{1,9},{9,17},{17,25},{25,1},{2,10},{10... | collective-permute-start | bytes 1069064 | tf_op jit(solution)/shard_map/ppermute | solution.py:1343
  43.8 31.4 %collective-permute-start.7 = (bf16[4,48,3712]{2,1,0:T(8,128)(2,1)S(1)}, bf16[4,48,3712]{2,1,0:T(8,128)(2,1)}, u32[]{:S(2)}, u32[]{:S(2)}) collective-permute-start(bf16[4,48,3712]{2,1,0:T(8,128)(2,1)S(1)} %pad_maximum_fusion.refs_0_.refs_13_.refs_5_), channel_id=1, source_target_pairs={{0,1},{1,0},{2,3},{3,2},{4,5},{5,4},{6,7},{7,6},{8,9},{9,8},{10,11... | collective-permute-start | bytes 4276232 | tf_op jit(solution)/shard_map/ppermute | solution.py:414
  43.8 33.8 %collective-permute-start.6 = (bf16[4,48,3712]{2,1,0:T(8,128)(2,1)S(1)}, bf16[4,48,3712]{2,1,0:T(8,128)(2,1)}, u32[]{:S(2)}, u32[]{:S(2)}) collective-permute-start(bf16[4,48,3712]{2,1,0:T(8,128)(2,1)S(1)} %pad_maximum_fusion.refs_0_.refs_13_.refs_5_), channel_id=1, source_target_pairs={{0,4},{1,5},{2,6},{3,7},{4,0},{5,1},{6,2},{7,3},{8,12},{9,13},{10,... | collective-permute-start | bytes 4276232 | tf_op jit(solution)/shard_map/ppermute | solution.py:410
  44.9 32.9 %collective-permute-start.5 = (bf16[4,48,3712]{2,1,0:T(8,128)(2,1)S(1)}, bf16[4,48,3712]{2,1,0:T(8,128)(2,1)}, u32[]{:S(2)}, u32[]{:S(2)}) collective-permute-start(bf16[4,48,3712]{2,1,0:T(8,128)(2,1)S(1)} %pad_maximum_fusion.refs_0_.refs_13_.refs_5_), channel_id=1, source_target_pairs={{0,2},{1,3},{2,0},{3,1},{4,6},{5,7},{6,4},{7,5},{8,10},{9,11},{10,... | collective-permute-start | bytes 4276232 | tf_op jit(solution)/shard_map/ppermute | solution.py:406
  45.5 29.7 %collective-permute-start.8 = (bf16[256,1536]{1,0:T(8,128)(2,1)S(1)}, bf16[256,1536]{1,0:T(8,128)(2,1)S(1)}, u32[]{:S(2)}, u32[]{:S(2)}) collective-permute-start(bf16[256,1536]{1,0:T(8,128)(2,1)S(1)} %slice.128.refs_2_.refs_4_.refs_8_.refs_24_), channel_id=1, source_target_pairs={{0,8},{8,16},{16,24},{24,0},{1,9},{9,17},{17,25},{25,1},{2,10},{10... | collective-permute-start | bytes 2359304 | tf_op jit(solution)/shard_map/ppermute | solution.py:1343
  45.6 29.6 %collective-permute-start.9 = (bf16[128,1536]{1,0:T(8,128)(2,1)S(1)}, bf16[128,1536]{1,0:T(8,128)(2,1)}, u32[]{:S(2)}, u32[]{:S(2)}) collective-permute-start(bf16[128,1536]{1,0:T(8,128)(2,1)S(1)} %slice.129.refs_6_.refs_8_.refs_12_.refs_28_), channel_id=1, source_target_pairs={{0,8},{8,16},{16,24},{24,0},{1,9},{9,17},{17,25},{25,1},{2,10},{10... | collective-permute-start | bytes 1179656 | tf_op jit(solution)/shard_map/ppermute | solution.py:1343
  77.8 25.2 %collective-permute-start.14 = (bf16[512,1536]{1,0:T(8,128)(2,1)}, bf16[512,1536]{1,0:T(8,128)(2,1)S(1)}, u32[]{:S(2)}, u32[]{:S(2)}) collective-permute-start(bf16[512,1536]{1,0:T(8,128)(2,1)} %copy-done.9), channel_id=1, source_target_pairs={{0,1},{1,0},{2,3},{3,2},{4,5},{5,4},{6,7},{7,6},{8,9},{9,8},{10,11... | collective-permute-start | bytes 4718600 | tf_op jit(solution)/shard_map/ppermute | solution.py:414
  79.4 23.6 %collective-permute-start.10 = (bf16[4,48,3712]{2,1,0:T(8,128)(2,1)S(1)}, bf16[4,48,3712]{2,1,0:T(8,128)(2,1)S(1)}, u32[]{:S(2)}, u32[]{:S(2)}) collective-permute-start(bf16[4,48,3712]{2,1,0:T(8,128)(2,1)S(1)} %broadcast_select_fusion.2), channel_id=1, source_target_pairs={{0,2},{1,5},{2,0},{3,7},{4,6},{5,1},{6,4},{7,3},{8,10},{9,13},{10,... | collective-permute-start | bytes 4276232 | tf_op jit(solution)/shard_map/ppermute | solution.py:422
  80.4 22.5 %collective-permute-start.11 = (bf16[4,48,3712]{2,1,0:T(8,128)(2,1)}, bf16[4,48,3712]{2,1,0:T(8,128)(2,1)S(1)}, u32[]{:S(2)}, u32[]{:S(2)}) collective-permute-start(bf16[4,48,3712]{2,1,0:T(8,128)(2,1)} %collective-permute-done.5.refs_2_.refs_15_.refs_7_), channel_id=1, source_target_pairs={{0,1},{1,0},{2,3},{3,2},{4,5},{5,4},{6,7},{7,6},{8,9},{9,8},{10,11... | collective-permute-start | bytes 4276232 | tf_op jit(solution)/shard_map/ppermute | solution.py:414
  81.2 21.8 %collective-permute-start.12 = (bf16[4,48,3712]{2,1,0:T(8,128)(2,1)}, bf16[4,48,3712]{2,1,0:T(8,128)(2,1)S(1)}, u32[]{:S(2)}, u32[]{:S(2)}) collective-permute-start(bf16[4,48,3712]{2,1,0:T(8,128)(2,1)} %collective-permute-done.6.refs_4_.refs_17_.refs_9_), channel_id=1, source_target_pairs={{0,1},{1,0},{2,3},{3,2},{4,5},{5,4},{6,7},{7,6},{8,9},{9,8},{10,11... | collective-permute-start | bytes 4276232 | tf_op jit(solution)/shard_map/ppermute | solution.py:414
  81.2 21.8 %collective-permute-start.13 = (bf16[256,1536]{1,0:T(8,128)(2,1)S(1)}, bf16[256,1536]{1,0:T(8,128)(2,1)S(1)}, u32[]{:S(2)}, u32[]{:S(2)}) collective-permute-start(bf16[256,1536]{1,0:T(8,128)(2,1)S(1)} %collective-permute-done.8.refs_3_.refs_5_.refs_9_.refs_25_), channel_id=1, source_target_pairs={{0,8},{8,16},{16,24},{24,0},{1,9},{9,17},{17,25},{25,1},{2,10},{10... | collective-permute-start | bytes 2359304 | tf_op jit(solution)/shard_map/ppermute | solution.py:1343
  103.1 28.5 %collective-permute-start.17 = (bf16[512,1536]{1,0:T(8,128)(2,1)}, bf16[512,1536]{1,0:T(8,128)(2,1)}, u32[]{:S(2)}, u32[]{:S(2)}) collective-permute-start(bf16[512,1536]{1,0:T(8,128)(2,1)} %refs_10_.1), channel_id=1, source_target_pairs={{0,1},{1,0},{2,3},{3,2},{4,5},{5,4},{6,7},{7,6},{8,9},{9,8},{10,11... | collective-permute-start | bytes 4718600 | tf_op jit(solution)/shard_map/ppermute | solution.py:414
  107.5 24.1 %collective-permute-start.16 = (bf16[512,1536]{1,0:T(8,128)(2,1)}, bf16[512,1536]{1,0:T(8,128)(2,1)}, u32[]{:S(2)}, u32[]{:S(2)}) collective-permute-start(bf16[512,1536]{1,0:T(8,128)(2,1)} %broadcast_select_fusion.1), channel_id=1, source_target_pairs={{0,2},{1,5},{2,0},{3,7},{4,6},{5,1},{6,4},{7,3},{8,10},{9,13},{10,... | collective-permute-start | bytes 4718600 | tf_op jit(solution)/shard_map/ppermute | solution.py:422
  108.1 23.6 %collective-permute-start.18 = (bf16[512,1536]{1,0:T(8,128)(2,1)}, bf16[512,1536]{1,0:T(8,128)(2,1)}, u32[]{:S(2)}, u32[]{:S(2)}) collective-permute-start(bf16[512,1536]{1,0:T(8,128)(2,1)} %collective-permute-done.3.refs_12_.refs_11_), channel_id=1, source_target_pairs={{0,1},{1,0},{2,3},{3,2},{4,5},{5,4},{6,7},{7,6},{8,9},{9,8},{10,11... | collective-permute-start | bytes 4718600 | tf_op jit(solution)/shard_map/ppermute | solution.py:414
  108.6 23.0 %collective-permute-start.19 = (bf16[256,1536]{1,0:T(8,128)(2,1)S(1)}, bf16[256,1536]{1,0:T(8,128)(2,1)S(1)}, u32[]{:S(2)}, u32[]{:S(2)}) collective-permute-start(bf16[256,1536]{1,0:T(8,128)(2,1)S(1)} %collective-permute-done.13.refs_4_.refs_6_.refs_10_.refs_26_), channel_id=1, source_target_pairs={{0,8},{8,16},{16,24},{24,0},{1,9},{9,17},{17,25},{25,1},{2,10},{10... | collective-permute-start | bytes 2359304 | tf_op jit(solution)/shard_map/ppermute | solution.py:1343
  132.6 28.5 %collective-permute-start.22 = (bf16[528,1536]{1,0:T(8,128)(2,1)}, bf16[528,1536]{1,0:T(8,128)(2,1)}, u32[]{:S(2)}, u32[]{:S(2)}) collective-permute-start(bf16[528,1536]{1,0:T(8,128)(2,1)} %get-tuple-element.313.refs_0_), channel_id=1, source_target_pairs={{0,1},{1,0},{2,3},{3,2},{4,5},{5,4},{6,7},{7,6},{8,9},{9,8},{10,11... | collective-permute-start | bytes 4866056 | tf_op jit(solution)/shard_map/ppermute | solution.py:414
  132.7 43.3 %collective-permute-start.21 = (bf16[528,1536]{1,0:T(8,128)(2,1)}, bf16[528,1536]{1,0:T(8,128)(2,1)S(1)}, u32[]{:S(2)}, u32[]{:S(2)}) collective-permute-start(bf16[528,1536]{1,0:T(8,128)(2,1)} %get-tuple-element.313.refs_0_), channel_id=1, source_target_pairs={{0,4},{1,5},{2,6},{3,7},{4,0},{5,1},{6,2},{7,3},{8,12},{9,13},{10,... | collective-permute-start | bytes 4866056 | tf_op jit(solution)/shard_map/ppermute | solution.py:410
  133.9 42.1 %collective-permute-start.20 = (bf16[528,1536]{1,0:T(8,128)(2,1)}, bf16[528,1536]{1,0:T(8,128)(2,1)}, u32[]{:S(2)}, u32[]{:S(2)}) collective-permute-start(bf16[528,1536]{1,0:T(8,128)(2,1)} %get-tuple-element.313.refs_0_), channel_id=1, source_target_pairs={{0,2},{1,3},{2,0},{3,1},{4,6},{5,7},{6,4},{7,5},{8,10},{9,11},{10,... | collective-permute-start | bytes 4866056 | tf_op jit(solution)/shard_map/ppermute | solution.py:406
  134.6 13.0 %collective-permute-start.23 = (bf16[128,1536]{1,0:T(8,128)(2,1)}, bf16[128,1536]{1,0:T(8,128)(2,1)S(1)}, u32[]{:S(2)}, u32[]{:S(2)}) collective-permute-start(bf16[128,1536]{1,0:T(8,128)(2,1)} %collective-permute-done.9.refs_7_.refs_9_.refs_13_.refs_29_), channel_id=1, source_target_pairs={{0,8},{8,16},{16,24},{24,0},{1,9},{9,17},{17,25},{25,1},{2,10},{10... | collective-permute-start | bytes 1179656 | tf_op jit(solution)/shard_map/ppermute | solution.py:1343
  147.6 11.9 %collective-permute-start.24 = (bf16[128,1536]{1,0:T(8,128)(2,1)S(1)}, bf16[128,1536]{1,0:T(8,128)(2,1)S(1)}, u32[]{:S(2)}, u32[]{:S(2)}) collective-permute-start(bf16[128,1536]{1,0:T(8,128)(2,1)S(1)} %collective-permute-done.23.refs_8_.refs_10_.refs_14_.refs_30_), channel_id=1, source_target_pairs={{0,8},{8,16},{16,24},{24,0},{1,9},{9,17},{17,25},{25,1},{2,10},{10... | collective-permute-start | bytes 1179656 | tf_op jit(solution)/shard_map/ppermute | solution.py:1343
  160.3 15.7 %collective-permute-start.25 = (bf16[192,1536]{1,0:T(8,128)(2,1)}, bf16[192,1536]{1,0:T(8,128)(2,1)}, u32[]{:S(2)}, u32[]{:S(2)}) collective-permute-start(bf16[192,1536]{1,0:T(8,128)(2,1)} %convert_bitcast_fusion.1.refs_2_.refs_16_.refs_32_.refs_6_), channel_id=1, source_target_pairs={{0,8},{8,16},{16,24},{24,0},{1,9},{9,17},{17,25},{25,1},{2,10},{10... | collective-permute-start | bytes 1769480 | tf_op jit(solution)/shard_map/ppermute | solution.py:1343
  177.9 23.0 %collective-permute-start.26 = (bf16[528,1536]{1,0:T(8,128)(2,1)}, bf16[528,1536]{1,0:T(8,128)(2,1)}, u32[]{:S(2)}, u32[]{:S(2)}) collective-permute-start(bf16[528,1536]{1,0:T(8,128)(2,1)} %broadcast_select_fusion), channel_id=1, source_target_pairs={{0,2},{1,5},{2,0},{3,7},{4,6},{5,1},{6,4},{7,3},{8,10},{9,13},{10,... | collective-permute-start | bytes 4866056 | tf_op jit(solution)/shard_map/ppermute | solution.py:422
  178.6 22.3 %collective-permute-start.27 = (bf16[192,1536]{1,0:T(8,128)(2,1)}, bf16[192,1536]{1,0:T(8,128)(2,1)}, u32[]{:S(2)}, u32[]{:S(2)}) collective-permute-start(bf16[192,1536]{1,0:T(8,128)(2,1)} %collective-permute-done.25.refs_3_.refs_17_.refs_33_.refs_7_), channel_id=1, source_target_pairs={{0,8},{8,16},{16,24},{24,0},{1,9},{9,17},{17,25},{25,1},{2,10},{10... | collective-permute-start | bytes 1769480 | tf_op jit(solution)/shard_map/ppermute | solution.py:1343
  201.1 18.2 %collective-permute-start.31 = (bf16[512,1536]{1,0:T(8,128)(2,1)}, bf16[512,1536]{1,0:T(8,128)(2,1)}, u32[]{:S(2)}, u32[]{:S(2)}) collective-permute-start(bf16[512,1536]{1,0:T(8,128)(2,1)} %collective-permute-done.16.refs_14_.refs_3_), channel_id=1, source_target_pairs={{0,1},{1,0},{2,3},{3,2},{4,5},{5,4},{6,7},{7,6},{8,9},{9,8},{10,11... | collective-permute-start | bytes 4718600 | tf_op jit(solution)/shard_map/ppermute | solution.py:414
  205.7 29.4 %collective-permute-start.32 = (bf16[192,1536]{1,0:T(8,128)(2,1)}, bf16[192,1536]{1,0:T(8,128)(2,1)}, u32[]{:S(2)}, u32[]{:S(2)}) collective-permute-start(bf16[192,1536]{1,0:T(8,128)(2,1)} %collective-permute-done.27.refs_4_.refs_18_.refs_34_.refs_8_), channel_id=1, source_target_pairs={{0,8},{8,16},{16,24},{24,0},{1,9},{9,17},{17,25},{25,1},{2,10},{10... | collective-permute-start | bytes 1769480 | tf_op jit(solution)/shard_map/ppermute | solution.py:1343
  243.8 18.3 %collective-permute-start.34 = (bf16[512,1536]{1,0:T(8,128)(2,1)}, bf16[512,1536]{1,0:T(8,128)(2,1)S(1)}, u32[]{:S(2)}, u32[]{:S(2)}) collective-permute-start(bf16[512,1536]{1,0:T(8,128)(2,1)} %get-tuple-element.357), channel_id=1, source_target_pairs={{0,1},{1,0},{2,3},{3,2},{4,5},{5,4},{6,7},{7,6},{8,9},{9,8},{10,11... | collective-permute-start | bytes 4718600 | tf_op jit(solution)/shard_map/ppermute | solution.py:414
  244.0 18.1 %collective-permute-start.33 = (bf16[192,1536]{1,0:T(8,128)(2,1)}, bf16[192,1536]{1,0:T(8,128)(2,1)}, u32[]{:S(2)}, u32[]{:S(2)}) collective-permute-start(bf16[192,1536]{1,0:T(8,128)(2,1)} %constant_dynamic-slice_fusion.2), channel_id=1, source_target_pairs={{0,8},{8,16},{16,24},{24,0},{1,9},{9,17},{17,25},{25,1},{2,10},{10... | collective-permute-start | bytes 1769480 | tf_op jit(solution)/shard_map/ppermute | solution.py:1343
  268.5 38.2 %collective-permute-start.36 = (bf16[528,1536]{1,0:T(8,128)(2,1)S(1)}, bf16[528,1536]{1,0:T(8,128)(2,1)}, u32[]{:S(2)}, u32[]{:S(2)}) collective-permute-start(bf16[528,1536]{1,0:T(8,128)(2,1)S(1)} %add_convert_fusion.4), channel_id=1, source_target_pairs={{0,2},{1,5},{2,0},{3,7},{4,6},{5,1},{6,4},{7,3},{8,10},{9,13},{10,... | collective-permute-start | bytes 4866056 | tf_op jit(solution)/shard_map/ppermute | solution.py:422
  269.3 37.3 %collective-permute-start.37 = (bf16[192,1536]{1,0:T(8,128)(2,1)}, bf16[192,1536]{1,0:T(8,128)(2,1)}, u32[]{:S(2)}, u32[]{:S(2)}) collective-permute-start(bf16[192,1536]{1,0:T(8,128)(2,1)} %add_convert_fusion.14), channel_id=1, source_target_pairs={{0,8},{8,16},{16,24},{24,0},{1,9},{9,17},{17,25},{25,1},{2,10},{10... | collective-permute-start | bytes 1769480 | tf_op jit(solution)/shard_map/ppermute | solution.py:1343
  306.7 16.2 %collective-permute-start.38 = (bf16[528,1536]{1,0:T(8,128)(2,1)}, bf16[528,1536]{1,0:T(8,128)(2,1)}, u32[]{:S(2)}, u32[]{:S(2)}) collective-permute-start(bf16[528,1536]{1,0:T(8,128)(2,1)} %get-tuple-element.396), channel_id=1, source_target_pairs={{0,1},{1,0},{2,3},{3,2},{4,5},{5,4},{6,7},{7,6},{8,9},{9,8},{10,11... | collective-permute-start | bytes 4866056 | tf_op jit(solution)/shard_map/ppermute | solution.py:414
  306.7 16.2 %collective-permute-start.39 = (bf16[528,1536]{1,0:T(8,128)(2,1)}, bf16[528,1536]{1,0:T(8,128)(2,1)}, u32[]{:S(2)}, u32[]{:S(2)}) collective-permute-start(bf16[528,1536]{1,0:T(8,128)(2,1)} %get-tuple-element.397), channel_id=1, source_target_pairs={{0,1},{1,0},{2,3},{3,2},{4,5},{5,4},{6,7},{7,6},{8,9},{9,8},{10,11... | collective-permute-start | bytes 4866056 | tf_op jit(solution)/shard_map/ppermute | solution.py:414
  307.2 15.7 %collective-permute-start.40 = (bf16[528,1536]{1,0:T(8,128)(2,1)}, bf16[528,1536]{1,0:T(8,128)(2,1)S(1)}, u32[]{:S(2)}, u32[]{:S(2)}) collective-permute-start(bf16[528,1536]{1,0:T(8,128)(2,1)} %get-tuple-element.398), channel_id=1, source_target_pairs={{0,1},{1,0},{2,3},{3,2},{4,5},{5,4},{6,7},{7,6},{8,9},{9,8},{10,11... | collective-permute-start | bytes 4866056 | tf_op jit(solution)/shard_map/ppermute | solution.py:414
  307.3 22.3 %collective-permute-start.41 = (bf16[512,1536]{1,0:T(8,128)(2,1)}, bf16[512,1536]{1,0:T(8,128)(2,1)}, u32[]{:S(2)}, u32[]{:S(2)}) collective-permute-start(bf16[512,1536]{1,0:T(8,128)(2,1)} %add_convert_fusion.8), channel_id=1, source_target_pairs={{0,2},{1,5},{2,0},{3,7},{4,6},{5,1},{6,4},{7,3},{8,10},{9,13},{10,... | collective-permute-start | bytes 4718600 | tf_op jit(solution)/shard_map/ppermute | solution.py:422
  329.6 35.8 %collective-permute-start.45 = (bf16[512,1536]{1,0:T(8,128)(2,1)}, bf16[512,1536]{1,0:T(8,128)(2,1)}, u32[]{:S(2)}, u32[]{:S(2)}) collective-permute-start(bf16[512,1536]{1,0:T(8,128)(2,1)} %get-tuple-element.434), channel_id=1, source_target_pairs={{0,1},{1,0},{2,3},{3,2},{4,5},{5,4},{6,7},{7,6},{8,9},{9,8},{10,11... | collective-permute-start | bytes 4718600 | tf_op jit(solution)/shard_map/ppermute | solution.py:414
  329.9 35.5 %collective-permute-start.46 = (bf16[512,1536]{1,0:T(8,128)(2,1)}, bf16[512,1536]{1,0:T(8,128)(2,1)}, u32[]{:S(2)}, u32[]{:S(2)}) collective-permute-start(bf16[512,1536]{1,0:T(8,128)(2,1)} %get-tuple-element.437), channel_id=1, source_target_pairs={{0,1},{1,0},{2,3},{3,2},{4,5},{5,4},{6,7},{7,6},{8,9},{9,8},{10,11... | collective-permute-start | bytes 4718600 | tf_op jit(solution)/shard_map/ppermute | solution.py:414
  330.2 41.0 %collective-permute-start.42 = (bf16[528,1536]{1,0:T(8,128)(2,1)}, bf16[528,1536]{1,0:T(8,128)(2,1)S(1)}, u32[]{:S(2)}, u32[]{:S(2)}) collective-permute-start(bf16[528,1536]{1,0:T(8,128)(2,1)} %get-tuple-element.420), channel_id=1, source_target_pairs={{0,2},{1,3},{2,0},{3,1},{4,6},{5,7},{6,4},{7,5},{8,10},{9,11},{10,... | collective-permute-start | bytes 4866056 | tf_op jit(solution)/shard_map/ppermute | solution.py:406
  332.0 39.3 %collective-permute-start.43 = (bf16[528,1536]{1,0:T(8,128)(2,1)}, bf16[528,1536]{1,0:T(8,128)(2,1)}, u32[]{:S(2)}, u32[]{:S(2)}) collective-permute-start(bf16[528,1536]{1,0:T(8,128)(2,1)} %get-tuple-element.421), channel_id=1, source_target_pairs={{0,4},{1,5},{2,6},{3,7},{4,0},{5,1},{6,2},{7,3},{8,12},{9,13},{10,... | collective-permute-start | bytes 4866056 | tf_op jit(solution)/shard_map/ppermute | solution.py:410
  333.0 38.3 %collective-permute-start.44 = (bf16[192,1536]{1,0:T(8,128)(2,1)}, bf16[192,1536]{1,0:T(8,128)(2,1)}, u32[]{:S(2)}, u32[]{:S(2)}) collective-permute-start(bf16[192,1536]{1,0:T(8,128)(2,1)} %add_convert_fusion.13), channel_id=1, source_target_pairs={{0,8},{8,16},{16,24},{24,0},{1,9},{9,17},{17,25},{25,1},{2,10},{10... | collective-permute-start | bytes 1769480 | tf_op jit(solution)/shard_map/ppermute | solution.py:1343
  371.3 40.2 %collective-permute-start.47 = (bf16[512,1536]{1,0:T(8,128)(2,1)}, bf16[512,1536]{1,0:T(8,128)(2,1)}, u32[]{:S(2)}, u32[]{:S(2)}) collective-permute-start(bf16[512,1536]{1,0:T(8,128)(2,1)} %get-tuple-element.453), channel_id=1, source_target_pairs={{0,1},{1,0},{2,3},{3,2},{4,5},{5,4},{6,7},{7,6},{8,9},{9,8},{10,11... | collective-permute-start | bytes 4718600 | tf_op jit(solution)/shard_map/ppermute | solution.py:414
  371.3 41.4 %collective-permute-start.51 = (bf16[512,1536]{1,0:T(8,128)(2,1)}, bf16[512,1536]{1,0:T(8,128)(2,1)}, u32[]{:S(2)}, u32[]{:S(2)}) collective-permute-start(bf16[512,1536]{1,0:T(8,128)(2,1)} %get-tuple-element.459), channel_id=1, source_target_pairs={{0,4},{1,5},{2,6},{3,7},{4,0},{5,1},{6,2},{7,3},{8,12},{9,13},{10,... | collective-permute-start | bytes 4718600 | tf_op jit(solution)/shard_map/ppermute | solution.py:410
  371.8 40.9 %collective-permute-start.50 = (bf16[512,1536]{1,0:T(8,128)(2,1)}, bf16[512,1536]{1,0:T(8,128)(2,1)}, u32[]{:S(2)}, u32[]{:S(2)}) collective-permute-start(bf16[512,1536]{1,0:T(8,128)(2,1)} %get-tuple-element.441), channel_id=1, source_target_pairs={{0,2},{1,3},{2,0},{3,1},{4,6},{5,7},{6,4},{7,5},{8,10},{9,11},{10,... | collective-permute-start | bytes 4718600 | tf_op jit(solution)/shard_map/ppermute | solution.py:406
  373.1 38.3 %collective-permute-start.48 = (bf16[240,1536]{1,0:T(8,128)(2,1)}, bf16[240,1536]{1,0:T(8,128)(2,1)}, u32[]{:S(2)}, u32[]{:S(2)}) collective-permute-start(bf16[240,1536]{1,0:T(8,128)(2,1)} %constant_dynamic-slice_fusion), channel_id=1, source_target_pairs={{0,8},{8,16},{16,24},{24,0},{1,9},{9,17},{17,25},{25,1},{2,10},{10... | collective-permute-start | bytes 2211848 | tf_op jit(solution)/shard_map/ppermute | solution.py:1343
  373.4 38.0 %collective-permute-start.49 = (bf16[144,1536]{1,0:T(8,128)(2,1)}, bf16[144,1536]{1,0:T(8,128)(2,1)}, u32[]{:S(2)}, u32[]{:S(2)}) collective-permute-start(bf16[144,1536]{1,0:T(8,128)(2,1)} %constant_dynamic-slice_fusion.1), channel_id=1, source_target_pairs={{0,8},{8,16},{16,24},{24,0},{1,9},{9,17},{17,25},{25,1},{2,10},{10... | collective-permute-start | bytes 1327112 | tf_op jit(solution)/shard_map/ppermute | solution.py:1343
  412.7 14.5 %collective-permute-start.52 = (bf16[4,4,48,2048]{3,2,1,0:T(8,128)(2,1)}, bf16[4,4,48,2048]{3,2,1,0:T(8,128)(2,1)}, u32[]{:S(2)}, u32[]{:S(2)}) collective-permute-start(bf16[4,4,48,2048]{3,2,1,0:T(8,128)(2,1)} %get-tuple-element.460), channel_id=1, source_target_pairs={{0,1},{1,0},{2,3},{3,2},{4,5},{5,4},{6,7},{7,6},{8,9},{9,8},{10,11... | collective-permute-start | bytes 9437192 | tf_op jit(solution)/shard_map/ppermute | solution.py:414
  412.8 14.4 %collective-permute-start.53 = (bf16[144,1536]{1,0:T(8,128)(2,1)S(1)}, bf16[144,1536]{1,0:T(8,128)(2,1)S(1)}, u32[]{:S(2)}, u32[]{:S(2)}) collective-permute-start(bf16[144,1536]{1,0:T(8,128)(2,1)S(1)} %add_convert_fusion.16), channel_id=1, source_target_pairs={{0,8},{8,16},{16,24},{24,0},{1,9},{9,17},{17,25},{25,1},{2,10},{10... | collective-permute-start | bytes 1327112 | tf_op jit(solution)/shard_map/ppermute | solution.py:1343
  429.0 24.7 %collective-permute-start.55 = (bf16[4,4,48,1664]{3,2,1,0:T(8,128)(2,1)}, bf16[4,4,48,1664]{3,2,1,0:T(8,128)(2,1)}, u32[]{:S(2)}, u32[]{:S(2)}) collective-permute-start(bf16[4,4,48,1664]{3,2,1,0:T(8,128)(2,1)} %get-tuple-element.472), channel_id=1, source_target_pairs={{0,1},{1,0},{2,3},{3,2},{4,5},{5,4},{6,7},{7,6},{8,9},{9,8},{10,11... | collective-permute-start | bytes 7667720 | tf_op jit(solution)/shard_map/ppermute | solution.py:414
  432.6 21.1 %collective-permute-start.56 = (bf16[240,1536]{1,0:T(8,128)(2,1)}, bf16[240,1536]{1,0:T(8,128)(2,1)}, u32[]{:S(2)}, u32[]{:S(2)}) collective-permute-start(bf16[240,1536]{1,0:T(8,128)(2,1)} %add_convert_fusion.11), channel_id=1, source_target_pairs={{0,8},{8,16},{16,24},{24,0},{1,9},{9,17},{17,25},{25,1},{2,10},{10... | collective-permute-start | bytes 2211848 | tf_op jit(solution)/shard_map/ppermute | solution.py:1343
  432.7 21.0 %collective-permute-start.54 = (bf16[4,48,2048]{2,1,0:T(8,128)(2,1)S(1)}, bf16[4,48,2048]{2,1,0:T(8,128)(2,1)}, u32[]{:S(2)}, u32[]{:S(2)}) collective-permute-start(bf16[4,48,2048]{2,1,0:T(8,128)(2,1)S(1)} %fusion.12), channel_id=1, source_target_pairs={{0,2},{1,5},{2,0},{3,7},{4,6},{5,1},{6,4},{7,3},{8,10},{9,13},{10,... | collective-permute-start | bytes 2359304 | tf_op jit(solution)/shard_map/ppermute | solution.py:422
  453.7 16.8 %collective-permute-start.61 = (bf16[144,1536]{1,0:T(8,128)(2,1)S(1)}, bf16[144,1536]{1,0:T(8,128)(2,1)S(1)}, u32[]{:S(2)}, u32[]{:S(2)}) collective-permute-start(bf16[144,1536]{1,0:T(8,128)(2,1)S(1)} %copy-done.41), channel_id=1, source_target_pairs={{0,8},{8,16},{16,24},{24,0},{1,9},{9,17},{17,25},{25,1},{2,10},{10... | collective-permute-start | bytes 1327112 | tf_op jit(solution)/shard_map/ppermute | solution.py:1343
  458.5 17.3 %collective-permute-start.59 = (bf16[4,48,1664]{2,1,0:T(8,128)(2,1)S(1)}, bf16[4,48,1664]{2,1,0:T(8,128)(2,1)S(1)}, u32[]{:S(2)}, u32[]{:S(2)}) collective-permute-start(bf16[4,48,1664]{2,1,0:T(8,128)(2,1)S(1)} %fusion.13), channel_id=1, source_target_pairs={{0,2},{1,5},{2,0},{3,7},{4,6},{5,1},{6,4},{7,3},{8,10},{9,13},{10,... | collective-permute-start | bytes 1916936 | tf_op jit(solution)/shard_map/ppermute | solution.py:422
  459.2 23.9 %collective-permute-start.60 = (bf16[240,1536]{1,0:T(8,128)(2,1)S(1)}, bf16[240,1536]{1,0:T(8,128)(2,1)S(1)}, u32[]{:S(2)}, u32[]{:S(2)}) collective-permute-start(bf16[240,1536]{1,0:T(8,128)(2,1)S(1)} %add_convert_fusion.10), channel_id=1, source_target_pairs={{0,8},{8,16},{16,24},{24,0},{1,9},{9,17},{17,25},{25,1},{2,10},{10... | collective-permute-start | bytes 2211848 | tf_op jit(solution)/shard_map/ppermute | solution.py:1343
  459.4 25.8 %collective-permute-start.57 = (bf16[4,48,2048]{2,1,0:T(8,128)(2,1)S(1)}, bf16[4,48,2048]{2,1,0:T(8,128)(2,1)S(1)}, u32[]{:S(2)}, u32[]{:S(2)}) collective-permute-start(bf16[4,48,2048]{2,1,0:T(8,128)(2,1)S(1)} %get-tuple-element.489), channel_id=1, source_target_pairs={{0,2},{1,3},{2,0},{3,1},{4,6},{5,7},{6,4},{7,5},{8,10},{9,11},{10,... | collective-permute-start | bytes 2359304 | tf_op jit(solution)/shard_map/ppermute | solution.py:406
  460.9 24.3 %collective-permute-start.58 = (bf16[4,48,2048]{2,1,0:T(8,128)(2,1)S(1)}, bf16[4,48,2048]{2,1,0:T(8,128)(2,1)S(1)}, u32[]{:S(2)}, u32[]{:S(2)}) collective-permute-start(bf16[4,48,2048]{2,1,0:T(8,128)(2,1)S(1)} %get-tuple-element.490), channel_id=1, source_target_pairs={{0,4},{1,5},{2,6},{3,7},{4,0},{5,1},{6,2},{7,3},{8,12},{9,13},{10,... | collective-permute-start | bytes 2359304 | tf_op jit(solution)/shard_map/ppermute | solution.py:410
  487.0 23.6 %collective-permute-start.65 = (bf16[4,48,1664]{2,1,0:T(8,128)(2,1)}, bf16[4,48,1664]{2,1,0:T(8,128)(2,1)S(1)}, u32[]{:S(2)}, u32[]{:S(2)}) collective-permute-start(bf16[4,48,1664]{2,1,0:T(8,128)(2,1)} %get-tuple-element.500), channel_id=1, source_target_pairs={{0,2},{1,3},{2,0},{3,1},{4,6},{5,7},{6,4},{7,5},{8,10},{9,11},{10,... | collective-permute-start | bytes 1916936 | tf_op jit(solution)/shard_map/ppermute | solution.py:406
  488.3 22.2 %collective-permute-start.66 = (bf16[4,48,1664]{2,1,0:T(8,128)(2,1)}, bf16[4,48,1664]{2,1,0:T(8,128)(2,1)S(1)}, u32[]{:S(2)}, u32[]{:S(2)}) collective-permute-start(bf16[4,48,1664]{2,1,0:T(8,128)(2,1)} %get-tuple-element.501), channel_id=1, source_target_pairs={{0,4},{1,5},{2,6},{3,7},{4,0},{5,1},{6,2},{7,3},{8,12},{9,13},{10,... | collective-permute-start | bytes 1916936 | tf_op jit(solution)/shard_map/ppermute | solution.py:410
  489.9 10.0 %collective-permute-start.64 = (bf16[48,2048]{1,0:T(8,128)(2,1)}, bf16[48,2048]{1,0:T(8,128)(2,1)}, u32[]{:S(2)}, u32[]{:S(2)}) collective-permute-start(bf16[48,2048]{1,0:T(8,128)(2,1)} %get-tuple-element.648), channel_id=1, source_target_pairs={{0,8},{8,16},{16,24},{24,0},{1,9},{9,17},{17,25},{25,1},{2,10},{10... | collective-permute-start | bytes 589832 | tf_op jit(solution)/shard_map/ppermute | solution.py:1570
  490.5 20.1 %collective-permute-start.62 = (bf16[48,2048]{1,0:T(8,128)(2,1)}, bf16[48,2048]{1,0:T(8,128)(2,1)}, u32[]{:S(2)}, u32[]{:S(2)}) collective-permute-start(bf16[48,2048]{1,0:T(8,128)(2,1)} %get-tuple-element.650), channel_id=1, source_target_pairs={{0,24},{8,0},{16,8},{24,16},{1,25},{9,1},{17,9},{25,17},{2,26},{10... | collective-permute-start | bytes 589832 | tf_op jit(solution)/shard_map/ppermute | solution.py:1570
  498.5 12.0 %collective-permute-start.63 = (bf16[48,2048]{1,0:T(8,128)(2,1)}, bf16[48,2048]{1,0:T(8,128)(2,1)}, u32[]{:S(2)}, u32[]{:S(2)}) collective-permute-start(bf16[48,2048]{1,0:T(8,128)(2,1)} %get-tuple-element.649), channel_id=1, source_target_pairs={{0,16},{8,24},{16,0},{24,8},{1,17},{9,25},{17,1},{25,9},{2,18},{10... | collective-permute-start | bytes 589832 | tf_op jit(solution)/shard_map/ppermute | solution.py:1570
  510.9 9.9 %collective-permute-start.67 = (bf16[48,1664]{1,0:T(8,128)(2,1)S(1)}, bf16[48,1664]{1,0:T(8,128)(2,1)S(1)}, u32[]{:S(2)}, u32[]{:S(2)}) collective-permute-start(bf16[48,1664]{1,0:T(8,128)(2,1)S(1)} %get-tuple-element.652), channel_id=1, source_target_pairs={{0,24},{8,0},{16,8},{24,16},{1,25},{9,1},{17,9},{25,17},{2,26},{10... | collective-permute-start | bytes 479240 | tf_op jit(solution)/shard_map/ppermute | solution.py:1570
  513.0 13.0 %collective-permute-start.68 = (bf16[48,1664]{1,0:T(8,128)(2,1)S(1)}, bf16[48,1664]{1,0:T(8,128)(2,1)S(1)}, u32[]{:S(2)}, u32[]{:S(2)}) collective-permute-start(bf16[48,1664]{1,0:T(8,128)(2,1)S(1)} %get-tuple-element.654), channel_id=1, source_target_pairs={{0,16},{8,24},{16,0},{24,8},{1,17},{9,25},{17,1},{25,9},{2,18},{10... | collective-permute-start | bytes 479240 | tf_op jit(solution)/shard_map/ppermute | solution.py:1570
  (66 other events, 572.7 us)
